TPU v7x, 128 devices: a whole 4x4x4 slice. The times are simulated.
128 devices in a mesh: dp: 8 (over y, core), expert: 16 (over z, x).
Axes of the slice: x: 4, y: 4, z: 4, core: 2. Of those that a mesh axis runs over, the one named last changes fastest.
Arguments:
- tokens: bfloat16 [16384, 4096], P(('dp', 'expert')), may hold values from -6 to 6
- expert_ids: int32 [16384, 4], P(('dp', 'expert')), may hold values from 0 to 15, as said below
- gate_values: float32 [16384, 4], P(('dp', 'expert')), may hold values from 0.1 to 1
- gate_weight: bfloat16 [16, 4096, 768], P('expert'), may hold values from -0.09375 to 0.09375
- up_weight: bfloat16 [16, 4096, 768], P('expert'), may hold values from -0.09375 to 0.09375
- down_weight: bfloat16 [16, 768, 4096], P('expert'), may hold values from -0.21875 to 0.21875
Outputs:
- mixed: bfloat16 [16384, 4096], P(('dp', 'expert'))
Inputs may be any that keep to these rules, and one draw needn't show every extreme that they name: `expert_ids`: each token names 4 different experts; at most 64 tokens of one device name one expert, and on every device exactly one expert is named by 64 of its tokens, the same expert for all devices of one index of dp.
All inputs are finite; a program needn't handle non-finite values.
Results may differ from a plain program's by a relative error of at most 0.0058.
Values may be sent and summed in bfloat16 or wider, within the bound.
No kernel may reach another device: no remote copies, remote signals or barrier semaphores. Data moves between devices by JAX's collectives and lax.ppermute only.
A program may use at most 128 MiB of HBM per device.

v0:
```python
import jax
import jax.numpy as jnp
from jax import lax
from jax.sharding import PartitionSpec as P

BLOCK = 128
OFFLOAD = 4


def from_partner(shard, axis, stride):
    return lax.ppermute(shard, axis, [(i, i ^ 1 << stride) for i in range(lax.axis_size(axis))])


def run_blocks(dense, blocks, w_gate, w_up, w_down):

    def step(index, done):
        part = lax.dynamic_slice_in_dim(dense, index * BLOCK, BLOCK, 0)
        gate_part = jnp.dot(part, w_gate, preferred_element_type=jnp.float32)
        up_part = jnp.dot(part, w_up, preferred_element_type=jnp.float32)
        hidden = (jax.nn.silu(gate_part) * up_part).astype(jnp.bfloat16)
        result = jnp.dot(hidden, w_down, preferred_element_type=jnp.float32).astype(jnp.bfloat16)
        return lax.dynamic_update_slice_in_dim(done, result, index * BLOCK, 0)

    return lax.fori_loop(0, blocks, step, jnp.zeros_like(dense))


def pack_rows(rows_in, valid_in):
    groups, width, depth = rows_in.shape
    total_rows = groups * width
    flattened = rows_in.reshape(total_rows, depth)
    valid_flat = valid_in.reshape(total_rows)
    packed_at = jnp.cumsum(valid_flat) - 1
    live_rows = jnp.sum(valid_flat)
    padded_rows = (-(-total_rows // BLOCK) + OFFLOAD) * BLOCK
    target = jnp.where(valid_flat == 1, packed_at, padded_rows)
    dense = jnp.zeros((padded_rows, depth), jnp.bfloat16).at[target].set(flattened, mode="drop")
    blocks = (live_rows + BLOCK - 1) // BLOCK
    return (dense, blocks, packed_at, valid_flat)


def unpack_rows(done, packed_at, valid_flat, shape_out):
    source = jnp.where(valid_flat == 1, packed_at, 0)
    picked = done[source]
    picked = jnp.where(valid_flat[:, None] == 1, picked, jnp.zeros((), jnp.bfloat16))
    return picked.reshape(shape_out)


def local(tokens, expert_ids, gate_values, gate_weight, up_weight, down_weight):
    experts_here = lax.axis_size("expert")
    tokens_here, chosen = expert_ids.shape
    depth = tokens.shape[1]
    capacity = 2 * tokens_here * chosen // experts_here
    w_gate = gate_weight[0]
    w_up = up_weight[0]
    w_down = down_weight[0]
    flat_ids = expert_ids.reshape(-1)
    onehot = (flat_ids[:, None] == jnp.arange(experts_here)[None, :]).astype(jnp.int32)
    order_in = jnp.sum(jnp.cumsum(onehot, axis=0) * onehot, axis=1) - 1
    slot_index = flat_ids * capacity + order_in
    source_rows = tokens[jnp.arange(tokens_here * chosen) // chosen]
    sending = (
        jnp.zeros((experts_here * capacity, depth), jnp.bfloat16).at[slot_index].set(source_rows)
    )
    sending = sending.reshape(experts_here, capacity, depth)
    valid = (
        jnp.zeros((experts_here * capacity,), jnp.int32)
        .at[slot_index]
        .set(1)
        .reshape(experts_here, capacity)
    )
    rows_in = lax.all_to_all(sending, "expert", split_axis=0, concat_axis=0, tiled=True)
    valid_in = lax.all_to_all(valid, "expert", split_axis=0, concat_axis=0, tiled=True)
    dense, blocks, packed_at, valid_flat = pack_rows(rows_in, valid_in)
    theirs = from_partner(blocks.reshape(1), "dp", 0)[0]
    sent_blocks = jnp.clip((blocks - theirs) // 2, 0, OFFLOAD)
    taken_blocks = jnp.clip((theirs - blocks) // 2, 0, OFFLOAD)
    start = (blocks - sent_blocks) * BLOCK
    outgoing = lax.dynamic_slice_in_dim(dense, start, OFFLOAD * BLOCK, 0)
    incoming = from_partner(outgoing, "dp", 0)
    local_done = run_blocks(dense, blocks - sent_blocks, w_gate, w_up, w_down)
    helped = run_blocks(incoming, taken_blocks, w_gate, w_up, w_down)
    returned = from_partner(helped, "dp", 0)
    done = lax.dynamic_update_slice_in_dim(local_done, returned, start, 0)
    results = unpack_rows(done, packed_at, valid_flat, rows_in.shape)
    back = lax.all_to_all(results, "expert", split_axis=0, concat_axis=0, tiled=True)
    back = back.reshape(experts_here * capacity, depth)
    picked_rows = back[slot_index].reshape(tokens_here, chosen, depth)
    mixed = jnp.zeros((tokens_here, depth), jnp.float32)
    for column in range(chosen):
        mixed = mixed + gate_values[:, column : column + 1] * picked_rows[:, column].astype(
            jnp.float32
        )
    return mixed.astype(jnp.bfloat16)


def solution(mesh):
    in_specs = (
        P(("dp", "expert"), None),
        P(("dp", "expert"), None),
        P(("dp", "expert"), None),
        P("expert", None, None),
        P("expert", None, None),
        P("expert", None, None),
    )
    out_specs = P(("dp", "expert"), None)
    return jax.shard_map(local, mesh=mesh, in_specs=in_specs, out_specs=out_specs, check_vma=False)
```

profile of v0, /device:TPU:9, one launch (start us, length us, event | category | flops | bytes accessed | tf_op | source)
XLA Modules:
  0.0 513.2 jit_solution(2569304148710022123)
XLA Ops:
  3.6 2.4 scatter_custom_fusion
  6.7 7.6 %all-to-all-start = ((s32[16,1,64]{2,1,0:T(1,128)}), s32[16,1,64]{2,1,0:T(1,128)S(1)}, u32[]{:S(2)}, u32[]{:S(2)}) async-start(s32[16,1,64]{2,1,0:T(1,128)} %all_to_all.12), calls=%async_computation | async-start | bytes 16384 | tf_op jit(solution)/shard_map/all_to_all | solution.py:72
  14.3 4.4 gather_fusion
  18.7 12.6 %scatter_custom_fusion.1 = bf16[1024,4096]{1,0:T(8,128)(2,1)} fusion(s32[512]{0:T(512)S(1)} %bitcast.91, bf16[512,4096]{1,0:T(8,128)(2,1)} %gather_fusion, bf16[]{:T(256)} %constant.93.clone.1), kind=kCustom, calls=%fused_computation.41 | custom fusion | bytes 8389120 | tf_op jit(solution)/shard_map/scatter | solution.py:62
  31.3 6.7 %all-to-all-start.1 = ((bf16[16,64,4096]{2,1,0:T(8,128)(2,1)}), bf16[16,64,4096]{2,1,0:T(8,128)(2,1)}, u32[]{:S(2)}, u32[]{:S(2)}) async-start(bf16[16,64,4096]{2,1,0:T(8,128)(2,1)} %bitcast.85), calls=%async_computation.1 | async-start | bytes 16777216 | tf_op jit(solution)/shard_map/all_to_all | solution.py:71
  38.5 1.3 fusion.47
  40.5 2.5 collective-permute-start
  44.5 115.2 %all-to-all-done.1 = bf16[16,64,4096]{2,1,0:T(8,128)(2,1)} async-done(((bf16[16,64,4096]{2,1,0:T(8,128)(2,1)}), bf16[16,64,4096]{2,1,0:T(8,128)(2,1)}, u32[]{:S(2)}, u32[]{:S(2)}) %all-to-all-start.1) | async-done | bytes 8388640 | tf_op jit(solution)/shard_map/all_to_all | solution.py:71
  159.6 20.1 %scatter_custom_fusion.2 = bf16[1536,4096]{1,0:T(8,128)(2,1)} fusion(s32[1024]{0:T(1024)S(1)} %bitcast.95, bf16[1024,4096]{1,0:T(8,128)(2,1)} %bitcast.12, bf16[]{:T(256)} %constant.93.clone.1), kind=kCustom, calls=%fused_computation.39 | custom fusion | bytes 12583424 | tf_op jit(solution)/shard_map/scatter | solution.py:36
  179.7 4.6 constant_dynamic-slice_fusion
  184.3 2.4 collective-permute-start.1
  187.4 6.5 %collective-permute-done.1 = bf16[512,4096]{1,0:T(8,128)(2,1)} collective-permute-done((bf16[512,4096]{1,0:T(8,128)(2,1)}, bf16[512,4096]{1,0:T(8,128)(2,1)}, u32[]{:S(2)}, u32[]{:S(2)}) %collective-permute-start.1) | collective-permute-done | bytes 4194336 | tf_op jit(solution)/shard_map/ppermute | solution.py:11
  193.8 2.5 broadcast_in_dim.33
  196.7 6.1 %broadcast.225 = bf16[1536,4096]{1,0:T(8,128)(2,1)} broadcast(bf16[]{:T(256)} %constant.93.clone.1), dimensions={} | broadcast | bytes 12582914 | tf_op jit(solution)/shard_map/broadcast.10
  202.7 50.3 %while.20 = (s32[]{:T(128)}, bf16[1536,4096]{1,0:T(8,128)(2,1)}, s32[]{:T(128)}, bf16[1536,4096]{1,0:T(8,128)(2,1)}, bf16[4096,768]{1,0:T(8,128)(2,1)}, /*index=...) while((s32[]{:T(128)}, bf16[1536,4096]{1,0:T(8,128)(2,1)}, ...), condition=%wide.region_10.11_spmd, body=%wide.region_9.10_spmd.sunk | while | flops 2417033216 | bytes 22807720 | solution.py:24
  202.7 4.1 fusion.75
  206.8 8.4 %fusion.76 = bf16[1536,4096]{1,0:T(8,128)(2,1)} fusion(bf16[1536,4096]{1,0:T(8,128)(2,1)} %get-tuple-element.223, s32[]{:T(128)S(6)} %select_n.127, bf16[768,4096]{1,0:T(8,128)(2,1)} %get-tuple-element.239, bf16[4096,768]{1,0:T(8,128)(2,1)} %get-tuple-element.238, bf16[1536,4096]{1,0:T(8,128)(2,1)} %get-tuple-element.236, f32[128,768]{1,0:T(8,128)S(1)} %fusion.75), kind=kOutput, calls=%fused_computation.7.clone.1 | convolution fusion | flops 1611726848 | bytes 15074304 | tf_op jit(solution)/shard_map/while/body/dot_general | solution.py:21
  215.3 4.1 fusion.75
  219.4 8.3 %fusion.76 = bf16[1536,4096]{1,0:T(8,128)(2,1)} fusion(bf16[1536,4096]{1,0:T(8,128)(2,1)} %get-tuple-element.223, s32[]{:T(128)S(6)} %select_n.127, bf16[768,4096]{1,0:T(8,128)(2,1)} %get-tuple-element.239, bf16[4096,768]{1,0:T(8,128)(2,1)} %get-tuple-element.238, bf16[1536,4096]{1,0:T(8,128)(2,1)} %get-tuple-element.236, f32[128,768]{1,0:T(8,128)S(1)} %fusion.75), kind=kOutput, calls=%fused_computation.7.clone.1 | convolution fusion | flops 1611726848 | bytes 15074304 | tf_op jit(solution)/shard_map/while/body/dot_general | solution.py:21
  227.7 4.1 fusion.75
  231.8 8.3 %fusion.76 = bf16[1536,4096]{1,0:T(8,128)(2,1)} fusion(bf16[1536,4096]{1,0:T(8,128)(2,1)} %get-tuple-element.223, s32[]{:T(128)S(6)} %select_n.127, bf16[768,4096]{1,0:T(8,128)(2,1)} %get-tuple-element.239, bf16[4096,768]{1,0:T(8,128)(2,1)} %get-tuple-element.238, bf16[1536,4096]{1,0:T(8,128)(2,1)} %get-tuple-element.236, f32[128,768]{1,0:T(8,128)S(1)} %fusion.75), kind=kOutput, calls=%fused_computation.7.clone.1 | convolution fusion | flops 1611726848 | bytes 15074304 | tf_op jit(solution)/shard_map/while/body/dot_general | solution.py:21
  240.2 4.1 fusion.75
  244.3 8.4 %fusion.76 = bf16[1536,4096]{1,0:T(8,128)(2,1)} fusion(bf16[1536,4096]{1,0:T(8,128)(2,1)} %get-tuple-element.223, s32[]{:T(128)S(6)} %select_n.127, bf16[768,4096]{1,0:T(8,128)(2,1)} %get-tuple-element.239, bf16[4096,768]{1,0:T(8,128)(2,1)} %get-tuple-element.238, bf16[1536,4096]{1,0:T(8,128)(2,1)} %get-tuple-element.236, f32[128,768]{1,0:T(8,128)S(1)} %fusion.75), kind=kOutput, calls=%fused_computation.7.clone.1 | convolution fusion | flops 1611726848 | bytes 15074304 | tf_op jit(solution)/shard_map/while/body/dot_general | solution.py:21
  253.0 4.6 constant_dynamic-update-slice_fusion
  257.7 21.3 %gather_fusion.1 = bf16[1024,4096]{1,0:T(8,128)(2,1)} fusion(bf16[1536,4096]{1,0:T(8,128)(2,1)} %constant_dynamic-update-slice_fusion, s32[1024]{0:T(1024)S(1)} %broadcast_clamp_fusion), kind=kCustom, calls=%fused_computation.1 | custom fusion | bytes 16781312 | tf_op jit(solution)/shard_map/gather | solution.py:43
  278.9 7.2 %broadcast_select_fusion = bf16[16,64,4096]{2,1,0:T(8,128)(2,1)} fusion(bf16[16,64,4096]{2,1,0:T(8,128)(2,1)} %bitcast.84, pred[16,64]{1,0:T(8,128)(4,1)S(1)} %fusion.55), kind=kLoop, calls=%fused_computation.38 | loop fusion | flops 4194304 | bytes 16778240 | tf_op jit(solution)/shard_map/jit(_where)/select_n | solution.py:44
  286.1 53.1 %all-to-all-start.2 = ((bf16[16,64,4096]{2,1,0:T(8,128)(2,1)}), bf16[16,64,4096]{2,1,0:T(8,128)(2,1)}, u32[]{:S(2)}, u32[]{:S(2)}) async-start(bf16[16,64,4096]{2,1,0:T(8,128)(2,1)} %broadcast_select_fusion), calls=%async_computation.2 | async-start | bytes 16777216 | tf_op jit(solution)/shard_map/all_to_all | solution.py:85
  339.3 129.0 %all-to-all-done.2 = bf16[16,64,4096]{2,1,0:T(8,128)(2,1)} async-done(((bf16[16,64,4096]{2,1,0:T(8,128)(2,1)}), bf16[16,64,4096]{2,1,0:T(8,128)(2,1)}, u32[]{:S(2)}, u32[]{:S(2)}) %all-to-all-start.2) | async-done | bytes 8388640 | tf_op jit(solution)/shard_map/all_to_all | solution.py:85
  468.3 13.0 %gather_fusion.2 = bf16[512,4096]{1,0:T(8,128)(2,1)} fusion(bf16[1024,4096]{1,0:T(8,128)(2,1)} %bitcast.18, s32[1024]{0:T(1024)S(1)} %pad_clamp_fusion), kind=kCustom, calls=%fused_computation.2 | custom fusion | bytes 8390656 | tf_op jit(solution)/shard_map/gather | solution.py:87
  481.3 7.2 %reshape.232 = bf16[128,4,4096]{2,1,0:T(4,128)(2,1)} reshape(bf16[512,4096]{1,0:T(8,128)(2,1)} %gather_fusion.2) | data formatting | bytes 8388608 | tf_op jit(solution)/shard_map/reshape | solution.py:87
  488.5 14.9 %fusion.48 = (bf16[128,1,4096]{2,1,0:T(2,128)(2,1)S(1)}, bf16[128,1,4096]{2,1,0:T(2,128)(2,1)S(1)}, bf16[128,1,4096]{2,1,0:T(2,128)(2,1)S(1)}, bf16[128,1,4096]{2,1,0:T(2,128)(2,1)S(1)}) fusion(bf16[128,4,4096]{2,1,0:T(4,128)(2,1)} %reshape.232), kind=kLoop, calls=%fused_computation.88 | loop fusion | bytes 8388608 | tf_op jit(solution)/shard_map/slice | solution.py:90
  503.4 9.6 %fusion.39 = bf16[128,4096]{1,0:T(8,128)(2,1)} fusion(bf16[128,1,4096]{2,1,0:T(2,128)(2,1)S(1)} %get-tuple-element.116, bf16[128,1,4096]{2,1,0:T(2,128)(2,1)S(1)} %get-tuple-element.114, bf16[128,1,4096]{2,1,0:T(2,128)(2,1)S(1)} %get-tuple-element.115, bf16[128,1,4096]{2,1,0:T(2,128)(2,1)S(1)} %get-tuple-element.113, f32[128]{0:T(128)S(1)} %get-tuple-element.121, ...), kind=kLoop, calls=%fused_computation.45 | loop fusion | flops 6291456 | bytes 5244928 | tf_op jit(solution)/shard_map/convert_element_type | solution.py:93
  (43 shorter events, 5.9 us)
Async XLA Ops:
  0.0 14.3 %copy-start = (bf16[128,4096]{1,0:T(8,128)(2,1)S(1)}, bf16[128,4096]{1,0:T(8,128)(2,1)}, u32[]{:S(2)}) copy-start(bf16[128,4096]{1,0:T(8,128)(2,1)} %param.10) | copy-start | bytes 3145732
  6.7 24.6 %all-to-all-start = ((s32[16,1,64]{2,1,0:T(1,128)}), s32[16,1,64]{2,1,0:T(1,128)S(1)}, u32[]{:S(2)}, u32[]{:S(2)}) async-start(s32[16,1,64]{2,1,0:T(1,128)} %all_to_all.12), calls=%async_computation | async-start | bytes 16384 | tf_op jit(solution)/shard_map/all_to_all | solution.py:72
  31.3 128.3 %all-to-all-start.1 = ((bf16[16,64,4096]{2,1,0:T(8,128)(2,1)}), bf16[16,64,4096]{2,1,0:T(8,128)(2,1)}, u32[]{:S(2)}, u32[]{:S(2)}) async-start(bf16[16,64,4096]{2,1,0:T(8,128)(2,1)} %bitcast.85), calls=%async_computation.1 | async-start | bytes 16777216 | tf_op jit(solution)/shard_map/all_to_all | solution.py:71
  40.5 3.3 collective-permute-start
  184.3 9.5 %collective-permute-start.1 = (bf16[512,4096]{1,0:T(8,128)(2,1)}, bf16[512,4096]{1,0:T(8,128)(2,1)}, u32[]{:S(2)}, u32[]{:S(2)}) collective-permute-start(bf16[512,4096]{1,0:T(8,128)(2,1)} %constant_dynamic-slice_fusion), channel_id=1, source_target_pairs={{0,16},{16,0},{32,48},{48,32},{64,80},{80,64},{96,112},{112,96},{1... | collective-permute-start | bytes 12582920 | tf_op jit(solution)/shard_map/ppermute | solution.py:11
  196.3 56.7 %collective-permute-start.2 = (bf16[512,4096]{1,0:T(8,128)(2,1)}, bf16[512,4096]{1,0:T(8,128)(2,1)}, u32[]{:S(2)}, u32[]{:S(2)}) collective-permute-start(bf16[512,4096]{1,0:T(8,128)(2,1)} %get-tuple-element.82), channel_id=1, source_target_pairs={{0,16},{16,0},{32,48},{48,32},{64,80},{80,64},{96,112},{112,96},{1... | collective-permute-start | bytes 12582920 | tf_op jit(solution)/shard_map/ppermute | solution.py:11
  286.1 53.1 %copy-start.2 = (f32[128,4]{0,1:T(4,128)S(1)}, f32[128,4]{0,1:T(4,128)}, u32[]{:S(2)}) copy-start(f32[128,4]{0,1:T(4,128)} %param.12) | copy-start | bytes 6148
  286.1 182.1 %all-to-all-start.2 = ((bf16[16,64,4096]{2,1,0:T(8,128)(2,1)}), bf16[16,64,4096]{2,1,0:T(8,128)(2,1)}, u32[]{:S(2)}, u32[]{:S(2)}) async-start(bf16[16,64,4096]{2,1,0:T(8,128)(2,1)} %broadcast_select_fusion), calls=%async_computation.2 | async-start | bytes 16777216 | tf_op jit(solution)/shard_map/all_to_all | solution.py:85
  488.5 24.5 %copy-start.1 = (bf16[128,4096]{1,0:T(8,128)(2,1)S(1)}, bf16[128,4096]{1,0:T(8,128)(2,1)}, u32[]{:S(2)}) copy-start(bf16[128,4096]{1,0:T(8,128)(2,1)} %param.10) | copy-start | bytes 3145732
where the time goes:
time: 522 us; the launch traced here: 513 us
  waiting for transfers between devices  251 us (48%)
  local copies, waits for them, and re-layouts  117 us (22%)
  starting transfers between devices  72.7 us (14%)
  matrix products  49.9 us (10%)
  other arithmetic  20.6 us (4%)
    all_to_all x1, waiting for transfers between devices, local(): lax.all_to_all(results, 'expert', split_axis=0, concat_axis=0, tiled=True)  129 us
    all_to_all x1, waiting for transfers between devices, local(): lax.all_to_all(sending, 'expert', split_axis=0, concat_axis=0, tiled=True)  115 us
    all_to_all x1, starting transfers between devices, local(): lax.all_to_all(results, 'expert', split_axis=0, concat_axis=0, tiled=True)  53.1 us
    dot_general x4, matrix products, step(): jnp.dot(hidden, w_down, preferred_element_type=jnp.float32)  33.5 us
    gather x1, local copies, waits for them, and re-layouts, unpack_rows(): picked = done[source]  21.3 us
    scatter x1, local copies, waits for them, and re-layouts, pack_rows(): jnp.zeros((padded_rows, depth), jnp.bfloat16).at[target]  20.1 us
    dot_general x4, matrix products, step(): gate_part = jnp.dot(part, w_gate, preferred_element_type=jnp.float32)  16.4 us
    slice x1, local copies, waits for them, and re-layouts, local(): picked_rows[:, column].astype(jnp.float32)  14.9 us
  transfers between devices with their start and end apart: 6, of which 3 were waited for; matrix products, arithmetic and copies ran while one was open for 15% of the time, Pallas kernels for 0%

commit v1 on v0

v1 whole, which is shorter than its diff:
```python
import functools

import jax
import jax.numpy as jnp
from jax import lax
from jax.experimental import pallas as pl
from jax.experimental.pallas import tpu as pltpu
from jax.sharding import Mesh, PartitionSpec as P

SIDE = 4
CAP = 64
CHUNKS = 2
ROWS = CAP // CHUNKS
PACK_TILE = 512
FF_TILE = 256
D_TILE = 512
SUM_TILE = 512
VMEM = 50 * 1024 * 1024


def shift(block, axis, step):
    return lax.ppermute(block, axis, [(i, (i + step) % SIDE) for i in range(SIDE)])


def slots_of(ids, expert):
    named = jnp.any(ids == expert[..., None, None], axis=-2)
    tokens = ids.shape[-1]
    before = (jnp.arange(tokens)[:, None] < jnp.arange(tokens)[None, :]).astype(jnp.bfloat16)
    rank = jnp.dot(named.astype(jnp.bfloat16), before, preferred_element_type=jnp.float32)
    return jnp.where(named, rank.astype(jnp.int32), -1)


def gather_axis(half, axis):
    rows = half.shape[0] // 2
    ahead = shift(half, axis, 1)
    behind = shift(half, axis, -1)
    low = shift(ahead[:rows], axis, 1)
    high = shift(behind[rows:], axis, -1)
    return (half, ahead, low, high, behind)


def pack_kernel(first, slot_ref, own, ahead, low, high, behind, *outs):
    tokens = own.shape[0]
    sources = (own[...], ahead[...], jnp.concatenate([low[...], high[...]], axis=0), behind[...])
    place = lax.broadcasted_iota(jnp.int32, (ROWS, tokens), 0) + first
    for source in range(SIDE):
        picks = [
            (slot_ref[source, dest : dest + 1, :] == place).astype(jnp.float32)
            for dest in range(SIDE)
        ]
        pick = jnp.concatenate(picks, axis=0).astype(jnp.bfloat16)
        rows = jnp.dot(pick, sources[source], preferred_element_type=jnp.float32)
        rows = rows.astype(jnp.bfloat16)
        for dest in range(SIDE):
            outs[dest][source] = rows[dest * ROWS : (dest + 1) * ROWS]


def pack(chunk, slots, blocks):
    tokens, width = blocks[0].shape
    tile = min(PACK_TILE, width)
    whole = pl.BlockSpec((SIDE, SIDE, tokens), lambda i: (0, 0, 0))
    specs = [pl.BlockSpec((b.shape[0], tile), lambda i: (0, i)) for b in blocks]
    out = jax.ShapeDtypeStruct((SIDE, ROWS, width), jnp.bfloat16)
    return pl.pallas_call(
        functools.partial(pack_kernel, chunk * ROWS),
        grid=(width // tile,),
        in_specs=[whole] + specs,
        out_specs=[pl.BlockSpec((SIDE, ROWS, tile), lambda i: (0, 0, i))] * SIDE,
        out_shape=[out] * SIDE,
        compiler_params=pltpu.CompilerParams(vmem_limit_bytes=VMEM),
        cost_estimate=pl.CostEstimate(
            flops=2 * SIDE * SIDE * ROWS * tokens * width,
            bytes_accessed=2 * SIDE * width * (tokens + SIDE * ROWS),
            transcendentals=0,
        ),
    )(slots, *blocks)


def expert_kernel(n_ff, n_half, scale_ref, wg_ref, wu_ref, wd_ref, *refs):
    a_in, b_in = refs[:SIDE], refs[SIDE : 2 * SIDE]
    a_out, b_out = refs[2 * SIDE : 3 * SIDE], refs[3 * SIDE : 4 * SIDE]
    x_ref, hidden_ref, sems = refs[4 * SIDE :]
    step = pl.program_id(0)
    half = x_ref.shape[-1] // 2
    count = SIDE * SIDE * ROWS

    @pl.when(step == 0)
    def _():
        copies = []
        for k in range(SIDE):
            copies.append(
                pltpu.make_async_copy(a_in[k], x_ref.at[:, k, :, :half], sems.at[k])
            )
            copies.append(
                pltpu.make_async_copy(b_in[k], x_ref.at[k, :, :, half:], sems.at[SIDE + k])
            )
        for copy in copies:
            copy.start()
        for copy in copies:
            copy.wait()

    for f in range(n_ff):

        @pl.when(step == f)
        def _(f=f):
            x = x_ref[...].reshape(count, 2 * half)
            gate = jnp.dot(x, wg_ref[...], preferred_element_type=jnp.float32)
            up = jnp.dot(x, wu_ref[...], preferred_element_type=jnp.float32)
            tile = gate.shape[1]
            hidden = gate / (1.0 + jnp.exp(-gate)) * up
            hidden_ref[:, f * tile : (f + 1) * tile] = hidden.astype(jnp.bfloat16)

    def down():
        out = jnp.dot(hidden_ref[...], wd_ref[...], preferred_element_type=jnp.float32)
        out = (out * scale_ref[...]).astype(jnp.bfloat16)
        return out.reshape(SIDE, SIDE, ROWS, out.shape[1])

    @pl.when((step >= n_ff) & (step < n_ff + n_half))
    def _():
        out = down()
        for k in range(SIDE):
            a_out[k][...] = out[:, k]

    @pl.when(step >= n_ff + n_half)
    def _():
        out = down()
        for k in range(SIDE):
            b_out[k][...] = out[k]


def expert(scale, w_gate, w_up, w_down, a_in, b_in):
    half = a_in[0].shape[-1]
    depth, ff = w_gate.shape
    count = SIDE * SIDE * ROWS
    n_ff = ff // FF_TILE
    d_tile = min(D_TILE, half)
    n_half = half // d_tile
    ff_spec = pl.BlockSpec((depth, FF_TILE), lambda i: (0, jnp.minimum(i, n_ff - 1)))
    wd_spec = pl.BlockSpec((ff, d_tile), lambda i: (0, jnp.maximum(i - n_ff, 0)))
    a_spec = pl.BlockSpec(
        (SIDE, ROWS, d_tile), lambda i: (0, 0, jnp.clip(i - n_ff, 0, n_half - 1))
    )
    b_spec = pl.BlockSpec(
        (SIDE, ROWS, d_tile), lambda i: (0, 0, jnp.clip(i - n_ff - n_half, 0, n_half - 1))
    )
    out = jax.ShapeDtypeStruct((SIDE, ROWS, half), jnp.bfloat16)
    done = pl.pallas_call(
        functools.partial(expert_kernel, n_ff, n_half),
        grid=(n_ff + 2 * n_half,),
        in_specs=[pl.BlockSpec((count, 1), lambda i: (0, 0)), ff_spec, ff_spec, wd_spec]
        + [pl.BlockSpec(memory_space=pl.ANY)] * (2 * SIDE),
        out_specs=[a_spec] * SIDE + [b_spec] * SIDE,
        out_shape=[out] * (2 * SIDE),
        scratch_shapes=[
            pltpu.VMEM((SIDE, SIDE, ROWS, depth), jnp.bfloat16),
            pltpu.VMEM((count, ff), jnp.bfloat16),
            pltpu.SemaphoreType.DMA((2 * SIDE,)),
        ],
        compiler_params=pltpu.CompilerParams(vmem_limit_bytes=VMEM),
        cost_estimate=pl.CostEstimate(
            flops=6 * count * depth * ff,
            bytes_accessed=6 * depth * ff + 4 * count * depth,
            transcendentals=count * ff,
        ),
    )(scale, w_gate, w_up, w_down, *a_in, *b_in)
    return done[:SIDE], done[SIDE:]


def sum_kernel(slot_ref, *refs):
    ins, outs = refs[: CHUNKS * SIDE], refs[CHUNKS * SIDE :]
    tokens = slot_ref.shape[-1]
    place = lax.broadcasted_iota(jnp.int32, (ROWS, tokens), 0)
    for source in range(SIDE):
        picks, rows = [], []
        for chunk in range(CHUNKS):
            for dest in range(SIDE):
                hit = slot_ref[source, dest : dest + 1, :] == place + chunk * ROWS
                picks.append(hit.astype(jnp.float32))
                rows.append(ins[chunk * SIDE + dest][source])
        pick = jnp.concatenate(picks, axis=0).T.astype(jnp.bfloat16)
        total = jnp.dot(
            pick, jnp.concatenate(rows, axis=0), preferred_element_type=jnp.float32
        )
        outs[source][...] = total.astype(jnp.bfloat16)


def sum_rows(slots, blocks):
    width = blocks[0].shape[-1]
    tokens = slots.shape[-1]
    tile = min(SUM_TILE, width)
    out = jax.ShapeDtypeStruct((tokens, width), jnp.bfloat16)
    return pl.pallas_call(
        sum_kernel,
        grid=(width // tile,),
        in_specs=[pl.BlockSpec((SIDE, SIDE, tokens), lambda i: (0, 0, 0))]
        + [pl.BlockSpec((SIDE, ROWS, tile), lambda i: (0, 0, i))] * len(blocks),
        out_specs=[pl.BlockSpec((tokens, tile), lambda i: (0, i))] * SIDE,
        out_shape=[out] * SIDE,
        compiler_params=pltpu.CompilerParams(vmem_limit_bytes=VMEM),
        cost_estimate=pl.CostEstimate(
            flops=2 * SIDE * SIDE * CAP * tokens * width,
            bytes_accessed=2 * SIDE * width * (tokens + SIDE * CAP),
            transcendentals=0,
        ),
    )(slots, *blocks)


def local(tokens, expert_ids, gate_values, gate_weight, up_weight, down_weight):
    half = tokens.shape[1] // 2
    z, x = lax.axis_index("z"), lax.axis_index("x")
    steps = jnp.arange(SIDE)

    a_rows = gather_axis(tokens[:, :half], "z")
    b_rows = gather_axis(tokens[:, half:], "x")

    top = expert_ids.shape[1]
    routing = jnp.concatenate([expert_ids.T.astype(jnp.float32), gate_values.T], axis=0)
    routing = lax.all_gather(routing, ("z", "x"), axis=0, tiled=False)
    routing = routing.reshape((SIDE, SIDE) + routing.shape[1:])
    routing = routing[(z - steps) % SIDE][:, (x - steps) % SIDE]
    ids, gates = routing[:, :, :top].astype(jnp.int32), routing[:, :, top:]

    a_slots = slots_of(
        jnp.broadcast_to(ids[:, :1], ids.shape),
        jnp.broadcast_to(z * SIDE + (x + steps) % SIDE, (SIDE, SIDE)),
    )
    b_slots = slots_of(
        jnp.broadcast_to(ids[0][:, None], ids.shape),
        jnp.broadcast_to((z + steps) % SIDE * SIDE + x, (SIDE, SIDE)),
    )
    here = jnp.full((SIDE, SIDE), z * SIDE + x)
    slots = slots_of(ids, here)
    weight = jnp.sum(jnp.where(ids == here[..., None, None], gates, 0.0), axis=2)
    hit = slots[:, :, None, :] == jnp.arange(CAP)[:, None]
    scale = jnp.sum(jnp.where(hit, weight[:, :, None, :], 0.0), axis=-1)

    w_gate, w_up, w_down = gate_weight[0], up_weight[0], down_weight[0]
    a_back, b_back = [], []
    for chunk in range(CHUNKS):
        a_out = pack(chunk, a_slots, a_rows)
        b_out = pack(chunk, b_slots, b_rows)
        a_in = [a_out[0]] + [shift(a_out[k], "x", k) for k in range(1, SIDE)]
        b_in = [b_out[0]] + [shift(b_out[k], "z", k) for k in range(1, SIDE)]
        part = scale[:, :, chunk * ROWS : (chunk + 1) * ROWS].reshape(-1, 1)
        a_done, b_done = expert(part, w_gate, w_up, w_down, a_in, b_in)
        a_back += [a_done[0]] + [shift(a_done[k], "x", -k) for k in range(1, SIDE)]
        b_back += [b_done[0]] + [shift(b_done[k], "z", -k) for k in range(1, SIDE)]

    a_sums = sum_rows(a_slots, a_back)
    b_sums = sum_rows(b_slots, b_back)
    a_home = [a_sums[0]] + [shift(a_sums[k], "z", -k) for k in range(1, SIDE)]
    b_home = [b_sums[0]] + [shift(b_sums[k], "x", -k) for k in range(1, SIDE)]
    mixed = [sum(part.astype(jnp.float32) for part in home) for home in (a_home, b_home)]
    return jnp.concatenate(mixed, axis=1).astype(jnp.bfloat16)


def solution(mesh):
    dp = mesh.devices.shape[0]
    grid = Mesh(mesh.devices.reshape(dp, SIDE, SIDE), ("dp", "z", "x"))
    rows, experts = ("dp", "z", "x"), ("z", "x")
    in_specs = (
        P(rows, None),
        P(rows, None),
        P(rows, None),
        P(experts, None, None),
        P(experts, None, None),
        P(experts, None, None),
    )
    return jax.shard_map(
        local, mesh=grid, in_specs=in_specs, out_specs=P(rows, None), check_vma=False
    )
```

time: 522 us -> 250 us (0.48)
  the two profiles are of different devices: /device:TPU:9 before, /device:TPU:0 now
where the time goes in v1:
time: 250 us
  waiting for transfers between devices  76.2 us (30%)
  starting transfers between devices  65.2 us (26%)
  Pallas kernels  63.1 us (25%)
  blocking collectives  29.2 us (12%)
  local copies, waits for them, and re-layouts  11.4 us (5%)
  other arithmetic  3.69 us (1%)
    ppermute x38, waiting for transfers between devices, shift(): lax.ppermute(block, axis, [(i, (i + step) % SIDE) for i in range(SIDE)])  76.2 us
    ppermute x38, starting transfers between devices, shift(): lax.ppermute(block, axis, [(i, (i + step) % SIDE) for i in range(SIDE)])  65.2 us
    pallas_call x2, Pallas kernels, expert(): pl.pallas_call(functools.partial(expert_kernel, n_ff, n_half), grid=(n_ff...  41.1 us
    all_gather x1, blocking collectives, local(): routing = lax.all_gather(routing, ('z', 'x'), axis=0, tiled=False)  29.2 us
    pallas_call x4, Pallas kernels, pack(): pl.pallas_call(functools.partial(pack_kernel, chunk * ROWS), grid=(width...  14.7 us
    pallas_call x2, Pallas kernels, sum_rows(): pl.pallas_call(sum_kernel, grid=(width // tile,), in_specs=[pl.BlockSpec(...  7.39 us
    unnamed x48, local copies, waits for them, and re-layouts  7.37 us
  transfers between devices with their start and end apart: 38, of which 15 were waited for; matrix products, arithmetic and copies ran while one was open for 2% of the time, Pallas kernels for 25%

profile of v1, /device:TPU:0, one launch (start us, length us, event | category | flops | bytes accessed | tf_op | source)
XLA Modules:
  0.0 249.6 jit_solution(15233795286365053936)
XLA Ops:
  3.3 2.2 collective-permute-start.2
  5.5 2.8 %collective-permute-start.9 = (bf16[128,2048]{1,0:T(8,128)(2,1)S(1)}, bf16[128,2048]{1,0:T(8,128)(2,1)}, u32[]{:S(2)}, u32[]{:S(2)}) collective-permute-start(bf16[128,2048]{1,0:T(8,128)(2,1)S(1)} %get-tuple-element.87.own), channel_id=1, source_target_pairs={{0,3},{1,0},{2,1},{3,2},{4,7},{5,4},{6,5},{7,6},{8,11},{9,8},{10,9... | collective-permute-start | bytes 1572872 | tf_op jit(solution)/shard_map/ppermute | solution.py:22
  9.7 29.2 %all-gather = f32[128,128]{1,0:T(8,128)S(1)} all-gather(f32[8,128]{1,0:T(8,128)S(1)} %pad_maximum_fusion.1), channel_id=2, replica_groups=mesh['dp'=8,'z'=4,'x'=4] {'z','x'}, dimensions={0}, use_global_device_ids=true | all-gather | bytes 69632 | tf_op jit(solution)/shard_map/all_gather | solution.py:218
  40.8 2.9 %collective-permute-start.3 = (bf16[64,2048]{1,0:T(8,128)(2,1)S(1)}, bf16[64,2048]{1,0:T(8,128)(2,1)S(1)}, u32[]{:S(2)}, u32[]{:S(2)}) collective-permute-start(bf16[64,2048]{1,0:T(8,128)(2,1)S(1)} %slice.57), channel_id=1, source_target_pairs={{0,12},{4,0},{8,4},{12,8},{1,13},{5,1},{9,5},{13,9},{2,14},{6,2},{... | collective-permute-start | bytes 786440 | tf_op jit(solution)/shard_map/ppermute | solution.py:22
  43.9 4.0 %collective-permute-done.1.low = bf16[64,2048]{1,0:T(8,128)(2,1)S(1)} collective-permute-done((bf16[64,2048]{1,0:T(8,128)(2,1)S(1)}, bf16[64,2048]{1,0:T(8,128)(2,1)S(1)}, u32[]{:S(2)}, u32[]{:S(2)}) %collective-permute-start.1) | collective-permute-done | bytes 262176 | tf_op jit(solution)/shard_map/ppermute | solution.py:22
  47.9 3.8 %shard_map.67 = (bf16[4,32,2048]{2,1,0:T(8,128)(2,1)S(1)}, bf16[4,32,2048]{2,1,0:T(8,128)(2,1)S(1)}, bf16[4,32,2048]{2,1,0:T(8,128)(2,1)S(1)}, bf16[4,32,2048]{2,1,0:T(8,128)(2,1)}) custom-call(s32[4,4,128]{2,1,0:T(4,128)S(1)} %fusion.2.slot_ref, bf16[128,2048]{1,0:T(8,128)(2,1)S(1)} %get-tuple-element.88.own, ...), custom_call_target="tpu_custom_call" | custom-call | flops 268435456 | bytes 4194304 | tf_op jit(solution)/shard_map/pallas_call | solution.py:64
  55.3 2.4 collective-permute-start.10
  58.0 3.2 %collective-permute-start.19 = (bf16[4,32,2048]{2,1,0:T(8,128)(2,1)}, bf16[4,32,2048]{2,1,0:T(8,128)(2,1)}, u32[]{:S(2)}, u32[]{:S(2)}) collective-permute-start(bf16[4,32,2048]{2,1,0:T(8,128)(2,1)} %get-tuple-element.60), channel_id=1, source_target_pairs={{0,3},{1,0},{2,1},{3,2},{4,7},{5,4},{6,5},{7,6},{8,11},{9,8},{10,9... | collective-permute-start | bytes 1572872 | tf_op jit(solution)/shard_map/ppermute | solution.py:22
  61.3 10.8 %collective-permute-done.10.high = bf16[64,2048]{1,0:T(8,128)(2,1)S(1)} collective-permute-done((bf16[64,2048]{1,0:T(8,128)(2,1)S(1)}, bf16[64,2048]{1,0:T(8,128)(2,1)S(1)}, u32[]{:S(2)}, u32[]{:S(2)}) %collective-permute-start.10) | collective-permute-done | bytes 262176 | tf_op jit(solution)/shard_map/ppermute | solution.py:22
  72.1 5.0 %collective-permute-done.8.low = bf16[64,2048]{1,0:T(8,128)(2,1)S(1)} collective-permute-done((bf16[64,2048]{1,0:T(8,128)(2,1)S(1)}, bf16[64,2048]{1,0:T(8,128)(2,1)S(1)}, u32[]{:S(2)}, u32[]{:S(2)}) %collective-permute-start.8) | collective-permute-done | bytes 262176 | tf_op jit(solution)/shard_map/ppermute | solution.py:22
  77.1 4.1 %shard_map.68 = (bf16[4,32,2048]{2,1,0:T(8,128)(2,1)S(1)}, bf16[4,32,2048]{2,1,0:T(8,128)(2,1)}, bf16[4,32,2048]{2,1,0:T(8,128)(2,1)}, bf16[4,32,2048]{2,1,0:T(8,128)(2,1)}) custom-call(s32[4,4,128]{2,1,0:T(4,128)S(1)} %fusion.slot_ref, bf16[128,2048]{1,0:T(8,128)(2,1)S(1)} %get-tuple-element.87.own, bf16[128,2048]{1,0:T(8,128)(2,1)S(1)} %collective-permute-done.7.ahead, ...), custom_call_target="tpu_custom_call" | custom-call | flops 268435456 | bytes 4194304 | tf_op jit(solution)/shard_map/pallas_call | solution.py:64
  81.9 4.4 %collective-permute-start.21 = (bf16[4,32,2048]{2,1,0:T(8,128)(2,1)}, bf16[4,32,2048]{2,1,0:T(8,128)(2,1)}, u32[]{:S(2)}, u32[]{:S(2)}) collective-permute-start(bf16[4,32,2048]{2,1,0:T(8,128)(2,1)} %get-tuple-element.63), channel_id=1, source_target_pairs={{0,8},{4,12},{8,0},{12,4},{1,9},{5,13},{9,1},{13,5},{2,10},{6,14},... | collective-permute-start | bytes 1572872 | tf_op jit(solution)/shard_map/ppermute | solution.py:22
  86.3 3.8 %shard_map.65 = (bf16[4,32,2048]{2,1,0:T(8,128)(2,1)S(1)}, bf16[4,32,2048]{2,1,0:T(8,128)(2,1)}, bf16[4,32,2048]{2,1,0:T(8,128)(2,1)S(1)}, bf16[4,32,2048]{2,1,0:T(8,128)(2,1)S(1)}) custom-call(s32[4,4,128]{2,1,0:T(4,128)S(1)} %fusion.slot_ref, bf16[128,2048]{1,0:T(8,128)(2,1)S(1)} %get-tuple-element.87.own, ...), custom_call_target="tpu_custom_call" | custom-call | flops 268435456 | bytes 4194304 | tf_op jit(solution)/shard_map/pallas_call | solution.py:64
  94.8 2.9 %shard_map.64 = (bf16[4,32,2048]{2,1,0:T(8,128)(2,1)S(1)}, bf16[4,32,2048]{2,1,0:T(8,128)(2,1)S(1)}, bf16[4,32,2048]{2,1,0:T(8,128)(2,1)S(1)}, bf16[4,32,2048]{2,1,0:T(8,128)(2,1)S(1)}) custom-call(s32[4,4,128]{2,1,0:T(4,128)S(1)} %fusion.2.slot_ref, bf16[128,2048]{1,0:T(8,128)(2,1)S(1)} %get-tuple-element.88.own, ...), custom_call_target="tpu_custom_call" | custom-call | flops 268435456 | bytes 4194304 | tf_op jit(solution)/shard_map/pallas_call | solution.py:64
  99.4 2.2 collective-permute-start.13
  101.6 8.3 %collective-permute-done.21.refs_6_ = bf16[4,32,2048]{2,1,0:T(8,128)(2,1)} collective-permute-done((bf16[4,32,2048]{2,1,0:T(8,128)(2,1)}, bf16[4,32,2048]{2,1,0:T(8,128)(2,1)}, u32[]{:S(2)}, u32[]{:S(2)}) %collective-permute-start.21) | collective-permute-done | bytes 524320 | tf_op jit(solution)/shard_map/ppermute | solution.py:22
  110.8 3.1 %collective-permute-start.5 = (bf16[4,32,2048]{2,1,0:T(8,128)(2,1)S(1)}, bf16[4,32,2048]{2,1,0:T(8,128)(2,1)S(1)}, u32[]{:S(2)}, u32[]{:S(2)}) collective-permute-start(bf16[4,32,2048]{2,1,0:T(8,128)(2,1)S(1)} %get-tuple-element.47), channel_id=1, source_target_pairs={{0,2},{1,3},{2,0},{3,1},{4,6},{5,7},{6,4},{7,5},{8,10},{9,11},{10,... | collective-permute-start | bytes 1572872 | tf_op jit(solution)/shard_map/ppermute | solution.py:22
  115.3 3.3 %collective-permute-start.6 = (bf16[4,32,2048]{2,1,0:T(8,128)(2,1)S(1)}, bf16[4,32,2048]{2,1,0:T(8,128)(2,1)S(1)}, u32[]{:S(2)}, u32[]{:S(2)}) collective-permute-start(bf16[4,32,2048]{2,1,0:T(8,128)(2,1)S(1)} %get-tuple-element.48), channel_id=1, source_target_pairs={{0,3},{1,0},{2,1},{3,2},{4,7},{5,4},{6,5},{7,6},{8,11},{9,8},{10,9... | collective-permute-start | bytes 1572872 | tf_op jit(solution)/shard_map/ppermute | solution.py:22
  118.6 20.5 %shard_map.69 = (bf16[4,32,2048]{2,1,0:T(8,128)(2,1)S(1)}, bf16[4,32,2048]{2,1,0:T(8,128)(2,1)S(1)}, bf16[4,32,2048]{2,1,0:T(8,128)(2,1)S(1)}, bf16[4,32,2048]{2...) custom-call(f32[512,1]{1,0:T(8,128)S(1)} %reshape.133.scale_ref, ...), custom_call_target="tpu_custom_call" | custom-call | flops 9663676416 | bytes 27262976 | tf_op jit(solution)/shard_map/pallas_call | solution.py:147
  144.0 20.6 %shard_map.66 = (bf16[4,32,2048]{2,1,0:T(8,128)(2,1)S(1)}, bf16[4,32,2048]{2,1,0:T(8,128)(2,1)S(1)}, bf16[4,32,2048]{2,1,0:T(8,128)(2,1)S(1)}, bf16[4,32,2048]{2...) custom-call(f32[512,1]{1,0:T(8,128)S(1)} %reshape.132.scale_ref, ...), custom_call_target="tpu_custom_call" | custom-call | flops 9663676416 | bytes 27262976 | tf_op jit(solution)/shard_map/pallas_call | solution.py:147
  164.5 2.7 %collective-permute-start.14 = (bf16[4,32,2048]{2,1,0:T(8,128)(2,1)S(1)}, bf16[4,32,2048]{2,1,0:T(8,128)(2,1)S(1)}, u32[]{:S(2)}, u32[]{:S(2)}) collective-permute-start(bf16[4,32,2048]{2,1,0:T(8,128)(2,1)S(1)} %get-tuple-element.54), channel_id=1, source_target_pairs={{0,3},{1,0},{2,1},{3,2},{4,7},{5,4},{6,5},{7,6},{8,11},{9,8},{10,9... | collective-permute-start | bytes 1572872 | tf_op jit(solution)/shard_map/ppermute | solution.py:22
  171.6 2.9 %collective-permute-start.33 = (bf16[4,32,2048]{2,1,0:T(8,128)(2,1)S(1)}, bf16[4,32,2048]{2,1,0:T(8,128)(2,1)S(1)}, u32[]{:S(2)}, u32[]{:S(2)}) collective-permute-start(bf16[4,32,2048]{2,1,0:T(8,128)(2,1)S(1)} %get-tuple-element.79), channel_id=1, source_target_pairs={{0,8},{4,12},{8,0},{12,4},{1,9},{5,13},{9,1},{13,5},{2,10},{6,14},... | collective-permute-start | bytes 1572872 | tf_op jit(solution)/shard_map/ppermute | solution.py:22
  174.6 5.0 %collective-permute-done.14.refs_1_ = bf16[4,32,2048]{2,1,0:T(8,128)(2,1)S(1)} collective-permute-done((bf16[4,32,2048]{2,1,0:T(8,128)(2,1)S(1)}, bf16[4,32,2048]{2,1,0:T(8,128)(2,1)S(1)}, u32[]{:S(2)}, u32[]{:S(2)}) %collective-permute-start.14) | collective-permute-done | bytes 524320 | tf_op jit(solution)/shard_map/ppermute | solution.py:22
  179.6 2.6 %collective-permute-start.34 = (bf16[4,32,2048]{2,1,0:T(8,128)(2,1)S(1)}, bf16[4,32,2048]{2,1,0:T(8,128)(2,1)S(1)}, u32[]{:S(2)}, u32[]{:S(2)}) collective-permute-start(bf16[4,32,2048]{2,1,0:T(8,128)(2,1)S(1)} %copy-done.18), channel_id=1, source_target_pairs={{0,4},{4,8},{8,12},{12,0},{1,5},{5,9},{9,13},{13,1},{2,6},{6,10},{... | collective-permute-start | bytes 1572872 | tf_op jit(solution)/shard_map/ppermute | solution.py:22
  186.2 3.7 %shard_map.70 = (bf16[128,2048]{1,0:T(8,128)(2,1)S(1)}, bf16[128,2048]{1,0:T(8,128)(2,1)S(1)}, bf16[128,2048]{1,0:T(8,128)(2,1)S(1)}, bf16[128,2048]{1,0:T(8,128)(2,1)S(1)}) custom-call(s32[4,4,128]{2,1,0:T(4,128)S(1)} %fusion.2.slot_ref, bf16[4,32,2048]{2,1,0:T(8,128)(2,1)S(1)} %get-tuple-element.53.refs_0_, ...), custom_call_target="tpu_custom_call" | custom-call | flops 536870912 | bytes 6291456 | tf_op jit(solution)/shard_map/pallas_call | solution.py:192
  189.9 9.4 %collective-permute-start.26 = (bf16[128,2048]{1,0:T(8,128)(2,1)S(1)}, bf16[128,2048]{1,0:T(8,128)(2,1)S(1)}, u32[]{:S(2)}, u32[]{:S(2)}) collective-permute-start(bf16[128,2048]{1,0:T(8,128)(2,1)S(1)} %get-tuple-element.70), channel_id=1, source_target_pairs={{0,12},{4,0},{8,4},{12,8},{1,13},{5,1},{9,5},{13,9},{2,14},{6,2},{... | collective-permute-start | bytes 1572872 | tf_op jit(solution)/shard_map/ppermute | solution.py:22
  199.3 4.2 %collective-permute-done.34.refs_7_ = bf16[4,32,2048]{2,1,0:T(8,128)(2,1)S(1)} collective-permute-done((bf16[4,32,2048]{2,1,0:T(8,128)(2,1)S(1)}, bf16[4,32,2048]{2,1,0:T(8,128)(2,1)S(1)}, u32[]{:S(2)}, u32[]{:S(2)}) %collective-permute-start.34) | collective-permute-done | bytes 524320 | tf_op jit(solution)/shard_map/ppermute | solution.py:22
  203.5 2.4 collective-permute-start.27
  207.9 18.0 %collective-permute-done.31.refs_3_ = bf16[4,32,2048]{2,1,0:T(8,128)(2,1)S(1)} collective-permute-done((bf16[4,32,2048]{2,1,0:T(8,128)(2,1)}, bf16[4,32,2048]{2,1,0:T(8,128)(2,1)S(1)}, u32[]{:S(2)}, u32[]{:S(2)}) %collective-permute-start.31) | collective-permute-done | bytes 524320 | tf_op jit(solution)/shard_map/ppermute | solution.py:22
  226.6 3.7 %shard_map.71 = (bf16[128,2048]{1,0:T(8,128)(2,1)S(1)}, bf16[128,2048]{1,0:T(8,128)(2,1)S(1)}, bf16[128,2048]{1,0:T(8,128)(2,1)S(1)}, bf16[128,2048]{1,0:T(8,128)(2,1)S(1)}) custom-call(s32[4,4,128]{2,1,0:T(4,128)S(1)} %fusion.slot_ref, bf16[4,32,2048]{2,1,0:T(8,128)(2,1)S(1)} %get-tuple-element.73.refs_0_, ...), custom_call_target="tpu_custom_call" | custom-call | flops 536870912 | bytes 6291456 | tf_op jit(solution)/shard_map/pallas_call | solution.py:192
  233.5 11.0 %collective-permute-done.35 = bf16[128,2048]{1,0:T(8,128)(2,1)S(1)} collective-permute-done((bf16[128,2048]{1,0:T(8,128)(2,1)S(1)}, bf16[128,2048]{1,0:T(8,128)(2,1)S(1)}, u32[]{:S(2)}, u32[]{:S(2)}) %collective-permute-start.35) | collective-permute-done | bytes 524320 | tf_op jit(solution)/shard_map/ppermute | solution.py:22
  244.5 3.7 %collective-permute-done.37 = bf16[128,2048]{1,0:T(8,128)(2,1)S(1)} collective-permute-done((bf16[128,2048]{1,0:T(8,128)(2,1)S(1)}, bf16[128,2048]{1,0:T(8,128)(2,1)S(1)}, u32[]{:S(2)}, u32[]{:S(2)}) %collective-permute-start.37) | collective-permute-done | bytes 524320 | tf_op jit(solution)/shard_map/ppermute | solution.py:22
  (132 shorter events, 40.7 us)
Async XLA Ops:
  1.3 38.9 %collective-permute-start = (bf16[128,2048]{1,0:T(8,128)(2,1)S(1)}, bf16[128,2048]{1,0:T(8,128)(2,1)S(1)}, u32[]{:S(2)}, u32[]{:S(2)}) collective-permute-start(bf16[128,2048]{1,0:T(8,128)(2,1)S(1)} %get-tuple-element.88.own), channel_id=1, source_target_pairs={{0,4},{4,8},{8,12},{12,0},{1,5},{5,9},{9,13},{13,1},{2,6},{6,10},{... | collective-permute-start | bytes 1572872 | tf_op jit(solution)/shard_map/ppermute | solution.py:22
  3.3 37.4 %collective-permute-start.2 = (bf16[128,2048]{1,0:T(8,128)(2,1)S(1)}, bf16[128,2048]{1,0:T(8,128)(2,1)S(1)}, u32[]{:S(2)}, u32[]{:S(2)}) collective-permute-start(bf16[128,2048]{1,0:T(8,128)(2,1)S(1)} %get-tuple-element.88.own), channel_id=1, source_target_pairs={{0,12},{4,0},{8,4},{12,8},{1,13},{5,1},{9,5},{13,9},{2,14},{6,2},{... | collective-permute-start | bytes 1572872 | tf_op jit(solution)/shard_map/ppermute | solution.py:22
  5.5 48.8 %collective-permute-start.9 = (bf16[128,2048]{1,0:T(8,128)(2,1)S(1)}, bf16[128,2048]{1,0:T(8,128)(2,1)}, u32[]{:S(2)}, u32[]{:S(2)}) collective-permute-start(bf16[128,2048]{1,0:T(8,128)(2,1)S(1)} %get-tuple-element.87.own), channel_id=1, source_target_pairs={{0,3},{1,0},{2,1},{3,2},{4,7},{5,4},{6,5},{7,6},{8,11},{9,8},{10,9... | collective-permute-start | bytes 1572872 | tf_op jit(solution)/shard_map/ppermute | solution.py:22
  8.3 49.4 %collective-permute-start.7 = (bf16[128,2048]{1,0:T(8,128)(2,1)S(1)}, bf16[128,2048]{1,0:T(8,128)(2,1)S(1)}, u32[]{:S(2)}, u32[]{:S(2)}) collective-permute-start(bf16[128,2048]{1,0:T(8,128)(2,1)S(1)} %get-tuple-element.87.own), channel_id=1, source_target_pairs={{0,1},{1,2},{2,3},{3,0},{4,5},{5,6},{6,7},{7,4},{8,9},{9,10},{10,1... | collective-permute-start | bytes 1572872 | tf_op jit(solution)/shard_map/ppermute | solution.py:22
  52.5 39.2 %collective-permute-start.17 = (bf16[4,32,2048]{2,1,0:T(8,128)(2,1)S(1)}, bf16[4,32,2048]{2,1,0:T(8,128)(2,1)S(1)}, u32[]{:S(2)}, u32[]{:S(2)}) collective-permute-start(bf16[4,32,2048]{2,1,0:T(8,128)(2,1)S(1)} %get-tuple-element.58), channel_id=1, source_target_pairs={{0,1},{1,2},{2,3},{3,0},{4,5},{5,6},{6,7},{7,4},{8,9},{9,10},{10,1... | collective-permute-start | bytes 1572872 | tf_op jit(solution)/shard_map/ppermute | solution.py:22
  52.5 39.2 %collective-permute-start.18 = (bf16[4,32,2048]{2,1,0:T(8,128)(2,1)S(1)}, bf16[4,32,2048]{2,1,0:T(8,128)(2,1)S(1)}, u32[]{:S(2)}, u32[]{:S(2)}) collective-permute-start(bf16[4,32,2048]{2,1,0:T(8,128)(2,1)S(1)} %get-tuple-element.59), channel_id=1, source_target_pairs={{0,2},{1,3},{2,0},{3,1},{4,6},{5,7},{6,4},{7,5},{8,10},{9,11},{10,... | collective-permute-start | bytes 1572872 | tf_op jit(solution)/shard_map/ppermute | solution.py:22
  55.3 16.8 %collective-permute-start.10 = (bf16[64,2048]{1,0:T(8,128)(2,1)S(1)}, bf16[64,2048]{1,0:T(8,128)(2,1)S(1)}, u32[]{:S(2)}, u32[]{:S(2)}) collective-permute-start(bf16[64,2048]{1,0:T(8,128)(2,1)S(1)} %slice.60), channel_id=1, source_target_pairs={{0,3},{1,0},{2,1},{3,2},{4,7},{5,4},{6,5},{7,6},{8,11},{9,8},{10,9... | collective-permute-start | bytes 786440 | tf_op jit(solution)/shard_map/ppermute | solution.py:22
  57.7 19.4 %collective-permute-start.8 = (bf16[64,2048]{1,0:T(8,128)(2,1)S(1)}, bf16[64,2048]{1,0:T(8,128)(2,1)S(1)}, u32[]{:S(2)}, u32[]{:S(2)}) collective-permute-start(bf16[64,2048]{1,0:T(8,128)(2,1)S(1)} %slice.59), channel_id=1, source_target_pairs={{0,1},{1,2},{2,3},{3,0},{4,5},{5,6},{6,7},{7,4},{8,9},{9,10},{10,1... | collective-permute-start | bytes 786440 | tf_op jit(solution)/shard_map/ppermute | solution.py:22
  58.0 40.5 %collective-permute-start.19 = (bf16[4,32,2048]{2,1,0:T(8,128)(2,1)}, bf16[4,32,2048]{2,1,0:T(8,128)(2,1)}, u32[]{:S(2)}, u32[]{:S(2)}) collective-permute-start(bf16[4,32,2048]{2,1,0:T(8,128)(2,1)} %get-tuple-element.60), channel_id=1, source_target_pairs={{0,3},{1,0},{2,1},{3,2},{4,7},{5,4},{6,5},{7,6},{8,11},{9,8},{10,9... | collective-permute-start | bytes 1572872 | tf_op jit(solution)/shard_map/ppermute | solution.py:22
  81.9 17.5 %collective-permute-start.20 = (bf16[4,32,2048]{2,1,0:T(8,128)(2,1)}, bf16[4,32,2048]{2,1,0:T(8,128)(2,1)}, u32[]{:S(2)}, u32[]{:S(2)}) collective-permute-start(bf16[4,32,2048]{2,1,0:T(8,128)(2,1)} %get-tuple-element.62), channel_id=1, source_target_pairs={{0,4},{4,8},{8,12},{12,0},{1,5},{5,9},{9,13},{13,1},{2,6},{6,10},{... | collective-permute-start | bytes 1572872 | tf_op jit(solution)/shard_map/ppermute | solution.py:22
  81.9 27.9 %collective-permute-start.21 = (bf16[4,32,2048]{2,1,0:T(8,128)(2,1)}, bf16[4,32,2048]{2,1,0:T(8,128)(2,1)}, u32[]{:S(2)}, u32[]{:S(2)}) collective-permute-start(bf16[4,32,2048]{2,1,0:T(8,128)(2,1)} %get-tuple-element.63), channel_id=1, source_target_pairs={{0,8},{4,12},{8,0},{12,4},{1,9},{5,13},{9,1},{13,5},{2,10},{6,14},... | collective-permute-start | bytes 1572872 | tf_op jit(solution)/shard_map/ppermute | solution.py:22
  91.8 19.1 %collective-permute-start.22 = (bf16[4,32,2048]{2,1,0:T(8,128)(2,1)}, bf16[4,32,2048]{2,1,0:T(8,128)(2,1)}, u32[]{:S(2)}, u32[]{:S(2)}) collective-permute-start(bf16[4,32,2048]{2,1,0:T(8,128)(2,1)} %get-tuple-element.64), channel_id=1, source_target_pairs={{0,12},{4,0},{8,4},{12,8},{1,13},{5,1},{9,5},{13,9},{2,14},{6,2},{... | collective-permute-start | bytes 1572872 | tf_op jit(solution)/shard_map/ppermute | solution.py:22
  91.8 23.5 %collective-permute-start.11 = (bf16[4,32,2048]{2,1,0:T(8,128)(2,1)}, bf16[4,32,2048]{2,1,0:T(8,128)(2,1)}, u32[]{:S(2)}, u32[]{:S(2)}) collective-permute-start(bf16[4,32,2048]{2,1,0:T(8,128)(2,1)} %get-tuple-element.50), channel_id=1, source_target_pairs={{0,4},{4,8},{8,12},{12,0},{1,5},{5,9},{9,13},{13,1},{2,6},{6,10},{... | collective-permute-start | bytes 1572872 | tf_op jit(solution)/shard_map/ppermute | solution.py:22
  98.5 42.2 %collective-permute-start.12 = (bf16[4,32,2048]{2,1,0:T(8,128)(2,1)}, bf16[4,32,2048]{2,1,0:T(8,128)(2,1)S(1)}, u32[]{:S(2)}, u32[]{:S(2)}) collective-permute-start(bf16[4,32,2048]{2,1,0:T(8,128)(2,1)} %copy-done.6), channel_id=1, source_target_pairs={{0,8},{4,12},{8,0},{12,4},{1,9},{5,13},{9,1},{13,5},{2,10},{6,14},... | collective-permute-start | bytes 1572872 | tf_op jit(solution)/shard_map/ppermute | solution.py:22
  99.4 41.3 %collective-permute-start.13 = (bf16[4,32,2048]{2,1,0:T(8,128)(2,1)S(1)}, bf16[4,32,2048]{2,1,0:T(8,128)(2,1)S(1)}, u32[]{:S(2)}, u32[]{:S(2)}) collective-permute-start(bf16[4,32,2048]{2,1,0:T(8,128)(2,1)S(1)} %get-tuple-element.52), channel_id=1, source_target_pairs={{0,12},{4,0},{8,4},{12,8},{1,13},{5,1},{9,5},{13,9},{2,14},{6,2},{... | collective-permute-start | bytes 1572872 | tf_op jit(solution)/shard_map/ppermute | solution.py:22
  109.8 31.8 %collective-permute-start.4 = (bf16[4,32,2048]{2,1,0:T(8,128)(2,1)S(1)}, bf16[4,32,2048]{2,1,0:T(8,128)(2,1)S(1)}, u32[]{:S(2)}, u32[]{:S(2)}) collective-permute-start(bf16[4,32,2048]{2,1,0:T(8,128)(2,1)S(1)} %get-tuple-element.46), channel_id=1, source_target_pairs={{0,1},{1,2},{2,3},{3,0},{4,5},{5,6},{6,7},{7,4},{8,9},{9,10},{10,1... | collective-permute-start | bytes 1572872 | tf_op jit(solution)/shard_map/ppermute | solution.py:22
  110.8 32.1 %collective-permute-start.5 = (bf16[4,32,2048]{2,1,0:T(8,128)(2,1)S(1)}, bf16[4,32,2048]{2,1,0:T(8,128)(2,1)S(1)}, u32[]{:S(2)}, u32[]{:S(2)}) collective-permute-start(bf16[4,32,2048]{2,1,0:T(8,128)(2,1)S(1)} %get-tuple-element.47), channel_id=1, source_target_pairs={{0,2},{1,3},{2,0},{3,1},{4,6},{5,7},{6,4},{7,5},{8,10},{9,11},{10,... | collective-permute-start | bytes 1572872 | tf_op jit(solution)/shard_map/ppermute | solution.py:22
  115.3 27.6 %collective-permute-start.6 = (bf16[4,32,2048]{2,1,0:T(8,128)(2,1)S(1)}, bf16[4,32,2048]{2,1,0:T(8,128)(2,1)S(1)}, u32[]{:S(2)}, u32[]{:S(2)}) collective-permute-start(bf16[4,32,2048]{2,1,0:T(8,128)(2,1)S(1)} %get-tuple-element.48), channel_id=1, source_target_pairs={{0,3},{1,0},{2,1},{3,2},{4,7},{5,4},{6,5},{7,6},{8,11},{9,8},{10,9... | collective-permute-start | bytes 1572872 | tf_op jit(solution)/shard_map/ppermute | solution.py:22
  140.7 28.1 %collective-permute-start.23 = (bf16[4,32,2048]{2,1,0:T(8,128)(2,1)S(1)}, bf16[4,32,2048]{2,1,0:T(8,128)(2,1)S(1)}, u32[]{:S(2)}, u32[]{:S(2)}) collective-permute-start(bf16[4,32,2048]{2,1,0:T(8,128)(2,1)S(1)} %get-tuple-element.66), channel_id=1, source_target_pairs={{0,3},{1,0},{2,1},{3,2},{4,7},{5,4},{6,5},{7,6},{8,11},{9,8},{10,9... | collective-permute-start | bytes 1572872 | tf_op jit(solution)/shard_map/ppermute | solution.py:22
  140.7 29.2 %collective-permute-start.24 = (bf16[4,32,2048]{2,1,0:T(8,128)(2,1)S(1)}, bf16[4,32,2048]{2,1,0:T(8,128)(2,1)S(1)}, u32[]{:S(2)}, u32[]{:S(2)}) collective-permute-start(bf16[4,32,2048]{2,1,0:T(8,128)(2,1)S(1)} %get-tuple-element.67), channel_id=1, source_target_pairs={{0,2},{1,3},{2,0},{3,1},{4,6},{5,7},{6,4},{7,5},{8,10},{9,11},{10,... | collective-permute-start | bytes 1572872 | tf_op jit(solution)/shard_map/ppermute | solution.py:22
  141.6 30.0 %collective-permute-start.25 = (bf16[4,32,2048]{2,1,0:T(8,128)(2,1)S(1)}, bf16[4,32,2048]{2,1,0:T(8,128)(2,1)S(1)}, u32[]{:S(2)}, u32[]{:S(2)}) collective-permute-start(bf16[4,32,2048]{2,1,0:T(8,128)(2,1)S(1)} %get-tuple-element.68), channel_id=1, source_target_pairs={{0,1},{1,2},{2,3},{3,0},{4,5},{5,6},{6,7},{7,4},{8,9},{9,10},{10,1... | collective-permute-start | bytes 1572872 | tf_op jit(solution)/shard_map/ppermute | solution.py:22
  164.5 15.0 %collective-permute-start.14 = (bf16[4,32,2048]{2,1,0:T(8,128)(2,1)S(1)}, bf16[4,32,2048]{2,1,0:T(8,128)(2,1)S(1)}, u32[]{:S(2)}, u32[]{:S(2)}) collective-permute-start(bf16[4,32,2048]{2,1,0:T(8,128)(2,1)S(1)} %get-tuple-element.54), channel_id=1, source_target_pairs={{0,3},{1,0},{2,1},{3,2},{4,7},{5,4},{6,5},{7,6},{8,11},{9,8},{10,9... | collective-permute-start | bytes 1572872 | tf_op jit(solution)/shard_map/ppermute | solution.py:22
  170.0 15.4 %collective-permute-start.32 = (bf16[4,32,2048]{2,1,0:T(8,128)(2,1)S(1)}, bf16[4,32,2048]{2,1,0:T(8,128)(2,1)S(1)}, u32[]{:S(2)}, u32[]{:S(2)}) collective-permute-start(bf16[4,32,2048]{2,1,0:T(8,128)(2,1)S(1)} %get-tuple-element.78), channel_id=1, source_target_pairs={{0,12},{4,0},{8,4},{12,8},{1,13},{5,1},{9,5},{13,9},{2,14},{6,2},{... | collective-permute-start | bytes 1572872 | tf_op jit(solution)/shard_map/ppermute | solution.py:22
  171.6 18.3 %collective-permute-start.33 = (bf16[4,32,2048]{2,1,0:T(8,128)(2,1)S(1)}, bf16[4,32,2048]{2,1,0:T(8,128)(2,1)S(1)}, u32[]{:S(2)}, u32[]{:S(2)}) collective-permute-start(bf16[4,32,2048]{2,1,0:T(8,128)(2,1)S(1)} %get-tuple-element.79), channel_id=1, source_target_pairs={{0,8},{4,12},{8,0},{12,4},{1,9},{5,13},{9,1},{13,5},{2,10},{6,14},... | collective-permute-start | bytes 1572872 | tf_op jit(solution)/shard_map/ppermute | solution.py:22
  179.6 23.9 %collective-permute-start.34 = (bf16[4,32,2048]{2,1,0:T(8,128)(2,1)S(1)}, bf16[4,32,2048]{2,1,0:T(8,128)(2,1)S(1)}, u32[]{:S(2)}, u32[]{:S(2)}) collective-permute-start(bf16[4,32,2048]{2,1,0:T(8,128)(2,1)S(1)} %copy-done.18), channel_id=1, source_target_pairs={{0,4},{4,8},{8,12},{12,0},{1,5},{5,9},{9,13},{13,1},{2,6},{6,10},{... | collective-permute-start | bytes 1572872 | tf_op jit(solution)/shard_map/ppermute | solution.py:22
  182.2 25.7 %collective-permute-start.29 = (bf16[4,32,2048]{2,1,0:T(8,128)(2,1)S(1)}, bf16[4,32,2048]{2,1,0:T(8,128)(2,1)S(1)}, u32[]{:S(2)}, u32[]{:S(2)}) collective-permute-start(bf16[4,32,2048]{2,1,0:T(8,128)(2,1)S(1)} %get-tuple-element.74), channel_id=1, source_target_pairs={{0,12},{4,0},{8,4},{12,8},{1,13},{5,1},{9,5},{13,9},{2,14},{6,2},{... | collective-permute-start | bytes 1572872 | tf_op jit(solution)/shard_map/ppermute | solution.py:22
  183.5 24.3 %collective-permute-start.30 = (bf16[4,32,2048]{2,1,0:T(8,128)(2,1)S(1)}, bf16[4,32,2048]{2,1,0:T(8,128)(2,1)S(1)}, u32[]{:S(2)}, u32[]{:S(2)}) collective-permute-start(bf16[4,32,2048]{2,1,0:T(8,128)(2,1)S(1)} %get-tuple-element.75), channel_id=1, source_target_pairs={{0,8},{4,12},{8,0},{12,4},{1,9},{5,13},{9,1},{13,5},{2,10},{6,14},... | collective-permute-start | bytes 1572872 | tf_op jit(solution)/shard_map/ppermute | solution.py:22
  185.3 40.5 %collective-permute-start.31 = (bf16[4,32,2048]{2,1,0:T(8,128)(2,1)}, bf16[4,32,2048]{2,1,0:T(8,128)(2,1)S(1)}, u32[]{:S(2)}, u32[]{:S(2)}) collective-permute-start(bf16[4,32,2048]{2,1,0:T(8,128)(2,1)} %get-tuple-element.76), channel_id=1, source_target_pairs={{0,4},{4,8},{8,12},{12,0},{1,5},{5,9},{9,13},{13,1},{2,6},{6,10},{... | collective-permute-start | bytes 1572872 | tf_op jit(solution)/shard_map/ppermute | solution.py:22
  189.9 42.2 %collective-permute-start.26 = (bf16[128,2048]{1,0:T(8,128)(2,1)S(1)}, bf16[128,2048]{1,0:T(8,128)(2,1)S(1)}, u32[]{:S(2)}, u32[]{:S(2)}) collective-permute-start(bf16[128,2048]{1,0:T(8,128)(2,1)S(1)} %get-tuple-element.70), channel_id=1, source_target_pairs={{0,12},{4,0},{8,4},{12,8},{1,13},{5,1},{9,5},{13,9},{2,14},{6,2},{... | collective-permute-start | bytes 1572872 | tf_op jit(solution)/shard_map/ppermute | solution.py:22
  203.5 29.6 %collective-permute-start.27 = (bf16[128,2048]{1,0:T(8,128)(2,1)S(1)}, bf16[128,2048]{1,0:T(8,128)(2,1)S(1)}, u32[]{:S(2)}, u32[]{:S(2)}) collective-permute-start(bf16[128,2048]{1,0:T(8,128)(2,1)S(1)} %get-tuple-element.71), channel_id=1, source_target_pairs={{0,8},{4,12},{8,0},{12,4},{1,9},{5,13},{9,1},{13,5},{2,10},{6,14},... | collective-permute-start | bytes 1572872 | tf_op jit(solution)/shard_map/ppermute | solution.py:22
  207.9 25.3 %collective-permute-start.28 = (bf16[128,2048]{1,0:T(8,128)(2,1)S(1)}, bf16[128,2048]{1,0:T(8,128)(2,1)S(1)}, u32[]{:S(2)}, u32[]{:S(2)}) collective-permute-start(bf16[128,2048]{1,0:T(8,128)(2,1)S(1)} %get-tuple-element.72), channel_id=1, source_target_pairs={{0,4},{4,8},{8,12},{12,0},{1,5},{5,9},{9,13},{13,1},{2,6},{6,10},{... | collective-permute-start | bytes 1572872 | tf_op jit(solution)/shard_map/ppermute | solution.py:22
  232.2 16.0 %collective-permute-start.37 = (bf16[128,2048]{1,0:T(8,128)(2,1)S(1)}, bf16[128,2048]{1,0:T(8,128)(2,1)S(1)}, u32[]{:S(2)}, u32[]{:S(2)}) collective-permute-start(bf16[128,2048]{1,0:T(8,128)(2,1)S(1)} %get-tuple-element.84), channel_id=1, source_target_pairs={{0,1},{1,2},{2,3},{3,0},{4,5},{5,6},{6,7},{7,4},{8,9},{9,10},{10,1... | collective-permute-start | bytes 1572872 | tf_op jit(solution)/shard_map/ppermute | solution.py:22
  (30 other events, 282.4 us)

commit v2 on v1

v2 whole, which is shorter than its diff:
```python
import functools

import jax
import jax.numpy as jnp
from jax import lax
from jax.experimental import pallas as pl
from jax.experimental.pallas import tpu as pltpu
from jax.sharding import Mesh, PartitionSpec as P

SIDE = 4
CAP = 64
CHUNKS = 2
ROWS = CAP // CHUNKS
PACK_TILE = 512
FF_TILE = 256
D_TILE = 512
SUM_TILE = 512
VMEM = 36 * 1024 * 1024
TILE = 128


def shift(block, axis, step):
    return lax.ppermute(block, axis, [(i, (i + step) % SIDE) for i in range(SIDE)])


def prepare_kernel(token_ref, id_ref, gate_ref, a_ref, b_ref):
    tokens, depth = token_ref.shape
    half = depth // 2
    top = id_ref.shape[1]
    lane = lax.broadcasted_iota(jnp.int32, (tokens, TILE), 1)
    row = lax.broadcasted_iota(jnp.int32, (tokens, tokens), 0)
    column = lax.broadcasted_iota(jnp.int32, (tokens, tokens), 1)
    ids = [id_ref[:, k : k + 1] for k in range(top)]
    named = jnp.zeros((tokens, TILE), jnp.float32)
    for k in range(top):
        named = named + (ids[k] == lane).astype(jnp.float32)
    before = (column < row).astype(jnp.float32).astype(jnp.bfloat16)
    rank = jnp.dot(before, named.astype(jnp.bfloat16), preferred_element_type=jnp.float32)
    facts = jnp.zeros((tokens, TILE), jnp.float32)
    for k in range(top):
        place = jnp.sum(jnp.where(ids[k] == lane, rank, 0.0), axis=1, keepdims=True)
        facts = jnp.where(lane == k, ids[k].astype(jnp.float32), facts)
        facts = jnp.where(lane == top + k, place, facts)
        rest = gate_ref[:, k : k + 1]
        for part in range(2, 5):
            term = rest.astype(jnp.bfloat16).astype(jnp.float32)
            facts = jnp.where(lane == part * top + k, term, facts)
            rest = rest - term
    facts = facts.astype(jnp.bfloat16)
    a_ref[:, :half] = token_ref[:, :half]
    b_ref[:, :half] = token_ref[:, half:]
    a_ref[:, half:] = facts
    b_ref[:, half:] = facts


def prepare(tokens, expert_ids, gate_values):
    rows, depth = tokens.shape
    out = jax.ShapeDtypeStruct((rows, depth // 2 + TILE), jnp.bfloat16)
    return pl.pallas_call(
        prepare_kernel,
        out_shape=[out, out],
        compiler_params=pltpu.CompilerParams(vmem_limit_bytes=VMEM),
        cost_estimate=pl.CostEstimate(
            flops=2 * rows * rows * TILE, bytes_accessed=4 * rows * depth, transcendentals=0
        ),
    )(tokens, expert_ids, gate_values)


def codes(facts, top):
    facts = facts.astype(jnp.float32)
    return [facts[:, k : k + 1] * CAP + facts[:, top + k : top + k + 1] for k in range(top)]


def targets(experts_ref, chunks, tokens):
    count = len(chunks) * SIDE * ROWS
    lane = lax.broadcasted_iota(jnp.int32, (tokens, count), 1)
    code = jnp.zeros((tokens, count), jnp.int32)
    for n, chunk in enumerate(chunks):
        for dest in range(SIDE):
            low = (n * SIDE + dest) * ROWS
            value = experts_ref[dest] * CAP + chunk * ROWS + lane - low
            code = jnp.where((lane >= low) & (lane < low + ROWS), value, code)
    return code.astype(jnp.float32)


def pack_kernel(chunk, top, experts_ref, *refs):
    sources, facts, outs = refs[:SIDE], refs[SIDE : 2 * SIDE], refs[2 * SIDE :]
    tokens = sources[0].shape[0]
    target = targets(experts_ref, (chunk,), tokens)
    for source in range(SIDE):
        pick = jnp.zeros(target.shape, jnp.float32)
        for code in codes(facts[source][...], top):
            pick = jnp.where(code == target, 1.0, pick)
        rows = jnp.dot(
            pick.T.astype(jnp.bfloat16), sources[source][...], preferred_element_type=jnp.float32
        ).astype(jnp.bfloat16)
        for dest in range(SIDE):
            outs[dest][source] = rows[dest * ROWS : (dest + 1) * ROWS]


def pack(chunk, top, experts, blocks):
    tokens, width = blocks[0].shape
    width -= TILE
    tile = min(PACK_TILE, width)
    last = width // TILE
    out = jax.ShapeDtypeStruct((SIDE, ROWS, width), jnp.bfloat16)
    return pl.pallas_call(
        functools.partial(pack_kernel, chunk, top),
        grid=(width // tile,),
        in_specs=[pl.BlockSpec(memory_space=pltpu.SMEM)]
        + [pl.BlockSpec((tokens, tile), lambda i: (0, i))] * SIDE
        + [pl.BlockSpec((tokens, TILE), lambda i: (0, last))] * SIDE,
        out_specs=[pl.BlockSpec((SIDE, ROWS, tile), lambda i: (0, 0, i))] * SIDE,
        out_shape=[out] * SIDE,
        compiler_params=pltpu.CompilerParams(vmem_limit_bytes=VMEM),
        cost_estimate=pl.CostEstimate(
            flops=2 * SIDE * SIDE * ROWS * tokens * width,
            bytes_accessed=2 * SIDE * width * (tokens + SIDE * ROWS),
            transcendentals=0,
        ),
    )(experts, *blocks, *blocks)


def expert_kernel(n_ff, n_half, wg_ref, wu_ref, wd_ref, *refs):
    a_in, b_in = refs[:SIDE], refs[SIDE : 2 * SIDE]
    a_out, b_out = refs[2 * SIDE : 3 * SIDE], refs[3 * SIDE : 4 * SIDE]
    x_ref, hidden_ref, sems = refs[4 * SIDE :]
    step = pl.program_id(0)
    half = x_ref.shape[-1] // 2
    count = SIDE * SIDE * ROWS

    @pl.when(step == 0)
    def _():
        copies = []
        for k in range(SIDE):
            copies.append(
                pltpu.make_async_copy(a_in[k], x_ref.at[:, k, :, :half], sems.at[k])
            )
            copies.append(
                pltpu.make_async_copy(b_in[k], x_ref.at[k, :, :, half:], sems.at[SIDE + k])
            )
        for copy in copies:
            copy.start()
        for copy in copies:
            copy.wait()

    for f in range(n_ff):

        @pl.when(step == f)
        def _(f=f):
            x = x_ref[...].reshape(count, 2 * half)
            gate = jnp.dot(x, wg_ref[...], preferred_element_type=jnp.float32)
            up = jnp.dot(x, wu_ref[...], preferred_element_type=jnp.float32)
            tile = gate.shape[1]
            hidden = gate / (1.0 + jnp.exp(-gate)) * up
            hidden_ref[:, f * tile : (f + 1) * tile] = hidden.astype(jnp.bfloat16)

    def down():
        out = jnp.dot(hidden_ref[...], wd_ref[...], preferred_element_type=jnp.float32)
        return out.astype(jnp.bfloat16).reshape(SIDE, SIDE, ROWS, out.shape[1])

    @pl.when((step >= n_ff) & (step < n_ff + n_half))
    def _():
        out = down()
        for k in range(SIDE):
            a_out[k][...] = out[:, k]

    @pl.when(step >= n_ff + n_half)
    def _():
        out = down()
        for k in range(SIDE):
            b_out[k][...] = out[k]


def expert(w_gate, w_up, w_down, a_in, b_in):
    half = a_in[0].shape[-1]
    depth, ff = w_gate.shape
    count = SIDE * SIDE * ROWS
    n_ff = ff // FF_TILE
    d_tile = min(D_TILE, half)
    n_half = half // d_tile
    ff_spec = pl.BlockSpec((depth, FF_TILE), lambda i: (0, jnp.minimum(i, n_ff - 1)))
    wd_spec = pl.BlockSpec((ff, d_tile), lambda i: (0, jnp.maximum(i - n_ff, 0)))
    a_spec = pl.BlockSpec(
        (SIDE, ROWS, d_tile), lambda i: (0, 0, jnp.clip(i - n_ff, 0, n_half - 1))
    )
    b_spec = pl.BlockSpec(
        (SIDE, ROWS, d_tile), lambda i: (0, 0, jnp.clip(i - n_ff - n_half, 0, n_half - 1))
    )
    out = jax.ShapeDtypeStruct((SIDE, ROWS, half), jnp.bfloat16)
    done = pl.pallas_call(
        functools.partial(expert_kernel, n_ff, n_half),
        grid=(n_ff + 2 * n_half,),
        in_specs=[ff_spec, ff_spec, wd_spec]
        + [pl.BlockSpec(memory_space=pl.ANY)] * (2 * SIDE),
        out_specs=[a_spec] * SIDE + [b_spec] * SIDE,
        out_shape=[out] * (2 * SIDE),
        scratch_shapes=[
            pltpu.VMEM((SIDE, SIDE, ROWS, depth), jnp.bfloat16),
            pltpu.VMEM((count, ff), jnp.bfloat16),
            pltpu.SemaphoreType.DMA((2 * SIDE,)),
        ],
        compiler_params=pltpu.CompilerParams(vmem_limit_bytes=VMEM),
        cost_estimate=pl.CostEstimate(
            flops=6 * count * depth * ff,
            bytes_accessed=6 * depth * ff + 4 * count * depth,
            transcendentals=count * ff,
        ),
    )(w_gate, w_up, w_down, *a_in, *b_in)
    return done[:SIDE], done[SIDE:]


def sum_kernel(top, experts_ref, *refs):
    count = CHUNKS * SIDE
    ins, facts, outs = refs[:count], refs[count : count + SIDE], refs[count + SIDE :]
    tokens = outs[0].shape[0]
    target = targets(experts_ref, tuple(range(CHUNKS)), tokens)
    for source in range(SIDE):
        about = facts[source][...]
        wide = about.astype(jnp.float32)
        weight = jnp.zeros(target.shape, jnp.float32)
        for k, code in enumerate(codes(about, top)):
            first, second, third = (
                wide[:, part * top + k : part * top + k + 1] for part in range(2, 5)
            )
            weight = jnp.where(code == target, first + second + third, weight)
        high = weight.astype(jnp.bfloat16)
        low = (weight - high.astype(jnp.float32)).astype(jnp.bfloat16)
        rows = jnp.concatenate([ref[source] for ref in ins], axis=0)
        total = jnp.dot(high, rows, preferred_element_type=jnp.float32)
        total = total + jnp.dot(low, rows, preferred_element_type=jnp.float32)
        outs[source][...] = total.astype(jnp.bfloat16)


def sum_rows(top, experts, facts, blocks):
    width = blocks[0].shape[-1]
    tokens = facts[0].shape[0]
    tile = min(SUM_TILE, width)
    last = width // TILE
    out = jax.ShapeDtypeStruct((tokens, width), jnp.bfloat16)
    return pl.pallas_call(
        functools.partial(sum_kernel, top),
        grid=(width // tile,),
        in_specs=[pl.BlockSpec(memory_space=pltpu.SMEM)]
        + [pl.BlockSpec((SIDE, ROWS, tile), lambda i: (0, 0, i))] * len(blocks)
        + [pl.BlockSpec((tokens, TILE), lambda i: (0, last))] * SIDE,
        out_specs=[pl.BlockSpec((tokens, tile), lambda i: (0, i))] * SIDE,
        out_shape=[out] * SIDE,
        compiler_params=pltpu.CompilerParams(vmem_limit_bytes=VMEM),
        cost_estimate=pl.CostEstimate(
            flops=4 * SIDE * SIDE * CAP * tokens * width,
            bytes_accessed=2 * SIDE * width * (tokens + SIDE * CAP),
            transcendentals=0,
        ),
    )(experts, *blocks, *facts)


def local(tokens, expert_ids, gate_values, gate_weight, up_weight, down_weight):
    top = expert_ids.shape[1]
    z, x = lax.axis_index("z"), lax.axis_index("x")
    steps = jnp.arange(SIDE, dtype=jnp.int32)
    a_experts = z * SIDE + (x + steps) % SIDE
    b_experts = (z + steps) % SIDE * SIDE + x

    a_half, b_half = prepare(tokens, expert_ids, gate_values)
    a_rows = [a_half] + [shift(a_half, "z", k) for k in range(1, SIDE)]
    b_rows = [b_half] + [shift(b_half, "x", k) for k in range(1, SIDE)]

    w_gate, w_up, w_down = gate_weight[0], up_weight[0], down_weight[0]
    a_back, b_back = [], []
    for chunk in range(CHUNKS):
        a_out = pack(chunk, top, a_experts, a_rows)
        b_out = pack(chunk, top, b_experts, b_rows)
        a_experts, b_experts, a_out, b_out = lax.optimization_barrier(
            (a_experts, b_experts, a_out, b_out)
        )
        a_in = [a_out[0]] + [shift(a_out[k], "x", k) for k in range(1, SIDE)]
        b_in = [b_out[0]] + [shift(b_out[k], "z", k) for k in range(1, SIDE)]
        a_done, b_done = expert(w_gate, w_up, w_down, a_in, b_in)
        a_back += [a_done[0]] + [shift(a_done[k], "x", -k) for k in range(1, SIDE)]
        b_back += [b_done[0]] + [shift(b_done[k], "z", -k) for k in range(1, SIDE)]

    a_sums = sum_rows(top, a_experts, a_rows, a_back)
    b_sums = sum_rows(top, b_experts, b_rows, b_back)
    a_home = [a_sums[0]] + [shift(a_sums[k], "z", -k) for k in range(1, SIDE)]
    b_home = [b_sums[0]] + [shift(b_sums[k], "x", -k) for k in range(1, SIDE)]
    mixed = [sum(part.astype(jnp.float32) for part in home) for home in (a_home, b_home)]
    return jnp.concatenate(mixed, axis=1).astype(jnp.bfloat16)


def solution(mesh):
    dp = mesh.devices.shape[0]
    grid = Mesh(mesh.devices.reshape(dp, SIDE, SIDE), ("dp", "z", "x"))
    rows, experts = ("dp", "z", "x"), ("z", "x")
    in_specs = (
        P(rows, None),
        P(rows, None),
        P(rows, None),
        P(experts, None, None),
        P(experts, None, None),
        P(experts, None, None),
    )
    return jax.shard_map(
        local, mesh=grid, in_specs=in_specs, out_specs=P(rows, None), check_vma=False
    )
```

time: 250 us -> 227 us (0.908)
  blocking collectives: 29.2 us -> 0 us
  waiting for transfers between devices: 76.2 us -> 100 us
  starting transfers between devices: 65.2 us -> 51.2 us
  local copies, waits for them, and re-layouts: 11.4 us -> 2.81 us
  Pallas kernels: 63.1 us -> 69.8 us
    all_gather x1 -> x0, blocking collectives: 29.2 us -> none  [local(): routing = lax.all_gather(routing, ('z', 'x'), axis=0, tiled=False)]
    ppermute x38 -> x36, waiting for transfers between devices: 76.2 us -> 100 us  [shift(): lax.ppermute(block, axis, [(i, (i + step) % SIDE) for i in range(SIDE)])]
    ppermute x38 -> x36, starting transfers between devices: 65.2 us -> 51.2 us  [shift(): lax.ppermute(block, axis, [(i, (i + step) % SIDE) for i in range(SIDE)])]
    pallas_call x6 -> x7, Pallas kernels: 22 us -> 35.5 us  [the longest x4 19.9 us: pack(): pl.pallas_call(functools.partial(pack_kernel, chunk, top), grid=(width //...]
    pallas_call x2, Pallas kernels: 41.1 us -> 34.3 us  [expert(): pl.pallas_call(functools.partial(expert_kernel, n_ff, n_half), grid=(n_ff...]
    unnamed x48 -> x8, local copies, waits for them, and re-layouts: 7.37 us -> 2.81 us
  transfers between devices with their start and end apart: 38 -> 36, of which waited for: 15 -> 14; matrix products, arithmetic and copies ran while one was open for 2% -> 0% of each run, Pallas kernels for 25% -> 28%
where the time goes in v2:
time: 227 us; the launch traced here: 226 us
  waiting for transfers between devices  100 us (44%)
  Pallas kernels  69.8 us (31%)
  starting transfers between devices  51.2 us (23%)
  local copies, waits for them, and re-layouts  2.81 us (1%)
    ppermute x36, waiting for transfers between devices, shift(): lax.ppermute(block, axis, [(i, (i + step) % SIDE) for i in range(SIDE)])  100 us
    ppermute x36, starting transfers between devices, shift(): lax.ppermute(block, axis, [(i, (i + step) % SIDE) for i in range(SIDE)])  51.2 us
    pallas_call x2, Pallas kernels, expert(): pl.pallas_call(functools.partial(expert_kernel, n_ff, n_half), grid=(n_ff...  34.3 us
    pallas_call x4, Pallas kernels, pack(): pl.pallas_call(functools.partial(pack_kernel, chunk, top), grid=(width //...  19.9 us
    pallas_call x2, Pallas kernels, sum_rows(): pl.pallas_call(functools.partial(sum_kernel, top), grid=(width // tile,),...  15 us
  transfers between devices with their start and end apart: 36, of which 14 were waited for; matrix products, arithmetic and copies ran while one was open for 0% of the time, Pallas kernels for 28%

profile of v2, /device:TPU:0, one launch (start us, length us, event | category | flops | bytes accessed | tf_op | source)
XLA Modules:
  0.0 226.0 jit_solution(2040461028939129616)
XLA Ops:
  3.4 2.9 %collective-permute-start.5 = (bf16[128,2176]{1,0:T(8,128)(2,1)S(1)}, bf16[128,2176]{1,0:T(8,128)(2,1)S(1)}, u32[]{:S(2)}, u32[]{:S(2)}) collective-permute-start(bf16[128,2176]{1,0:T(8,128)(2,1)S(1)} %get-tuple-element.72.refs_0_.refs_4_.refs_8_), channel_id=1, source_target_pairs={{0,3},{1,0},{2,1},{3,2},{4,7},{5,4},{6,5},{7,6},{8,11},{9,8},{10,9... | collective-permute-start | bytes 1671176 | tf_op jit(solution)/shard_map/ppermute | solution.py:23
  8.0 4.0 %collective-permute-start.2 = (bf16[128,2176]{1,0:T(8,128)(2,1)S(1)}, bf16[128,2176]{1,0:T(8,128)(2,1)S(1)}, u32[]{:S(2)}, u32[]{:S(2)}) collective-permute-start(bf16[128,2176]{1,0:T(8,128)(2,1)S(1)} %get-tuple-element.67.refs_0_.refs_4_.refs_8_), channel_id=1, source_target_pairs={{0,12},{4,0},{8,4},{12,8},{1,13},{5,1},{9,5},{13,9},{2,14},{6,2},{... | collective-permute-start | bytes 1671176 | tf_op jit(solution)/shard_map/ppermute | solution.py:23
  12.0 18.1 %collective-permute-done.5.refs_3_.refs_7_.refs_11_ = bf16[128,2176]{1,0:T(8,128)(2,1)S(1)} collective-permute-done((bf16[128,2176]{1,0:T(8,128)(2,1)S(1)}, bf16[128,2176]{1,0:T(8,128)(2,1)S(1)}, u32[]{:S(2)}, u32[]{:S(2)}) %collective-permute-start.5) | collective-permute-done | bytes 557088 | tf_op jit(solution)/shard_map/ppermute | solution.py:23
  30.1 2.0 collective-permute-start
  33.8 4.8 %shard_map.66 = (bf16[4,32,2048]{2,1,0:T(8,128)(2,1)S(1)}, bf16[4,32,2048]{2,1,0:T(8,128)(2,1)S(1)}, bf16[4,32,2048]{2,1,0:T(8,128)(2,1)S(1)}, bf16[4,32,2048]{2,1,0:T(8,128)(2,1)S(1)}) custom-call(s32[4]{0:T(128)S(1)} %get-tuple-element.116.experts_ref, bf16[128,2176]{1,0:T(8,128)(2,1)S(1)} %get-tuple-element.72.refs_0_.refs_4_.refs_8_, ...), custom_call_target="tpu_custom_call" | custom-call | flops 268435456 | bytes 4194304 | tf_op jit(solution)/shard_map/pallas_call | solution.py:107
  38.7 3.1 %collective-permute-done.refs_1_.refs_5_.refs_9_ = bf16[128,2176]{1,0:T(8,128)(2,1)} collective-permute-done((bf16[128,2176]{1,0:T(8,128)(2,1)S(1)}, bf16[128,2176]{1,0:T(8,128)(2,1)}, u32[]{:S(2)}, u32[]{:S(2)}) %collective-permute-start) | collective-permute-done | bytes 557088 | tf_op jit(solution)/shard_map/ppermute | solution.py:23
  41.8 5.2 %shard_map.65 = (bf16[4,32,2048]{2,1,0:T(8,128)(2,1)S(1)}, bf16[4,32,2048]{2,1,0:T(8,128)(2,1)S(1)}, bf16[4,32,2048]{2,1,0:T(8,128)(2,1)S(1)}, bf16[4,32,2048]{2,1,0:T(8,128)(2,1)S(1)}) custom-call(s32[4]{0:T(128)S(1)} %get-tuple-element.87.experts_ref, bf16[128,2176]{1,0:T(8,128)(2,1)S(1)} %get-tuple-element.67.refs_0_.refs_4_.refs_8_, ...), custom_call_target="tpu_custom_call" | custom-call | flops 268435456 | bytes 4194304 | tf_op jit(solution)/shard_map/pallas_call | solution.py:107
  47.1 9.4 %collective-permute-start.7 = (bf16[4,32,2048]{2,1,0:T(8,128)(2,1)S(1)}, bf16[4,32,2048]{2,1,0:T(8,128)(2,1)S(1)}, u32[]{:S(2)}, u32[]{:S(2)}) collective-permute-start(bf16[4,32,2048]{2,1,0:T(8,128)(2,1)S(1)} %get-tuple-element.90), channel_id=1, source_target_pairs={{0,2},{1,3},{2,0},{3,1},{4,6},{5,7},{6,4},{7,5},{8,10},{9,11},{10,... | collective-permute-start | bytes 1572872 | tf_op jit(solution)/shard_map/ppermute | solution.py:23
  56.5 3.2 %collective-permute-start.10 = (bf16[4,32,2048]{2,1,0:T(8,128)(2,1)S(1)}, bf16[4,32,2048]{2,1,0:T(8,128)(2,1)S(1)}, u32[]{:S(2)}, u32[]{:S(2)}) collective-permute-start(bf16[4,32,2048]{2,1,0:T(8,128)(2,1)S(1)} %get-tuple-element.94), channel_id=1, source_target_pairs={{0,8},{4,12},{8,0},{12,4},{1,9},{5,13},{9,1},{13,5},{2,10},{6,14},... | collective-permute-start | bytes 1572872 | tf_op jit(solution)/shard_map/ppermute | solution.py:23
  59.7 5.0 %shard_map.67 = (bf16[4,32,2048]{2,1,0:T(8,128)(2,1)S(1)}, bf16[4,32,2048]{2,1,0:T(8,128)(2,1)S(1)}, bf16[4,32,2048]{2,1,0:T(8,128)(2,1)S(1)}, bf16[4,32,2048]{2,1,0:T(8,128)(2,1)S(1)}) custom-call(s32[4]{0:T(128)S(1)} %get-tuple-element.87.experts_ref, bf16[128,2176]{1,0:T(8,128)(2,1)S(1)} %get-tuple-element.67.refs_0_.refs_4_.refs_8_, ...), custom_call_target="tpu_custom_call" | custom-call | flops 268435456 | bytes 4194304 | tf_op jit(solution)/shard_map/pallas_call | solution.py:107
  64.8 4.9 %shard_map.68 = (bf16[4,32,2048]{2,1,0:T(8,128)(2,1)S(1)}, bf16[4,32,2048]{2,1,0:T(8,128)(2,1)S(1)}, bf16[4,32,2048]{2,1,0:T(8,128)(2,1)S(1)}, bf16[4,32,2048]{2,1,0:T(8,128)(2,1)S(1)}) custom-call(s32[4]{0:T(128)S(1)} %get-tuple-element.116.experts_ref, bf16[128,2176]{1,0:T(8,128)(2,1)S(1)} %get-tuple-element.72.refs_0_.refs_4_.refs_8_, ...), custom_call_target="tpu_custom_call" | custom-call | flops 268435456 | bytes 4194304 | tf_op jit(solution)/shard_map/pallas_call | solution.py:107
  70.6 9.4 %collective-permute-done.7.refs_2_ = bf16[4,32,2048]{2,1,0:T(8,128)(2,1)S(1)} collective-permute-done((bf16[4,32,2048]{2,1,0:T(8,128)(2,1)S(1)}, bf16[4,32,2048]{2,1,0:T(8,128)(2,1)S(1)}, u32[]{:S(2)}, u32[]{:S(2)}) %collective-permute-start.7) | collective-permute-done | bytes 524320 | tf_op jit(solution)/shard_map/ppermute | solution.py:23
  80.7 2.7 %collective-permute-start.17 = (bf16[4,32,2048]{2,1,0:T(8,128)(2,1)S(1)}, bf16[4,32,2048]{2,1,0:T(8,128)(2,1)S(1)}, u32[]{:S(2)}, u32[]{:S(2)}) collective-permute-start(bf16[4,32,2048]{2,1,0:T(8,128)(2,1)S(1)} %get-tuple-element.103), channel_id=1, source_target_pairs={{0,3},{1,0},{2,1},{3,2},{4,7},{5,4},{6,5},{7,6},{8,11},{9,8},{10,9... | collective-permute-start | bytes 1572872 | tf_op jit(solution)/shard_map/ppermute | solution.py:23
  83.4 3.2 %collective-permute-start.19 = (bf16[4,32,2048]{2,1,0:T(8,128)(2,1)S(1)}, bf16[4,32,2048]{2,1,0:T(8,128)(2,1)S(1)}, u32[]{:S(2)}, u32[]{:S(2)}) collective-permute-start(bf16[4,32,2048]{2,1,0:T(8,128)(2,1)S(1)} %get-tuple-element.106), channel_id=1, source_target_pairs={{0,8},{4,12},{8,0},{12,4},{1,9},{5,13},{9,1},{13,5},{2,10},{6,14},... | collective-permute-start | bytes 1572872 | tf_op jit(solution)/shard_map/ppermute | solution.py:23
  86.6 15.6 %collective-permute-done.15.refs_1_ = bf16[4,32,2048]{2,1,0:T(8,128)(2,1)S(1)} collective-permute-done((bf16[4,32,2048]{2,1,0:T(8,128)(2,1)S(1)}, bf16[4,32,2048]{2,1,0:T(8,128)(2,1)S(1)}, u32[]{:S(2)}, u32[]{:S(2)}) %collective-permute-start.15) | collective-permute-done | bytes 524320 | tf_op jit(solution)/shard_map/ppermute | solution.py:23
  103.6 17.2 %shard_map.69 = (bf16[4,32,2048]{2,1,0:T(8,128)(2,1)S(1)}, bf16[4,32,2048]{2,1,0:T(8,128)(2,1)S(1)}, bf16[4,32,2048]{2,1,0:T(8,128)(2,1)S(1)}, bf16[4,32,2048]{2...) custom-call(bf16[4096,768]{1,0:T(8,128)(2,1)S(1)} %bitcast.5, ...), custom_call_target="tpu_custom_call" | custom-call | flops 9663676416 | bytes 27262976 | tf_op jit(solution)/shard_map/pallas_call | solution.py:191
  121.0 2.0 collective-permute-start.14
  123.2 17.2 %shard_map.70 = (bf16[4,32,2048]{2,1,0:T(8,128)(2,1)S(1)}, bf16[4,32,2048]{2,1,0:T(8,128)(2,1)S(1)}, bf16[4,32,2048]{2,1,0:T(8,128)(2,1)S(1)}, bf16[4,32,2048]{2...) custom-call(bf16[4096,768]{1,0:T(8,128)(2,1)S(1)} %bitcast.6, ...), custom_call_target="tpu_custom_call" | custom-call | flops 9663676416 | bytes 27262976 | tf_op jit(solution)/shard_map/pallas_call | solution.py:191
  140.4 3.0 %collective-permute-start.21 = (bf16[4,32,2048]{2,1,0:T(8,128)(2,1)S(1)}, bf16[4,32,2048]{2,1,0:T(8,128)(2,1)S(1)}, u32[]{:S(2)}, u32[]{:S(2)}) collective-permute-start(bf16[4,32,2048]{2,1,0:T(8,128)(2,1)S(1)} %get-tuple-element.109), channel_id=1, source_target_pairs={{0,3},{1,0},{2,1},{3,2},{4,7},{5,4},{6,5},{7,6},{8,11},{9,8},{10,9... | collective-permute-start | bytes 1572872 | tf_op jit(solution)/shard_map/ppermute | solution.py:23
  145.9 2.5 %collective-permute-done.14.refs_3_ = bf16[4,32,2048]{2,1,0:T(8,128)(2,1)S(1)} collective-permute-done((bf16[4,32,2048]{2,1,0:T(8,128)(2,1)S(1)}, bf16[4,32,2048]{2,1,0:T(8,128)(2,1)S(1)}, u32[]{:S(2)}, u32[]{:S(2)}) %collective-permute-start.14) | collective-permute-done | bytes 524320 | tf_op jit(solution)/shard_map/ppermute | solution.py:23
  149.6 8.3 %collective-permute-done.21.refs_5_ = bf16[4,32,2048]{2,1,0:T(8,128)(2,1)S(1)} collective-permute-done((bf16[4,32,2048]{2,1,0:T(8,128)(2,1)S(1)}, bf16[4,32,2048]{2,1,0:T(8,128)(2,1)S(1)}, u32[]{:S(2)}, u32[]{:S(2)}) %collective-permute-start.21) | collective-permute-done | bytes 524320 | tf_op jit(solution)/shard_map/ppermute | solution.py:23
  158.1 2.4 %collective-permute-start.31 = (bf16[4,32,2048]{2,1,0:T(8,128)(2,1)S(1)}, bf16[4,32,2048]{2,1,0:T(8,128)(2,1)S(1)}, u32[]{:S(2)}, u32[]{:S(2)}) collective-permute-start(bf16[4,32,2048]{2,1,0:T(8,128)(2,1)S(1)} %get-tuple-element.123), channel_id=1, source_target_pairs={{0,8},{4,12},{8,0},{12,4},{1,9},{5,13},{9,1},{13,5},{2,10},{6,14},... | collective-permute-start | bytes 1572872 | tf_op jit(solution)/shard_map/ppermute | solution.py:23
  161.5 7.6 %shard_map.71 = (bf16[128,2048]{1,0:T(8,128)(2,1)S(1)}, bf16[128,2048]{1,0:T(8,128)(2,1)S(1)}, bf16[128,2048]{1,0:T(8,128)(2,1)S(1)}, bf16[128,2048]{1,0:T(8,128)(2,1)S(1)}) custom-call(s32[4]{0:T(128)S(1)} %get-tuple-element.87.experts_ref, bf16[4,32,2048]{2,1,0:T(8,128)(2,1)S(1)} %get-tuple-element.96.refs_0_, ...), custom_call_target="tpu_custom_call" | custom-call | flops 1073741824 | bytes 6291456 | tf_op jit(solution)/shard_map/pallas_call | solution.py:241
  169.1 2.3 %collective-permute-start.24 = (bf16[128,2048]{1,0:T(8,128)(2,1)S(1)}, bf16[128,2048]{1,0:T(8,128)(2,1)S(1)}, u32[]{:S(2)}, u32[]{:S(2)}) collective-permute-start(bf16[128,2048]{1,0:T(8,128)(2,1)S(1)} %get-tuple-element.113), channel_id=1, source_target_pairs={{0,12},{4,0},{8,4},{12,8},{1,13},{5,1},{9,5},{13,9},{2,14},{6,2},{... | collective-permute-start | bytes 1572872 | tf_op jit(solution)/shard_map/ppermute | solution.py:23
  171.4 7.2 %collective-permute-done.29.refs_3_ = bf16[4,32,2048]{2,1,0:T(8,128)(2,1)S(1)} collective-permute-done((bf16[4,32,2048]{2,1,0:T(8,128)(2,1)S(1)}, bf16[4,32,2048]{2,1,0:T(8,128)(2,1)S(1)}, u32[]{:S(2)}, u32[]{:S(2)}) %collective-permute-start.29) | collective-permute-done | bytes 524320 | tf_op jit(solution)/shard_map/ppermute | solution.py:23
  178.7 2.4 %collective-permute-done.30.refs_5_ = bf16[4,32,2048]{2,1,0:T(8,128)(2,1)S(1)} collective-permute-done((bf16[4,32,2048]{2,1,0:T(8,128)(2,1)S(1)}, bf16[4,32,2048]{2,1,0:T(8,128)(2,1)S(1)}, u32[]{:S(2)}, u32[]{:S(2)}) %collective-permute-start.30) | collective-permute-done | bytes 524320 | tf_op jit(solution)/shard_map/ppermute | solution.py:23
  181.1 2.7 %collective-permute-done.31.refs_6_ = bf16[4,32,2048]{2,1,0:T(8,128)(2,1)S(1)} collective-permute-done((bf16[4,32,2048]{2,1,0:T(8,128)(2,1)S(1)}, bf16[4,32,2048]{2,1,0:T(8,128)(2,1)S(1)}, u32[]{:S(2)}, u32[]{:S(2)}) %collective-permute-start.31) | collective-permute-done | bytes 524320 | tf_op jit(solution)/shard_map/ppermute | solution.py:23
  183.8 13.6 %collective-permute-done.32.refs_7_ = bf16[4,32,2048]{2,1,0:T(8,128)(2,1)S(1)} collective-permute-done((bf16[4,32,2048]{2,1,0:T(8,128)(2,1)S(1)}, bf16[4,32,2048]{2,1,0:T(8,128)(2,1)S(1)}, u32[]{:S(2)}, u32[]{:S(2)}) %collective-permute-start.32) | collective-permute-done | bytes 524320 | tf_op jit(solution)/shard_map/ppermute | solution.py:23
  197.4 7.4 %shard_map.72 = (bf16[128,2048]{1,0:T(8,128)(2,1)S(1)}, bf16[128,2048]{1,0:T(8,128)(2,1)S(1)}, bf16[128,2048]{1,0:T(8,128)(2,1)S(1)}, bf16[128,2048]{1,0:T(8,128)(2,1)S(1)}) custom-call(s32[4]{0:T(128)S(1)} %get-tuple-element.116.experts_ref, bf16[4,32,2048]{2,1,0:T(8,128)(2,1)S(1)} %get-tuple-element.117.refs_0_, ...), custom_call_target="tpu_custom_call" | custom-call | flops 1073741824 | bytes 6291456 | tf_op jit(solution)/shard_map/pallas_call | solution.py:241
  204.9 3.7 %collective-permute-start.33 = (bf16[128,2048]{1,0:T(8,128)(2,1)S(1)}, bf16[128,2048]{1,0:T(8,128)(2,1)S(1)}, u32[]{:S(2)}, u32[]{:S(2)}) collective-permute-start(bf16[128,2048]{1,0:T(8,128)(2,1)S(1)} %get-tuple-element.126), channel_id=1, source_target_pairs={{0,3},{1,0},{2,1},{3,2},{4,7},{5,4},{6,5},{7,6},{8,11},{9,8},{10,9... | collective-permute-start | bytes 1572872 | tf_op jit(solution)/shard_map/ppermute | solution.py:23
  209.8 11.0 %collective-permute-done.33 = bf16[128,2048]{1,0:T(8,128)(2,1)S(1)} collective-permute-done((bf16[128,2048]{1,0:T(8,128)(2,1)S(1)}, bf16[128,2048]{1,0:T(8,128)(2,1)S(1)}, u32[]{:S(2)}, u32[]{:S(2)}) %collective-permute-start.33) | collective-permute-done | bytes 524320 | tf_op jit(solution)/shard_map/ppermute | solution.py:23
  220.9 3.7 %collective-permute-done.35 = bf16[128,2048]{1,0:T(8,128)(2,1)S(1)} collective-permute-done((bf16[128,2048]{1,0:T(8,128)(2,1)S(1)}, bf16[128,2048]{1,0:T(8,128)(2,1)S(1)}, u32[]{:S(2)}, u32[]{:S(2)}) %collective-permute-start.35) | collective-permute-done | bytes 524320 | tf_op jit(solution)/shard_map/ppermute | solution.py:23
  (62 shorter events, 18.0 us)
Async XLA Ops:
  3.4 26.7 %collective-permute-start.5 = (bf16[128,2176]{1,0:T(8,128)(2,1)S(1)}, bf16[128,2176]{1,0:T(8,128)(2,1)S(1)}, u32[]{:S(2)}, u32[]{:S(2)}) collective-permute-start(bf16[128,2176]{1,0:T(8,128)(2,1)S(1)} %get-tuple-element.72.refs_0_.refs_4_.refs_8_), channel_id=1, source_target_pairs={{0,3},{1,0},{2,1},{3,2},{4,7},{5,4},{6,5},{7,6},{8,11},{9,8},{10,9... | collective-permute-start | bytes 1671176 | tf_op jit(solution)/shard_map/ppermute | solution.py:23
  6.3 25.8 %collective-permute-start.4 = (bf16[128,2176]{1,0:T(8,128)(2,1)S(1)}, bf16[128,2176]{1,0:T(8,128)(2,1)S(1)}, u32[]{:S(2)}, u32[]{:S(2)}) collective-permute-start(bf16[128,2176]{1,0:T(8,128)(2,1)S(1)} %get-tuple-element.72.refs_0_.refs_4_.refs_8_), channel_id=1, source_target_pairs={{0,2},{1,3},{2,0},{3,1},{4,6},{5,7},{6,4},{7,5},{8,10},{9,11},{10,... | collective-permute-start | bytes 1671176 | tf_op jit(solution)/shard_map/ppermute | solution.py:23
  7.1 26.7 %collective-permute-start.3 = (bf16[128,2176]{1,0:T(8,128)(2,1)S(1)}, bf16[128,2176]{1,0:T(8,128)(2,1)S(1)}, u32[]{:S(2)}, u32[]{:S(2)}) collective-permute-start(bf16[128,2176]{1,0:T(8,128)(2,1)S(1)} %get-tuple-element.72.refs_0_.refs_4_.refs_8_), channel_id=1, source_target_pairs={{0,1},{1,2},{2,3},{3,0},{4,5},{5,6},{6,7},{7,4},{8,9},{9,10},{10,1... | collective-permute-start | bytes 1671176 | tf_op jit(solution)/shard_map/ppermute | solution.py:23
  8.0 30.7 %collective-permute-start.2 = (bf16[128,2176]{1,0:T(8,128)(2,1)S(1)}, bf16[128,2176]{1,0:T(8,128)(2,1)S(1)}, u32[]{:S(2)}, u32[]{:S(2)}) collective-permute-start(bf16[128,2176]{1,0:T(8,128)(2,1)S(1)} %get-tuple-element.67.refs_0_.refs_4_.refs_8_), channel_id=1, source_target_pairs={{0,12},{4,0},{8,4},{12,8},{1,13},{5,1},{9,5},{13,9},{2,14},{6,2},{... | collective-permute-start | bytes 1671176 | tf_op jit(solution)/shard_map/ppermute | solution.py:23
  12.0 26.6 %collective-permute-start.1 = (bf16[128,2176]{1,0:T(8,128)(2,1)S(1)}, bf16[128,2176]{1,0:T(8,128)(2,1)}, u32[]{:S(2)}, u32[]{:S(2)}) collective-permute-start(bf16[128,2176]{1,0:T(8,128)(2,1)S(1)} %get-tuple-element.67.refs_0_.refs_4_.refs_8_), channel_id=1, source_target_pairs={{0,8},{4,12},{8,0},{12,4},{1,9},{5,13},{9,1},{13,5},{2,10},{6,14},... | collective-permute-start | bytes 1671176 | tf_op jit(solution)/shard_map/ppermute | solution.py:23
  47.0 22.6 %collective-permute-start.6 = (bf16[4,32,2048]{2,1,0:T(8,128)(2,1)S(1)}, bf16[4,32,2048]{2,1,0:T(8,128)(2,1)S(1)}, u32[]{:S(2)}, u32[]{:S(2)}) collective-permute-start(bf16[4,32,2048]{2,1,0:T(8,128)(2,1)S(1)} %get-tuple-element.89), channel_id=1, source_target_pairs={{0,1},{1,2},{2,3},{3,0},{4,5},{5,6},{6,7},{7,4},{8,9},{9,10},{10,1... | collective-permute-start | bytes 1572872 | tf_op jit(solution)/shard_map/ppermute | solution.py:23
  47.1 32.9 %collective-permute-start.7 = (bf16[4,32,2048]{2,1,0:T(8,128)(2,1)S(1)}, bf16[4,32,2048]{2,1,0:T(8,128)(2,1)S(1)}, u32[]{:S(2)}, u32[]{:S(2)}) collective-permute-start(bf16[4,32,2048]{2,1,0:T(8,128)(2,1)S(1)} %get-tuple-element.90), channel_id=1, source_target_pairs={{0,2},{1,3},{2,0},{3,1},{4,6},{5,7},{6,4},{7,5},{8,10},{9,11},{10,... | collective-permute-start | bytes 1572872 | tf_op jit(solution)/shard_map/ppermute | solution.py:23
  56.5 23.5 %collective-permute-start.8 = (bf16[4,32,2048]{2,1,0:T(8,128)(2,1)S(1)}, bf16[4,32,2048]{2,1,0:T(8,128)(2,1)S(1)}, u32[]{:S(2)}, u32[]{:S(2)}) collective-permute-start(bf16[4,32,2048]{2,1,0:T(8,128)(2,1)S(1)} %get-tuple-element.91), channel_id=1, source_target_pairs={{0,3},{1,0},{2,1},{3,2},{4,7},{5,4},{6,5},{7,6},{8,11},{9,8},{10,9... | collective-permute-start | bytes 1572872 | tf_op jit(solution)/shard_map/ppermute | solution.py:23
  56.5 24.1 %collective-permute-start.9 = (bf16[4,32,2048]{2,1,0:T(8,128)(2,1)S(1)}, bf16[4,32,2048]{2,1,0:T(8,128)(2,1)S(1)}, u32[]{:S(2)}, u32[]{:S(2)}) collective-permute-start(bf16[4,32,2048]{2,1,0:T(8,128)(2,1)S(1)} %get-tuple-element.93), channel_id=1, source_target_pairs={{0,4},{4,8},{8,12},{12,0},{1,5},{5,9},{9,13},{13,1},{2,6},{6,10},{... | collective-permute-start | bytes 1572872 | tf_op jit(solution)/shard_map/ppermute | solution.py:23
  56.5 26.8 %collective-permute-start.10 = (bf16[4,32,2048]{2,1,0:T(8,128)(2,1)S(1)}, bf16[4,32,2048]{2,1,0:T(8,128)(2,1)S(1)}, u32[]{:S(2)}, u32[]{:S(2)}) collective-permute-start(bf16[4,32,2048]{2,1,0:T(8,128)(2,1)S(1)} %get-tuple-element.94), channel_id=1, source_target_pairs={{0,8},{4,12},{8,0},{12,4},{1,9},{5,13},{9,1},{13,5},{2,10},{6,14},... | collective-permute-start | bytes 1572872 | tf_op jit(solution)/shard_map/ppermute | solution.py:23
  80.0 22.1 %collective-permute-start.15 = (bf16[4,32,2048]{2,1,0:T(8,128)(2,1)S(1)}, bf16[4,32,2048]{2,1,0:T(8,128)(2,1)S(1)}, u32[]{:S(2)}, u32[]{:S(2)}) collective-permute-start(bf16[4,32,2048]{2,1,0:T(8,128)(2,1)S(1)} %get-tuple-element.101), channel_id=1, source_target_pairs={{0,1},{1,2},{2,3},{3,0},{4,5},{5,6},{6,7},{7,4},{8,9},{9,10},{10,1... | collective-permute-start | bytes 1572872 | tf_op jit(solution)/shard_map/ppermute | solution.py:23
  80.0 40.8 %collective-permute-start.16 = (bf16[4,32,2048]{2,1,0:T(8,128)(2,1)S(1)}, bf16[4,32,2048]{2,1,0:T(8,128)(2,1)S(1)}, u32[]{:S(2)}, u32[]{:S(2)}) collective-permute-start(bf16[4,32,2048]{2,1,0:T(8,128)(2,1)S(1)} %get-tuple-element.102), channel_id=1, source_target_pairs={{0,2},{1,3},{2,0},{3,1},{4,6},{5,7},{6,4},{7,5},{8,10},{9,11},{10,... | collective-permute-start | bytes 1572872 | tf_op jit(solution)/shard_map/ppermute | solution.py:23
  80.7 40.2 %collective-permute-start.17 = (bf16[4,32,2048]{2,1,0:T(8,128)(2,1)S(1)}, bf16[4,32,2048]{2,1,0:T(8,128)(2,1)S(1)}, u32[]{:S(2)}, u32[]{:S(2)}) collective-permute-start(bf16[4,32,2048]{2,1,0:T(8,128)(2,1)S(1)} %get-tuple-element.103), channel_id=1, source_target_pairs={{0,3},{1,0},{2,1},{3,2},{4,7},{5,4},{6,5},{7,6},{8,11},{9,8},{10,9... | collective-permute-start | bytes 1572872 | tf_op jit(solution)/shard_map/ppermute | solution.py:23
  83.4 37.7 %collective-permute-start.18 = (bf16[4,32,2048]{2,1,0:T(8,128)(2,1)S(1)}, bf16[4,32,2048]{2,1,0:T(8,128)(2,1)S(1)}, u32[]{:S(2)}, u32[]{:S(2)}) collective-permute-start(bf16[4,32,2048]{2,1,0:T(8,128)(2,1)S(1)} %get-tuple-element.105), channel_id=1, source_target_pairs={{0,4},{4,8},{8,12},{12,0},{1,5},{5,9},{9,13},{13,1},{2,6},{6,10},{... | collective-permute-start | bytes 1572872 | tf_op jit(solution)/shard_map/ppermute | solution.py:23
  83.4 39.6 %collective-permute-start.19 = (bf16[4,32,2048]{2,1,0:T(8,128)(2,1)S(1)}, bf16[4,32,2048]{2,1,0:T(8,128)(2,1)S(1)}, u32[]{:S(2)}, u32[]{:S(2)}) collective-permute-start(bf16[4,32,2048]{2,1,0:T(8,128)(2,1)S(1)} %get-tuple-element.106), channel_id=1, source_target_pairs={{0,8},{4,12},{8,0},{12,4},{1,9},{5,13},{9,1},{13,5},{2,10},{6,14},... | collective-permute-start | bytes 1572872 | tf_op jit(solution)/shard_map/ppermute | solution.py:23
  102.1 21.1 %collective-permute-start.20 = (bf16[4,32,2048]{2,1,0:T(8,128)(2,1)S(1)}, bf16[4,32,2048]{2,1,0:T(8,128)(2,1)S(1)}, u32[]{:S(2)}, u32[]{:S(2)}) collective-permute-start(bf16[4,32,2048]{2,1,0:T(8,128)(2,1)S(1)} %get-tuple-element.107), channel_id=1, source_target_pairs={{0,12},{4,0},{8,4},{12,8},{1,13},{5,1},{9,5},{13,9},{2,14},{6,2},{... | collective-permute-start | bytes 1572872 | tf_op jit(solution)/shard_map/ppermute | solution.py:23
  120.8 22.5 %collective-permute-start.12 = (bf16[4,32,2048]{2,1,0:T(8,128)(2,1)S(1)}, bf16[4,32,2048]{2,1,0:T(8,128)(2,1)S(1)}, u32[]{:S(2)}, u32[]{:S(2)}) collective-permute-start(bf16[4,32,2048]{2,1,0:T(8,128)(2,1)S(1)} %get-tuple-element.97), channel_id=1, source_target_pairs={{0,3},{1,0},{2,1},{3,2},{4,7},{5,4},{6,5},{7,6},{8,11},{9,8},{10,9... | collective-permute-start | bytes 1572872 | tf_op jit(solution)/shard_map/ppermute | solution.py:23
  120.9 23.7 %collective-permute-start.13 = (bf16[4,32,2048]{2,1,0:T(8,128)(2,1)S(1)}, bf16[4,32,2048]{2,1,0:T(8,128)(2,1)S(1)}, u32[]{:S(2)}, u32[]{:S(2)}) collective-permute-start(bf16[4,32,2048]{2,1,0:T(8,128)(2,1)S(1)} %get-tuple-element.98), channel_id=1, source_target_pairs={{0,2},{1,3},{2,0},{3,1},{4,6},{5,7},{6,4},{7,5},{8,10},{9,11},{10,... | collective-permute-start | bytes 1572872 | tf_op jit(solution)/shard_map/ppermute | solution.py:23
  121.0 27.4 %collective-permute-start.14 = (bf16[4,32,2048]{2,1,0:T(8,128)(2,1)S(1)}, bf16[4,32,2048]{2,1,0:T(8,128)(2,1)S(1)}, u32[]{:S(2)}, u32[]{:S(2)}) collective-permute-start(bf16[4,32,2048]{2,1,0:T(8,128)(2,1)S(1)} %get-tuple-element.99), channel_id=1, source_target_pairs={{0,1},{1,2},{2,3},{3,0},{4,5},{5,6},{6,7},{7,4},{8,9},{9,10},{10,1... | collective-permute-start | bytes 1572872 | tf_op jit(solution)/shard_map/ppermute | solution.py:23
  123.0 25.4 %collective-permute-start.27 = (bf16[4,32,2048]{2,1,0:T(8,128)(2,1)S(1)}, bf16[4,32,2048]{2,1,0:T(8,128)(2,1)S(1)}, u32[]{:S(2)}, u32[]{:S(2)}) collective-permute-start(bf16[4,32,2048]{2,1,0:T(8,128)(2,1)S(1)} %get-tuple-element.118), channel_id=1, source_target_pairs={{0,12},{4,0},{8,4},{12,8},{1,13},{5,1},{9,5},{13,9},{2,14},{6,2},{... | collective-permute-start | bytes 1572872 | tf_op jit(solution)/shard_map/ppermute | solution.py:23
  140.4 17.5 %collective-permute-start.21 = (bf16[4,32,2048]{2,1,0:T(8,128)(2,1)S(1)}, bf16[4,32,2048]{2,1,0:T(8,128)(2,1)S(1)}, u32[]{:S(2)}, u32[]{:S(2)}) collective-permute-start(bf16[4,32,2048]{2,1,0:T(8,128)(2,1)S(1)} %get-tuple-element.109), channel_id=1, source_target_pairs={{0,3},{1,0},{2,1},{3,2},{4,7},{5,4},{6,5},{7,6},{8,11},{9,8},{10,9... | collective-permute-start | bytes 1572872 | tf_op jit(solution)/shard_map/ppermute | solution.py:23
  144.6 15.9 %collective-permute-start.23 = (bf16[4,32,2048]{2,1,0:T(8,128)(2,1)S(1)}, bf16[4,32,2048]{2,1,0:T(8,128)(2,1)S(1)}, u32[]{:S(2)}, u32[]{:S(2)}) collective-permute-start(bf16[4,32,2048]{2,1,0:T(8,128)(2,1)S(1)} %get-tuple-element.111), channel_id=1, source_target_pairs={{0,1},{1,2},{2,3},{3,0},{4,5},{5,6},{6,7},{7,4},{8,9},{9,10},{10,1... | collective-permute-start | bytes 1572872 | tf_op jit(solution)/shard_map/ppermute | solution.py:23
  148.4 20.7 %collective-permute-start.28 = (bf16[4,32,2048]{2,1,0:T(8,128)(2,1)S(1)}, bf16[4,32,2048]{2,1,0:T(8,128)(2,1)S(1)}, u32[]{:S(2)}, u32[]{:S(2)}) collective-permute-start(bf16[4,32,2048]{2,1,0:T(8,128)(2,1)S(1)} %get-tuple-element.119), channel_id=1, source_target_pairs={{0,8},{4,12},{8,0},{12,4},{1,9},{5,13},{9,1},{13,5},{2,10},{6,14},... | collective-permute-start | bytes 1572872 | tf_op jit(solution)/shard_map/ppermute | solution.py:23
  148.4 30.2 %collective-permute-start.29 = (bf16[4,32,2048]{2,1,0:T(8,128)(2,1)S(1)}, bf16[4,32,2048]{2,1,0:T(8,128)(2,1)S(1)}, u32[]{:S(2)}, u32[]{:S(2)}) collective-permute-start(bf16[4,32,2048]{2,1,0:T(8,128)(2,1)S(1)} %get-tuple-element.120), channel_id=1, source_target_pairs={{0,4},{4,8},{8,12},{12,0},{1,5},{5,9},{9,13},{13,1},{2,6},{6,10},{... | collective-permute-start | bytes 1572872 | tf_op jit(solution)/shard_map/ppermute | solution.py:23
  157.9 23.3 %collective-permute-start.30 = (bf16[4,32,2048]{2,1,0:T(8,128)(2,1)S(1)}, bf16[4,32,2048]{2,1,0:T(8,128)(2,1)S(1)}, u32[]{:S(2)}, u32[]{:S(2)}) collective-permute-start(bf16[4,32,2048]{2,1,0:T(8,128)(2,1)S(1)} %get-tuple-element.122), channel_id=1, source_target_pairs={{0,12},{4,0},{8,4},{12,8},{1,13},{5,1},{9,5},{13,9},{2,14},{6,2},{... | collective-permute-start | bytes 1572872 | tf_op jit(solution)/shard_map/ppermute | solution.py:23
  158.1 25.8 %collective-permute-start.31 = (bf16[4,32,2048]{2,1,0:T(8,128)(2,1)S(1)}, bf16[4,32,2048]{2,1,0:T(8,128)(2,1)S(1)}, u32[]{:S(2)}, u32[]{:S(2)}) collective-permute-start(bf16[4,32,2048]{2,1,0:T(8,128)(2,1)S(1)} %get-tuple-element.123), channel_id=1, source_target_pairs={{0,8},{4,12},{8,0},{12,4},{1,9},{5,13},{9,1},{13,5},{2,10},{6,14},... | collective-permute-start | bytes 1572872 | tf_op jit(solution)/shard_map/ppermute | solution.py:23
  160.5 37.0 %collective-permute-start.32 = (bf16[4,32,2048]{2,1,0:T(8,128)(2,1)S(1)}, bf16[4,32,2048]{2,1,0:T(8,128)(2,1)S(1)}, u32[]{:S(2)}, u32[]{:S(2)}) collective-permute-start(bf16[4,32,2048]{2,1,0:T(8,128)(2,1)S(1)} %get-tuple-element.124), channel_id=1, source_target_pairs={{0,4},{4,8},{8,12},{12,0},{1,5},{5,9},{9,13},{13,1},{2,6},{6,10},{... | collective-permute-start | bytes 1572872 | tf_op jit(solution)/shard_map/ppermute | solution.py:23
  169.1 39.4 %collective-permute-start.24 = (bf16[128,2048]{1,0:T(8,128)(2,1)S(1)}, bf16[128,2048]{1,0:T(8,128)(2,1)S(1)}, u32[]{:S(2)}, u32[]{:S(2)}) collective-permute-start(bf16[128,2048]{1,0:T(8,128)(2,1)S(1)} %get-tuple-element.113), channel_id=1, source_target_pairs={{0,12},{4,0},{8,4},{12,8},{1,13},{5,1},{9,5},{13,9},{2,14},{6,2},{... | collective-permute-start | bytes 1572872 | tf_op jit(solution)/shard_map/ppermute | solution.py:23
  178.7 30.8 %collective-permute-start.25 = (bf16[128,2048]{1,0:T(8,128)(2,1)S(1)}, bf16[128,2048]{1,0:T(8,128)(2,1)S(1)}, u32[]{:S(2)}, u32[]{:S(2)}) collective-permute-start(bf16[128,2048]{1,0:T(8,128)(2,1)S(1)} %get-tuple-element.114), channel_id=1, source_target_pairs={{0,8},{4,12},{8,0},{12,4},{1,9},{5,13},{9,1},{13,5},{2,10},{6,14},... | collective-permute-start | bytes 1572872 | tf_op jit(solution)/shard_map/ppermute | solution.py:23
  181.1 28.4 %collective-permute-start.26 = (bf16[128,2048]{1,0:T(8,128)(2,1)S(1)}, bf16[128,2048]{1,0:T(8,128)(2,1)S(1)}, u32[]{:S(2)}, u32[]{:S(2)}) collective-permute-start(bf16[128,2048]{1,0:T(8,128)(2,1)S(1)} %get-tuple-element.115), channel_id=1, source_target_pairs={{0,4},{4,8},{8,12},{12,0},{1,5},{5,9},{9,13},{13,1},{2,6},{6,10},{... | collective-permute-start | bytes 1572872 | tf_op jit(solution)/shard_map/ppermute | solution.py:23
  204.9 16.0 %collective-permute-start.33 = (bf16[128,2048]{1,0:T(8,128)(2,1)S(1)}, bf16[128,2048]{1,0:T(8,128)(2,1)S(1)}, u32[]{:S(2)}, u32[]{:S(2)}) collective-permute-start(bf16[128,2048]{1,0:T(8,128)(2,1)S(1)} %get-tuple-element.126), channel_id=1, source_target_pairs={{0,3},{1,0},{2,1},{3,2},{4,7},{5,4},{6,5},{7,6},{8,11},{9,8},{10,9... | collective-permute-start | bytes 1572872 | tf_op jit(solution)/shard_map/ppermute | solution.py:23
  208.6 16.0 %collective-permute-start.35 = (bf16[128,2048]{1,0:T(8,128)(2,1)S(1)}, bf16[128,2048]{1,0:T(8,128)(2,1)S(1)}, u32[]{:S(2)}, u32[]{:S(2)}) collective-permute-start(bf16[128,2048]{1,0:T(8,128)(2,1)S(1)} %get-tuple-element.128), channel_id=1, source_target_pairs={{0,1},{1,2},{2,3},{3,0},{4,5},{5,6},{6,7},{7,4},{8,9},{9,10},{10,1... | collective-permute-start | bytes 1572872 | tf_op jit(solution)/shard_map/ppermute | solution.py:23
  (7 other events, 172.1 us)

commit v3 on v2

--- a/solution.py
+++ b/solution.py
@@ -11,12 +11,12 @@
 CAP = 64
 CHUNKS = 2
 ROWS = CAP // CHUNKS
+TILE = 128
 PACK_TILE = 512
 FF_TILE = 256
-D_TILE = 512
+D_TILE = 1024
 SUM_TILE = 512
 VMEM = 36 * 1024 * 1024
-TILE = 128
 
 
 def shift(block, axis, step):
@@ -26,22 +26,24 @@
 def prepare_kernel(token_ref, id_ref, gate_ref, a_ref, b_ref):
     tokens, depth = token_ref.shape
     half = depth // 2
-    top = id_ref.shape[1]
+    top = id_ref.shape[0]
+    given = jnp.concatenate([id_ref[...].astype(jnp.float32), gate_ref[...]], axis=0).T
     lane = lax.broadcasted_iota(jnp.int32, (tokens, TILE), 1)
+    number = lane.astype(jnp.float32)
     row = lax.broadcasted_iota(jnp.int32, (tokens, tokens), 0)
     column = lax.broadcasted_iota(jnp.int32, (tokens, tokens), 1)
-    ids = [id_ref[:, k : k + 1] for k in range(top)]
+    ids = [given[:, k : k + 1] for k in range(top)]
     named = jnp.zeros((tokens, TILE), jnp.float32)
     for k in range(top):
-        named = named + (ids[k] == lane).astype(jnp.float32)
-    before = (column < row).astype(jnp.float32).astype(jnp.bfloat16)
+        named = jnp.where(ids[k] == number, 1.0, named)
+    before = jnp.where(column < row, 1.0, 0.0).astype(jnp.bfloat16)
     rank = jnp.dot(before, named.astype(jnp.bfloat16), preferred_element_type=jnp.float32)
     facts = jnp.zeros((tokens, TILE), jnp.float32)
     for k in range(top):
-        place = jnp.sum(jnp.where(ids[k] == lane, rank, 0.0), axis=1, keepdims=True)
-        facts = jnp.where(lane == k, ids[k].astype(jnp.float32), facts)
+        place = jnp.sum(jnp.where(ids[k] == number, rank, 0.0), axis=1, keepdims=True)
+        facts = jnp.where(lane == k, ids[k], facts)
         facts = jnp.where(lane == top + k, place, facts)
-        rest = gate_ref[:, k : k + 1]
+        rest = given[:, top + k : top + k + 1]
         for part in range(2, 5):
             term = rest.astype(jnp.bfloat16).astype(jnp.float32)
             facts = jnp.where(lane == part * top + k, term, facts)
@@ -63,7 +65,7 @@
         cost_estimate=pl.CostEstimate(
             flops=2 * rows * rows * TILE, bytes_accessed=4 * rows * depth, transcendentals=0
         ),
-    )(tokens, expert_ids, gate_values)
+    )(tokens, expert_ids.T, gate_values.T)
 
 
 def codes(facts, top):
@@ -84,15 +86,22 @@
 
 
 def pack_kernel(chunk, top, experts_ref, *refs):
-    sources, facts, outs = refs[:SIDE], refs[SIDE : 2 * SIDE], refs[2 * SIDE :]
+    sources, facts = refs[:SIDE], refs[SIDE : 2 * SIDE]
+    outs, pick_ref = refs[2 * SIDE : -1], refs[-1]
     tokens = sources[0].shape[0]
-    target = targets(experts_ref, (chunk,), tokens)
+
+    @pl.when(pl.program_id(0) == 0)
+    def _():
+        target = targets(experts_ref, (chunk,), tokens)
+        for source in range(SIDE):
+            pick = jnp.zeros(target.shape, jnp.float32)
+            for code in codes(facts[source][...], top):
+                pick = jnp.where(code == target, 1.0, pick)
+            pick_ref[source] = pick.T.astype(jnp.bfloat16)
+
     for source in range(SIDE):
-        pick = jnp.zeros(target.shape, jnp.float32)
-        for code in codes(facts[source][...], top):
-            pick = jnp.where(code == target, 1.0, pick)
         rows = jnp.dot(
-            pick.T.astype(jnp.bfloat16), sources[source][...], preferred_element_type=jnp.float32
+            pick_ref[source], sources[source][...], preferred_element_type=jnp.float32
         ).astype(jnp.bfloat16)
         for dest in range(SIDE):
             outs[dest][source] = rows[dest * ROWS : (dest + 1) * ROWS]
@@ -112,6 +121,7 @@
         + [pl.BlockSpec((tokens, TILE), lambda i: (0, last))] * SIDE,
         out_specs=[pl.BlockSpec((SIDE, ROWS, tile), lambda i: (0, 0, i))] * SIDE,
         out_shape=[out] * SIDE,
+        scratch_shapes=[pltpu.VMEM((SIDE, SIDE * ROWS, tokens), jnp.bfloat16)],
         compiler_params=pltpu.CompilerParams(vmem_limit_bytes=VMEM),
         cost_estimate=pl.CostEstimate(
             flops=2 * SIDE * SIDE * ROWS * tokens * width,
@@ -212,23 +222,30 @@
 
 def sum_kernel(top, experts_ref, *refs):
     count = CHUNKS * SIDE
-    ins, facts, outs = refs[:count], refs[count : count + SIDE], refs[count + SIDE :]
-    tokens = outs[0].shape[0]
-    target = targets(experts_ref, tuple(range(CHUNKS)), tokens)
+    ins, facts = refs[:count], refs[count : count + SIDE]
+    outs, high_ref, low_ref = refs[count + SIDE : -2], refs[-2], refs[-1]
+    tokens = high_ref.shape[1]
+
+    @pl.when(pl.program_id(0) == 0)
+    def _():
+        target = targets(experts_ref, tuple(range(CHUNKS)), tokens)
+        for source in range(SIDE):
+            about = facts[source][...]
+            wide = about.astype(jnp.float32)
+            weight = jnp.zeros(target.shape, jnp.float32)
+            for k, code in enumerate(codes(about, top)):
+                first, second, third = (
+                    wide[:, part * top + k : part * top + k + 1] for part in range(2, 5)
+                )
+                weight = jnp.where(code == target, first + second + third, weight)
+            high = weight.astype(jnp.bfloat16)
+            high_ref[source] = high
+            low_ref[source] = (weight - high.astype(jnp.float32)).astype(jnp.bfloat16)
+
     for source in range(SIDE):
-        about = facts[source][...]
-        wide = about.astype(jnp.float32)
-        weight = jnp.zeros(target.shape, jnp.float32)
-        for k, code in enumerate(codes(about, top)):
-            first, second, third = (
-                wide[:, part * top + k : part * top + k + 1] for part in range(2, 5)
-            )
-            weight = jnp.where(code == target, first + second + third, weight)
-        high = weight.astype(jnp.bfloat16)
-        low = (weight - high.astype(jnp.float32)).astype(jnp.bfloat16)
         rows = jnp.concatenate([ref[source] for ref in ins], axis=0)
-        total = jnp.dot(high, rows, preferred_element_type=jnp.float32)
-        total = total + jnp.dot(low, rows, preferred_element_type=jnp.float32)
+        total = jnp.dot(high_ref[source], rows, preferred_element_type=jnp.float32)
+        total = total + jnp.dot(low_ref[source], rows, preferred_element_type=jnp.float32)
         outs[source][...] = total.astype(jnp.bfloat16)
 
 
@@ -238,6 +255,7 @@
     tile = min(SUM_TILE, width)
     last = width // TILE
     out = jax.ShapeDtypeStruct((tokens, width), jnp.bfloat16)
+    weights = pltpu.VMEM((SIDE, tokens, SIDE * CAP), jnp.bfloat16)
     return pl.pallas_call(
         functools.partial(sum_kernel, top),
         grid=(width // tile,),
@@ -246,6 +264,7 @@
         + [pl.BlockSpec((tokens, TILE), lambda i: (0, last))] * SIDE,
         out_specs=[pl.BlockSpec((tokens, tile), lambda i: (0, i))] * SIDE,
         out_shape=[out] * SIDE,
+        scratch_shapes=[weights, weights],
         compiler_params=pltpu.CompilerParams(vmem_limit_bytes=VMEM),
         cost_estimate=pl.CostEstimate(
             flops=4 * SIDE * SIDE * CAP * tokens * width,
@@ -268,20 +287,24 @@
 
     w_gate, w_up, w_down = gate_weight[0], up_weight[0], down_weight[0]
     a_back, b_back = [], []
+    a_done = None
     for chunk in range(CHUNKS):
-        a_out = pack(chunk, top, a_experts, a_rows)
-        b_out = pack(chunk, top, b_experts, b_rows)
+        a_out = list(pack(chunk, top, a_experts, a_rows))
+        b_out = list(pack(chunk, top, b_experts, b_rows))
         a_experts, b_experts, a_out, b_out = lax.optimization_barrier(
             (a_experts, b_experts, a_out, b_out)
         )
+        if chunk:
+            b_out[2], a_done[0] = lax.optimization_barrier((b_out[2], a_done[0]))
         a_in = [a_out[0]] + [shift(a_out[k], "x", k) for k in range(1, SIDE)]
         b_in = [b_out[0]] + [shift(b_out[k], "z", k) for k in range(1, SIDE)]
         a_done, b_done = expert(w_gate, w_up, w_down, a_in, b_in)
-        a_back += [a_done[0]] + [shift(a_done[k], "x", -k) for k in range(1, SIDE)]
-        b_back += [b_done[0]] + [shift(b_done[k], "z", -k) for k in range(1, SIDE)]
-
-    a_sums = sum_rows(top, a_experts, a_rows, a_back)
-    b_sums = sum_rows(top, b_experts, b_rows, b_back)
+        a_done = list(a_done)
+        a_back.append([a_done[0]] + [shift(a_done[k], "x", -k) for k in range(1, SIDE)])
+        b_back.append([b_done[0]] + [shift(b_done[k], "z", -k) for k in range(1, SIDE)])
+
+    a_sums = sum_rows(top, a_experts, a_rows, sum(a_back, []))
+    b_sums = sum_rows(top, b_experts, b_rows, sum(b_back, []))
     a_home = [a_sums[0]] + [shift(a_sums[k], "z", -k) for k in range(1, SIDE)]
     b_home = [b_sums[0]] + [shift(b_sums[k], "x", -k) for k in range(1, SIDE)]
     mixed = [sum(part.astype(jnp.float32) for part in home) for home in (a_home, b_home)]

time: 227 us -> 217 us (0.956)
  Pallas kernels: 69.8 us -> 54.9 us
  starting transfers between devices: 51.2 us -> 56.8 us
    pallas_call x2, Pallas kernels: 15 us -> 9.13 us  [sum_rows(): pl.pallas_call(functools.partial(sum_kernel, top), grid=(width // tile,),...]
    ppermute x36, starting transfers between devices: 51.2 us -> 56.8 us  [shift(): lax.ppermute(block, axis, [(i, (i + step) % SIDE) for i in range(SIDE)])]
    pallas_call x4, Pallas kernels: 19.9 us -> 14.8 us  [pack(): pl.pallas_call(functools.partial(pack_kernel, chunk, top), grid=(width //...]
    pallas_call x2, Pallas kernels: 34.3 us -> 30.4 us  [expert(): pl.pallas_call(functools.partial(expert_kernel, n_ff, n_half), grid=(n_ff...]
  transfers between devices with their start and end apart: 36 -> 36, of which waited for: 14 -> 18; matrix products, arithmetic and copies ran while one was open for 0% -> 0% of each run, Pallas kernels for 28% -> 23%
where the time goes in v3:
time: 217 us; the launch traced here: 216 us
  waiting for transfers between devices  99.7 us (46%)
  starting transfers between devices  56.8 us (26%)
  Pallas kernels  54.9 us (25%)
  local copies, waits for them, and re-layouts  2.6 us (1%)
    ppermute x36, waiting for transfers between devices, shift(): lax.ppermute(block, axis, [(i, (i + step) % SIDE) for i in range(SIDE)])  99.7 us
    ppermute x36, starting transfers between devices, shift(): lax.ppermute(block, axis, [(i, (i + step) % SIDE) for i in range(SIDE)])  56.8 us
    pallas_call x2, Pallas kernels, expert(): pl.pallas_call(functools.partial(expert_kernel, n_ff, n_half), grid=(n_ff...  30.4 us
    pallas_call x4, Pallas kernels, pack(): pl.pallas_call(functools.partial(pack_kernel, chunk, top), grid=(width //...  14.8 us
    pallas_call x2, Pallas kernels, sum_rows(): pl.pallas_call(functools.partial(sum_kernel, top), grid=(width // tile,),...  9.13 us
  transfers between devices with their start and end apart: 36, of which 18 were waited for; matrix products, arithmetic and copies ran while one was open for 0% of the time, Pallas kernels for 23%

profile of v3, /device:TPU:0, one launch (start us, length us, event | category | flops | bytes accessed | tf_op | source)
XLA Modules:
  0.0 215.9 jit_solution(12441590087557651420)
XLA Ops:
  3.2 2.9 %collective-permute-start.5 = (bf16[128,2176]{1,0:T(8,128)(2,1)S(1)}, bf16[128,2176]{1,0:T(8,128)(2,1)S(1)}, u32[]{:S(2)}, u32[]{:S(2)}) collective-permute-start(bf16[128,2176]{1,0:T(8,128)(2,1)S(1)} %get-tuple-element.73.refs_0_.refs_4_.refs_8_), channel_id=1, source_target_pairs={{0,3},{1,0},{2,1},{3,2},{4,7},{5,4},{6,5},{7,6},{8,11},{9,8},{10,9... | collective-permute-start | bytes 1671176 | tf_op jit(solution)/shard_map/ppermute | solution.py:23
  7.8 4.0 %collective-permute-start.2 = (bf16[128,2176]{1,0:T(8,128)(2,1)S(1)}, bf16[128,2176]{1,0:T(8,128)(2,1)S(1)}, u32[]{:S(2)}, u32[]{:S(2)}) collective-permute-start(bf16[128,2176]{1,0:T(8,128)(2,1)S(1)} %get-tuple-element.68.refs_0_.refs_4_.refs_8_), channel_id=1, source_target_pairs={{0,12},{4,0},{8,4},{12,8},{1,13},{5,1},{9,5},{13,9},{2,14},{6,2},{... | collective-permute-start | bytes 1671176 | tf_op jit(solution)/shard_map/ppermute | solution.py:23
  11.8 18.1 %collective-permute-done.5.refs_3_.refs_7_.refs_11_ = bf16[128,2176]{1,0:T(8,128)(2,1)S(1)} collective-permute-done((bf16[128,2176]{1,0:T(8,128)(2,1)S(1)}, bf16[128,2176]{1,0:T(8,128)(2,1)S(1)}, u32[]{:S(2)}, u32[]{:S(2)}) %collective-permute-start.5) | collective-permute-done | bytes 557088 | tf_op jit(solution)/shard_map/ppermute | solution.py:23
  33.6 3.3 %shard_map.66 = (bf16[4,32,2048]{2,1,0:T(8,128)(2,1)S(1)}, bf16[4,32,2048]{2,1,0:T(8,128)(2,1)S(1)}, bf16[4,32,2048]{2,1,0:T(8,128)(2,1)S(1)}, bf16[4,32,2048]{2,1,0:T(8,128)(2,1)S(1)}) custom-call(s32[4]{0:T(128)S(1)} %get-tuple-element.118.experts_ref, bf16[128,2176]{1,0:T(8,128)(2,1)S(1)} %get-tuple-element.73.refs_0_.refs_4_.refs_8_, ...), custom_call_target="tpu_custom_call" | custom-call | flops 268435456 | bytes 4194304 | tf_op jit(solution)/shard_map/pallas_call | solution.py:116
  36.9 4.7 %collective-permute-done.refs_1_.refs_5_.refs_9_ = bf16[128,2176]{1,0:T(8,128)(2,1)} collective-permute-done((bf16[128,2176]{1,0:T(8,128)(2,1)S(1)}, bf16[128,2176]{1,0:T(8,128)(2,1)}, u32[]{:S(2)}, u32[]{:S(2)}) %collective-permute-start) | collective-permute-done | bytes 557088 | tf_op jit(solution)/shard_map/ppermute | solution.py:23
  41.6 4.2 %shard_map.65 = (bf16[4,32,2048]{2,1,0:T(8,128)(2,1)S(1)}, bf16[4,32,2048]{2,1,0:T(8,128)(2,1)S(1)}, bf16[4,32,2048]{2,1,0:T(8,128)(2,1)S(1)}, bf16[4,32,2048]{2,1,0:T(8,128)(2,1)S(1)}) custom-call(s32[4]{0:T(128)S(1)} %get-tuple-element.88.experts_ref, bf16[128,2176]{1,0:T(8,128)(2,1)S(1)} %get-tuple-element.68.refs_0_.refs_4_.refs_8_, ...), custom_call_target="tpu_custom_call" | custom-call | flops 268435456 | bytes 4194304 | tf_op jit(solution)/shard_map/pallas_call | solution.py:116
  45.9 9.5 %collective-permute-start.7 = (bf16[4,32,2048]{2,1,0:T(8,128)(2,1)S(1)}, bf16[4,32,2048]{2,1,0:T(8,128)(2,1)S(1)}, u32[]{:S(2)}, u32[]{:S(2)}) collective-permute-start(bf16[4,32,2048]{2,1,0:T(8,128)(2,1)S(1)} %get-tuple-element.91), channel_id=1, source_target_pairs={{0,2},{1,3},{2,0},{3,1},{4,6},{5,7},{6,4},{7,5},{8,10},{9,11},{10,... | collective-permute-start | bytes 1572872 | tf_op jit(solution)/shard_map/ppermute | solution.py:23
  55.4 3.2 %collective-permute-start.10 = (bf16[4,32,2048]{2,1,0:T(8,128)(2,1)S(1)}, bf16[4,32,2048]{2,1,0:T(8,128)(2,1)S(1)}, u32[]{:S(2)}, u32[]{:S(2)}) collective-permute-start(bf16[4,32,2048]{2,1,0:T(8,128)(2,1)S(1)} %get-tuple-element.95), channel_id=1, source_target_pairs={{0,8},{4,12},{8,0},{12,4},{1,9},{5,13},{9,1},{13,5},{2,10},{6,14},... | collective-permute-start | bytes 1572872 | tf_op jit(solution)/shard_map/ppermute | solution.py:23
  58.6 7.3 %collective-permute-done.6.refs_1_ = bf16[4,32,2048]{2,1,0:T(8,128)(2,1)S(1)} collective-permute-done((bf16[4,32,2048]{2,1,0:T(8,128)(2,1)S(1)}, bf16[4,32,2048]{2,1,0:T(8,128)(2,1)S(1)}, u32[]{:S(2)}, u32[]{:S(2)}) %collective-permute-start.6) | collective-permute-done | bytes 524320 | tf_op jit(solution)/shard_map/ppermute | solution.py:23
  67.6 4.0 %shard_map.67 = (bf16[4,32,2048]{2,1,0:T(8,128)(2,1)S(1)}, bf16[4,32,2048]{2,1,0:T(8,128)(2,1)S(1)}, bf16[4,32,2048]{2,1,0:T(8,128)(2,1)S(1)}, bf16[4,32,2048]{2,1,0:T(8,128)(2,1)S(1)}) custom-call(s32[4]{0:T(128)S(1)} %get-tuple-element.88.experts_ref, bf16[128,2176]{1,0:T(8,128)(2,1)S(1)} %get-tuple-element.68.refs_0_.refs_4_.refs_8_, ...), custom_call_target="tpu_custom_call" | custom-call | flops 268435456 | bytes 4194304 | tf_op jit(solution)/shard_map/pallas_call | solution.py:116
  71.6 3.3 %shard_map.68 = (bf16[4,32,2048]{2,1,0:T(8,128)(2,1)S(1)}, bf16[4,32,2048]{2,1,0:T(8,128)(2,1)S(1)}, bf16[4,32,2048]{2,1,0:T(8,128)(2,1)S(1)}, bf16[4,32,2048]{2,1,0:T(8,128)(2,1)S(1)}) custom-call(s32[4]{0:T(128)S(1)} %get-tuple-element.118.experts_ref, bf16[128,2176]{1,0:T(8,128)(2,1)S(1)} %get-tuple-element.73.refs_0_.refs_4_.refs_8_, ...), custom_call_target="tpu_custom_call" | custom-call | flops 268435456 | bytes 4194304 | tf_op jit(solution)/shard_map/pallas_call | solution.py:116
  75.0 3.9 %collective-permute-done.7.refs_2_ = bf16[4,32,2048]{2,1,0:T(8,128)(2,1)S(1)} collective-permute-done((bf16[4,32,2048]{2,1,0:T(8,128)(2,1)S(1)}, bf16[4,32,2048]{2,1,0:T(8,128)(2,1)S(1)}, u32[]{:S(2)}, u32[]{:S(2)}) %collective-permute-start.7) | collective-permute-done | bytes 524320 | tf_op jit(solution)/shard_map/ppermute | solution.py:23
  82.2 3.2 %collective-permute-start.20 = (bf16[4,32,2048]{2,1,0:T(8,128)(2,1)S(1)}, bf16[4,32,2048]{2,1,0:T(8,128)(2,1)S(1)}, u32[]{:S(2)}, u32[]{:S(2)}) collective-permute-start(bf16[4,32,2048]{2,1,0:T(8,128)(2,1)S(1)} %get-tuple-element.109), channel_id=1, source_target_pairs={{0,12},{4,0},{8,4},{12,8},{1,13},{5,1},{9,5},{13,9},{2,14},{6,2},{... | collective-permute-start | bytes 1572872 | tf_op jit(solution)/shard_map/ppermute | solution.py:23
  85.4 15.2 %shard_map.69 = (bf16[4,32,2048]{2,1,0:T(8,128)(2,1)S(1)}, bf16[4,32,2048]{2,1,0:T(8,128)(2,1)S(1)}, bf16[4,32,2048]{2,1,0:T(8,128)(2,1)S(1)}, bf16[4,32,2048]{2...) custom-call(bf16[4096,768]{1,0:T(8,128)(2,1)S(1)} %bitcast.9, ...), custom_call_target="tpu_custom_call" | custom-call | flops 9663676416 | bytes 27262976 | tf_op jit(solution)/shard_map/pallas_call | solution.py:201
  102.1 3.4 %collective-permute-done.17.refs_3_ = bf16[4,32,2048]{2,1,0:T(8,128)(2,1)S(1)} collective-permute-done((bf16[4,32,2048]{2,1,0:T(8,128)(2,1)S(1)}, bf16[4,32,2048]{2,1,0:T(8,128)(2,1)S(1)}, u32[]{:S(2)}, u32[]{:S(2)}) %collective-permute-start.17) | collective-permute-done | bytes 524320 | tf_op jit(solution)/shard_map/ppermute | solution.py:23
  108.1 4.0 %collective-permute-done.19.refs_6_ = bf16[4,32,2048]{2,1,0:T(8,128)(2,1)S(1)} collective-permute-done((bf16[4,32,2048]{2,1,0:T(8,128)(2,1)S(1)}, bf16[4,32,2048]{2,1,0:T(8,128)(2,1)S(1)}, u32[]{:S(2)}, u32[]{:S(2)}) %collective-permute-start.19) | collective-permute-done | bytes 524320 | tf_op jit(solution)/shard_map/ppermute | solution.py:23
  112.1 15.2 %shard_map.70 = (bf16[4,32,2048]{2,1,0:T(8,128)(2,1)S(1)}, bf16[4,32,2048]{2,1,0:T(8,128)(2,1)S(1)}, bf16[4,32,2048]{2,1,0:T(8,128)(2,1)S(1)}, bf16[4,32,2048]{2...) custom-call(bf16[4096,768]{1,0:T(8,128)(2,1)S(1)} %bitcast.10, ...), custom_call_target="tpu_custom_call" | custom-call | flops 9663676416 | bytes 27262976 | tf_op jit(solution)/shard_map/pallas_call | solution.py:201
  127.7 4.4 %collective-permute-start.22 = (bf16[4,32,2048]{2,1,0:T(8,128)(2,1)S(1)}, bf16[4,32,2048]{2,1,0:T(8,128)(2,1)S(1)}, u32[]{:S(2)}, u32[]{:S(2)}) collective-permute-start(bf16[4,32,2048]{2,1,0:T(8,128)(2,1)S(1)} %get-tuple-element.112), channel_id=1, source_target_pairs={{0,2},{1,3},{2,0},{3,1},{4,6},{5,7},{6,4},{7,5},{8,10},{9,11},{10,... | collective-permute-start | bytes 1572872 | tf_op jit(solution)/shard_map/ppermute | solution.py:23
  132.4 4.3 %collective-permute-start.29 = (bf16[4,32,2048]{2,1,0:T(8,128)(2,1)S(1)}, bf16[4,32,2048]{2,1,0:T(8,128)(2,1)S(1)}, u32[]{:S(2)}, u32[]{:S(2)}) collective-permute-start(bf16[4,32,2048]{2,1,0:T(8,128)(2,1)S(1)} %get-tuple-element.122), channel_id=1, source_target_pairs={{0,4},{4,8},{8,12},{12,0},{1,5},{5,9},{9,13},{13,1},{2,6},{6,10},{... | collective-permute-start | bytes 1572872 | tf_op jit(solution)/shard_map/ppermute | solution.py:23
  136.7 6.0 %collective-permute-done.21.refs_5_ = bf16[4,32,2048]{2,1,0:T(8,128)(2,1)S(1)} collective-permute-done((bf16[4,32,2048]{2,1,0:T(8,128)(2,1)S(1)}, bf16[4,32,2048]{2,1,0:T(8,128)(2,1)S(1)}, u32[]{:S(2)}, u32[]{:S(2)}) %collective-permute-start.21) | collective-permute-done | bytes 524320 | tf_op jit(solution)/shard_map/ppermute | solution.py:23
  145.2 6.7 %collective-permute-done.23.refs_7_ = bf16[4,32,2048]{2,1,0:T(8,128)(2,1)S(1)} collective-permute-done((bf16[4,32,2048]{2,1,0:T(8,128)(2,1)S(1)}, bf16[4,32,2048]{2,1,0:T(8,128)(2,1)S(1)}, u32[]{:S(2)}, u32[]{:S(2)}) %collective-permute-start.23) | collective-permute-done | bytes 524320 | tf_op jit(solution)/shard_map/ppermute | solution.py:23
  151.9 4.7 %shard_map.71 = (bf16[128,2048]{1,0:T(8,128)(2,1)S(1)}, bf16[128,2048]{1,0:T(8,128)(2,1)S(1)}, bf16[128,2048]{1,0:T(8,128)(2,1)S(1)}, bf16[128,2048]{1,0:T(8,128)(2,1)S(1)}) custom-call(s32[4]{0:T(128)S(1)} %get-tuple-element.88.experts_ref, bf16[4,32,2048]{2,1,0:T(8,128)(2,1)S(1)} %get-tuple-element.97.refs_0_, ...), custom_call_target="tpu_custom_call" | custom-call | flops 1073741824 | bytes 6291456 | tf_op jit(solution)/shard_map/pallas_call | solution.py:259
  156.6 3.3 %collective-permute-start.24 = (bf16[128,2048]{1,0:T(8,128)(2,1)S(1)}, bf16[128,2048]{1,0:T(8,128)(2,1)S(1)}, u32[]{:S(2)}, u32[]{:S(2)}) collective-permute-start(bf16[128,2048]{1,0:T(8,128)(2,1)S(1)} %get-tuple-element.115), channel_id=1, source_target_pairs={{0,12},{4,0},{8,4},{12,8},{1,13},{5,1},{9,5},{13,9},{2,14},{6,2},{... | collective-permute-start | bytes 1572872 | tf_op jit(solution)/shard_map/ppermute | solution.py:23
  159.9 2.8 %collective-permute-start.25 = (bf16[128,2048]{1,0:T(8,128)(2,1)S(1)}, bf16[128,2048]{1,0:T(8,128)(2,1)S(1)}, u32[]{:S(2)}, u32[]{:S(2)}) collective-permute-start(bf16[128,2048]{1,0:T(8,128)(2,1)S(1)} %get-tuple-element.116), channel_id=1, source_target_pairs={{0,8},{4,12},{8,0},{12,4},{1,9},{5,13},{9,1},{13,5},{2,10},{6,14},... | collective-permute-start | bytes 1572872 | tf_op jit(solution)/shard_map/ppermute | solution.py:23
  162.8 8.2 %collective-permute-done.31.refs_6_ = bf16[4,32,2048]{2,1,0:T(8,128)(2,1)S(1)} collective-permute-done((bf16[4,32,2048]{2,1,0:T(8,128)(2,1)S(1)}, bf16[4,32,2048]{2,1,0:T(8,128)(2,1)S(1)}, u32[]{:S(2)}, u32[]{:S(2)}) %collective-permute-start.31) | collective-permute-done | bytes 524320 | tf_op jit(solution)/shard_map/ppermute | solution.py:23
  171.0 11.3 %collective-permute-done.32.refs_7_ = bf16[4,32,2048]{2,1,0:T(8,128)(2,1)S(1)} collective-permute-done((bf16[4,32,2048]{2,1,0:T(8,128)(2,1)S(1)}, bf16[4,32,2048]{2,1,0:T(8,128)(2,1)S(1)}, u32[]{:S(2)}, u32[]{:S(2)}) %collective-permute-start.32) | collective-permute-done | bytes 524320 | tf_op jit(solution)/shard_map/ppermute | solution.py:23
  182.3 4.4 %shard_map.72 = (bf16[128,2048]{1,0:T(8,128)(2,1)S(1)}, bf16[128,2048]{1,0:T(8,128)(2,1)S(1)}, bf16[128,2048]{1,0:T(8,128)(2,1)S(1)}, bf16[128,2048]{1,0:T(8,128)(2,1)S(1)}) custom-call(s32[4]{0:T(128)S(1)} %get-tuple-element.118.experts_ref, bf16[4,32,2048]{2,1,0:T(8,128)(2,1)S(1)} %get-tuple-element.119.refs_0_, ...), custom_call_target="tpu_custom_call" | custom-call | flops 1073741824 | bytes 6291456 | tf_op jit(solution)/shard_map/pallas_call | solution.py:259
  186.7 3.0 %collective-permute-start.33 = (bf16[128,2048]{1,0:T(8,128)(2,1)S(1)}, bf16[128,2048]{1,0:T(8,128)(2,1)S(1)}, u32[]{:S(2)}, u32[]{:S(2)}) collective-permute-start(bf16[128,2048]{1,0:T(8,128)(2,1)S(1)} %get-tuple-element.128), channel_id=1, source_target_pairs={{0,3},{1,0},{2,1},{3,2},{4,7},{5,4},{6,5},{7,6},{8,11},{9,8},{10,9... | collective-permute-start | bytes 1572872 | tf_op jit(solution)/shard_map/ppermute | solution.py:23
  190.6 2.9 %collective-permute-done.25 = bf16[128,2048]{1,0:T(8,128)(2,1)S(1)} collective-permute-done((bf16[128,2048]{1,0:T(8,128)(2,1)S(1)}, bf16[128,2048]{1,0:T(8,128)(2,1)S(1)}, u32[]{:S(2)}, u32[]{:S(2)}) %collective-permute-start.25) | collective-permute-done | bytes 524320 | tf_op jit(solution)/shard_map/ppermute | solution.py:23
  193.5 6.4 %collective-permute-done.26 = bf16[128,2048]{1,0:T(8,128)(2,1)S(1)} collective-permute-done((bf16[128,2048]{1,0:T(8,128)(2,1)S(1)}, bf16[128,2048]{1,0:T(8,128)(2,1)S(1)}, u32[]{:S(2)}, u32[]{:S(2)}) %collective-permute-start.26) | collective-permute-done | bytes 524320 | tf_op jit(solution)/shard_map/ppermute | solution.py:23
  200.2 10.9 %collective-permute-done.33 = bf16[128,2048]{1,0:T(8,128)(2,1)S(1)} collective-permute-done((bf16[128,2048]{1,0:T(8,128)(2,1)S(1)}, bf16[128,2048]{1,0:T(8,128)(2,1)S(1)}, u32[]{:S(2)}, u32[]{:S(2)}) %collective-permute-start.33) | collective-permute-done | bytes 524320 | tf_op jit(solution)/shard_map/ppermute | solution.py:23
  211.1 3.4 %collective-permute-done.35 = bf16[128,2048]{1,0:T(8,128)(2,1)S(1)} collective-permute-done((bf16[128,2048]{1,0:T(8,128)(2,1)S(1)}, bf16[128,2048]{1,0:T(8,128)(2,1)S(1)}, u32[]{:S(2)}, u32[]{:S(2)}) %collective-permute-start.35) | collective-permute-done | bytes 524320 | tf_op jit(solution)/shard_map/ppermute | solution.py:23
  (64 shorter events, 23.6 us)
Async XLA Ops:
  3.2 26.7 %collective-permute-start.5 = (bf16[128,2176]{1,0:T(8,128)(2,1)S(1)}, bf16[128,2176]{1,0:T(8,128)(2,1)S(1)}, u32[]{:S(2)}, u32[]{:S(2)}) collective-permute-start(bf16[128,2176]{1,0:T(8,128)(2,1)S(1)} %get-tuple-element.73.refs_0_.refs_4_.refs_8_), channel_id=1, source_target_pairs={{0,3},{1,0},{2,1},{3,2},{4,7},{5,4},{6,5},{7,6},{8,11},{9,8},{10,9... | collective-permute-start | bytes 1671176 | tf_op jit(solution)/shard_map/ppermute | solution.py:23
  6.1 25.8 %collective-permute-start.4 = (bf16[128,2176]{1,0:T(8,128)(2,1)S(1)}, bf16[128,2176]{1,0:T(8,128)(2,1)S(1)}, u32[]{:S(2)}, u32[]{:S(2)}) collective-permute-start(bf16[128,2176]{1,0:T(8,128)(2,1)S(1)} %get-tuple-element.73.refs_0_.refs_4_.refs_8_), channel_id=1, source_target_pairs={{0,2},{1,3},{2,0},{3,1},{4,6},{5,7},{6,4},{7,5},{8,10},{9,11},{10,... | collective-permute-start | bytes 1671176 | tf_op jit(solution)/shard_map/ppermute | solution.py:23
  6.9 26.7 %collective-permute-start.3 = (bf16[128,2176]{1,0:T(8,128)(2,1)S(1)}, bf16[128,2176]{1,0:T(8,128)(2,1)S(1)}, u32[]{:S(2)}, u32[]{:S(2)}) collective-permute-start(bf16[128,2176]{1,0:T(8,128)(2,1)S(1)} %get-tuple-element.73.refs_0_.refs_4_.refs_8_), channel_id=1, source_target_pairs={{0,1},{1,2},{2,3},{3,0},{4,5},{5,6},{6,7},{7,4},{8,9},{9,10},{10,1... | collective-permute-start | bytes 1671176 | tf_op jit(solution)/shard_map/ppermute | solution.py:23
  7.8 29.1 %collective-permute-start.2 = (bf16[128,2176]{1,0:T(8,128)(2,1)S(1)}, bf16[128,2176]{1,0:T(8,128)(2,1)S(1)}, u32[]{:S(2)}, u32[]{:S(2)}) collective-permute-start(bf16[128,2176]{1,0:T(8,128)(2,1)S(1)} %get-tuple-element.68.refs_0_.refs_4_.refs_8_), channel_id=1, source_target_pairs={{0,12},{4,0},{8,4},{12,8},{1,13},{5,1},{9,5},{13,9},{2,14},{6,2},{... | collective-permute-start | bytes 1671176 | tf_op jit(solution)/shard_map/ppermute | solution.py:23
  11.8 25.1 %collective-permute-start.1 = (bf16[128,2176]{1,0:T(8,128)(2,1)S(1)}, bf16[128,2176]{1,0:T(8,128)(2,1)}, u32[]{:S(2)}, u32[]{:S(2)}) collective-permute-start(bf16[128,2176]{1,0:T(8,128)(2,1)S(1)} %get-tuple-element.68.refs_0_.refs_4_.refs_8_), channel_id=1, source_target_pairs={{0,8},{4,12},{8,0},{12,4},{1,9},{5,13},{9,1},{13,5},{2,10},{6,14},... | collective-permute-start | bytes 1671176 | tf_op jit(solution)/shard_map/ppermute | solution.py:23
  45.8 20.0 %collective-permute-start.6 = (bf16[4,32,2048]{2,1,0:T(8,128)(2,1)S(1)}, bf16[4,32,2048]{2,1,0:T(8,128)(2,1)S(1)}, u32[]{:S(2)}, u32[]{:S(2)}) collective-permute-start(bf16[4,32,2048]{2,1,0:T(8,128)(2,1)S(1)} %get-tuple-element.90), channel_id=1, source_target_pairs={{0,1},{1,2},{2,3},{3,0},{4,5},{5,6},{6,7},{7,4},{8,9},{9,10},{10,1... | collective-permute-start | bytes 1572872 | tf_op jit(solution)/shard_map/ppermute | solution.py:23
  45.9 33.0 %collective-permute-start.7 = (bf16[4,32,2048]{2,1,0:T(8,128)(2,1)S(1)}, bf16[4,32,2048]{2,1,0:T(8,128)(2,1)S(1)}, u32[]{:S(2)}, u32[]{:S(2)}) collective-permute-start(bf16[4,32,2048]{2,1,0:T(8,128)(2,1)S(1)} %get-tuple-element.91), channel_id=1, source_target_pairs={{0,2},{1,3},{2,0},{3,1},{4,6},{5,7},{6,4},{7,5},{8,10},{9,11},{10,... | collective-permute-start | bytes 1572872 | tf_op jit(solution)/shard_map/ppermute | solution.py:23
  55.4 23.5 %collective-permute-start.8 = (bf16[4,32,2048]{2,1,0:T(8,128)(2,1)S(1)}, bf16[4,32,2048]{2,1,0:T(8,128)(2,1)S(1)}, u32[]{:S(2)}, u32[]{:S(2)}) collective-permute-start(bf16[4,32,2048]{2,1,0:T(8,128)(2,1)S(1)} %get-tuple-element.92), channel_id=1, source_target_pairs={{0,3},{1,0},{2,1},{3,2},{4,7},{5,4},{6,5},{7,6},{8,11},{9,8},{10,9... | collective-permute-start | bytes 1572872 | tf_op jit(solution)/shard_map/ppermute | solution.py:23
  55.4 24.2 %collective-permute-start.9 = (bf16[4,32,2048]{2,1,0:T(8,128)(2,1)S(1)}, bf16[4,32,2048]{2,1,0:T(8,128)(2,1)S(1)}, u32[]{:S(2)}, u32[]{:S(2)}) collective-permute-start(bf16[4,32,2048]{2,1,0:T(8,128)(2,1)S(1)} %get-tuple-element.94), channel_id=1, source_target_pairs={{0,4},{4,8},{8,12},{12,0},{1,5},{5,9},{9,13},{13,1},{2,6},{6,10},{... | collective-permute-start | bytes 1572872 | tf_op jit(solution)/shard_map/ppermute | solution.py:23
  55.4 26.8 %collective-permute-start.10 = (bf16[4,32,2048]{2,1,0:T(8,128)(2,1)S(1)}, bf16[4,32,2048]{2,1,0:T(8,128)(2,1)S(1)}, u32[]{:S(2)}, u32[]{:S(2)}) collective-permute-start(bf16[4,32,2048]{2,1,0:T(8,128)(2,1)S(1)} %get-tuple-element.95), channel_id=1, source_target_pairs={{0,8},{4,12},{8,0},{12,4},{1,9},{5,13},{9,1},{13,5},{2,10},{6,14},... | collective-permute-start | bytes 1572872 | tf_op jit(solution)/shard_map/ppermute | solution.py:23
  78.9 22.1 %collective-permute-start.15 = (bf16[4,32,2048]{2,1,0:T(8,128)(2,1)S(1)}, bf16[4,32,2048]{2,1,0:T(8,128)(2,1)S(1)}, u32[]{:S(2)}, u32[]{:S(2)}) collective-permute-start(bf16[4,32,2048]{2,1,0:T(8,128)(2,1)S(1)} %get-tuple-element.102), channel_id=1, source_target_pairs={{0,1},{1,2},{2,3},{3,0},{4,5},{5,6},{6,7},{7,4},{8,9},{9,10},{10,1... | collective-permute-start | bytes 1572872 | tf_op jit(solution)/shard_map/ppermute | solution.py:23
  78.9 23.2 %collective-permute-start.16 = (bf16[4,32,2048]{2,1,0:T(8,128)(2,1)S(1)}, bf16[4,32,2048]{2,1,0:T(8,128)(2,1)S(1)}, u32[]{:S(2)}, u32[]{:S(2)}) collective-permute-start(bf16[4,32,2048]{2,1,0:T(8,128)(2,1)S(1)} %get-tuple-element.103), channel_id=1, source_target_pairs={{0,2},{1,3},{2,0},{3,1},{4,6},{5,7},{6,4},{7,5},{8,10},{9,11},{10,... | collective-permute-start | bytes 1572872 | tf_op jit(solution)/shard_map/ppermute | solution.py:23
  79.5 26.0 %collective-permute-start.17 = (bf16[4,32,2048]{2,1,0:T(8,128)(2,1)S(1)}, bf16[4,32,2048]{2,1,0:T(8,128)(2,1)S(1)}, u32[]{:S(2)}, u32[]{:S(2)}) collective-permute-start(bf16[4,32,2048]{2,1,0:T(8,128)(2,1)S(1)} %get-tuple-element.104), channel_id=1, source_target_pairs={{0,3},{1,0},{2,1},{3,2},{4,7},{5,4},{6,5},{7,6},{8,11},{9,8},{10,9... | collective-permute-start | bytes 1572872 | tf_op jit(solution)/shard_map/ppermute | solution.py:23
  82.2 23.4 %collective-permute-start.18 = (bf16[4,32,2048]{2,1,0:T(8,128)(2,1)S(1)}, bf16[4,32,2048]{2,1,0:T(8,128)(2,1)S(1)}, u32[]{:S(2)}, u32[]{:S(2)}) collective-permute-start(bf16[4,32,2048]{2,1,0:T(8,128)(2,1)S(1)} %get-tuple-element.106), channel_id=1, source_target_pairs={{0,4},{4,8},{8,12},{12,0},{1,5},{5,9},{9,13},{13,1},{2,6},{6,10},{... | collective-permute-start | bytes 1572872 | tf_op jit(solution)/shard_map/ppermute | solution.py:23
  82.2 24.4 %collective-permute-start.20 = (bf16[4,32,2048]{2,1,0:T(8,128)(2,1)S(1)}, bf16[4,32,2048]{2,1,0:T(8,128)(2,1)S(1)}, u32[]{:S(2)}, u32[]{:S(2)}) collective-permute-start(bf16[4,32,2048]{2,1,0:T(8,128)(2,1)S(1)} %get-tuple-element.109), channel_id=1, source_target_pairs={{0,12},{4,0},{8,4},{12,8},{1,13},{5,1},{9,5},{13,9},{2,14},{6,2},{... | collective-permute-start | bytes 1572872 | tf_op jit(solution)/shard_map/ppermute | solution.py:23
  102.1 25.6 %collective-permute-start.12 = (bf16[4,32,2048]{2,1,0:T(8,128)(2,1)S(1)}, bf16[4,32,2048]{2,1,0:T(8,128)(2,1)S(1)}, u32[]{:S(2)}, u32[]{:S(2)}) collective-permute-start(bf16[4,32,2048]{2,1,0:T(8,128)(2,1)S(1)} %get-tuple-element.98), channel_id=1, source_target_pairs={{0,3},{1,0},{2,1},{3,2},{4,7},{5,4},{6,5},{7,6},{8,11},{9,8},{10,9... | collective-permute-start | bytes 1572872 | tf_op jit(solution)/shard_map/ppermute | solution.py:23
  105.5 26.5 %collective-permute-start.13 = (bf16[4,32,2048]{2,1,0:T(8,128)(2,1)S(1)}, bf16[4,32,2048]{2,1,0:T(8,128)(2,1)S(1)}, u32[]{:S(2)}, u32[]{:S(2)}) collective-permute-start(bf16[4,32,2048]{2,1,0:T(8,128)(2,1)S(1)} %get-tuple-element.99), channel_id=1, source_target_pairs={{0,2},{1,3},{2,0},{3,1},{4,6},{5,7},{6,4},{7,5},{8,10},{9,11},{10,... | collective-permute-start | bytes 1572872 | tf_op jit(solution)/shard_map/ppermute | solution.py:23
  105.6 26.5 %collective-permute-start.14 = (bf16[4,32,2048]{2,1,0:T(8,128)(2,1)S(1)}, bf16[4,32,2048]{2,1,0:T(8,128)(2,1)S(1)}, u32[]{:S(2)}, u32[]{:S(2)}) collective-permute-start(bf16[4,32,2048]{2,1,0:T(8,128)(2,1)S(1)} %get-tuple-element.100), channel_id=1, source_target_pairs={{0,1},{1,2},{2,3},{3,0},{4,5},{5,6},{6,7},{7,4},{8,9},{9,10},{10,1... | collective-permute-start | bytes 1572872 | tf_op jit(solution)/shard_map/ppermute | solution.py:23
  106.6 25.8 %collective-permute-start.27 = (bf16[4,32,2048]{2,1,0:T(8,128)(2,1)S(1)}, bf16[4,32,2048]{2,1,0:T(8,128)(2,1)S(1)}, u32[]{:S(2)}, u32[]{:S(2)}) collective-permute-start(bf16[4,32,2048]{2,1,0:T(8,128)(2,1)S(1)} %get-tuple-element.120), channel_id=1, source_target_pairs={{0,12},{4,0},{8,4},{12,8},{1,13},{5,1},{9,5},{13,9},{2,14},{6,2},{... | collective-permute-start | bytes 1572872 | tf_op jit(solution)/shard_map/ppermute | solution.py:23
  127.7 17.2 %collective-permute-start.22 = (bf16[4,32,2048]{2,1,0:T(8,128)(2,1)S(1)}, bf16[4,32,2048]{2,1,0:T(8,128)(2,1)S(1)}, u32[]{:S(2)}, u32[]{:S(2)}) collective-permute-start(bf16[4,32,2048]{2,1,0:T(8,128)(2,1)S(1)} %get-tuple-element.112), channel_id=1, source_target_pairs={{0,2},{1,3},{2,0},{3,1},{4,6},{5,7},{6,4},{7,5},{8,10},{9,11},{10,... | collective-permute-start | bytes 1572872 | tf_op jit(solution)/shard_map/ppermute | solution.py:23
  132.0 19.9 %collective-permute-start.23 = (bf16[4,32,2048]{2,1,0:T(8,128)(2,1)S(1)}, bf16[4,32,2048]{2,1,0:T(8,128)(2,1)S(1)}, u32[]{:S(2)}, u32[]{:S(2)}) collective-permute-start(bf16[4,32,2048]{2,1,0:T(8,128)(2,1)S(1)} %get-tuple-element.113), channel_id=1, source_target_pairs={{0,1},{1,2},{2,3},{3,0},{4,5},{5,6},{6,7},{7,4},{8,9},{9,10},{10,1... | collective-permute-start | bytes 1572872 | tf_op jit(solution)/shard_map/ppermute | solution.py:23
  132.0 24.6 %collective-permute-start.28 = (bf16[4,32,2048]{2,1,0:T(8,128)(2,1)S(1)}, bf16[4,32,2048]{2,1,0:T(8,128)(2,1)S(1)}, u32[]{:S(2)}, u32[]{:S(2)}) collective-permute-start(bf16[4,32,2048]{2,1,0:T(8,128)(2,1)S(1)} %get-tuple-element.121), channel_id=1, source_target_pairs={{0,8},{4,12},{8,0},{12,4},{1,9},{5,13},{9,1},{13,5},{2,10},{6,14},... | collective-permute-start | bytes 1572872 | tf_op jit(solution)/shard_map/ppermute | solution.py:23
  132.4 27.5 %collective-permute-start.29 = (bf16[4,32,2048]{2,1,0:T(8,128)(2,1)S(1)}, bf16[4,32,2048]{2,1,0:T(8,128)(2,1)S(1)}, u32[]{:S(2)}, u32[]{:S(2)}) collective-permute-start(bf16[4,32,2048]{2,1,0:T(8,128)(2,1)S(1)} %get-tuple-element.122), channel_id=1, source_target_pairs={{0,4},{4,8},{8,12},{12,0},{1,5},{5,9},{9,13},{13,1},{2,6},{6,10},{... | collective-permute-start | bytes 1572872 | tf_op jit(solution)/shard_map/ppermute | solution.py:23
  142.8 20.0 %collective-permute-start.30 = (bf16[4,32,2048]{2,1,0:T(8,128)(2,1)S(1)}, bf16[4,32,2048]{2,1,0:T(8,128)(2,1)S(1)}, u32[]{:S(2)}, u32[]{:S(2)}) collective-permute-start(bf16[4,32,2048]{2,1,0:T(8,128)(2,1)S(1)} %get-tuple-element.124), channel_id=1, source_target_pairs={{0,12},{4,0},{8,4},{12,8},{1,13},{5,1},{9,5},{13,9},{2,14},{6,2},{... | collective-permute-start | bytes 1572872 | tf_op jit(solution)/shard_map/ppermute | solution.py:23
  144.9 26.1 %collective-permute-start.31 = (bf16[4,32,2048]{2,1,0:T(8,128)(2,1)S(1)}, bf16[4,32,2048]{2,1,0:T(8,128)(2,1)S(1)}, u32[]{:S(2)}, u32[]{:S(2)}) collective-permute-start(bf16[4,32,2048]{2,1,0:T(8,128)(2,1)S(1)} %get-tuple-element.125), channel_id=1, source_target_pairs={{0,8},{4,12},{8,0},{12,4},{1,9},{5,13},{9,1},{13,5},{2,10},{6,14},... | collective-permute-start | bytes 1572872 | tf_op jit(solution)/shard_map/ppermute | solution.py:23
  151.9 30.3 %collective-permute-start.32 = (bf16[4,32,2048]{2,1,0:T(8,128)(2,1)S(1)}, bf16[4,32,2048]{2,1,0:T(8,128)(2,1)S(1)}, u32[]{:S(2)}, u32[]{:S(2)}) collective-permute-start(bf16[4,32,2048]{2,1,0:T(8,128)(2,1)S(1)} %get-tuple-element.126), channel_id=1, source_target_pairs={{0,4},{4,8},{8,12},{12,0},{1,5},{5,9},{9,13},{13,1},{2,6},{6,10},{... | collective-permute-start | bytes 1572872 | tf_op jit(solution)/shard_map/ppermute | solution.py:23
  156.6 33.0 %collective-permute-start.24 = (bf16[128,2048]{1,0:T(8,128)(2,1)S(1)}, bf16[128,2048]{1,0:T(8,128)(2,1)S(1)}, u32[]{:S(2)}, u32[]{:S(2)}) collective-permute-start(bf16[128,2048]{1,0:T(8,128)(2,1)S(1)} %get-tuple-element.115), channel_id=1, source_target_pairs={{0,12},{4,0},{8,4},{12,8},{1,13},{5,1},{9,5},{13,9},{2,14},{6,2},{... | collective-permute-start | bytes 1572872 | tf_op jit(solution)/shard_map/ppermute | solution.py:23
  159.9 33.6 %collective-permute-start.25 = (bf16[128,2048]{1,0:T(8,128)(2,1)S(1)}, bf16[128,2048]{1,0:T(8,128)(2,1)S(1)}, u32[]{:S(2)}, u32[]{:S(2)}) collective-permute-start(bf16[128,2048]{1,0:T(8,128)(2,1)S(1)} %get-tuple-element.116), channel_id=1, source_target_pairs={{0,8},{4,12},{8,0},{12,4},{1,9},{5,13},{9,1},{13,5},{2,10},{6,14},... | collective-permute-start | bytes 1572872 | tf_op jit(solution)/shard_map/ppermute | solution.py:23
  162.8 37.1 %collective-permute-start.26 = (bf16[128,2048]{1,0:T(8,128)(2,1)S(1)}, bf16[128,2048]{1,0:T(8,128)(2,1)S(1)}, u32[]{:S(2)}, u32[]{:S(2)}) collective-permute-start(bf16[128,2048]{1,0:T(8,128)(2,1)S(1)} %get-tuple-element.117), channel_id=1, source_target_pairs={{0,4},{4,8},{8,12},{12,0},{1,5},{5,9},{9,13},{13,1},{2,6},{6,10},{... | collective-permute-start | bytes 1572872 | tf_op jit(solution)/shard_map/ppermute | solution.py:23
  186.7 24.4 %collective-permute-start.33 = (bf16[128,2048]{1,0:T(8,128)(2,1)S(1)}, bf16[128,2048]{1,0:T(8,128)(2,1)S(1)}, u32[]{:S(2)}, u32[]{:S(2)}) collective-permute-start(bf16[128,2048]{1,0:T(8,128)(2,1)S(1)} %get-tuple-element.128), channel_id=1, source_target_pairs={{0,3},{1,0},{2,1},{3,2},{4,7},{5,4},{6,5},{7,6},{8,11},{9,8},{10,9... | collective-permute-start | bytes 1572872 | tf_op jit(solution)/shard_map/ppermute | solution.py:23
  189.7 21.5 %collective-permute-start.34 = (bf16[128,2048]{1,0:T(8,128)(2,1)S(1)}, bf16[128,2048]{1,0:T(8,128)(2,1)S(1)}, u32[]{:S(2)}, u32[]{:S(2)}) collective-permute-start(bf16[128,2048]{1,0:T(8,128)(2,1)S(1)} %get-tuple-element.129), channel_id=1, source_target_pairs={{0,2},{1,3},{2,0},{3,1},{4,6},{5,7},{6,4},{7,5},{8,10},{9,11},{10,... | collective-permute-start | bytes 1572872 | tf_op jit(solution)/shard_map/ppermute | solution.py:23
  189.7 24.8 %collective-permute-start.35 = (bf16[128,2048]{1,0:T(8,128)(2,1)S(1)}, bf16[128,2048]{1,0:T(8,128)(2,1)S(1)}, u32[]{:S(2)}, u32[]{:S(2)}) collective-permute-start(bf16[128,2048]{1,0:T(8,128)(2,1)S(1)} %get-tuple-element.130), channel_id=1, source_target_pairs={{0,1},{1,2},{2,3},{3,0},{4,5},{5,6},{6,7},{7,4},{8,9},{9,10},{10,1... | collective-permute-start | bytes 1572872 | tf_op jit(solution)/shard_map/ppermute | solution.py:23
  (9 other events, 140.7 us)

commit v4 on v3

--- a/solution.py
+++ b/solution.py
@@ -12,7 +12,7 @@
 CHUNKS = 2
 ROWS = CAP // CHUNKS
 TILE = 128
-PACK_TILE = 512
+PACK_TILE = 1024
 FF_TILE = 256
 D_TILE = 1024
 SUM_TILE = 512
@@ -21,6 +21,14 @@
 
 def shift(block, axis, step):
     return lax.ppermute(block, axis, [(i, (i + step) % SIDE) for i in range(SIDE)])
+
+
+def both_ways(a_blocks, b_blocks, a_axis, b_axis, sign):
+    a_moved, b_moved = list(a_blocks), list(b_blocks)
+    for k in (1, 3, 2):
+        a_moved[k] = shift(a_blocks[k], a_axis, sign * k)
+        b_moved[k] = shift(b_blocks[k], b_axis, sign * k)
+    return a_moved, b_moved
 
 
 def prepare_kernel(token_ref, id_ref, gate_ref, a_ref, b_ref):
@@ -73,26 +81,26 @@
     return [facts[:, k : k + 1] * CAP + facts[:, top + k : top + k + 1] for k in range(top)]
 
 
-def targets(experts_ref, chunks, tokens):
+def targets(places_ref, first, chunks, tokens):
     count = len(chunks) * SIDE * ROWS
     lane = lax.broadcasted_iota(jnp.int32, (tokens, count), 1)
     code = jnp.zeros((tokens, count), jnp.int32)
     for n, chunk in enumerate(chunks):
         for dest in range(SIDE):
             low = (n * SIDE + dest) * ROWS
-            value = experts_ref[dest] * CAP + chunk * ROWS + lane - low
+            value = places_ref[first + dest] * CAP + chunk * ROWS + lane - low
             code = jnp.where((lane >= low) & (lane < low + ROWS), value, code)
     return code.astype(jnp.float32)
 
 
-def pack_kernel(chunk, top, experts_ref, *refs):
+def pack_kernel(chunk, top, places_ref, *refs):
     sources, facts = refs[:SIDE], refs[SIDE : 2 * SIDE]
     outs, pick_ref = refs[2 * SIDE : -1], refs[-1]
     tokens = sources[0].shape[0]
 
     @pl.when(pl.program_id(0) == 0)
     def _():
-        target = targets(experts_ref, (chunk,), tokens)
+        target = targets(places_ref, 0, (chunk,), tokens)
         for source in range(SIDE):
             pick = jnp.zeros(target.shape, jnp.float32)
             for code in codes(facts[source][...], top):
@@ -107,28 +115,44 @@
             outs[dest][source] = rows[dest * ROWS : (dest + 1) * ROWS]
 
 
-def pack(chunk, top, experts, blocks):
-    tokens, width = blocks[0].shape
-    width -= TILE
+def wide_specs(tokens, tile):
+    return [
+        pl.BlockSpec((tokens, tile), lambda i, places, k=k: (places[SIDE + k], i))
+        for k in range(SIDE)
+    ]
+
+
+def fact_specs(tokens, last):
+    return [
+        pl.BlockSpec((tokens, TILE), lambda i, places, k=k: (places[SIDE + k], last))
+        for k in range(SIDE)
+    ]
+
+
+def pack(chunk, top, places, blocks):
+    width = blocks[0].shape[1] - TILE
+    tokens = blocks[-1].shape[0]
+    if len(blocks) == 1:
+        blocks, tokens = list(blocks) * SIDE, tokens // SIDE
     tile = min(PACK_TILE, width)
-    last = width // TILE
     out = jax.ShapeDtypeStruct((SIDE, ROWS, width), jnp.bfloat16)
     return pl.pallas_call(
         functools.partial(pack_kernel, chunk, top),
-        grid=(width // tile,),
-        in_specs=[pl.BlockSpec(memory_space=pltpu.SMEM)]
-        + [pl.BlockSpec((tokens, tile), lambda i: (0, i))] * SIDE
-        + [pl.BlockSpec((tokens, TILE), lambda i: (0, last))] * SIDE,
-        out_specs=[pl.BlockSpec((SIDE, ROWS, tile), lambda i: (0, 0, i))] * SIDE,
+        grid_spec=pltpu.PrefetchScalarGridSpec(
+            num_scalar_prefetch=1,
+            grid=(width // tile,),
+            in_specs=wide_specs(tokens, tile) + fact_specs(tokens, width // TILE),
+            out_specs=[pl.BlockSpec((SIDE, ROWS, tile), lambda i, places: (0, 0, i))] * SIDE,
+            scratch_shapes=[pltpu.VMEM((SIDE, SIDE * ROWS, tokens), jnp.bfloat16)],
+        ),
         out_shape=[out] * SIDE,
-        scratch_shapes=[pltpu.VMEM((SIDE, SIDE * ROWS, tokens), jnp.bfloat16)],
         compiler_params=pltpu.CompilerParams(vmem_limit_bytes=VMEM),
         cost_estimate=pl.CostEstimate(
             flops=2 * SIDE * SIDE * ROWS * tokens * width,
             bytes_accessed=2 * SIDE * width * (tokens + SIDE * ROWS),
             transcendentals=0,
         ),
-    )(experts, *blocks, *blocks)
+    )(places, *blocks, *blocks)
 
 
 def expert_kernel(n_ff, n_half, wg_ref, wu_ref, wd_ref, *refs):
@@ -220,95 +244,115 @@
     return done[:SIDE], done[SIDE:]
 
 
-def sum_kernel(top, experts_ref, *refs):
+def weigh(places_ref, first, top, facts, high_ref, low_ref):
+    tokens = high_ref.shape[1]
+    target = targets(places_ref, first, tuple(range(CHUNKS)), tokens)
+    for source in range(SIDE):
+        about = facts[source][...]
+        wide = about.astype(jnp.float32)
+        weight = jnp.zeros(target.shape, jnp.float32)
+        for k, code in enumerate(codes(about, top)):
+            one, two, three = (
+                wide[:, part * top + k : part * top + k + 1] for part in range(2, 5)
+            )
+            weight = jnp.where(code == target, one + two + three, weight)
+        high = weight.astype(jnp.bfloat16)
+        high_ref[source] = high
+        low_ref[source] = (weight - high.astype(jnp.float32)).astype(jnp.bfloat16)
+
+
+def sum_kernel(top, places_ref, *refs):
     count = CHUNKS * SIDE
-    ins, facts = refs[:count], refs[count : count + SIDE]
-    outs, high_ref, low_ref = refs[count + SIDE : -2], refs[-2], refs[-1]
-    tokens = high_ref.shape[1]
+    a_in, b_in, refs = refs[:count], refs[count : 2 * count], refs[2 * count :]
+    a_facts, b_facts, refs = refs[:SIDE], refs[SIDE : 2 * SIDE], refs[2 * SIDE :]
+    a_out, b_out, (high_ref, low_ref) = refs[0], refs[1 : 1 + SIDE], refs[1 + SIDE :]
 
     @pl.when(pl.program_id(0) == 0)
     def _():
-        target = targets(experts_ref, tuple(range(CHUNKS)), tokens)
-        for source in range(SIDE):
-            about = facts[source][...]
-            wide = about.astype(jnp.float32)
-            weight = jnp.zeros(target.shape, jnp.float32)
-            for k, code in enumerate(codes(about, top)):
-                first, second, third = (
-                    wide[:, part * top + k : part * top + k + 1] for part in range(2, 5)
-                )
-                weight = jnp.where(code == target, first + second + third, weight)
-            high = weight.astype(jnp.bfloat16)
-            high_ref[source] = high
-            low_ref[source] = (weight - high.astype(jnp.float32)).astype(jnp.bfloat16)
+        weigh(places_ref, 0, top, a_facts, high_ref.at[0], low_ref.at[0])
+        weigh(places_ref, 2 * SIDE, top, b_facts, high_ref.at[1], low_ref.at[1])
+
+    def total(half, source, ins):
+        rows = jnp.concatenate([ref[source] for ref in ins], axis=0)
+        out = jnp.dot(high_ref[half, source], rows, preferred_element_type=jnp.float32)
+        low = jnp.dot(low_ref[half, source], rows, preferred_element_type=jnp.float32)
+        return (out + low).astype(jnp.bfloat16)
 
     for source in range(SIDE):
-        rows = jnp.concatenate([ref[source] for ref in ins], axis=0)
-        total = jnp.dot(high_ref[source], rows, preferred_element_type=jnp.float32)
-        total = total + jnp.dot(low_ref[source], rows, preferred_element_type=jnp.float32)
-        outs[source][...] = total.astype(jnp.bfloat16)
-
-
-def sum_rows(top, experts, facts, blocks):
-    width = blocks[0].shape[-1]
-    tokens = facts[0].shape[0]
+        a_out[places_ref[SIDE + source]] = total(0, source, a_in)
+        b_out[source][...] = total(1, source, b_in)
+
+
+def sum_rows(top, places, a_facts, b_facts, a_blocks, b_blocks):
+    width = a_blocks[0].shape[-1]
+    tokens = b_facts[0].shape[0]
     tile = min(SUM_TILE, width)
     last = width // TILE
-    out = jax.ShapeDtypeStruct((tokens, width), jnp.bfloat16)
-    weights = pltpu.VMEM((SIDE, tokens, SIDE * CAP), jnp.bfloat16)
-    return pl.pallas_call(
+    block = pl.BlockSpec((SIDE, ROWS, tile), lambda i, places: (0, 0, i))
+    weights = pltpu.VMEM((2, SIDE, tokens, SIDE * CAP), jnp.bfloat16)
+    done = pl.pallas_call(
         functools.partial(sum_kernel, top),
-        grid=(width // tile,),
-        in_specs=[pl.BlockSpec(memory_space=pltpu.SMEM)]
-        + [pl.BlockSpec((SIDE, ROWS, tile), lambda i: (0, 0, i))] * len(blocks)
-        + [pl.BlockSpec((tokens, TILE), lambda i: (0, last))] * SIDE,
-        out_specs=[pl.BlockSpec((tokens, tile), lambda i: (0, i))] * SIDE,
-        out_shape=[out] * SIDE,
-        scratch_shapes=[weights, weights],
+        grid_spec=pltpu.PrefetchScalarGridSpec(
+            num_scalar_prefetch=1,
+            grid=(width // tile,),
+            in_specs=[block] * (len(a_blocks) + len(b_blocks))
+            + fact_specs(tokens, last)
+            + [pl.BlockSpec((tokens, TILE), lambda i, places: (0, last))] * SIDE,
+            out_specs=[pl.BlockSpec((SIDE, tokens, tile), lambda i, places: (0, 0, i))]
+            + [pl.BlockSpec((tokens, tile), lambda i, places: (0, i))] * SIDE,
+            scratch_shapes=[weights, weights],
+        ),
+        out_shape=[pltpu.HBM((SIDE, tokens, width), jnp.bfloat16)]
+        + [jax.ShapeDtypeStruct((tokens, width), jnp.bfloat16)] * SIDE,
         compiler_params=pltpu.CompilerParams(vmem_limit_bytes=VMEM),
         cost_estimate=pl.CostEstimate(
-            flops=4 * SIDE * SIDE * CAP * tokens * width,
-            bytes_accessed=2 * SIDE * width * (tokens + SIDE * CAP),
+            flops=8 * SIDE * SIDE * CAP * tokens * width,
+            bytes_accessed=4 * SIDE * width * (tokens + SIDE * CAP),
             transcendentals=0,
         ),
-    )(experts, *blocks, *facts)
+    )(places, *a_blocks, *b_blocks, *[a_facts] * SIDE, *b_facts)
+    return done[0], done[1:]
 
 
 def local(tokens, expert_ids, gate_values, gate_weight, up_weight, down_weight):
-    top = expert_ids.shape[1]
+    count, top = expert_ids.shape
     z, x = lax.axis_index("z"), lax.axis_index("x")
     steps = jnp.arange(SIDE, dtype=jnp.int32)
-    a_experts = z * SIDE + (x + steps) % SIDE
-    b_experts = (z + steps) % SIDE * SIDE + x
+    a_places = jnp.concatenate([z * SIDE + (x + steps) % SIDE, (z - steps) % SIDE])
+    b_places = jnp.concatenate([(z + steps) % SIDE * SIDE + x, steps * 0])
 
     a_half, b_half = prepare(tokens, expert_ids, gate_values)
-    a_rows = [a_half] + [shift(a_half, "z", k) for k in range(1, SIDE)]
+    a_rows = lax.all_gather(a_half, "z", axis=0, tiled=True)
+    a_rows = pltpu.with_memory_space_constraint(a_rows, pltpu.HBM)
     b_rows = [b_half] + [shift(b_half, "x", k) for k in range(1, SIDE)]
 
-    w_gate, w_up, w_down = gate_weight[0], up_weight[0], down_weight[0]
+    weights = gate_weight[0], up_weight[0], down_weight[0]
+    weights = [pltpu.with_memory_space_constraint(w, pltpu.HBM) for w in weights]
     a_back, b_back = [], []
     a_done = None
     for chunk in range(CHUNKS):
-        a_out = list(pack(chunk, top, a_experts, a_rows))
-        b_out = list(pack(chunk, top, b_experts, b_rows))
-        a_experts, b_experts, a_out, b_out = lax.optimization_barrier(
-            (a_experts, b_experts, a_out, b_out)
+        a_out = list(pack(chunk, top, a_places, [a_rows]))
+        b_out = list(pack(chunk, top, b_places, b_rows))
+        a_places, b_places, a_out, b_out = lax.optimization_barrier(
+            (a_places, b_places, a_out, b_out)
         )
         if chunk:
             b_out[2], a_done[0] = lax.optimization_barrier((b_out[2], a_done[0]))
-        a_in = [a_out[0]] + [shift(a_out[k], "x", k) for k in range(1, SIDE)]
-        b_in = [b_out[0]] + [shift(b_out[k], "z", k) for k in range(1, SIDE)]
-        a_done, b_done = expert(w_gate, w_up, w_down, a_in, b_in)
+        a_in, b_in = both_ways(a_out, b_out, "x", "z", 1)
+        a_done, b_done = expert(*weights, a_in, b_in)
         a_done = list(a_done)
-        a_back.append([a_done[0]] + [shift(a_done[k], "x", -k) for k in range(1, SIDE)])
-        b_back.append([b_done[0]] + [shift(b_done[k], "z", -k) for k in range(1, SIDE)])
-
-    a_sums = sum_rows(top, a_experts, a_rows, sum(a_back, []))
-    b_sums = sum_rows(top, b_experts, b_rows, sum(b_back, []))
-    a_home = [a_sums[0]] + [shift(a_sums[k], "z", -k) for k in range(1, SIDE)]
+        a_home, b_home = both_ways(a_done, b_done, "x", "z", -1)
+        a_back += a_home
+        b_back += b_home
+
+    places = jnp.concatenate([a_places, b_places])
+    a_sums, b_sums = sum_rows(top, places, a_rows, b_rows, a_back, b_back)
+    a_mixed = lax.psum_scatter(
+        a_sums.reshape(SIDE * count, -1), "z", scatter_dimension=0, tiled=True
+    )
     b_home = [b_sums[0]] + [shift(b_sums[k], "x", -k) for k in range(1, SIDE)]
-    mixed = [sum(part.astype(jnp.float32) for part in home) for home in (a_home, b_home)]
-    return jnp.concatenate(mixed, axis=1).astype(jnp.bfloat16)
+    b_mixed = sum(part.astype(jnp.float32) for part in b_home).astype(jnp.bfloat16)
+    return jnp.concatenate([a_mixed, b_mixed], axis=1)
 
 
 def solution(mesh):

time: 217 us -> 225 us (1.037)
  between operations: 0.17 us -> 13.6 us
  waiting for transfers between devices: 99.7 us -> 92.3 us
  local copies, waits for them, and re-layouts: 2.6 us -> 5.79 us
  starting transfers between devices: 56.8 us -> 54.1 us
    ppermute x36 -> x30, waiting for transfers between devices: 99.7 us -> 90.8 us  [shift(): lax.ppermute(block, axis, [(i, (i + step) % SIDE) for i in range(SIDE)])]
    unnamed x10 -> x18, local copies, waits for them, and re-layouts: 2.6 us -> 5.78 us
    ppermute x36 -> x30, starting transfers between devices: 56.8 us -> 54 us  [shift(): lax.ppermute(block, axis, [(i, (i + step) % SIDE) for i in range(SIDE)])]
    pallas_call x6 -> x5, Pallas kernels: 23.9 us -> 22.8 us  [the longest x4 13.4 us: pack(): pl.pallas_call(functools.partial(pack_kernel, chunk, top), grid_spec=pltp...]
  transfers between devices with their start and end apart: 36 -> 32, of which waited for: 18 -> 17; matrix products, arithmetic and copies ran while one was open for 0% -> 0% of each run, Pallas kernels for 23% -> 18%
where the time goes in v4:
time: 225 us; the launch traced here: 223 us
  waiting for transfers between devices  92.3 us (41%)
  Pallas kernels  55.1 us (24%)
  starting transfers between devices  54.1 us (24%)
  between operations  13.6 us (6%)
  local copies, waits for them, and re-layouts  5.79 us (3%)
  other arithmetic  2.6 us (1%)
    ppermute x30, waiting for transfers between devices, shift(): lax.ppermute(block, axis, [(i, (i + step) % SIDE) for i in range(SIDE)])  90.8 us
    ppermute x30, starting transfers between devices, shift(): lax.ppermute(block, axis, [(i, (i + step) % SIDE) for i in range(SIDE)])  54 us
    pallas_call x2, Pallas kernels, expert(): pl.pallas_call(functools.partial(expert_kernel, n_ff, n_half), grid=(n_ff...  31 us
    pallas_call x4, Pallas kernels, pack(): pl.pallas_call(functools.partial(pack_kernel, chunk, top), grid_spec=pltp...  13.4 us
    pallas_call x1, Pallas kernels, sum_rows(): pl.pallas_call(functools.partial(sum_kernel, top), grid_spec=pltpu.Prefet...  9.34 us
    unnamed x18, local copies, waits for them, and re-layouts  5.78 us
  transfers between devices with their start and end apart: 32, of which 17 were waited for; matrix products, arithmetic and copies ran while one was open for 0% of the time, Pallas kernels for 18%

profile of v4, /device:TPU:0, one launch (start us, length us, event | category | flops | bytes accessed | tf_op | source)
XLA Modules:
  0.0 223.5 jit_solution(16827860638908146785)
XLA Ops:
  10.6 2.9 %collective-permute-start.2 = (bf16[128,2176]{1,0:T(8,128)(2,1)S(1)}, bf16[128,2176]{1,0:T(8,128)(2,1)S(1)}, u32[]{:S(2)}, u32[]{:S(2)}) collective-permute-start(bf16[128,2176]{1,0:T(8,128)(2,1)S(1)} %get-tuple-element.70.refs_0_.refs_4_.refs_20_), channel_id=1, source_target_pairs={{0,3},{1,0},{2,1},{3,2},{4,7},{5,4},{6,5},{7,6},{8,11},{9,8},{10,9... | collective-permute-start | bytes 1671176 | tf_op jit(solution)/shard_map/ppermute | solution.py:23
  15.3 22.0 %collective-permute-done.2.refs_3_.refs_7_.refs_23_ = bf16[128,2176]{1,0:T(8,128)(2,1)S(1)} collective-permute-done((bf16[128,2176]{1,0:T(8,128)(2,1)S(1)}, bf16[128,2176]{1,0:T(8,128)(2,1)S(1)}, u32[]{:S(2)}, u32[]{:S(2)}) %collective-permute-start.2) | collective-permute-done | bytes 557088 | tf_op jit(solution)/shard_map/ppermute | solution.py:23
  37.3 3.7 %collective-permute-done.refs_1_.refs_5_.refs_21_ = bf16[128,2176]{1,0:T(8,128)(2,1)S(1)} collective-permute-done((bf16[128,2176]{1,0:T(8,128)(2,1)S(1)}, bf16[128,2176]{1,0:T(8,128)(2,1)S(1)}, u32[]{:S(2)}, u32[]{:S(2)}) %collective-permute-start) | collective-permute-done | bytes 557088 | tf_op jit(solution)/shard_map/ppermute | solution.py:23
  41.0 2.9 %shard_map.66 = (bf16[4,32,2048]{2,1,0:T(8,128)(2,1)S(1)}, bf16[4,32,2048]{2,1,0:T(8,128)(2,1)S(1)}, bf16[4,32,2048]{2,1,0:T(8,128)(2,1)S(1)}, bf16[4,32,2048]{2,1,0:T(8,128)(2,1)S(1)}) custom-call(s32[8]{0:T(128)S(1)} %concatenate.13.places_ref, bf16[128,2176]{1,0:T(8,128)(2,1)S(1)} %get-tuple-element.70.refs_0_.refs_4_.refs_20_, ...), custom_call_target="tpu_custom_call" | custom-call | flops 268435456 | bytes 4194304 | tf_op jit(solution)/shard_map/pallas_call | solution.py:139
  45.6 3.8 %shard_map.65 = (bf16[4,32,2048]{2,1,0:T(8,128)(2,1)S(1)}, bf16[4,32,2048]{2,1,0:T(8,128)(2,1)S(1)}, bf16[4,32,2048]{2,1,0:T(8,128)(2,1)S(1)}, bf16[4,32,2048]{2,1,0:T(8,128)(2,1)S(1)}) custom-call(s32[8]{0:T(128)S(1)} %pad_add_fusion.places_ref, ...), custom_call_target="tpu_custom_call" | custom-call | flops 268435456 | bytes 4194304 | tf_op jit(solution)/shard_map/pallas_call | solution.py:139
  50.6 2.7 %collective-permute-start.4 = (bf16[4,32,2048]{2,1,0:T(8,128)(2,1)S(1)}, bf16[4,32,2048]{2,1,0:T(8,128)(2,1)S(1)}, u32[]{:S(2)}, u32[]{:S(2)}) collective-permute-start(bf16[4,32,2048]{2,1,0:T(8,128)(2,1)S(1)} %get-tuple-element.89), channel_id=1, source_target_pairs={{0,2},{1,3},{2,0},{3,1},{4,6},{5,7},{6,4},{7,5},{8,10},{9,11},{10,... | collective-permute-start | bytes 1572872 | tf_op jit(solution)/shard_map/ppermute | solution.py:23
  55.2 3.1 %collective-permute-start.7 = (bf16[4,32,2048]{2,1,0:T(8,128)(2,1)S(1)}, bf16[4,32,2048]{2,1,0:T(8,128)(2,1)S(1)}, u32[]{:S(2)}, u32[]{:S(2)}) collective-permute-start(bf16[4,32,2048]{2,1,0:T(8,128)(2,1)S(1)} %copy-done.4), channel_id=1, source_target_pairs={{0,8},{4,12},{8,0},{12,4},{1,9},{5,13},{9,1},{13,5},{2,10},{6,14},... | collective-permute-start | bytes 1572872 | tf_op jit(solution)/shard_map/ppermute | solution.py:23
  58.4 7.0 %collective-permute-done.3.refs_1_ = bf16[4,32,2048]{2,1,0:T(8,128)(2,1)S(1)} collective-permute-done((bf16[4,32,2048]{2,1,0:T(8,128)(2,1)S(1)}, bf16[4,32,2048]{2,1,0:T(8,128)(2,1)S(1)}, u32[]{:S(2)}, u32[]{:S(2)}) %collective-permute-start.3) | collective-permute-done | bytes 524320 | tf_op jit(solution)/shard_map/ppermute | solution.py:23
  65.4 14.5 %collective-permute-start.8 = (bf16[4,32,2048]{2,1,0:T(8,128)(2,1)S(1)}, bf16[4,32,2048]{2,1,0:T(8,128)(2,1)S(1)}, u32[]{:S(2)}, u32[]{:S(2)}) collective-permute-start(bf16[4,32,2048]{2,1,0:T(8,128)(2,1)S(1)} %get-tuple-element.94), channel_id=1, source_target_pairs={{0,12},{4,0},{8,4},{12,8},{1,13},{5,1},{9,5},{13,9},{2,14},{6,2},{... | collective-permute-start | bytes 1572872 | tf_op jit(solution)/shard_map/ppermute | solution.py:23
  79.9 3.8 %shard_map.67 = (bf16[4,32,2048]{2,1,0:T(8,128)(2,1)S(1)}, bf16[4,32,2048]{2,1,0:T(8,128)(2,1)S(1)}, bf16[4,32,2048]{2,1,0:T(8,128)(2,1)S(1)}, bf16[4,32,2048]{2,1,0:T(8,128)(2,1)S(1)}) custom-call(s32[8]{0:T(128)S(1)} %pad_add_fusion.places_ref, ...), custom_call_target="tpu_custom_call" | custom-call | flops 268435456 | bytes 4194304 | tf_op jit(solution)/shard_map/pallas_call | solution.py:139
  83.6 2.9 %shard_map.68 = (bf16[4,32,2048]{2,1,0:T(8,128)(2,1)S(1)}, bf16[4,32,2048]{2,1,0:T(8,128)(2,1)S(1)}, bf16[4,32,2048]{2,1,0:T(8,128)(2,1)S(1)}, bf16[4,32,2048]{2,1,0:T(8,128)(2,1)S(1)}) custom-call(s32[8]{0:T(128)S(1)} %concatenate.13.places_ref, bf16[128,2176]{1,0:T(8,128)(2,1)S(1)} %get-tuple-element.70.refs_0_.refs_4_.refs_20_, ...), custom_call_target="tpu_custom_call" | custom-call | flops 268435456 | bytes 4194304 | tf_op jit(solution)/shard_map/pallas_call | solution.py:139
  87.7 2.3 %collective-permute-start.14 = (bf16[4,32,2048]{2,1,0:T(8,128)(2,1)S(1)}, bf16[4,32,2048]{2,1,0:T(8,128)(2,1)S(1)}, u32[]{:S(2)}, u32[]{:S(2)}) collective-permute-start(bf16[4,32,2048]{2,1,0:T(8,128)(2,1)S(1)} %get-tuple-element.102), channel_id=1, source_target_pairs={{0,3},{1,0},{2,1},{3,2},{4,7},{5,4},{6,5},{7,6},{8,11},{9,8},{10,9... | collective-permute-start | bytes 1572872 | tf_op jit(solution)/shard_map/ppermute | solution.py:23
  90.5 3.7 %collective-permute-start.17 = (bf16[4,32,2048]{2,1,0:T(8,128)(2,1)S(1)}, bf16[4,32,2048]{2,1,0:T(8,128)(2,1)S(1)}, u32[]{:S(2)}, u32[]{:S(2)}) collective-permute-start(bf16[4,32,2048]{2,1,0:T(8,128)(2,1)S(1)} %get-tuple-element.107), channel_id=1, source_target_pairs={{0,12},{4,0},{8,4},{12,8},{1,13},{5,1},{9,5},{13,9},{2,14},{6,2},{... | collective-permute-start | bytes 1572872 | tf_op jit(solution)/shard_map/ppermute | solution.py:23
  94.2 15.5 %shard_map.69 = (bf16[4,32,2048]{2,1,0:T(8,128)(2,1)S(1)}, bf16[4,32,2048]{2,1,0:T(8,128)(2,1)S(1)}, bf16[4,32,2048]{2,1,0:T(8,128)(2,1)S(1)}, bf16[4,32,2048]{2...) custom-call(bf16[4096,768]{1,0:T(8,128)(2,1)} %bitcast.9, ...), custom_call_target="tpu_custom_call" | custom-call | flops 9663676416 | bytes 27262976 | tf_op jit(solution)/shard_map/pallas_call | solution.py:225
  109.7 2.3 %collective-permute-done.12.refs_1_ = bf16[4,32,2048]{2,1,0:T(8,128)(2,1)S(1)} collective-permute-done((bf16[4,32,2048]{2,1,0:T(8,128)(2,1)S(1)}, bf16[4,32,2048]{2,1,0:T(8,128)(2,1)S(1)}, u32[]{:S(2)}, u32[]{:S(2)}) %collective-permute-start.12) | collective-permute-done | bytes 524320 | tf_op jit(solution)/shard_map/ppermute | solution.py:23
  113.4 2.7 %collective-permute-start.11 = (bf16[4,32,2048]{2,1,0:T(8,128)(2,1)S(1)}, bf16[4,32,2048]{2,1,0:T(8,128)(2,1)S(1)}, u32[]{:S(2)}, u32[]{:S(2)}) collective-permute-start(bf16[4,32,2048]{2,1,0:T(8,128)(2,1)S(1)} %get-tuple-element.98), channel_id=1, source_target_pairs={{0,1},{1,2},{2,3},{3,0},{4,5},{5,6},{6,7},{7,4},{8,9},{9,10},{10,1... | collective-permute-start | bytes 1572872 | tf_op jit(solution)/shard_map/ppermute | solution.py:23
  116.4 8.9 %collective-permute-done.16.refs_6_ = bf16[4,32,2048]{2,1,0:T(8,128)(2,1)S(1)} collective-permute-done((bf16[4,32,2048]{2,1,0:T(8,128)(2,1)S(1)}, bf16[4,32,2048]{2,1,0:T(8,128)(2,1)S(1)}, u32[]{:S(2)}, u32[]{:S(2)}) %collective-permute-start.16) | collective-permute-done | bytes 524320 | tf_op jit(solution)/shard_map/ppermute | solution.py:23
  125.6 15.5 %shard_map.70 = (bf16[4,32,2048]{2,1,0:T(8,128)(2,1)S(1)}, bf16[4,32,2048]{2,1,0:T(8,128)(2,1)S(1)}, bf16[4,32,2048]{2,1,0:T(8,128)(2,1)S(1)}, bf16[4,32,2048]{2...) custom-call(bf16[4096,768]{1,0:T(8,128)(2,1)} %bitcast.10, ...), custom_call_target="tpu_custom_call" | custom-call | flops 9663676416 | bytes 27262976 | tf_op jit(solution)/shard_map/pallas_call | solution.py:225
  141.1 3.9 %collective-permute-start.23 = (bf16[4,32,2048]{2,1,0:T(8,128)(2,1)S(1)}, bf16[4,32,2048]{2,1,0:T(8,128)(2,1)S(1)}, u32[]{:S(2)}, u32[]{:S(2)}) collective-permute-start(bf16[4,32,2048]{2,1,0:T(8,128)(2,1)S(1)} %get-tuple-element.115), channel_id=1, source_target_pairs={{0,4},{4,8},{8,12},{12,0},{1,5},{5,9},{9,13},{13,1},{2,6},{6,10},{... | collective-permute-start | bytes 1572872 | tf_op jit(solution)/shard_map/ppermute | solution.py:23
  145.2 2.0 collective-permute-start.20
  147.2 2.3 %collective-permute-start.24 = (bf16[4,32,2048]{2,1,0:T(8,128)(2,1)S(1)}, bf16[4,32,2048]{2,1,0:T(8,128)(2,1)S(1)}, u32[]{:S(2)}, u32[]{:S(2)}) collective-permute-start(bf16[4,32,2048]{2,1,0:T(8,128)(2,1)S(1)} %get-tuple-element.117), channel_id=1, source_target_pairs={{0,12},{4,0},{8,4},{12,8},{1,13},{5,1},{9,5},{13,9},{2,14},{6,2},{... | collective-permute-start | bytes 1572872 | tf_op jit(solution)/shard_map/ppermute | solution.py:23
  149.5 3.9 %collective-permute-done.23.refs_11_ = bf16[4,32,2048]{2,1,0:T(8,128)(2,1)S(1)} collective-permute-done((bf16[4,32,2048]{2,1,0:T(8,128)(2,1)S(1)}, bf16[4,32,2048]{2,1,0:T(8,128)(2,1)S(1)}, u32[]{:S(2)}, u32[]{:S(2)}) %collective-permute-start.23) | collective-permute-done | bytes 524320 | tf_op jit(solution)/shard_map/ppermute | solution.py:23
  153.4 2.4 %collective-permute-start.25 = (bf16[4,32,2048]{2,1,0:T(8,128)(2,1)S(1)}, bf16[4,32,2048]{2,1,0:T(8,128)(2,1)S(1)}, u32[]{:S(2)}, u32[]{:S(2)}) collective-permute-start(bf16[4,32,2048]{2,1,0:T(8,128)(2,1)S(1)} %get-tuple-element.118), channel_id=1, source_target_pairs={{0,8},{4,12},{8,0},{12,4},{1,9},{5,13},{9,1},{13,5},{2,10},{6,14},... | collective-permute-start | bytes 1572872 | tf_op jit(solution)/shard_map/ppermute | solution.py:23
  155.8 2.3 %collective-permute-done.18.refs_5_ = bf16[4,32,2048]{2,1,0:T(8,128)(2,1)S(1)} collective-permute-done((bf16[4,32,2048]{2,1,0:T(8,128)(2,1)S(1)}, bf16[4,32,2048]{2,1,0:T(8,128)(2,1)S(1)}, u32[]{:S(2)}, u32[]{:S(2)}) %collective-permute-start.18) | collective-permute-done | bytes 524320 | tf_op jit(solution)/shard_map/ppermute | solution.py:23
  160.1 5.3 %collective-permute-done.20.refs_7_ = bf16[4,32,2048]{2,1,0:T(8,128)(2,1)S(1)} collective-permute-done((bf16[4,32,2048]{2,1,0:T(8,128)(2,1)S(1)}, bf16[4,32,2048]{2,1,0:T(8,128)(2,1)S(1)}, u32[]{:S(2)}, u32[]{:S(2)}) %collective-permute-start.20) | collective-permute-done | bytes 524320 | tf_op jit(solution)/shard_map/ppermute | solution.py:23
  165.4 2.8 %collective-permute-done.24.refs_13_ = bf16[4,32,2048]{2,1,0:T(8,128)(2,1)S(1)} collective-permute-done((bf16[4,32,2048]{2,1,0:T(8,128)(2,1)S(1)}, bf16[4,32,2048]{2,1,0:T(8,128)(2,1)S(1)}, u32[]{:S(2)}, u32[]{:S(2)}) %collective-permute-start.24) | collective-permute-done | bytes 524320 | tf_op jit(solution)/shard_map/ppermute | solution.py:23
  169.7 6.4 %collective-permute-done.26.refs_15_ = bf16[4,32,2048]{2,1,0:T(8,128)(2,1)S(1)} collective-permute-done((bf16[4,32,2048]{2,1,0:T(8,128)(2,1)S(1)}, bf16[4,32,2048]{2,1,0:T(8,128)(2,1)S(1)}, u32[]{:S(2)}, u32[]{:S(2)}) %collective-permute-start.26) | collective-permute-done | bytes 524320 | tf_op jit(solution)/shard_map/ppermute | solution.py:23
  176.2 9.3 %shard_map.71 = (bf16[4,128,2048]{2,1,0:T(8,128)(2,1)}, bf16[128,2048]{1,0:T(8,128)(2,1)S(1)}, bf16[128,2048]{1,0:T(8,128)(2,1)S(1)}, bf16[128,2048]{1,0:T(8,128)(2,1)S(1)}, bf16[128,2048]{1,0:T(8,128)(2,1)S(1)}) custom-call(s32[16]{0:T(128)S(1)} %pad_add_fusion.1.places_ref, bf16[4,32,2048]{2,1,0:T(8,128)(2,1)S(1)} %get-tuple-element.95.refs_0_, ...), custom_call_target="tpu_custom_call" | custom-call | flops 2147483648 | bytes 12582912 | tf_op jit(solution)/shard_map/pallas_call | solution.py:293
  187.3 1.9 collective-permute-start.29
  189.2 13.0 %collective-permute-done.27 = bf16[128,2048]{1,0:T(8,128)(2,1)S(1)} collective-permute-done((bf16[128,2048]{1,0:T(8,128)(2,1)}, bf16[128,2048]{1,0:T(8,128)(2,1)S(1)}, u32[]{:S(2)}, u32[]{:S(2)}) %collective-permute-start.27) | collective-permute-done | bytes 524320 | tf_op jit(solution)/shard_map/ppermute | solution.py:23
  203.9 8.8 %collective-permute-done.29 = bf16[128,2048]{1,0:T(8,128)(2,1)S(1)} collective-permute-done((bf16[128,2048]{1,0:T(8,128)(2,1)S(1)}, bf16[128,2048]{1,0:T(8,128)(2,1)S(1)}, u32[]{:S(2)}, u32[]{:S(2)}) %collective-permute-start.29) | collective-permute-done | bytes 524320 | tf_op jit(solution)/shard_map/ppermute | solution.py:23
  214.5 2.1 pad_maximum_fusion
  (67 shorter events, 23.1 us)
Async XLA Ops:
  6.5 39.0 %all-gather.2.cloned.1.call-start = ((), (), s32[]{:S(2)}) async-start(), calls=%async_computation.1 | async-start | bytes 2785280 | tf_op jit(solution)/shard_map/all_gather | solution.py:325
  10.6 204.0 %reduce-scatter.2.cloned.1.call-start = ((), (), s32[]{:S(2)}) async-start(), calls=%async_computation.2 | async-start | bytes 2621440 | tf_op jit(solution)/shard_map/reduce_scatter | solution.py:350
  10.6 26.7 %collective-permute-start.2 = (bf16[128,2176]{1,0:T(8,128)(2,1)S(1)}, bf16[128,2176]{1,0:T(8,128)(2,1)S(1)}, u32[]{:S(2)}, u32[]{:S(2)}) collective-permute-start(bf16[128,2176]{1,0:T(8,128)(2,1)S(1)} %get-tuple-element.70.refs_0_.refs_4_.refs_20_), channel_id=1, source_target_pairs={{0,3},{1,0},{2,1},{3,2},{4,7},{5,4},{6,5},{7,6},{8,11},{9,8},{10,9... | collective-permute-start | bytes 1671176 | tf_op jit(solution)/shard_map/ppermute | solution.py:23
  13.5 23.8 %collective-permute-start.1 = (bf16[128,2176]{1,0:T(8,128)(2,1)S(1)}, bf16[128,2176]{1,0:T(8,128)(2,1)S(1)}, u32[]{:S(2)}, u32[]{:S(2)}) collective-permute-start(bf16[128,2176]{1,0:T(8,128)(2,1)S(1)} %get-tuple-element.70.refs_0_.refs_4_.refs_20_), channel_id=1, source_target_pairs={{0,2},{1,3},{2,0},{3,1},{4,6},{5,7},{6,4},{7,5},{8,10},{9,11},{10,... | collective-permute-start | bytes 1671176 | tf_op jit(solution)/shard_map/ppermute | solution.py:23
  14.3 26.7 %collective-permute-start = (bf16[128,2176]{1,0:T(8,128)(2,1)S(1)}, bf16[128,2176]{1,0:T(8,128)(2,1)S(1)}, u32[]{:S(2)}, u32[]{:S(2)}) collective-permute-start(bf16[128,2176]{1,0:T(8,128)(2,1)S(1)} %get-tuple-element.70.refs_0_.refs_4_.refs_20_), channel_id=1, source_target_pairs={{0,1},{1,2},{2,3},{3,0},{4,5},{5,6},{6,7},{7,4},{8,9},{9,10},{10,1... | collective-permute-start | bytes 1671176 | tf_op jit(solution)/shard_map/ppermute | solution.py:23
  49.3 16.0 %collective-permute-start.3 = (bf16[4,32,2048]{2,1,0:T(8,128)(2,1)S(1)}, bf16[4,32,2048]{2,1,0:T(8,128)(2,1)S(1)}, u32[]{:S(2)}, u32[]{:S(2)}) collective-permute-start(bf16[4,32,2048]{2,1,0:T(8,128)(2,1)S(1)} %get-tuple-element.88), channel_id=1, source_target_pairs={{0,1},{1,2},{2,3},{3,0},{4,5},{5,6},{6,7},{7,4},{8,9},{9,10},{10,1... | collective-permute-start | bytes 1572872 | tf_op jit(solution)/shard_map/ppermute | solution.py:23
  50.6 36.0 %collective-permute-start.4 = (bf16[4,32,2048]{2,1,0:T(8,128)(2,1)S(1)}, bf16[4,32,2048]{2,1,0:T(8,128)(2,1)S(1)}, u32[]{:S(2)}, u32[]{:S(2)}) collective-permute-start(bf16[4,32,2048]{2,1,0:T(8,128)(2,1)S(1)} %get-tuple-element.89), channel_id=1, source_target_pairs={{0,2},{1,3},{2,0},{3,1},{4,6},{5,7},{6,4},{7,5},{8,10},{9,11},{10,... | collective-permute-start | bytes 1572872 | tf_op jit(solution)/shard_map/ppermute | solution.py:23
  53.3 33.4 %collective-permute-start.5 = (bf16[4,32,2048]{2,1,0:T(8,128)(2,1)S(1)}, bf16[4,32,2048]{2,1,0:T(8,128)(2,1)S(1)}, u32[]{:S(2)}, u32[]{:S(2)}) collective-permute-start(bf16[4,32,2048]{2,1,0:T(8,128)(2,1)S(1)} %get-tuple-element.90), channel_id=1, source_target_pairs={{0,3},{1,0},{2,1},{3,2},{4,7},{5,4},{6,5},{7,6},{8,11},{9,8},{10,9... | collective-permute-start | bytes 1572872 | tf_op jit(solution)/shard_map/ppermute | solution.py:23
  54.8 32.9 %collective-permute-start.6 = (bf16[4,32,2048]{2,1,0:T(8,128)(2,1)S(1)}, bf16[4,32,2048]{2,1,0:T(8,128)(2,1)S(1)}, u32[]{:S(2)}, u32[]{:S(2)}) collective-permute-start(bf16[4,32,2048]{2,1,0:T(8,128)(2,1)S(1)} %copy-done.6), channel_id=1, source_target_pairs={{0,4},{4,8},{8,12},{12,0},{1,5},{5,9},{9,13},{13,1},{2,6},{6,10},{... | collective-permute-start | bytes 1572872 | tf_op jit(solution)/shard_map/ppermute | solution.py:23
  55.2 34.7 %collective-permute-start.7 = (bf16[4,32,2048]{2,1,0:T(8,128)(2,1)S(1)}, bf16[4,32,2048]{2,1,0:T(8,128)(2,1)S(1)}, u32[]{:S(2)}, u32[]{:S(2)}) collective-permute-start(bf16[4,32,2048]{2,1,0:T(8,128)(2,1)S(1)} %copy-done.4), channel_id=1, source_target_pairs={{0,8},{4,12},{8,0},{12,4},{1,9},{5,13},{9,1},{13,5},{2,10},{6,14},... | collective-permute-start | bytes 1572872 | tf_op jit(solution)/shard_map/ppermute | solution.py:23
  65.4 25.1 %collective-permute-start.8 = (bf16[4,32,2048]{2,1,0:T(8,128)(2,1)S(1)}, bf16[4,32,2048]{2,1,0:T(8,128)(2,1)S(1)}, u32[]{:S(2)}, u32[]{:S(2)}) collective-permute-start(bf16[4,32,2048]{2,1,0:T(8,128)(2,1)S(1)} %get-tuple-element.94), channel_id=1, source_target_pairs={{0,12},{4,0},{8,4},{12,8},{1,13},{5,1},{9,5},{13,9},{2,14},{6,2},{... | collective-permute-start | bytes 1572872 | tf_op jit(solution)/shard_map/ppermute | solution.py:23
  86.6 25.3 %collective-permute-start.12 = (bf16[4,32,2048]{2,1,0:T(8,128)(2,1)S(1)}, bf16[4,32,2048]{2,1,0:T(8,128)(2,1)S(1)}, u32[]{:S(2)}, u32[]{:S(2)}) collective-permute-start(bf16[4,32,2048]{2,1,0:T(8,128)(2,1)S(1)} %get-tuple-element.100), channel_id=1, source_target_pairs={{0,1},{1,2},{2,3},{3,0},{4,5},{5,6},{6,7},{7,4},{8,9},{9,10},{10,1... | collective-permute-start | bytes 1572872 | tf_op jit(solution)/shard_map/ppermute | solution.py:23
  86.7 25.3 %collective-permute-start.13 = (bf16[4,32,2048]{2,1,0:T(8,128)(2,1)S(1)}, bf16[4,32,2048]{2,1,0:T(8,128)(2,1)S(1)}, u32[]{:S(2)}, u32[]{:S(2)}) collective-permute-start(bf16[4,32,2048]{2,1,0:T(8,128)(2,1)S(1)} %get-tuple-element.101), channel_id=1, source_target_pairs={{0,2},{1,3},{2,0},{3,1},{4,6},{5,7},{6,4},{7,5},{8,10},{9,11},{10,... | collective-permute-start | bytes 1572872 | tf_op jit(solution)/shard_map/ppermute | solution.py:23
  87.7 24.9 %collective-permute-start.14 = (bf16[4,32,2048]{2,1,0:T(8,128)(2,1)S(1)}, bf16[4,32,2048]{2,1,0:T(8,128)(2,1)S(1)}, u32[]{:S(2)}, u32[]{:S(2)}) collective-permute-start(bf16[4,32,2048]{2,1,0:T(8,128)(2,1)S(1)} %get-tuple-element.102), channel_id=1, source_target_pairs={{0,3},{1,0},{2,1},{3,2},{4,7},{5,4},{6,5},{7,6},{8,11},{9,8},{10,9... | collective-permute-start | bytes 1572872 | tf_op jit(solution)/shard_map/ppermute | solution.py:23
  90.0 23.5 %collective-permute-start.15 = (bf16[4,32,2048]{2,1,0:T(8,128)(2,1)S(1)}, bf16[4,32,2048]{2,1,0:T(8,128)(2,1)S(1)}, u32[]{:S(2)}, u32[]{:S(2)}) collective-permute-start(bf16[4,32,2048]{2,1,0:T(8,128)(2,1)S(1)} %get-tuple-element.104), channel_id=1, source_target_pairs={{0,4},{4,8},{8,12},{12,0},{1,5},{5,9},{9,13},{13,1},{2,6},{6,10},{... | collective-permute-start | bytes 1572872 | tf_op jit(solution)/shard_map/ppermute | solution.py:23
  90.5 25.7 %collective-permute-start.17 = (bf16[4,32,2048]{2,1,0:T(8,128)(2,1)S(1)}, bf16[4,32,2048]{2,1,0:T(8,128)(2,1)S(1)}, u32[]{:S(2)}, u32[]{:S(2)}) collective-permute-start(bf16[4,32,2048]{2,1,0:T(8,128)(2,1)S(1)} %get-tuple-element.107), channel_id=1, source_target_pairs={{0,12},{4,0},{8,4},{12,8},{1,13},{5,1},{9,5},{13,9},{2,14},{6,2},{... | collective-permute-start | bytes 1572872 | tf_op jit(solution)/shard_map/ppermute | solution.py:23
  111.9 13.4 %collective-permute-start.16 = (bf16[4,32,2048]{2,1,0:T(8,128)(2,1)S(1)}, bf16[4,32,2048]{2,1,0:T(8,128)(2,1)S(1)}, u32[]{:S(2)}, u32[]{:S(2)}) collective-permute-start(bf16[4,32,2048]{2,1,0:T(8,128)(2,1)S(1)} %get-tuple-element.106), channel_id=1, source_target_pairs={{0,8},{4,12},{8,0},{12,4},{1,9},{5,13},{9,1},{13,5},{2,10},{6,14},... | collective-permute-start | bytes 1572872 | tf_op jit(solution)/shard_map/ppermute | solution.py:23
  111.9 29.2 %collective-permute-start.9 = (bf16[4,32,2048]{2,1,0:T(8,128)(2,1)S(1)}, bf16[4,32,2048]{2,1,0:T(8,128)(2,1)S(1)}, u32[]{:S(2)}, u32[]{:S(2)}) collective-permute-start(bf16[4,32,2048]{2,1,0:T(8,128)(2,1)S(1)} %get-tuple-element.96), channel_id=1, source_target_pairs={{0,3},{1,0},{2,1},{3,2},{4,7},{5,4},{6,5},{7,6},{8,11},{9,8},{10,9... | collective-permute-start | bytes 1572872 | tf_op jit(solution)/shard_map/ppermute | solution.py:23
  112.6 32.5 %collective-permute-start.10 = (bf16[4,32,2048]{2,1,0:T(8,128)(2,1)S(1)}, bf16[4,32,2048]{2,1,0:T(8,128)(2,1)S(1)}, u32[]{:S(2)}, u32[]{:S(2)}) collective-permute-start(bf16[4,32,2048]{2,1,0:T(8,128)(2,1)S(1)} %get-tuple-element.97), channel_id=1, source_target_pairs={{0,2},{1,3},{2,0},{3,1},{4,6},{5,7},{6,4},{7,5},{8,10},{9,11},{10,... | collective-permute-start | bytes 1572872 | tf_op jit(solution)/shard_map/ppermute | solution.py:23
  113.4 31.6 %collective-permute-start.11 = (bf16[4,32,2048]{2,1,0:T(8,128)(2,1)S(1)}, bf16[4,32,2048]{2,1,0:T(8,128)(2,1)S(1)}, u32[]{:S(2)}, u32[]{:S(2)}) collective-permute-start(bf16[4,32,2048]{2,1,0:T(8,128)(2,1)S(1)} %get-tuple-element.98), channel_id=1, source_target_pairs={{0,1},{1,2},{2,3},{3,0},{4,5},{5,6},{6,7},{7,4},{8,9},{9,10},{10,1... | collective-permute-start | bytes 1572872 | tf_op jit(solution)/shard_map/ppermute | solution.py:23
  116.1 29.0 %collective-permute-start.21 = (bf16[4,32,2048]{2,1,0:T(8,128)(2,1)S(1)}, bf16[4,32,2048]{2,1,0:T(8,128)(2,1)S(1)}, u32[]{:S(2)}, u32[]{:S(2)}) collective-permute-start(bf16[4,32,2048]{2,1,0:T(8,128)(2,1)S(1)} %get-tuple-element.113), channel_id=1, source_target_pairs={{0,12},{4,0},{8,4},{12,8},{1,13},{5,1},{9,5},{13,9},{2,14},{6,2},{... | collective-permute-start | bytes 1572872 | tf_op jit(solution)/shard_map/ppermute | solution.py:23
  125.3 21.8 %collective-permute-start.22 = (bf16[4,32,2048]{2,1,0:T(8,128)(2,1)S(1)}, bf16[4,32,2048]{2,1,0:T(8,128)(2,1)S(1)}, u32[]{:S(2)}, u32[]{:S(2)}) collective-permute-start(bf16[4,32,2048]{2,1,0:T(8,128)(2,1)S(1)} %get-tuple-element.114), channel_id=1, source_target_pairs={{0,8},{4,12},{8,0},{12,4},{1,9},{5,13},{9,1},{13,5},{2,10},{6,14},... | collective-permute-start | bytes 1572872 | tf_op jit(solution)/shard_map/ppermute | solution.py:23
  141.1 12.3 %collective-permute-start.23 = (bf16[4,32,2048]{2,1,0:T(8,128)(2,1)S(1)}, bf16[4,32,2048]{2,1,0:T(8,128)(2,1)S(1)}, u32[]{:S(2)}, u32[]{:S(2)}) collective-permute-start(bf16[4,32,2048]{2,1,0:T(8,128)(2,1)S(1)} %get-tuple-element.115), channel_id=1, source_target_pairs={{0,4},{4,8},{8,12},{12,0},{1,5},{5,9},{9,13},{13,1},{2,6},{6,10},{... | collective-permute-start | bytes 1572872 | tf_op jit(solution)/shard_map/ppermute | solution.py:23
  145.1 13.1 %collective-permute-start.18 = (bf16[4,32,2048]{2,1,0:T(8,128)(2,1)S(1)}, bf16[4,32,2048]{2,1,0:T(8,128)(2,1)S(1)}, u32[]{:S(2)}, u32[]{:S(2)}) collective-permute-start(bf16[4,32,2048]{2,1,0:T(8,128)(2,1)S(1)} %get-tuple-element.109), channel_id=1, source_target_pairs={{0,3},{1,0},{2,1},{3,2},{4,7},{5,4},{6,5},{7,6},{8,11},{9,8},{10,9... | collective-permute-start | bytes 1572872 | tf_op jit(solution)/shard_map/ppermute | solution.py:23
  145.1 15.0 %collective-permute-start.19 = (bf16[4,32,2048]{2,1,0:T(8,128)(2,1)S(1)}, bf16[4,32,2048]{2,1,0:T(8,128)(2,1)S(1)}, u32[]{:S(2)}, u32[]{:S(2)}) collective-permute-start(bf16[4,32,2048]{2,1,0:T(8,128)(2,1)S(1)} %get-tuple-element.110), channel_id=1, source_target_pairs={{0,2},{1,3},{2,0},{3,1},{4,6},{5,7},{6,4},{7,5},{8,10},{9,11},{10,... | collective-permute-start | bytes 1572872 | tf_op jit(solution)/shard_map/ppermute | solution.py:23
  145.2 20.2 %collective-permute-start.20 = (bf16[4,32,2048]{2,1,0:T(8,128)(2,1)S(1)}, bf16[4,32,2048]{2,1,0:T(8,128)(2,1)S(1)}, u32[]{:S(2)}, u32[]{:S(2)}) collective-permute-start(bf16[4,32,2048]{2,1,0:T(8,128)(2,1)S(1)} %get-tuple-element.111), channel_id=1, source_target_pairs={{0,1},{1,2},{2,3},{3,0},{4,5},{5,6},{6,7},{7,4},{8,9},{9,10},{10,1... | collective-permute-start | bytes 1572872 | tf_op jit(solution)/shard_map/ppermute | solution.py:23
  147.2 20.9 %collective-permute-start.24 = (bf16[4,32,2048]{2,1,0:T(8,128)(2,1)S(1)}, bf16[4,32,2048]{2,1,0:T(8,128)(2,1)S(1)}, u32[]{:S(2)}, u32[]{:S(2)}) collective-permute-start(bf16[4,32,2048]{2,1,0:T(8,128)(2,1)S(1)} %get-tuple-element.117), channel_id=1, source_target_pairs={{0,12},{4,0},{8,4},{12,8},{1,13},{5,1},{9,5},{13,9},{2,14},{6,2},{... | collective-permute-start | bytes 1572872 | tf_op jit(solution)/shard_map/ppermute | solution.py:23
  153.4 16.4 %collective-permute-start.25 = (bf16[4,32,2048]{2,1,0:T(8,128)(2,1)S(1)}, bf16[4,32,2048]{2,1,0:T(8,128)(2,1)S(1)}, u32[]{:S(2)}, u32[]{:S(2)}) collective-permute-start(bf16[4,32,2048]{2,1,0:T(8,128)(2,1)S(1)} %get-tuple-element.118), channel_id=1, source_target_pairs={{0,8},{4,12},{8,0},{12,4},{1,9},{5,13},{9,1},{13,5},{2,10},{6,14},... | collective-permute-start | bytes 1572872 | tf_op jit(solution)/shard_map/ppermute | solution.py:23
  158.2 18.0 %collective-permute-start.26 = (bf16[4,32,2048]{2,1,0:T(8,128)(2,1)S(1)}, bf16[4,32,2048]{2,1,0:T(8,128)(2,1)S(1)}, u32[]{:S(2)}, u32[]{:S(2)}) collective-permute-start(bf16[4,32,2048]{2,1,0:T(8,128)(2,1)S(1)} %get-tuple-element.119), channel_id=1, source_target_pairs={{0,4},{4,8},{8,12},{12,0},{1,5},{5,9},{9,13},{13,1},{2,6},{6,10},{... | collective-permute-start | bytes 1572872 | tf_op jit(solution)/shard_map/ppermute | solution.py:23
  187.1 15.1 %collective-permute-start.27 = (bf16[128,2048]{1,0:T(8,128)(2,1)}, bf16[128,2048]{1,0:T(8,128)(2,1)S(1)}, u32[]{:S(2)}, u32[]{:S(2)}) collective-permute-start(bf16[128,2048]{1,0:T(8,128)(2,1)} %copy-done.8), channel_id=1, source_target_pairs={{0,3},{1,0},{2,1},{3,2},{4,7},{5,4},{6,5},{7,6},{8,11},{9,8},{10,9... | collective-permute-start | bytes 1572872 | tf_op jit(solution)/shard_map/ppermute | solution.py:23
  187.2 16.7 %collective-permute-start.28 = (bf16[128,2048]{1,0:T(8,128)(2,1)}, bf16[128,2048]{1,0:T(8,128)(2,1)S(1)}, u32[]{:S(2)}, u32[]{:S(2)}) collective-permute-start(bf16[128,2048]{1,0:T(8,128)(2,1)} %copy-done.7), channel_id=1, source_target_pairs={{0,2},{1,3},{2,0},{3,1},{4,6},{5,7},{6,4},{7,5},{8,10},{9,11},{10,... | collective-permute-start | bytes 1572872 | tf_op jit(solution)/shard_map/ppermute | solution.py:23
  187.3 25.4 %collective-permute-start.29 = (bf16[128,2048]{1,0:T(8,128)(2,1)S(1)}, bf16[128,2048]{1,0:T(8,128)(2,1)S(1)}, u32[]{:S(2)}, u32[]{:S(2)}) collective-permute-start(bf16[128,2048]{1,0:T(8,128)(2,1)S(1)} %get-tuple-element.124), channel_id=1, source_target_pairs={{0,1},{1,2},{2,3},{3,0},{4,5},{5,6},{6,7},{7,4},{8,9},{9,10},{10,1... | collective-permute-start | bytes 1572872 | tf_op jit(solution)/shard_map/ppermute | solution.py:23
  (9 other events, 24.6 us)
Sparse Core Ops, SparseCore 0:
  10.7 34.5 all-gather.1
  187.3 27.2 reduce-scatter.1

commit v5 on v3

--- a/solution.py
+++ b/solution.py
@@ -12,15 +12,39 @@
 CHUNKS = 2
 ROWS = CAP // CHUNKS
 TILE = 128
-PACK_TILE = 512
 FF_TILE = 256
 D_TILE = 1024
-SUM_TILE = 512
 VMEM = 36 * 1024 * 1024
 
 
 def shift(block, axis, step):
     return lax.ppermute(block, axis, [(i, (i + step) % SIDE) for i in range(SIDE)])
+
+
+def gather_line(half, axis):
+    rows = half.shape[0] // 2
+    if axis == "z":
+        ahead, behind = shift(half, axis, 1), shift(half, axis, 3)
+        return [half, ahead, shift(half, axis, 2), behind]
+    ahead, behind = shift(half, axis, 1), shift(half, axis, -1)
+    low = shift(ahead[:rows], axis, 1)
+    high = shift(behind[rows:], axis, -1)
+    return [half, ahead, low, high, behind]
+
+
+def line_rows(refs, column=slice(None)):
+    if len(refs) == SIDE:
+        return [ref[:, column] for ref in refs]
+    own, ahead, low, high, behind = [ref[:, column] for ref in refs]
+    return [own, ahead, jnp.concatenate([low, high], axis=0), behind]
+
+
+def both_ways(a_blocks, b_blocks, a_axis, b_axis, sign):
+    a_moved, b_moved = list(a_blocks), list(b_blocks)
+    for k in (1, 3, 2):
+        a_moved[k] = shift(a_blocks[k], a_axis, sign * k)
+        b_moved[k] = shift(b_blocks[k], b_axis, sign * k)
+    return a_moved, b_moved
 
 
 def prepare_kernel(token_ref, id_ref, gate_ref, a_ref, b_ref):
@@ -43,11 +67,7 @@
         place = jnp.sum(jnp.where(ids[k] == number, rank, 0.0), axis=1, keepdims=True)
         facts = jnp.where(lane == k, ids[k], facts)
         facts = jnp.where(lane == top + k, place, facts)
-        rest = given[:, top + k : top + k + 1]
-        for part in range(2, 5):
-            term = rest.astype(jnp.bfloat16).astype(jnp.float32)
-            facts = jnp.where(lane == part * top + k, term, facts)
-            rest = rest - term
+        facts = jnp.where(lane == 2 * top + k, given[:, top + k : top + k + 1], facts)
     facts = facts.astype(jnp.bfloat16)
     a_ref[:, :half] = token_ref[:, :half]
     b_ref[:, :half] = token_ref[:, half:]
@@ -73,35 +93,31 @@
     return [facts[:, k : k + 1] * CAP + facts[:, top + k : top + k + 1] for k in range(top)]
 
 
-def targets(experts_ref, chunks, tokens):
+def targets(experts_ref, first, chunks, tokens):
     count = len(chunks) * SIDE * ROWS
     lane = lax.broadcasted_iota(jnp.int32, (tokens, count), 1)
     code = jnp.zeros((tokens, count), jnp.int32)
     for n, chunk in enumerate(chunks):
         for dest in range(SIDE):
             low = (n * SIDE + dest) * ROWS
-            value = experts_ref[dest] * CAP + chunk * ROWS + lane - low
+            value = experts_ref[first + dest] * CAP + chunk * ROWS + lane - low
             code = jnp.where((lane >= low) & (lane < low + ROWS), value, code)
     return code.astype(jnp.float32)
 
 
 def pack_kernel(chunk, top, experts_ref, *refs):
-    sources, facts = refs[:SIDE], refs[SIDE : 2 * SIDE]
-    outs, pick_ref = refs[2 * SIDE : -1], refs[-1]
-    tokens = sources[0].shape[0]
-
-    @pl.when(pl.program_id(0) == 0)
-    def _():
-        target = targets(experts_ref, (chunk,), tokens)
-        for source in range(SIDE):
-            pick = jnp.zeros(target.shape, jnp.float32)
-            for code in codes(facts[source][...], top):
-                pick = jnp.where(code == target, 1.0, pick)
-            pick_ref[source] = pick.T.astype(jnp.bfloat16)
-
+    blocks, outs = refs[:-SIDE], refs[-SIDE:]
+    tokens = blocks[0].shape[0]
+    width = outs[0].shape[-1]
+    target = targets(experts_ref, 0, (chunk,), tokens)
+    facts = line_rows(blocks, slice(width, width + TILE))
+    rows_in = line_rows(blocks, slice(0, width))
     for source in range(SIDE):
+        pick = jnp.zeros(target.shape, jnp.float32)
+        for code in codes(facts[source], top):
+            pick = jnp.where(code == target, 1.0, pick)
         rows = jnp.dot(
-            pick_ref[source], sources[source][...], preferred_element_type=jnp.float32
+            pick.T.astype(jnp.bfloat16), rows_in[source], preferred_element_type=jnp.float32
         ).astype(jnp.bfloat16)
         for dest in range(SIDE):
             outs[dest][source] = rows[dest * ROWS : (dest + 1) * ROWS]
@@ -110,25 +126,20 @@
 def pack(chunk, top, experts, blocks):
     tokens, width = blocks[0].shape
     width -= TILE
-    tile = min(PACK_TILE, width)
-    last = width // TILE
     out = jax.ShapeDtypeStruct((SIDE, ROWS, width), jnp.bfloat16)
     return pl.pallas_call(
         functools.partial(pack_kernel, chunk, top),
-        grid=(width // tile,),
         in_specs=[pl.BlockSpec(memory_space=pltpu.SMEM)]
-        + [pl.BlockSpec((tokens, tile), lambda i: (0, i))] * SIDE
-        + [pl.BlockSpec((tokens, TILE), lambda i: (0, last))] * SIDE,
-        out_specs=[pl.BlockSpec((SIDE, ROWS, tile), lambda i: (0, 0, i))] * SIDE,
+        + [pl.BlockSpec(memory_space=pltpu.VMEM)] * len(blocks),
+        out_specs=[pl.BlockSpec(memory_space=pltpu.VMEM)] * SIDE,
         out_shape=[out] * SIDE,
-        scratch_shapes=[pltpu.VMEM((SIDE, SIDE * ROWS, tokens), jnp.bfloat16)],
         compiler_params=pltpu.CompilerParams(vmem_limit_bytes=VMEM),
         cost_estimate=pl.CostEstimate(
             flops=2 * SIDE * SIDE * ROWS * tokens * width,
             bytes_accessed=2 * SIDE * width * (tokens + SIDE * ROWS),
             transcendentals=0,
         ),
-    )(experts, *blocks, *blocks)
+    )(experts, *blocks)
 
 
 def expert_kernel(n_ff, n_half, wg_ref, wu_ref, wd_ref, *refs):
@@ -220,58 +231,53 @@
     return done[:SIDE], done[SIDE:]
 
 
-def sum_kernel(top, experts_ref, *refs):
-    count = CHUNKS * SIDE
-    ins, facts = refs[:count], refs[count : count + SIDE]
-    outs, high_ref, low_ref = refs[count + SIDE : -2], refs[-2], refs[-1]
-    tokens = high_ref.shape[1]
-
-    @pl.when(pl.program_id(0) == 0)
-    def _():
-        target = targets(experts_ref, tuple(range(CHUNKS)), tokens)
+def sum_kernel(top, counts, experts_ref, *refs):
+    groups = []
+    for count in counts:
+        groups.append(refs[:count])
+        refs = refs[count:]
+    a_in, b_in, a_facts, b_facts, a_out, b_out = groups
+    tokens = a_out[0].shape[0]
+    for first, ins, blocks, outs in ((0, a_in, a_facts, a_out), (SIDE, b_in, b_facts, b_out)):
+        target = targets(experts_ref, first, tuple(range(CHUNKS)), tokens)
+        facts = line_rows(blocks)
         for source in range(SIDE):
-            about = facts[source][...]
-            wide = about.astype(jnp.float32)
+            wide = facts[source].astype(jnp.float32)
             weight = jnp.zeros(target.shape, jnp.float32)
-            for k, code in enumerate(codes(about, top)):
-                first, second, third = (
-                    wide[:, part * top + k : part * top + k + 1] for part in range(2, 5)
-                )
-                weight = jnp.where(code == target, first + second + third, weight)
-            high = weight.astype(jnp.bfloat16)
-            high_ref[source] = high
-            low_ref[source] = (weight - high.astype(jnp.float32)).astype(jnp.bfloat16)
-
-    for source in range(SIDE):
-        rows = jnp.concatenate([ref[source] for ref in ins], axis=0)
-        total = jnp.dot(high_ref[source], rows, preferred_element_type=jnp.float32)
-        total = total + jnp.dot(low_ref[source], rows, preferred_element_type=jnp.float32)
-        outs[source][...] = total.astype(jnp.bfloat16)
-
-
-def sum_rows(top, experts, facts, blocks):
-    width = blocks[0].shape[-1]
-    tokens = facts[0].shape[0]
-    tile = min(SUM_TILE, width)
+            for k, code in enumerate(codes(wide, top)):
+                gate = wide[:, 2 * top + k : 2 * top + k + 1]
+                weight = jnp.where(code == target, gate, weight)
+            rows = jnp.concatenate([ref[source] for ref in ins], axis=0)
+            total = jnp.dot(
+                weight.astype(jnp.bfloat16), rows, preferred_element_type=jnp.float32
+            )
+            outs[source][...] = total.astype(jnp.bfloat16)
+
+
+def sum_rows(top, experts, a_facts, b_facts, a_blocks, b_blocks):
+    width = a_blocks[0].shape[-1]
+    tokens = a_facts[0].shape[0]
+    facts = [*a_facts, *b_facts]
     last = width // TILE
+    whole = pl.BlockSpec(memory_space=pltpu.VMEM)
     out = jax.ShapeDtypeStruct((tokens, width), jnp.bfloat16)
-    weights = pltpu.VMEM((SIDE, tokens, SIDE * CAP), jnp.bfloat16)
-    return pl.pallas_call(
-        functools.partial(sum_kernel, top),
-        grid=(width // tile,),
+    counts = (len(a_blocks), len(b_blocks), len(a_facts), len(b_facts), SIDE, SIDE)
+    done = pl.pallas_call(
+        functools.partial(sum_kernel, top, counts),
+        grid=(1,),
         in_specs=[pl.BlockSpec(memory_space=pltpu.SMEM)]
-        + [pl.BlockSpec((SIDE, ROWS, tile), lambda i: (0, 0, i))] * len(blocks)
-        + [pl.BlockSpec((tokens, TILE), lambda i: (0, last))] * SIDE,
-        out_specs=[pl.BlockSpec((tokens, tile), lambda i: (0, i))] * SIDE,
-        out_shape=[out] * SIDE,
-        scratch_shapes=[weights, weights],
+        + [whole] * (len(a_blocks) + len(b_blocks))
+        + [pl.BlockSpec((f.shape[0], TILE), lambda i: (0, last)) for f in facts],
+        out_specs=[whole] * (2 * SIDE),
+        out_shape=[out] * (2 * SIDE),
         compiler_params=pltpu.CompilerParams(vmem_limit_bytes=VMEM),
         cost_estimate=pl.CostEstimate(
             flops=4 * SIDE * SIDE * CAP * tokens * width,
-            bytes_accessed=2 * SIDE * width * (tokens + SIDE * CAP),
+            bytes_accessed=4 * SIDE * width * (tokens + SIDE * CAP),
             transcendentals=0,
         ),
-    )(experts, *blocks, *facts)
+    )(experts, *a_blocks, *b_blocks, *facts)
+    return done[:SIDE], done[SIDE:]
 
 
 def local(tokens, expert_ids, gate_values, gate_weight, up_weight, down_weight):
@@ -282,10 +288,11 @@
     b_experts = (z + steps) % SIDE * SIDE + x
 
     a_half, b_half = prepare(tokens, expert_ids, gate_values)
-    a_rows = [a_half] + [shift(a_half, "z", k) for k in range(1, SIDE)]
-    b_rows = [b_half] + [shift(b_half, "x", k) for k in range(1, SIDE)]
-
-    w_gate, w_up, w_down = gate_weight[0], up_weight[0], down_weight[0]
+    b_rows = gather_line(b_half, "x")
+    a_rows = gather_line(a_half, "z")
+
+    weights = gate_weight[0], up_weight[0], down_weight[0]
+    weights = [pltpu.with_memory_space_constraint(w, pltpu.HBM) for w in weights]
     a_back, b_back = [], []
     a_done = None
     for chunk in range(CHUNKS):
@@ -296,17 +303,16 @@
         )
         if chunk:
             b_out[2], a_done[0] = lax.optimization_barrier((b_out[2], a_done[0]))
-        a_in = [a_out[0]] + [shift(a_out[k], "x", k) for k in range(1, SIDE)]
-        b_in = [b_out[0]] + [shift(b_out[k], "z", k) for k in range(1, SIDE)]
-        a_done, b_done = expert(w_gate, w_up, w_down, a_in, b_in)
+        a_in, b_in = both_ways(a_out, b_out, "x", "z", 1)
+        a_done, b_done = expert(*weights, a_in, b_in)
         a_done = list(a_done)
-        a_back.append([a_done[0]] + [shift(a_done[k], "x", -k) for k in range(1, SIDE)])
-        b_back.append([b_done[0]] + [shift(b_done[k], "z", -k) for k in range(1, SIDE)])
-
-    a_sums = sum_rows(top, a_experts, a_rows, sum(a_back, []))
-    b_sums = sum_rows(top, b_experts, b_rows, sum(b_back, []))
-    a_home = [a_sums[0]] + [shift(a_sums[k], "z", -k) for k in range(1, SIDE)]
-    b_home = [b_sums[0]] + [shift(b_sums[k], "x", -k) for k in range(1, SIDE)]
+        a_home, b_home = both_ways(a_done, b_done, "x", "z", -1)
+        a_back += a_home
+        b_back += b_home
+
+    experts = jnp.concatenate([a_experts, b_experts])
+    a_sums, b_sums = sum_rows(top, experts, a_rows, b_rows, a_back, b_back)
+    a_home, b_home = both_ways(a_sums, b_sums, "z", "x", -1)
     mixed = [sum(part.astype(jnp.float32) for part in home) for home in (a_home, b_home)]
     return jnp.concatenate(mixed, axis=1).astype(jnp.bfloat16)
 

time: 217 us -> 190 us (0.88)
  Pallas kernels: 54.9 us -> 43.5 us
  waiting for transfers between devices: 99.7 us -> 90.8 us
  starting transfers between devices: 56.8 us -> 48.6 us
    pallas_call x6 -> x5, Pallas kernels: 23.9 us -> 12 us  [the longest x4 8.99 us: pack(): pl.pallas_call(functools.partial(pack_kernel, chunk, top), in_specs=[pl.B...]
    ppermute x36 -> x37, waiting for transfers between devices: 99.7 us -> 90.8 us  [shift(): lax.ppermute(block, axis, [(i, (i + step) % SIDE) for i in range(SIDE)])]
    ppermute x36 -> x37, starting transfers between devices: 56.8 us -> 48.6 us  [shift(): lax.ppermute(block, axis, [(i, (i + step) % SIDE) for i in range(SIDE)])]
  transfers between devices with their start and end apart: 36 -> 37, of which waited for: 18 -> 16; matrix products, arithmetic and copies ran while one was open for 0% -> 1% of each run, Pallas kernels for 23% -> 20%
where the time goes in v5:
time: 190 us; the launch traced here: 189 us
  waiting for transfers between devices  90.8 us (48%)
  starting transfers between devices  48.6 us (26%)
  Pallas kernels  43.5 us (23%)
  local copies, waits for them, and re-layouts  4.04 us (2%)
    ppermute x37, waiting for transfers between devices, shift(): lax.ppermute(block, axis, [(i, (i + step) % SIDE) for i in range(SIDE)])  90.8 us
    ppermute x37, starting transfers between devices, shift(): lax.ppermute(block, axis, [(i, (i + step) % SIDE) for i in range(SIDE)])  48.6 us
    pallas_call x2, Pallas kernels, expert(): pl.pallas_call(functools.partial(expert_kernel, n_ff, n_half), grid=(n_ff...  31 us
    pallas_call x4, Pallas kernels, pack(): pl.pallas_call(functools.partial(pack_kernel, chunk, top), in_specs=[pl.B...  8.99 us
  transfers between devices with their start and end apart: 37, of which 16 were waited for; matrix products, arithmetic and copies ran while one was open for 1% of the time, Pallas kernels for 20%

profile of v5, /device:TPU:0, one launch (start us, length us, event | category | flops | bytes accessed | tf_op | source)
XLA Modules:
  0.0 188.9 jit_solution(17823548000379774147)
XLA Ops:
  3.1 2.9 %collective-permute-start.5 = (bf16[128,2176]{1,0:T(8,128)(2,1)S(1)}, bf16[128,2176]{1,0:T(8,128)(2,1)S(1)}, u32[]{:S(2)}, u32[]{:S(2)}) collective-permute-start(bf16[128,2176]{1,0:T(8,128)(2,1)S(1)} %get-tuple-element.73.refs_0_.refs_20_), channel_id=1, source_target_pairs={{0,3},{1,0},{2,1},{3,2},{4,7},{5,4},{6,5},{7,6},{8,11},{9,8},{10,9... | collective-permute-start | bytes 1671176 | tf_op jit(solution)/shard_map/ppermute | solution.py:21
  6.0 4.0 %collective-permute-start.2 = (bf16[128,2176]{1,0:T(8,128)(2,1)S(1)}, bf16[128,2176]{1,0:T(8,128)(2,1)S(1)}, u32[]{:S(2)}, u32[]{:S(2)}) collective-permute-start(bf16[128,2176]{1,0:T(8,128)(2,1)S(1)} %get-tuple-element.68.refs_0_.refs_16_), channel_id=1, source_target_pairs={{0,12},{4,0},{8,4},{12,8},{1,13},{5,1},{9,5},{13,9},{2,14},{6,2},{... | collective-permute-start | bytes 1671176 | tf_op jit(solution)/shard_map/ppermute | solution.py:21
  11.3 6.6 %collective-permute-done.5.refs_4_.refs_24_ = bf16[128,2176]{1,0:T(8,128)(2,1)S(1)} collective-permute-done((bf16[128,2176]{1,0:T(8,128)(2,1)S(1)}, bf16[128,2176]{1,0:T(8,128)(2,1)S(1)}, u32[]{:S(2)}, u32[]{:S(2)}) %collective-permute-start.5) | collective-permute-done | bytes 557088 | tf_op jit(solution)/shard_map/ppermute | solution.py:21
  18.7 3.7 %collective-permute-start.6 = (bf16[64,2176]{1,0:T(8,128)(2,1)}, bf16[64,2176]{1,0:T(8,128)(2,1)}, u32[]{:S(2)}, u32[]{:S(2)}) collective-permute-start(bf16[64,2176]{1,0:T(8,128)(2,1)} %slice.9), channel_id=1, source_target_pairs={{0,3},{1,0},{2,1},{3,2},{4,7},{5,4},{6,5},{7,6},{8,11},{9,8},{10,9... | collective-permute-start | bytes 835592 | tf_op jit(solution)/shard_map/ppermute | solution.py:21
  23.1 10.5 %collective-permute-done.2.refs_3_.refs_19_ = bf16[128,2176]{1,0:T(8,128)(2,1)S(1)} collective-permute-done((bf16[128,2176]{1,0:T(8,128)(2,1)S(1)}, bf16[128,2176]{1,0:T(8,128)(2,1)S(1)}, u32[]{:S(2)}, u32[]{:S(2)}) %collective-permute-start.2) | collective-permute-done | bytes 557088 | tf_op jit(solution)/shard_map/ppermute | solution.py:21
  33.6 3.5 %collective-permute-done.refs_1_.refs_17_ = bf16[128,2176]{1,0:T(8,128)(2,1)} collective-permute-done((bf16[128,2176]{1,0:T(8,128)(2,1)S(1)}, bf16[128,2176]{1,0:T(8,128)(2,1)}, u32[]{:S(2)}, u32[]{:S(2)}) %collective-permute-start) | collective-permute-done | bytes 557088 | tf_op jit(solution)/shard_map/ppermute | solution.py:21
  37.1 2.3 %shard_map.65 = (bf16[4,32,2048]{2,1,0:T(8,128)(2,1)S(1)}, bf16[4,32,2048]{2,1,0:T(8,128)(2,1)S(1)}, bf16[4,32,2048]{2,1,0:T(8,128)(2,1)S(1)}, bf16[4,32,2048]{2,1,0:T(8,128)(2,1)S(1)}) custom-call(s32[4]{0:T(128)S(1)} %get-tuple-element.88.experts_ref, bf16[128,2176]{1,0:T(8,128)(2,1)S(1)} %get-tuple-element.68.refs_0_.refs_16_, ...), custom_call_target="tpu_custom_call" | custom-call | flops 268435456 | bytes 4194304 | tf_op jit(solution)/shard_map/pallas_call | solution.py:130
  39.4 2.2 %shard_map.66 = (bf16[4,32,2048]{2,1,0:T(8,128)(2,1)S(1)}, bf16[4,32,2048]{2,1,0:T(8,128)(2,1)S(1)}, bf16[4,32,2048]{2,1,0:T(8,128)(2,1)S(1)}, bf16[4,32,2048]{2,1,0:T(8,128)(2,1)S(1)}) custom-call(s32[4]{0:T(128)S(1)} %get-tuple-element.89.experts_ref, bf16[128,2176]{1,0:T(8,128)(2,1)S(1)} %get-tuple-element.73.refs_0_.refs_20_, ...), custom_call_target="tpu_custom_call" | custom-call | flops 268435456 | bytes 4194304 | tf_op jit(solution)/shard_map/pallas_call | solution.py:130
  42.2 3.9 %collective-permute-start.8 = (bf16[4,32,2048]{2,1,0:T(8,128)(2,1)S(1)}, bf16[4,32,2048]{2,1,0:T(8,128)(2,1)S(1)}, u32[]{:S(2)}, u32[]{:S(2)}) collective-permute-start(bf16[4,32,2048]{2,1,0:T(8,128)(2,1)S(1)} %get-tuple-element.92), channel_id=1, source_target_pairs={{0,2},{1,3},{2,0},{3,1},{4,6},{5,7},{6,4},{7,5},{8,10},{9,11},{10,... | collective-permute-start | bytes 1572872 | tf_op jit(solution)/shard_map/ppermute | solution.py:21
  46.4 2.4 %collective-permute-start.11 = (bf16[4,32,2048]{2,1,0:T(8,128)(2,1)S(1)}, bf16[4,32,2048]{2,1,0:T(8,128)(2,1)S(1)}, u32[]{:S(2)}, u32[]{:S(2)}) collective-permute-start(bf16[4,32,2048]{2,1,0:T(8,128)(2,1)S(1)} %get-tuple-element.96), channel_id=1, source_target_pairs={{0,8},{4,12},{8,0},{12,4},{1,9},{5,13},{9,1},{13,5},{2,10},{6,14},... | collective-permute-start | bytes 1572872 | tf_op jit(solution)/shard_map/ppermute | solution.py:21
  48.8 7.9 %collective-permute-done.7.refs_1_ = bf16[4,32,2048]{2,1,0:T(8,128)(2,1)S(1)} collective-permute-done((bf16[4,32,2048]{2,1,0:T(8,128)(2,1)S(1)}, bf16[4,32,2048]{2,1,0:T(8,128)(2,1)S(1)}, u32[]{:S(2)}, u32[]{:S(2)}) %collective-permute-start.7) | collective-permute-done | bytes 524320 | tf_op jit(solution)/shard_map/ppermute | solution.py:21
  57.9 2.2 %shard_map.67 = (bf16[4,32,2048]{2,1,0:T(8,128)(2,1)S(1)}, bf16[4,32,2048]{2,1,0:T(8,128)(2,1)S(1)}, bf16[4,32,2048]{2,1,0:T(8,128)(2,1)S(1)}, bf16[4,32,2048]{2,1,0:T(8,128)(2,1)S(1)}) custom-call(s32[4]{0:T(128)S(1)} %get-tuple-element.88.experts_ref, bf16[128,2176]{1,0:T(8,128)(2,1)S(1)} %get-tuple-element.68.refs_0_.refs_16_, ...), custom_call_target="tpu_custom_call" | custom-call | flops 268435456 | bytes 4194304 | tf_op jit(solution)/shard_map/pallas_call | solution.py:130
  60.2 2.2 %shard_map.68 = (bf16[4,32,2048]{2,1,0:T(8,128)(2,1)S(1)}, bf16[4,32,2048]{2,1,0:T(8,128)(2,1)S(1)}, bf16[4,32,2048]{2,1,0:T(8,128)(2,1)S(1)}, bf16[4,32,2048]{2,1,0:T(8,128)(2,1)S(1)}) custom-call(s32[4]{0:T(128)S(1)} %get-tuple-element.89.experts_ref, bf16[128,2176]{1,0:T(8,128)(2,1)S(1)} %get-tuple-element.73.refs_0_.refs_20_, ...), custom_call_target="tpu_custom_call" | custom-call | flops 268435456 | bytes 4194304 | tf_op jit(solution)/shard_map/pallas_call | solution.py:130
  62.4 7.2 %collective-permute-done.8.refs_2_ = bf16[4,32,2048]{2,1,0:T(8,128)(2,1)S(1)} collective-permute-done((bf16[4,32,2048]{2,1,0:T(8,128)(2,1)S(1)}, bf16[4,32,2048]{2,1,0:T(8,128)(2,1)S(1)}, u32[]{:S(2)}, u32[]{:S(2)}) %collective-permute-start.8) | collective-permute-done | bytes 524320 | tf_op jit(solution)/shard_map/ppermute | solution.py:21
  72.9 3.2 %collective-permute-start.21 = (bf16[4,32,2048]{2,1,0:T(8,128)(2,1)S(1)}, bf16[4,32,2048]{2,1,0:T(8,128)(2,1)S(1)}, u32[]{:S(2)}, u32[]{:S(2)}) collective-permute-start(bf16[4,32,2048]{2,1,0:T(8,128)(2,1)S(1)} %get-tuple-element.110), channel_id=1, source_target_pairs={{0,12},{4,0},{8,4},{12,8},{1,13},{5,1},{9,5},{13,9},{2,14},{6,2},{... | collective-permute-start | bytes 1572872 | tf_op jit(solution)/shard_map/ppermute | solution.py:21
  76.2 15.5 %shard_map.69 = (bf16[4,32,2048]{2,1,0:T(8,128)(2,1)S(1)}, bf16[4,32,2048]{2,1,0:T(8,128)(2,1)S(1)}, bf16[4,32,2048]{2,1,0:T(8,128)(2,1)S(1)}, bf16[4,32,2048]{2...) custom-call(bf16[4096,768]{1,0:T(8,128)(2,1)} %bitcast.7, ...), custom_call_target="tpu_custom_call" | custom-call | flops 9663676416 | bytes 27262976 | tf_op jit(solution)/shard_map/pallas_call | solution.py:212
  91.7 2.2 %collective-permute-done.16.refs_1_ = bf16[4,32,2048]{2,1,0:T(8,128)(2,1)S(1)} collective-permute-done((bf16[4,32,2048]{2,1,0:T(8,128)(2,1)S(1)}, bf16[4,32,2048]{2,1,0:T(8,128)(2,1)S(1)}, u32[]{:S(2)}, u32[]{:S(2)}) %collective-permute-start.16) | collective-permute-done | bytes 524320 | tf_op jit(solution)/shard_map/ppermute | solution.py:21
  95.3 3.2 %collective-permute-start.14 = (bf16[4,32,2048]{2,1,0:T(8,128)(2,1)S(1)}, bf16[4,32,2048]{2,1,0:T(8,128)(2,1)S(1)}, u32[]{:S(2)}, u32[]{:S(2)}) collective-permute-start(bf16[4,32,2048]{2,1,0:T(8,128)(2,1)S(1)} %get-tuple-element.100), channel_id=1, source_target_pairs={{0,2},{1,3},{2,0},{3,1},{4,6},{5,7},{6,4},{7,5},{8,10},{9,11},{10,... | collective-permute-start | bytes 1572872 | tf_op jit(solution)/shard_map/ppermute | solution.py:21
  98.6 6.8 %collective-permute-done.20.refs_6_ = bf16[4,32,2048]{2,1,0:T(8,128)(2,1)S(1)} collective-permute-done((bf16[4,32,2048]{2,1,0:T(8,128)(2,1)S(1)}, bf16[4,32,2048]{2,1,0:T(8,128)(2,1)S(1)}, u32[]{:S(2)}, u32[]{:S(2)}) %collective-permute-start.20) | collective-permute-done | bytes 524320 | tf_op jit(solution)/shard_map/ppermute | solution.py:21
  105.4 3.1 %collective-permute-start.26 = (bf16[4,32,2048]{2,1,0:T(8,128)(2,1)S(1)}, bf16[4,32,2048]{2,1,0:T(8,128)(2,1)S(1)}, u32[]{:S(2)}, u32[]{:S(2)}) collective-permute-start(bf16[4,32,2048]{2,1,0:T(8,128)(2,1)S(1)} %get-tuple-element.117), channel_id=1, source_target_pairs={{0,8},{4,12},{8,0},{12,4},{1,9},{5,13},{9,1},{13,5},{2,10},{6,14},... | collective-permute-start | bytes 1572872 | tf_op jit(solution)/shard_map/ppermute | solution.py:21
  108.5 15.5 %shard_map.70 = (bf16[4,32,2048]{2,1,0:T(8,128)(2,1)S(1)}, bf16[4,32,2048]{2,1,0:T(8,128)(2,1)S(1)}, bf16[4,32,2048]{2,1,0:T(8,128)(2,1)S(1)}, bf16[4,32,2048]{2...) custom-call(bf16[4096,768]{1,0:T(8,128)(2,1)} %bitcast.8, ...), custom_call_target="tpu_custom_call" | custom-call | flops 9663676416 | bytes 27262976 | tf_op jit(solution)/shard_map/pallas_call | solution.py:212
  124.6 3.0 %collective-permute-start.23 = (bf16[4,32,2048]{2,1,0:T(8,128)(2,1)S(1)}, bf16[4,32,2048]{2,1,0:T(8,128)(2,1)S(1)}, u32[]{:S(2)}, u32[]{:S(2)}) collective-permute-start(bf16[4,32,2048]{2,1,0:T(8,128)(2,1)S(1)} %get-tuple-element.113), channel_id=1, source_target_pairs={{0,2},{1,3},{2,0},{3,1},{4,6},{5,7},{6,4},{7,5},{8,10},{9,11},{10,... | collective-permute-start | bytes 1572872 | tf_op jit(solution)/shard_map/ppermute | solution.py:21
  129.6 12.2 %collective-permute-done.27.refs_11_ = bf16[4,32,2048]{2,1,0:T(8,128)(2,1)S(1)} collective-permute-done((bf16[4,32,2048]{2,1,0:T(8,128)(2,1)S(1)}, bf16[4,32,2048]{2,1,0:T(8,128)(2,1)S(1)}, u32[]{:S(2)}, u32[]{:S(2)}) %collective-permute-start.27) | collective-permute-done | bytes 524320 | tf_op jit(solution)/shard_map/ppermute | solution.py:21
  141.9 5.7 %collective-permute-done.24.refs_7_ = bf16[4,32,2048]{2,1,0:T(8,128)(2,1)S(1)} collective-permute-done((bf16[4,32,2048]{2,1,0:T(8,128)(2,1)S(1)}, bf16[4,32,2048]{2,1,0:T(8,128)(2,1)S(1)}, u32[]{:S(2)}, u32[]{:S(2)}) %collective-permute-start.24) | collective-permute-done | bytes 524320 | tf_op jit(solution)/shard_map/ppermute | solution.py:21
  148.6 4.2 %collective-permute-done.29.refs_14_ = bf16[4,32,2048]{2,1,0:T(8,128)(2,1)S(1)} collective-permute-done((bf16[4,32,2048]{2,1,0:T(8,128)(2,1)S(1)}, bf16[4,32,2048]{2,1,0:T(8,128)(2,1)S(1)}, u32[]{:S(2)}, u32[]{:S(2)}) %collective-permute-start.29) | collective-permute-done | bytes 524320 | tf_op jit(solution)/shard_map/ppermute | solution.py:21
  152.8 5.6 %collective-permute-done.30.refs_15_ = bf16[4,32,2048]{2,1,0:T(8,128)(2,1)S(1)} collective-permute-done((bf16[4,32,2048]{2,1,0:T(8,128)(2,1)S(1)}, bf16[4,32,2048]{2,1,0:T(8,128)(2,1)S(1)}, u32[]{:S(2)}, u32[]{:S(2)}) %collective-permute-start.30) | collective-permute-done | bytes 524320 | tf_op jit(solution)/shard_map/ppermute | solution.py:21
  158.3 3.0 %shard_map.71 = (bf16[128,2048]{1,0:T(8,128)(2,1)S(1)}, bf16[128,2048]{1,0:T(8,128)(2,1)S(1)}, bf16[128,2048]{1,0:T(8,128)(2,1)S(1)}, bf16[128,2048]{1,0:T(8,128...) custom-call(s32[8]{0:T(128)S(1)} %pad_add_fusion.experts_ref, ...), custom_call_target="tpu_custom_call" | custom-call | flops 1073741824 | bytes 12582912 | tf_op jit(solution)/shard_map/pallas_call | solution.py:265
  163.4 5.0 %collective-permute-start.35 = (bf16[128,2048]{1,0:T(8,128)(2,1)S(1)}, bf16[128,2048]{1,0:T(8,128)(2,1)S(1)}, u32[]{:S(2)}, u32[]{:S(2)}) collective-permute-start(bf16[128,2048]{1,0:T(8,128)(2,1)S(1)} %get-tuple-element.129), channel_id=1, source_target_pairs={{0,2},{1,3},{2,0},{3,1},{4,6},{5,7},{6,4},{7,5},{8,10},{9,11},{10,... | collective-permute-start | bytes 1572872 | tf_op jit(solution)/shard_map/ppermute | solution.py:21
  168.4 7.3 %collective-permute-done.31 = bf16[128,2048]{1,0:T(8,128)(2,1)S(1)} collective-permute-done((bf16[128,2048]{1,0:T(8,128)(2,1)S(1)}, bf16[128,2048]{1,0:T(8,128)(2,1)S(1)}, u32[]{:S(2)}, u32[]{:S(2)}) %collective-permute-start.31) | collective-permute-done | bytes 524320 | tf_op jit(solution)/shard_map/ppermute | solution.py:21
  175.8 2.5 %collective-permute-start.36 = (bf16[128,2048]{1,0:T(8,128)(2,1)S(1)}, bf16[128,2048]{1,0:T(8,128)(2,1)S(1)}, u32[]{:S(2)}, u32[]{:S(2)}) collective-permute-start(bf16[128,2048]{1,0:T(8,128)(2,1)S(1)} %get-tuple-element.130), channel_id=1, source_target_pairs={{0,1},{1,2},{2,3},{3,0},{4,5},{5,6},{6,7},{7,4},{8,9},{9,10},{10,1... | collective-permute-start | bytes 1572872 | tf_op jit(solution)/shard_map/ppermute | solution.py:21
  178.3 4.7 %collective-permute-done.33 = bf16[128,2048]{1,0:T(8,128)(2,1)S(1)} collective-permute-done((bf16[128,2048]{1,0:T(8,128)(2,1)S(1)}, bf16[128,2048]{1,0:T(8,128)(2,1)S(1)}, u32[]{:S(2)}, u32[]{:S(2)}) %collective-permute-start.33) | collective-permute-done | bytes 524320 | tf_op jit(solution)/shard_map/ppermute | solution.py:21
  183.3 4.1 %collective-permute-done.36 = bf16[128,2048]{1,0:T(8,128)(2,1)S(1)} collective-permute-done((bf16[128,2048]{1,0:T(8,128)(2,1)S(1)}, bf16[128,2048]{1,0:T(8,128)(2,1)S(1)}, u32[]{:S(2)}, u32[]{:S(2)}) %collective-permute-start.36) | collective-permute-done | bytes 524320 | tf_op jit(solution)/shard_map/ppermute | solution.py:21
  (63 shorter events, 20.3 us)
Async XLA Ops:
  6.0 16.3 %collective-permute-start.3 = (bf16[128,2176]{1,0:T(8,128)(2,1)S(1)}, bf16[128,2176]{1,0:T(8,128)(2,1)S(1)}, u32[]{:S(2)}, u32[]{:S(2)}) collective-permute-start(bf16[128,2176]{1,0:T(8,128)(2,1)S(1)} %get-tuple-element.73.refs_0_.refs_20_), channel_id=1, source_target_pairs={{0,1},{1,2},{2,3},{3,0},{4,5},{5,6},{6,7},{7,4},{8,9},{9,10},{10,1... | collective-permute-start | bytes 1671176 | tf_op jit(solution)/shard_map/ppermute | solution.py:21
  6.0 27.6 %collective-permute-start.2 = (bf16[128,2176]{1,0:T(8,128)(2,1)S(1)}, bf16[128,2176]{1,0:T(8,128)(2,1)S(1)}, u32[]{:S(2)}, u32[]{:S(2)}) collective-permute-start(bf16[128,2176]{1,0:T(8,128)(2,1)S(1)} %get-tuple-element.68.refs_0_.refs_16_), channel_id=1, source_target_pairs={{0,12},{4,0},{8,4},{12,8},{1,13},{5,1},{9,5},{13,9},{2,14},{6,2},{... | collective-permute-start | bytes 1671176 | tf_op jit(solution)/shard_map/ppermute | solution.py:21
  10.1 23.5 %collective-permute-start.1 = (bf16[128,2176]{1,0:T(8,128)(2,1)S(1)}, bf16[128,2176]{1,0:T(8,128)(2,1)S(1)}, u32[]{:S(2)}, u32[]{:S(2)}) collective-permute-start(bf16[128,2176]{1,0:T(8,128)(2,1)S(1)} %get-tuple-element.68.refs_0_.refs_16_), channel_id=1, source_target_pairs={{0,8},{4,12},{8,0},{12,4},{1,9},{5,13},{9,1},{13,5},{2,10},{6,14},... | collective-permute-start | bytes 1671176 | tf_op jit(solution)/shard_map/ppermute | solution.py:21
  10.1 27.1 %collective-permute-start = (bf16[128,2176]{1,0:T(8,128)(2,1)S(1)}, bf16[128,2176]{1,0:T(8,128)(2,1)}, u32[]{:S(2)}, u32[]{:S(2)}) collective-permute-start(bf16[128,2176]{1,0:T(8,128)(2,1)S(1)} %get-tuple-element.68.refs_0_.refs_16_), channel_id=1, source_target_pairs={{0,4},{4,8},{8,12},{12,0},{1,5},{5,9},{9,13},{13,1},{2,6},{6,10},{... | collective-permute-start | bytes 1671176 | tf_op jit(solution)/shard_map/ppermute | solution.py:21
  18.7 20.8 %collective-permute-start.6 = (bf16[64,2176]{1,0:T(8,128)(2,1)}, bf16[64,2176]{1,0:T(8,128)(2,1)}, u32[]{:S(2)}, u32[]{:S(2)}) collective-permute-start(bf16[64,2176]{1,0:T(8,128)(2,1)} %slice.9), channel_id=1, source_target_pairs={{0,3},{1,0},{2,1},{3,2},{4,7},{5,4},{6,5},{7,6},{8,11},{9,8},{10,9... | collective-permute-start | bytes 835592 | tf_op jit(solution)/shard_map/ppermute | solution.py:21
  23.1 16.3 %collective-permute-start.4 = (bf16[64,2176]{1,0:T(8,128)(2,1)}, bf16[64,2176]{1,0:T(8,128)(2,1)}, u32[]{:S(2)}, u32[]{:S(2)}) collective-permute-start(bf16[64,2176]{1,0:T(8,128)(2,1)} %slice.8), channel_id=1, source_target_pairs={{0,1},{1,2},{2,3},{3,0},{4,5},{5,6},{6,7},{7,4},{8,9},{9,10},{10,1... | collective-permute-start | bytes 835592 | tf_op jit(solution)/shard_map/ppermute | solution.py:21
  41.7 14.9 %collective-permute-start.7 = (bf16[4,32,2048]{2,1,0:T(8,128)(2,1)S(1)}, bf16[4,32,2048]{2,1,0:T(8,128)(2,1)S(1)}, u32[]{:S(2)}, u32[]{:S(2)}) collective-permute-start(bf16[4,32,2048]{2,1,0:T(8,128)(2,1)S(1)} %get-tuple-element.91), channel_id=1, source_target_pairs={{0,1},{1,2},{2,3},{3,0},{4,5},{5,6},{6,7},{7,4},{8,9},{9,10},{10,1... | collective-permute-start | bytes 1572872 | tf_op jit(solution)/shard_map/ppermute | solution.py:21
  42.2 27.4 %collective-permute-start.8 = (bf16[4,32,2048]{2,1,0:T(8,128)(2,1)S(1)}, bf16[4,32,2048]{2,1,0:T(8,128)(2,1)S(1)}, u32[]{:S(2)}, u32[]{:S(2)}) collective-permute-start(bf16[4,32,2048]{2,1,0:T(8,128)(2,1)S(1)} %get-tuple-element.92), channel_id=1, source_target_pairs={{0,2},{1,3},{2,0},{3,1},{4,6},{5,7},{6,4},{7,5},{8,10},{9,11},{10,... | collective-permute-start | bytes 1572872 | tf_op jit(solution)/shard_map/ppermute | solution.py:21
  46.2 23.4 %collective-permute-start.9 = (bf16[4,32,2048]{2,1,0:T(8,128)(2,1)S(1)}, bf16[4,32,2048]{2,1,0:T(8,128)(2,1)S(1)}, u32[]{:S(2)}, u32[]{:S(2)}) collective-permute-start(bf16[4,32,2048]{2,1,0:T(8,128)(2,1)S(1)} %get-tuple-element.93), channel_id=1, source_target_pairs={{0,3},{1,0},{2,1},{3,2},{4,7},{5,4},{6,5},{7,6},{8,11},{9,8},{10,9... | collective-permute-start | bytes 1572872 | tf_op jit(solution)/shard_map/ppermute | solution.py:21
  46.4 25.2 %collective-permute-start.10 = (bf16[4,32,2048]{2,1,0:T(8,128)(2,1)S(1)}, bf16[4,32,2048]{2,1,0:T(8,128)(2,1)S(1)}, u32[]{:S(2)}, u32[]{:S(2)}) collective-permute-start(bf16[4,32,2048]{2,1,0:T(8,128)(2,1)S(1)} %get-tuple-element.95), channel_id=1, source_target_pairs={{0,4},{4,8},{8,12},{12,0},{1,5},{5,9},{9,13},{13,1},{2,6},{6,10},{... | collective-permute-start | bytes 1572872 | tf_op jit(solution)/shard_map/ppermute | solution.py:21
  46.4 26.5 %collective-permute-start.11 = (bf16[4,32,2048]{2,1,0:T(8,128)(2,1)S(1)}, bf16[4,32,2048]{2,1,0:T(8,128)(2,1)S(1)}, u32[]{:S(2)}, u32[]{:S(2)}) collective-permute-start(bf16[4,32,2048]{2,1,0:T(8,128)(2,1)S(1)} %get-tuple-element.96), channel_id=1, source_target_pairs={{0,8},{4,12},{8,0},{12,4},{1,9},{5,13},{9,1},{13,5},{2,10},{6,14},... | collective-permute-start | bytes 1572872 | tf_op jit(solution)/shard_map/ppermute | solution.py:21
  56.6 16.3 %collective-permute-start.12 = (bf16[4,32,2048]{2,1,0:T(8,128)(2,1)S(1)}, bf16[4,32,2048]{2,1,0:T(8,128)(2,1)S(1)}, u32[]{:S(2)}, u32[]{:S(2)}) collective-permute-start(bf16[4,32,2048]{2,1,0:T(8,128)(2,1)S(1)} %get-tuple-element.97), channel_id=1, source_target_pairs={{0,12},{4,0},{8,4},{12,8},{1,13},{5,1},{9,5},{13,9},{2,14},{6,2},{... | collective-permute-start | bytes 1572872 | tf_op jit(solution)/shard_map/ppermute | solution.py:21
  69.6 24.3 %collective-permute-start.16 = (bf16[4,32,2048]{2,1,0:T(8,128)(2,1)S(1)}, bf16[4,32,2048]{2,1,0:T(8,128)(2,1)S(1)}, u32[]{:S(2)}, u32[]{:S(2)}) collective-permute-start(bf16[4,32,2048]{2,1,0:T(8,128)(2,1)S(1)} %get-tuple-element.103), channel_id=1, source_target_pairs={{0,1},{1,2},{2,3},{3,0},{4,5},{5,6},{6,7},{7,4},{8,9},{9,10},{10,1... | collective-permute-start | bytes 1572872 | tf_op jit(solution)/shard_map/ppermute | solution.py:21
  69.6 25.6 %collective-permute-start.17 = (bf16[4,32,2048]{2,1,0:T(8,128)(2,1)S(1)}, bf16[4,32,2048]{2,1,0:T(8,128)(2,1)S(1)}, u32[]{:S(2)}, u32[]{:S(2)}) collective-permute-start(bf16[4,32,2048]{2,1,0:T(8,128)(2,1)S(1)} %get-tuple-element.104), channel_id=1, source_target_pairs={{0,2},{1,3},{2,0},{3,1},{4,6},{5,7},{6,4},{7,5},{8,10},{9,11},{10,... | collective-permute-start | bytes 1572872 | tf_op jit(solution)/shard_map/ppermute | solution.py:21
  71.5 23.7 %collective-permute-start.18 = (bf16[4,32,2048]{2,1,0:T(8,128)(2,1)S(1)}, bf16[4,32,2048]{2,1,0:T(8,128)(2,1)S(1)}, u32[]{:S(2)}, u32[]{:S(2)}) collective-permute-start(bf16[4,32,2048]{2,1,0:T(8,128)(2,1)S(1)} %get-tuple-element.105), channel_id=1, source_target_pairs={{0,3},{1,0},{2,1},{3,2},{4,7},{5,4},{6,5},{7,6},{8,11},{9,8},{10,9... | collective-permute-start | bytes 1572872 | tf_op jit(solution)/shard_map/ppermute | solution.py:21
  72.9 25.5 %collective-permute-start.19 = (bf16[4,32,2048]{2,1,0:T(8,128)(2,1)S(1)}, bf16[4,32,2048]{2,1,0:T(8,128)(2,1)S(1)}, u32[]{:S(2)}, u32[]{:S(2)}) collective-permute-start(bf16[4,32,2048]{2,1,0:T(8,128)(2,1)S(1)} %get-tuple-element.107), channel_id=1, source_target_pairs={{0,4},{4,8},{8,12},{12,0},{1,5},{5,9},{9,13},{13,1},{2,6},{6,10},{... | collective-permute-start | bytes 1572872 | tf_op jit(solution)/shard_map/ppermute | solution.py:21
  72.9 25.6 %collective-permute-start.21 = (bf16[4,32,2048]{2,1,0:T(8,128)(2,1)S(1)}, bf16[4,32,2048]{2,1,0:T(8,128)(2,1)S(1)}, u32[]{:S(2)}, u32[]{:S(2)}) collective-permute-start(bf16[4,32,2048]{2,1,0:T(8,128)(2,1)S(1)} %get-tuple-element.110), channel_id=1, source_target_pairs={{0,12},{4,0},{8,4},{12,8},{1,13},{5,1},{9,5},{13,9},{2,14},{6,2},{... | collective-permute-start | bytes 1572872 | tf_op jit(solution)/shard_map/ppermute | solution.py:21
  95.3 28.8 %collective-permute-start.13 = (bf16[4,32,2048]{2,1,0:T(8,128)(2,1)S(1)}, bf16[4,32,2048]{2,1,0:T(8,128)(2,1)S(1)}, u32[]{:S(2)}, u32[]{:S(2)}) collective-permute-start(bf16[4,32,2048]{2,1,0:T(8,128)(2,1)S(1)} %get-tuple-element.99), channel_id=1, source_target_pairs={{0,3},{1,0},{2,1},{3,2},{4,7},{5,4},{6,5},{7,6},{8,11},{9,8},{10,9... | collective-permute-start | bytes 1572872 | tf_op jit(solution)/shard_map/ppermute | solution.py:21
  95.3 29.3 %collective-permute-start.14 = (bf16[4,32,2048]{2,1,0:T(8,128)(2,1)S(1)}, bf16[4,32,2048]{2,1,0:T(8,128)(2,1)S(1)}, u32[]{:S(2)}, u32[]{:S(2)}) collective-permute-start(bf16[4,32,2048]{2,1,0:T(8,128)(2,1)S(1)} %get-tuple-element.100), channel_id=1, source_target_pairs={{0,2},{1,3},{2,0},{3,1},{4,6},{5,7},{6,4},{7,5},{8,10},{9,11},{10,... | collective-permute-start | bytes 1572872 | tf_op jit(solution)/shard_map/ppermute | solution.py:21
  98.4 26.2 %collective-permute-start.15 = (bf16[4,32,2048]{2,1,0:T(8,128)(2,1)S(1)}, bf16[4,32,2048]{2,1,0:T(8,128)(2,1)S(1)}, u32[]{:S(2)}, u32[]{:S(2)}) collective-permute-start(bf16[4,32,2048]{2,1,0:T(8,128)(2,1)S(1)} %get-tuple-element.101), channel_id=1, source_target_pairs={{0,1},{1,2},{2,3},{3,0},{4,5},{5,6},{6,7},{7,4},{8,9},{9,10},{10,1... | collective-permute-start | bytes 1572872 | tf_op jit(solution)/shard_map/ppermute | solution.py:21
  98.6 29.0 %collective-permute-start.25 = (bf16[4,32,2048]{2,1,0:T(8,128)(2,1)S(1)}, bf16[4,32,2048]{2,1,0:T(8,128)(2,1)S(1)}, u32[]{:S(2)}, u32[]{:S(2)}) collective-permute-start(bf16[4,32,2048]{2,1,0:T(8,128)(2,1)S(1)} %get-tuple-element.116), channel_id=1, source_target_pairs={{0,12},{4,0},{8,4},{12,8},{1,13},{5,1},{9,5},{13,9},{2,14},{6,2},{... | collective-permute-start | bytes 1572872 | tf_op jit(solution)/shard_map/ppermute | solution.py:21
  105.4 22.1 %collective-permute-start.26 = (bf16[4,32,2048]{2,1,0:T(8,128)(2,1)S(1)}, bf16[4,32,2048]{2,1,0:T(8,128)(2,1)S(1)}, u32[]{:S(2)}, u32[]{:S(2)}) collective-permute-start(bf16[4,32,2048]{2,1,0:T(8,128)(2,1)S(1)} %get-tuple-element.117), channel_id=1, source_target_pairs={{0,8},{4,12},{8,0},{12,4},{1,9},{5,13},{9,1},{13,5},{2,10},{6,14},... | collective-permute-start | bytes 1572872 | tf_op jit(solution)/shard_map/ppermute | solution.py:21
  124.0 17.8 %collective-permute-start.27 = (bf16[4,32,2048]{2,1,0:T(8,128)(2,1)S(1)}, bf16[4,32,2048]{2,1,0:T(8,128)(2,1)S(1)}, u32[]{:S(2)}, u32[]{:S(2)}) collective-permute-start(bf16[4,32,2048]{2,1,0:T(8,128)(2,1)S(1)} %get-tuple-element.118), channel_id=1, source_target_pairs={{0,4},{4,8},{8,12},{12,0},{1,5},{5,9},{9,13},{13,1},{2,6},{6,10},{... | collective-permute-start | bytes 1572872 | tf_op jit(solution)/shard_map/ppermute | solution.py:21
  124.6 17.2 %collective-permute-start.22 = (bf16[4,32,2048]{2,1,0:T(8,128)(2,1)S(1)}, bf16[4,32,2048]{2,1,0:T(8,128)(2,1)S(1)}, u32[]{:S(2)}, u32[]{:S(2)}) collective-permute-start(bf16[4,32,2048]{2,1,0:T(8,128)(2,1)S(1)} %get-tuple-element.112), channel_id=1, source_target_pairs={{0,3},{1,0},{2,1},{3,2},{4,7},{5,4},{6,5},{7,6},{8,11},{9,8},{10,9... | collective-permute-start | bytes 1572872 | tf_op jit(solution)/shard_map/ppermute | solution.py:21
  124.6 17.3 %collective-permute-start.23 = (bf16[4,32,2048]{2,1,0:T(8,128)(2,1)S(1)}, bf16[4,32,2048]{2,1,0:T(8,128)(2,1)S(1)}, u32[]{:S(2)}, u32[]{:S(2)}) collective-permute-start(bf16[4,32,2048]{2,1,0:T(8,128)(2,1)S(1)} %get-tuple-element.113), channel_id=1, source_target_pairs={{0,2},{1,3},{2,0},{3,1},{4,6},{5,7},{6,4},{7,5},{8,10},{9,11},{10,... | collective-permute-start | bytes 1572872 | tf_op jit(solution)/shard_map/ppermute | solution.py:21
  127.5 20.0 %collective-permute-start.24 = (bf16[4,32,2048]{2,1,0:T(8,128)(2,1)S(1)}, bf16[4,32,2048]{2,1,0:T(8,128)(2,1)S(1)}, u32[]{:S(2)}, u32[]{:S(2)}) collective-permute-start(bf16[4,32,2048]{2,1,0:T(8,128)(2,1)S(1)} %get-tuple-element.114), channel_id=1, source_target_pairs={{0,1},{1,2},{2,3},{3,0},{4,5},{5,6},{6,7},{7,4},{8,9},{9,10},{10,1... | collective-permute-start | bytes 1572872 | tf_op jit(solution)/shard_map/ppermute | solution.py:21
  127.6 21.0 %collective-permute-start.28 = (bf16[4,32,2048]{2,1,0:T(8,128)(2,1)S(1)}, bf16[4,32,2048]{2,1,0:T(8,128)(2,1)S(1)}, u32[]{:S(2)}, u32[]{:S(2)}) collective-permute-start(bf16[4,32,2048]{2,1,0:T(8,128)(2,1)S(1)} %get-tuple-element.120), channel_id=1, source_target_pairs={{0,12},{4,0},{8,4},{12,8},{1,13},{5,1},{9,5},{13,9},{2,14},{6,2},{... | collective-permute-start | bytes 1572872 | tf_op jit(solution)/shard_map/ppermute | solution.py:21
  141.8 16.5 %collective-permute-start.30 = (bf16[4,32,2048]{2,1,0:T(8,128)(2,1)S(1)}, bf16[4,32,2048]{2,1,0:T(8,128)(2,1)S(1)}, u32[]{:S(2)}, u32[]{:S(2)}) collective-permute-start(bf16[4,32,2048]{2,1,0:T(8,128)(2,1)S(1)} %get-tuple-element.122), channel_id=1, source_target_pairs={{0,4},{4,8},{8,12},{12,0},{1,5},{5,9},{9,13},{13,1},{2,6},{6,10},{... | collective-permute-start | bytes 1572872 | tf_op jit(solution)/shard_map/ppermute | solution.py:21
  161.9 16.4 %collective-permute-start.32 = (bf16[128,2048]{1,0:T(8,128)(2,1)S(1)}, bf16[128,2048]{1,0:T(8,128)(2,1)S(1)}, u32[]{:S(2)}, u32[]{:S(2)}) collective-permute-start(bf16[128,2048]{1,0:T(8,128)(2,1)S(1)} %get-tuple-element.125), channel_id=1, source_target_pairs={{0,8},{4,12},{8,0},{12,4},{1,9},{5,13},{9,1},{13,5},{2,10},{6,14},... | collective-permute-start | bytes 1572872 | tf_op jit(solution)/shard_map/ppermute | solution.py:21
  162.6 20.4 %collective-permute-start.33 = (bf16[128,2048]{1,0:T(8,128)(2,1)S(1)}, bf16[128,2048]{1,0:T(8,128)(2,1)S(1)}, u32[]{:S(2)}, u32[]{:S(2)}) collective-permute-start(bf16[128,2048]{1,0:T(8,128)(2,1)S(1)} %get-tuple-element.126), channel_id=1, source_target_pairs={{0,4},{4,8},{8,12},{12,0},{1,5},{5,9},{9,13},{13,1},{2,6},{6,10},{... | collective-permute-start | bytes 1572872 | tf_op jit(solution)/shard_map/ppermute | solution.py:21
  163.4 19.9 %collective-permute-start.34 = (bf16[128,2048]{1,0:T(8,128)(2,1)S(1)}, bf16[128,2048]{1,0:T(8,128)(2,1)S(1)}, u32[]{:S(2)}, u32[]{:S(2)}) collective-permute-start(bf16[128,2048]{1,0:T(8,128)(2,1)S(1)} %get-tuple-element.128), channel_id=1, source_target_pairs={{0,3},{1,0},{2,1},{3,2},{4,7},{5,4},{6,5},{7,6},{8,11},{9,8},{10,9... | collective-permute-start | bytes 1572872 | tf_op jit(solution)/shard_map/ppermute | solution.py:21
  163.4 19.9 %collective-permute-start.35 = (bf16[128,2048]{1,0:T(8,128)(2,1)S(1)}, bf16[128,2048]{1,0:T(8,128)(2,1)S(1)}, u32[]{:S(2)}, u32[]{:S(2)}) collective-permute-start(bf16[128,2048]{1,0:T(8,128)(2,1)S(1)} %get-tuple-element.129), channel_id=1, source_target_pairs={{0,2},{1,3},{2,0},{3,1},{4,6},{5,7},{6,4},{7,5},{8,10},{9,11},{10,... | collective-permute-start | bytes 1572872 | tf_op jit(solution)/shard_map/ppermute | solution.py:21
  (8 other events, 66.0 us)

commit v6 on v5

--- a/solution.py
+++ b/solution.py
@@ -23,9 +23,6 @@
 
 def gather_line(half, axis):
     rows = half.shape[0] // 2
-    if axis == "z":
-        ahead, behind = shift(half, axis, 1), shift(half, axis, 3)
-        return [half, ahead, shift(half, axis, 2), behind]
     ahead, behind = shift(half, axis, 1), shift(half, axis, -1)
     low = shift(ahead[:rows], axis, 1)
     high = shift(behind[rows:], axis, -1)
@@ -33,8 +30,6 @@
 
 
 def line_rows(refs, column=slice(None)):
-    if len(refs) == SIDE:
-        return [ref[:, column] for ref in refs]
     own, ahead, low, high, behind = [ref[:, column] for ref in refs]
     return [own, ahead, jnp.concatenate([low, high], axis=0), behind]
 
@@ -45,6 +40,10 @@
         a_moved[k] = shift(a_blocks[k], a_axis, sign * k)
         b_moved[k] = shift(b_blocks[k], b_axis, sign * k)
     return a_moved, b_moved
+
+
+def in_hbm(*arrays):
+    return [pltpu.with_memory_space_constraint(array, pltpu.HBM) for array in arrays]
 
 
 def prepare_kernel(token_ref, id_ref, gate_ref, a_ref, b_ref):
@@ -78,14 +77,22 @@
 def prepare(tokens, expert_ids, gate_values):
     rows, depth = tokens.shape
     out = jax.ShapeDtypeStruct((rows, depth // 2 + TILE), jnp.bfloat16)
+    top = expert_ids.shape[1]
     return pl.pallas_call(
         prepare_kernel,
+        grid=(1,),
+        in_specs=[
+            pl.BlockSpec((rows, depth), lambda i: (0, 0)),
+            pl.BlockSpec((top, rows), lambda i: (0, 0)),
+            pl.BlockSpec((top, rows), lambda i: (0, 0)),
+        ],
+        out_specs=[pl.BlockSpec(out.shape, lambda i: (0, 0))] * 2,
         out_shape=[out, out],
         compiler_params=pltpu.CompilerParams(vmem_limit_bytes=VMEM),
         cost_estimate=pl.CostEstimate(
             flops=2 * rows * rows * TILE, bytes_accessed=4 * rows * depth, transcendentals=0
         ),
-    )(tokens, expert_ids.T, gate_values.T)
+    )(*in_hbm(tokens, expert_ids.T, gate_values.T))
 
 
 def codes(facts, top):
@@ -142,15 +149,13 @@
     )(experts, *blocks)
 
 
-def expert_kernel(n_ff, n_half, wg_ref, wu_ref, wd_ref, *refs):
+def hidden_kernel(wg_ref, wu_ref, *refs):
     a_in, b_in = refs[:SIDE], refs[SIDE : 2 * SIDE]
-    a_out, b_out = refs[2 * SIDE : 3 * SIDE], refs[3 * SIDE : 4 * SIDE]
-    x_ref, hidden_ref, sems = refs[4 * SIDE :]
-    step = pl.program_id(0)
+    hidden_ref, x_ref, sems = refs[2 * SIDE :]
     half = x_ref.shape[-1] // 2
     count = SIDE * SIDE * ROWS
 
-    @pl.when(step == 0)
+    @pl.when(pl.program_id(0) == 0)
     def _():
         copies = []
         for k in range(SIDE):
@@ -165,69 +170,75 @@
         for copy in copies:
             copy.wait()
 
-    for f in range(n_ff):
-
-        @pl.when(step == f)
-        def _(f=f):
-            x = x_ref[...].reshape(count, 2 * half)
-            gate = jnp.dot(x, wg_ref[...], preferred_element_type=jnp.float32)
-            up = jnp.dot(x, wu_ref[...], preferred_element_type=jnp.float32)
-            tile = gate.shape[1]
-            hidden = gate / (1.0 + jnp.exp(-gate)) * up
-            hidden_ref[:, f * tile : (f + 1) * tile] = hidden.astype(jnp.bfloat16)
-
-    def down():
-        out = jnp.dot(hidden_ref[...], wd_ref[...], preferred_element_type=jnp.float32)
-        return out.astype(jnp.bfloat16).reshape(SIDE, SIDE, ROWS, out.shape[1])
-
-    @pl.when((step >= n_ff) & (step < n_ff + n_half))
+    x = x_ref[...].reshape(count, 2 * half)
+    gate = jnp.dot(x, wg_ref[...], preferred_element_type=jnp.float32)
+    up = jnp.dot(x, wu_ref[...], preferred_element_type=jnp.float32)
+    hidden_ref[...] = (gate / (1.0 + jnp.exp(-gate)) * up).astype(jnp.bfloat16)
+
+
+def hidden_rows(w_gate, w_up, a_in, b_in):
+    depth, ff = w_gate.shape
+    count = SIDE * SIDE * ROWS
+    weight = pl.BlockSpec((depth, FF_TILE), lambda i: (0, i))
+    return pl.pallas_call(
+        hidden_kernel,
+        grid=(ff // FF_TILE,),
+        in_specs=[weight, weight] + [pl.BlockSpec(memory_space=pl.ANY)] * (2 * SIDE),
+        out_specs=pl.BlockSpec((count, FF_TILE), lambda i: (0, i)),
+        out_shape=jax.ShapeDtypeStruct((count, ff), jnp.bfloat16),
+        scratch_shapes=[
+            pltpu.VMEM((SIDE, SIDE, ROWS, depth), jnp.bfloat16),
+            pltpu.SemaphoreType.DMA((2 * SIDE,)),
+        ],
+        compiler_params=pltpu.CompilerParams(vmem_limit_bytes=VMEM),
+        cost_estimate=pl.CostEstimate(
+            flops=4 * count * depth * ff,
+            bytes_accessed=4 * depth * ff + 2 * count * depth,
+            transcendentals=count * ff,
+        ),
+    )(w_gate, w_up, *a_in, *b_in)
+
+
+def down_kernel(n_half, hidden_ref, wd_ref, *refs):
+    a_out, b_out = refs[:SIDE], refs[SIDE:]
+    out = jnp.dot(hidden_ref[...], wd_ref[...], preferred_element_type=jnp.float32)
+    out = out.astype(jnp.bfloat16).reshape(SIDE, SIDE, ROWS, out.shape[1])
+
+    @pl.when(pl.program_id(0) < n_half)
     def _():
-        out = down()
         for k in range(SIDE):
             a_out[k][...] = out[:, k]
 
-    @pl.when(step >= n_ff + n_half)
+    @pl.when(pl.program_id(0) >= n_half)
     def _():
-        out = down()
         for k in range(SIDE):
             b_out[k][...] = out[k]
 
 
-def expert(w_gate, w_up, w_down, a_in, b_in):
-    half = a_in[0].shape[-1]
-    depth, ff = w_gate.shape
-    count = SIDE * SIDE * ROWS
-    n_ff = ff // FF_TILE
-    d_tile = min(D_TILE, half)
-    n_half = half // d_tile
-    ff_spec = pl.BlockSpec((depth, FF_TILE), lambda i: (0, jnp.minimum(i, n_ff - 1)))
-    wd_spec = pl.BlockSpec((ff, d_tile), lambda i: (0, jnp.maximum(i - n_ff, 0)))
-    a_spec = pl.BlockSpec(
-        (SIDE, ROWS, d_tile), lambda i: (0, 0, jnp.clip(i - n_ff, 0, n_half - 1))
-    )
-    b_spec = pl.BlockSpec(
-        (SIDE, ROWS, d_tile), lambda i: (0, 0, jnp.clip(i - n_ff - n_half, 0, n_half - 1))
-    )
+def down_rows(hidden, w_down):
+    count, ff = hidden.shape
+    half = w_down.shape[1] // 2
+    tile = min(D_TILE, half)
+    n_half = half // tile
+    a_spec = pl.BlockSpec((SIDE, ROWS, tile), lambda i: (0, 0, jnp.minimum(i, n_half - 1)))
+    b_spec = pl.BlockSpec((SIDE, ROWS, tile), lambda i: (0, 0, jnp.maximum(i - n_half, 0)))
     out = jax.ShapeDtypeStruct((SIDE, ROWS, half), jnp.bfloat16)
     done = pl.pallas_call(
-        functools.partial(expert_kernel, n_ff, n_half),
-        grid=(n_ff + 2 * n_half,),
-        in_specs=[ff_spec, ff_spec, wd_spec]
-        + [pl.BlockSpec(memory_space=pl.ANY)] * (2 * SIDE),
+        functools.partial(down_kernel, n_half),
+        grid=(2 * n_half,),
+        in_specs=[
+            pl.BlockSpec((count, ff), lambda i: (0, 0)),
+            pl.BlockSpec((ff, tile), lambda i: (0, i)),
+        ],
         out_specs=[a_spec] * SIDE + [b_spec] * SIDE,
         out_shape=[out] * (2 * SIDE),
-        scratch_shapes=[
-            pltpu.VMEM((SIDE, SIDE, ROWS, depth), jnp.bfloat16),
-            pltpu.VMEM((count, ff), jnp.bfloat16),
-            pltpu.SemaphoreType.DMA((2 * SIDE,)),
-        ],
-        compiler_params=pltpu.CompilerParams(vmem_limit_bytes=VMEM),
-        cost_estimate=pl.CostEstimate(
-            flops=6 * count * depth * ff,
-            bytes_accessed=6 * depth * ff + 4 * count * depth,
-            transcendentals=count * ff,
-        ),
-    )(w_gate, w_up, w_down, *a_in, *b_in)
+        compiler_params=pltpu.CompilerParams(vmem_limit_bytes=VMEM),
+        cost_estimate=pl.CostEstimate(
+            flops=4 * count * half * ff,
+            bytes_accessed=4 * half * ff + 4 * count * half,
+            transcendentals=0,
+        ),
+    )(hidden, w_down)
     return done[:SIDE], done[SIDE:]
 
 
@@ -291,10 +302,8 @@
     b_rows = gather_line(b_half, "x")
     a_rows = gather_line(a_half, "z")
 
-    weights = gate_weight[0], up_weight[0], down_weight[0]
-    weights = [pltpu.with_memory_space_constraint(w, pltpu.HBM) for w in weights]
+    w_gate, w_up, w_down = in_hbm(gate_weight[0], up_weight[0], down_weight[0])
     a_back, b_back = [], []
-    a_done = None
     for chunk in range(CHUNKS):
         a_out = list(pack(chunk, top, a_experts, a_rows))
         b_out = list(pack(chunk, top, b_experts, b_rows))
@@ -302,13 +311,18 @@
             (a_experts, b_experts, a_out, b_out)
         )
         if chunk:
-            b_out[2], a_done[0] = lax.optimization_barrier((b_out[2], a_done[0]))
+            b_out[2], hidden = lax.optimization_barrier((b_out[2], hidden))
+            a_done, b_done = down_rows(hidden, w_down)
+            a_home, b_home = both_ways(a_done, b_done, "x", "z", -1)
+            a_back += a_home
+            b_back += b_home
         a_in, b_in = both_ways(a_out, b_out, "x", "z", 1)
-        a_done, b_done = expert(*weights, a_in, b_in)
-        a_done = list(a_done)
-        a_home, b_home = both_ways(a_done, b_done, "x", "z", -1)
-        a_back += a_home
-        b_back += b_home
+        hidden = hidden_rows(w_gate, w_up, a_in, b_in)
+    hidden, a_back[1] = lax.optimization_barrier((hidden, a_back[1]))
+    a_done, b_done = down_rows(hidden, w_down)
+    a_home, b_home = both_ways(a_done, b_done, "x", "z", -1)
+    a_back += a_home
+    b_back += b_home
 
     experts = jnp.concatenate([a_experts, b_experts])
     a_sums, b_sums = sum_rows(top, experts, a_rows, b_rows, a_back, b_back)

time: 190 us -> 181 us (0.953)
  waiting for transfers between devices: 90.8 us -> 61.1 us
  starting transfers between devices: 48.6 us -> 68.4 us
  Pallas kernels: 43.5 us -> 46.2 us
    ppermute x37 -> x38, waiting for transfers between devices: 90.8 us -> 61.1 us  [shift(): lax.ppermute(block, axis, [(i, (i + step) % SIDE) for i in range(SIDE)])]
    ppermute x37 -> x38, starting transfers between devices: 48.6 us -> 68.4 us  [shift(): lax.ppermute(block, axis, [(i, (i + step) % SIDE) for i in range(SIDE)])]
    pallas_call x3 -> x5, Pallas kernels: 31.5 us -> 34.3 us  [the longest x2 19.5 us: hidden_rows(): pl.pallas_call(hidden_kernel, grid=(ff // FF_TILE,), in_specs=[weight, we...]
    unnamed x6 -> x0, local copies, waits for them, and re-layouts: 2.59 us -> none
  transfers between devices with their start and end apart: 37 -> 38, of which waited for: 16 -> 13; matrix products, arithmetic and copies ran while one was open for 1% -> 2% of each run, Pallas kernels for 20% -> 22%
where the time goes in v6:
time: 181 us
  starting transfers between devices  68.4 us (38%)
  waiting for transfers between devices  61.1 us (34%)
  Pallas kernels  46.2 us (26%)
  local copies, waits for them, and re-layouts  2.92 us (2%)
  other arithmetic  1.81 us (1%)
    ppermute x38, starting transfers between devices, shift(): lax.ppermute(block, axis, [(i, (i + step) % SIDE) for i in range(SIDE)])  68.4 us
    ppermute x38, waiting for transfers between devices, shift(): lax.ppermute(block, axis, [(i, (i + step) % SIDE) for i in range(SIDE)])  61.1 us
    pallas_call x2, Pallas kernels, hidden_rows(): pl.pallas_call(hidden_kernel, grid=(ff // FF_TILE,), in_specs=[weight, we...  19.5 us
    pallas_call x2, Pallas kernels, down_rows(): pl.pallas_call(functools.partial(down_kernel, n_half), grid=(2 * n_half,)...  13 us
    pallas_call x4, Pallas kernels, pack(): pl.pallas_call(functools.partial(pack_kernel, chunk, top), in_specs=[pl.B...  8.95 us
  transfers between devices with their start and end apart: 38, of which 13 were waited for; matrix products, arithmetic and copies ran while one was open for 2% of the time, Pallas kernels for 22%

profile of v6, /device:TPU:0, one launch (start us, length us, event | category | flops | bytes accessed | tf_op | source)
XLA Modules:
  0.0 180.7 jit_solution(619078518021817537)
XLA Ops:
  1.8 2.9 %collective-permute-start.6 = (bf16[128,2176]{1,0:T(8,128)(2,1)S(1)}, bf16[128,2176]{1,0:T(8,128)(2,1)S(1)}, u32[]{:S(2)}, u32[]{:S(2)}) collective-permute-start(bf16[128,2176]{1,0:T(8,128)(2,1)S(1)} %get-tuple-element.76.refs_0_.refs_21_), channel_id=1, source_target_pairs={{0,3},{1,0},{2,1},{3,2},{4,7},{5,4},{6,5},{7,6},{8,11},{9,8},{10,9... | collective-permute-start | bytes 1671176 | tf_op jit(solution)/shard_map/ppermute | solution.py:21
  4.8 4.0 %collective-permute-start.2 = (bf16[128,2176]{1,0:T(8,128)(2,1)S(1)}, bf16[128,2176]{1,0:T(8,128)(2,1)S(1)}, u32[]{:S(2)}, u32[]{:S(2)}) collective-permute-start(bf16[128,2176]{1,0:T(8,128)(2,1)S(1)} %get-tuple-element.71.refs_0_.refs_16_), channel_id=1, source_target_pairs={{0,12},{4,0},{8,4},{12,8},{1,13},{5,1},{9,5},{13,9},{2,14},{6,2},{... | collective-permute-start | bytes 1671176 | tf_op jit(solution)/shard_map/ppermute | solution.py:21
  8.8 7.8 %collective-permute-done.6.refs_4_.refs_25_ = bf16[128,2176]{1,0:T(8,128)(2,1)S(1)} collective-permute-done((bf16[128,2176]{1,0:T(8,128)(2,1)S(1)}, bf16[128,2176]{1,0:T(8,128)(2,1)S(1)}, u32[]{:S(2)}, u32[]{:S(2)}) %collective-permute-start.6) | collective-permute-done | bytes 557088 | tf_op jit(solution)/shard_map/ppermute | solution.py:21
  17.4 3.7 %collective-permute-start.7 = (bf16[64,2176]{1,0:T(8,128)(2,1)}, bf16[64,2176]{1,0:T(8,128)(2,1)}, u32[]{:S(2)}, u32[]{:S(2)}) collective-permute-start(bf16[64,2176]{1,0:T(8,128)(2,1)} %slice.19), channel_id=1, source_target_pairs={{0,3},{1,0},{2,1},{3,2},{4,7},{5,4},{6,5},{7,6},{8,11},{9,8},{10,9... | collective-permute-start | bytes 835592 | tf_op jit(solution)/shard_map/ppermute | solution.py:21
  22.5 4.0 %collective-permute-start.3 = (bf16[64,2176]{1,0:T(8,128)(2,1)}, bf16[64,2176]{1,0:T(8,128)(2,1)}, u32[]{:S(2)}, u32[]{:S(2)}) collective-permute-start(bf16[64,2176]{1,0:T(8,128)(2,1)} %slice.17), channel_id=1, source_target_pairs={{0,12},{4,0},{8,4},{12,8},{1,13},{5,1},{9,5},{13,9},{2,14},{6,2},{... | collective-permute-start | bytes 835592 | tf_op jit(solution)/shard_map/ppermute | solution.py:21
  27.3 3.2 %collective-permute-done.5.refs_2_.refs_23_ = bf16[64,2176]{1,0:T(8,128)(2,1)} collective-permute-done((bf16[64,2176]{1,0:T(8,128)(2,1)}, bf16[64,2176]{1,0:T(8,128)(2,1)}, u32[]{:S(2)}, u32[]{:S(2)}) %collective-permute-start.5) | collective-permute-done | bytes 278560 | tf_op jit(solution)/shard_map/ppermute | solution.py:21
  30.6 2.2 %shard_map.66 = (bf16[4,32,2048]{2,1,0:T(8,128)(2,1)S(1)}, bf16[4,32,2048]{2,1,0:T(8,128)(2,1)S(1)}, bf16[4,32,2048]{2,1,0:T(8,128)(2,1)S(1)}, bf16[4,32,2048]{2,1,0:T(8,128)(2,1)S(1)}) custom-call(s32[4]{0:T(128)S(1)} %get-tuple-element.92.experts_ref, bf16[128,2176]{1,0:T(8,128)(2,1)S(1)} %get-tuple-element.76.refs_0_.refs_21_, ...), custom_call_target="tpu_custom_call" | custom-call | flops 268435456 | bytes 4194304 | tf_op jit(solution)/shard_map/pallas_call | solution.py:137
  32.8 3.0 %collective-permute-done.1.refs_2_.refs_18_ = bf16[64,2176]{1,0:T(8,128)(2,1)} collective-permute-done((bf16[64,2176]{1,0:T(8,128)(2,1)}, bf16[64,2176]{1,0:T(8,128)(2,1)}, u32[]{:S(2)}, u32[]{:S(2)}) %collective-permute-start.1) | collective-permute-done | bytes 278560 | tf_op jit(solution)/shard_map/ppermute | solution.py:21
  35.8 2.2 %shard_map.65 = (bf16[4,32,2048]{2,1,0:T(8,128)(2,1)S(1)}, bf16[4,32,2048]{2,1,0:T(8,128)(2,1)S(1)}, bf16[4,32,2048]{2,1,0:T(8,128)(2,1)S(1)}, bf16[4,32,2048]{2,1,0:T(8,128)(2,1)S(1)}) custom-call(s32[4]{0:T(128)S(1)} %get-tuple-element.91.experts_ref, bf16[128,2176]{1,0:T(8,128)(2,1)S(1)} %get-tuple-element.71.refs_0_.refs_16_, ...), custom_call_target="tpu_custom_call" | custom-call | flops 268435456 | bytes 4194304 | tf_op jit(solution)/shard_map/pallas_call | solution.py:137
  38.1 4.4 %collective-permute-start.9 = (bf16[4,32,2048]{2,1,0:T(8,128)(2,1)S(1)}, bf16[4,32,2048]{2,1,0:T(8,128)(2,1)S(1)}, u32[]{:S(2)}, u32[]{:S(2)}) collective-permute-start(bf16[4,32,2048]{2,1,0:T(8,128)(2,1)S(1)} %get-tuple-element.96), channel_id=1, source_target_pairs={{0,2},{1,3},{2,0},{3,1},{4,6},{5,7},{6,4},{7,5},{8,10},{9,11},{10,... | collective-permute-start | bytes 1572872 | tf_op jit(solution)/shard_map/ppermute | solution.py:21
  43.9 9.7 %collective-permute-done.8.refs_1_ = bf16[4,32,2048]{2,1,0:T(8,128)(2,1)S(1)} collective-permute-done((bf16[4,32,2048]{2,1,0:T(8,128)(2,1)S(1)}, bf16[4,32,2048]{2,1,0:T(8,128)(2,1)S(1)}, u32[]{:S(2)}, u32[]{:S(2)}) %collective-permute-start.8) | collective-permute-done | bytes 524320 | tf_op jit(solution)/shard_map/ppermute | solution.py:21
  53.6 9.5 %collective-permute-start.13 = (bf16[4,32,2048]{2,1,0:T(8,128)(2,1)S(1)}, bf16[4,32,2048]{2,1,0:T(8,128)(2,1)S(1)}, u32[]{:S(2)}, u32[]{:S(2)}) collective-permute-start(bf16[4,32,2048]{2,1,0:T(8,128)(2,1)S(1)} %get-tuple-element.101), channel_id=1, source_target_pairs={{0,12},{4,0},{8,4},{12,8},{1,13},{5,1},{9,5},{13,9},{2,14},{6,2},{... | collective-permute-start | bytes 1572872 | tf_op jit(solution)/shard_map/ppermute | solution.py:21
  63.0 2.2 %shard_map.67 = (bf16[4,32,2048]{2,1,0:T(8,128)(2,1)S(1)}, bf16[4,32,2048]{2,1,0:T(8,128)(2,1)S(1)}, bf16[4,32,2048]{2,1,0:T(8,128)(2,1)S(1)}, bf16[4,32,2048]{2,1,0:T(8,128)(2,1)S(1)}) custom-call(s32[4]{0:T(128)S(1)} %get-tuple-element.91.experts_ref, bf16[128,2176]{1,0:T(8,128)(2,1)S(1)} %get-tuple-element.71.refs_0_.refs_16_, ...), custom_call_target="tpu_custom_call" | custom-call | flops 268435456 | bytes 4194304 | tf_op jit(solution)/shard_map/pallas_call | solution.py:137
  65.3 2.2 %shard_map.68 = (bf16[4,32,2048]{2,1,0:T(8,128)(2,1)S(1)}, bf16[4,32,2048]{2,1,0:T(8,128)(2,1)S(1)}, bf16[4,32,2048]{2,1,0:T(8,128)(2,1)S(1)}, bf16[4,32,2048]{2,1,0:T(8,128)(2,1)S(1)}) custom-call(s32[4]{0:T(128)S(1)} %get-tuple-element.92.experts_ref, bf16[128,2176]{1,0:T(8,128)(2,1)S(1)} %get-tuple-element.76.refs_0_.refs_21_, ...), custom_call_target="tpu_custom_call" | custom-call | flops 268435456 | bytes 4194304 | tf_op jit(solution)/shard_map/pallas_call | solution.py:137
  68.5 2.4 %collective-permute-start.16 = (bf16[4,32,2048]{2,1,0:T(8,128)(2,1)S(1)}, bf16[4,32,2048]{2,1,0:T(8,128)(2,1)S(1)}, u32[]{:S(2)}, u32[]{:S(2)}) collective-permute-start(bf16[4,32,2048]{2,1,0:T(8,128)(2,1)S(1)} %get-tuple-element.107), channel_id=1, source_target_pairs={{0,3},{1,0},{2,1},{3,2},{4,7},{5,4},{6,5},{7,6},{8,11},{9,8},{10,9... | collective-permute-start | bytes 1572872 | tf_op jit(solution)/shard_map/ppermute | solution.py:21
  70.9 3.6 %collective-permute-start.19 = (bf16[4,32,2048]{2,1,0:T(8,128)(2,1)S(1)}, bf16[4,32,2048]{2,1,0:T(8,128)(2,1)S(1)}, u32[]{:S(2)}, u32[]{:S(2)}) collective-permute-start(bf16[4,32,2048]{2,1,0:T(8,128)(2,1)S(1)} %get-tuple-element.111), channel_id=1, source_target_pairs={{0,12},{4,0},{8,4},{12,8},{1,13},{5,1},{9,5},{13,9},{2,14},{6,2},{... | collective-permute-start | bytes 1572872 | tf_op jit(solution)/shard_map/ppermute | solution.py:21
  74.6 9.7 %shard_map.69.hidden_ref = bf16[512,768]{1,0:T(8,128)(2,1)S(1)} custom-call(bf16[4096,768]{1,0:T(8,128)(2,1)} %bitcast.7, bf16[4096,768]{1,0:T(8,128)(2,1)} %bitcast.9, bf16[4,32,2048]{2,1,0:T(8,128)(2,1)S(1)} %get-tuple-element.94.refs_0_, bf16[4,32,2048]{2,1,0:T(8,128)(2,1)S(1)} %collective-permute-done.8.refs_1_, ...), custom_call_target="tpu_custom_call" | custom-call | flops 6442450944 | bytes 16777216 | tf_op jit(solution)/shard_map/pallas_call | solution.py:183
  84.3 2.2 %collective-permute-done.14.refs_1_ = bf16[4,32,2048]{2,1,0:T(8,128)(2,1)S(1)} collective-permute-done((bf16[4,32,2048]{2,1,0:T(8,128)(2,1)S(1)}, bf16[4,32,2048]{2,1,0:T(8,128)(2,1)S(1)}, u32[]{:S(2)}, u32[]{:S(2)}) %collective-permute-start.14) | collective-permute-done | bytes 524320 | tf_op jit(solution)/shard_map/ppermute | solution.py:21
  86.6 6.5 %shard_map.70 = (bf16[4,32,2048]{2,1,0:T(8,128)(2,1)S(1)}, bf16[4,32,2048]{2,1,0:T(8,128)(2,1)S(1)}, bf16[4,32,2048]{2,1,0:T(8,128)(2,1)S(1)}, bf16[4,32,2048]{2...) custom-call(bf16[512,768]{1,0:T(8,128)(2,1)S(1)} %shard_map.69.hidde, ...), custom_call_target="tpu_custom_call" | custom-call | flops 3221225472 | bytes 10485760 | tf_op jit(solution)/shard_map/pallas_call | solution.py:226
  99.0 9.7 %shard_map.71.hidden_ref = bf16[512,768]{1,0:T(8,128)(2,1)S(1)} custom-call(bf16[4096,768]{1,0:T(8,128)(2,1)} %bitcast.8, bf16[4096,768]{1,0:T(8,128)(2,1)} %bitcast.10, bf16[4,32,2048]{2,1,0:T(8,128)(2,1)S(1)} %get-tuple-element.104.refs_0_, bf16[4,32,2048]{2,1,0:T(8,128)(2,1)S(1)} %collective-permute-done.14.refs_1_, ...), custom_call_target="tpu_custom_call" | custom-call | flops 6442450944 | bytes 16777216 | tf_op jit(solution)/shard_map/pallas_call | solution.py:183
  110.0 6.5 %shard_map.72 = (bf16[4,32,2048]{2,1,0:T(8,128)(2,1)S(1)}, bf16[4,32,2048]{2,1,0:T(8,128)(2,1)S(1)}, bf16[4,32,2048]{2,1,0:T(8,128)(2,1)S(1)}, bf16[4,32,2048]{2...) custom-call(bf16[512,768]{1,0:T(8,128)(2,1)S(1)} %shard_map.71.hidde, ...), custom_call_target="tpu_custom_call" | custom-call | flops 3221225472 | bytes 10485760 | tf_op jit(solution)/shard_map/pallas_call | solution.py:226
  116.6 2.7 %collective-permute-start.23 = (bf16[4,32,2048]{2,1,0:T(8,128)(2,1)S(1)}, bf16[4,32,2048]{2,1,0:T(8,128)(2,1)S(1)}, u32[]{:S(2)}, u32[]{:S(2)}) collective-permute-start(bf16[4,32,2048]{2,1,0:T(8,128)(2,1)S(1)} %get-tuple-element.118), channel_id=1, source_target_pairs={{0,3},{1,0},{2,1},{3,2},{4,7},{5,4},{6,5},{7,6},{8,11},{9,8},{10,9... | collective-permute-start | bytes 1572872 | tf_op jit(solution)/shard_map/ppermute | solution.py:21
  124.1 3.4 %collective-permute-start.30 = (bf16[4,32,2048]{2,1,0:T(8,128)(2,1)S(1)}, bf16[4,32,2048]{2,1,0:T(8,128)(2,1)S(1)}, u32[]{:S(2)}, u32[]{:S(2)}) collective-permute-start(bf16[4,32,2048]{2,1,0:T(8,128)(2,1)S(1)} %get-tuple-element.127), channel_id=1, source_target_pairs={{0,8},{4,12},{8,0},{12,4},{1,9},{5,13},{9,1},{13,5},{2,10},{6,14},... | collective-permute-start | bytes 1572872 | tf_op jit(solution)/shard_map/ppermute | solution.py:21
  127.5 6.5 %collective-permute-done.23.refs_5_ = bf16[4,32,2048]{2,1,0:T(8,128)(2,1)S(1)} collective-permute-done((bf16[4,32,2048]{2,1,0:T(8,128)(2,1)S(1)}, bf16[4,32,2048]{2,1,0:T(8,128)(2,1)S(1)}, u32[]{:S(2)}, u32[]{:S(2)}) %collective-permute-start.23) | collective-permute-done | bytes 524320 | tf_op jit(solution)/shard_map/ppermute | solution.py:21
  134.1 4.4 %collective-permute-done.25.refs_7_ = bf16[4,32,2048]{2,1,0:T(8,128)(2,1)S(1)} collective-permute-done((bf16[4,32,2048]{2,1,0:T(8,128)(2,1)S(1)}, bf16[4,32,2048]{2,1,0:T(8,128)(2,1)S(1)}, u32[]{:S(2)}, u32[]{:S(2)}) %collective-permute-start.25) | collective-permute-done | bytes 524320 | tf_op jit(solution)/shard_map/ppermute | solution.py:21
  138.4 7.0 %collective-permute-done.31.refs_15_ = bf16[4,32,2048]{2,1,0:T(8,128)(2,1)S(1)} collective-permute-done((bf16[4,32,2048]{2,1,0:T(8,128)(2,1)S(1)}, bf16[4,32,2048]{2,1,0:T(8,128)(2,1)S(1)}, u32[]{:S(2)}, u32[]{:S(2)}) %collective-permute-start.31) | collective-permute-done | bytes 524320 | tf_op jit(solution)/shard_map/ppermute | solution.py:21
  145.5 3.0 %shard_map.73 = (bf16[128,2048]{1,0:T(8,128)(2,1)S(1)}, bf16[128,2048]{1,0:T(8,128)(2,1)S(1)}, bf16[128,2048]{1,0:T(8,128)(2,1)S(1)}, bf16[128,2048]{1,0:T(8,128...) custom-call(s32[8]{0:T(128)S(1)} %pad_add_fusion.experts_ref, ...), custom_call_target="tpu_custom_call" | custom-call | flops 1073741824 | bytes 12582912 | tf_op jit(solution)/shard_map/pallas_call | solution.py:276
  148.4 2.6 %collective-permute-start.32 = (bf16[128,2048]{1,0:T(8,128)(2,1)S(1)}, bf16[128,2048]{1,0:T(8,128)(2,1)S(1)}, u32[]{:S(2)}, u32[]{:S(2)}) collective-permute-start(bf16[128,2048]{1,0:T(8,128)(2,1)S(1)} %get-tuple-element.130), channel_id=1, source_target_pairs={{0,12},{4,0},{8,4},{12,8},{1,13},{5,1},{9,5},{13,9},{2,14},{6,2},{... | collective-permute-start | bytes 1572872 | tf_op jit(solution)/shard_map/ppermute | solution.py:21
  152.0 10.9 %collective-permute-start.35 = (bf16[128,2048]{1,0:T(8,128)(2,1)S(1)}, bf16[128,2048]{1,0:T(8,128)(2,1)S(1)}, u32[]{:S(2)}, u32[]{:S(2)}) collective-permute-start(bf16[128,2048]{1,0:T(8,128)(2,1)S(1)} %get-tuple-element.134), channel_id=1, source_target_pairs={{0,3},{1,0},{2,1},{3,2},{4,7},{5,4},{6,5},{7,6},{8,11},{9,8},{10,9... | collective-permute-start | bytes 1572872 | tf_op jit(solution)/shard_map/ppermute | solution.py:21
  163.8 3.3 %collective-permute-done.34 = bf16[128,2048]{1,0:T(8,128)(2,1)S(1)} collective-permute-done((bf16[128,2048]{1,0:T(8,128)(2,1)S(1)}, bf16[128,2048]{1,0:T(8,128)(2,1)S(1)}, u32[]{:S(2)}, u32[]{:S(2)}) %collective-permute-start.34) | collective-permute-done | bytes 524320 | tf_op jit(solution)/shard_map/ppermute | solution.py:21
  167.4 7.8 %collective-permute-done.35 = bf16[128,2048]{1,0:T(8,128)(2,1)S(1)} collective-permute-done((bf16[128,2048]{1,0:T(8,128)(2,1)S(1)}, bf16[128,2048]{1,0:T(8,128)(2,1)S(1)}, u32[]{:S(2)}, u32[]{:S(2)}) %collective-permute-start.35) | collective-permute-done | bytes 524320 | tf_op jit(solution)/shard_map/ppermute | solution.py:21
  175.3 4.0 %collective-permute-done.37 = bf16[128,2048]{1,0:T(8,128)(2,1)S(1)} collective-permute-done((bf16[128,2048]{1,0:T(8,128)(2,1)S(1)}, bf16[128,2048]{1,0:T(8,128)(2,1)S(1)}, u32[]{:S(2)}, u32[]{:S(2)}) %collective-permute-start.37) | collective-permute-done | bytes 524320 | tf_op jit(solution)/shard_map/ppermute | solution.py:21
  (63 shorter events, 22.7 us)
Async XLA Ops:
  1.8 14.8 %collective-permute-start.6 = (bf16[128,2176]{1,0:T(8,128)(2,1)S(1)}, bf16[128,2176]{1,0:T(8,128)(2,1)S(1)}, u32[]{:S(2)}, u32[]{:S(2)}) collective-permute-start(bf16[128,2176]{1,0:T(8,128)(2,1)S(1)} %get-tuple-element.76.refs_0_.refs_21_), channel_id=1, source_target_pairs={{0,3},{1,0},{2,1},{3,2},{4,7},{5,4},{6,5},{7,6},{8,11},{9,8},{10,9... | collective-permute-start | bytes 1671176 | tf_op jit(solution)/shard_map/ppermute | solution.py:21
  4.7 16.3 %collective-permute-start.4 = (bf16[128,2176]{1,0:T(8,128)(2,1)S(1)}, bf16[128,2176]{1,0:T(8,128)(2,1)S(1)}, u32[]{:S(2)}, u32[]{:S(2)}) collective-permute-start(bf16[128,2176]{1,0:T(8,128)(2,1)S(1)} %get-tuple-element.76.refs_0_.refs_21_), channel_id=1, source_target_pairs={{0,1},{1,2},{2,3},{3,0},{4,5},{5,6},{6,7},{7,4},{8,9},{9,10},{10,1... | collective-permute-start | bytes 1671176 | tf_op jit(solution)/shard_map/ppermute | solution.py:21
  4.8 17.1 %collective-permute-start.2 = (bf16[128,2176]{1,0:T(8,128)(2,1)S(1)}, bf16[128,2176]{1,0:T(8,128)(2,1)S(1)}, u32[]{:S(2)}, u32[]{:S(2)}) collective-permute-start(bf16[128,2176]{1,0:T(8,128)(2,1)S(1)} %get-tuple-element.71.refs_0_.refs_16_), channel_id=1, source_target_pairs={{0,12},{4,0},{8,4},{12,8},{1,13},{5,1},{9,5},{13,9},{2,14},{6,2},{... | collective-permute-start | bytes 1671176 | tf_op jit(solution)/shard_map/ppermute | solution.py:21
  8.8 17.8 %collective-permute-start = (bf16[128,2176]{1,0:T(8,128)(2,1)S(1)}, bf16[128,2176]{1,0:T(8,128)(2,1)S(1)}, u32[]{:S(2)}, u32[]{:S(2)}) collective-permute-start(bf16[128,2176]{1,0:T(8,128)(2,1)S(1)} %get-tuple-element.71.refs_0_.refs_16_), channel_id=1, source_target_pairs={{0,4},{4,8},{8,12},{12,0},{1,5},{5,9},{9,13},{13,1},{2,6},{6,10},{... | collective-permute-start | bytes 1671176 | tf_op jit(solution)/shard_map/ppermute | solution.py:21
  38.0 15.5 %collective-permute-start.8 = (bf16[4,32,2048]{2,1,0:T(8,128)(2,1)S(1)}, bf16[4,32,2048]{2,1,0:T(8,128)(2,1)S(1)}, u32[]{:S(2)}, u32[]{:S(2)}) collective-permute-start(bf16[4,32,2048]{2,1,0:T(8,128)(2,1)S(1)} %get-tuple-element.95), channel_id=1, source_target_pairs={{0,1},{1,2},{2,3},{3,0},{4,5},{5,6},{6,7},{7,4},{8,9},{9,10},{10,1... | collective-permute-start | bytes 1572872 | tf_op jit(solution)/shard_map/ppermute | solution.py:21
  38.1 29.4 %collective-permute-start.9 = (bf16[4,32,2048]{2,1,0:T(8,128)(2,1)S(1)}, bf16[4,32,2048]{2,1,0:T(8,128)(2,1)S(1)}, u32[]{:S(2)}, u32[]{:S(2)}) collective-permute-start(bf16[4,32,2048]{2,1,0:T(8,128)(2,1)S(1)} %get-tuple-element.96), channel_id=1, source_target_pairs={{0,2},{1,3},{2,0},{3,1},{4,6},{5,7},{6,4},{7,5},{8,10},{9,11},{10,... | collective-permute-start | bytes 1572872 | tf_op jit(solution)/shard_map/ppermute | solution.py:21
  42.5 25.1 %collective-permute-start.10 = (bf16[4,32,2048]{2,1,0:T(8,128)(2,1)S(1)}, bf16[4,32,2048]{2,1,0:T(8,128)(2,1)S(1)}, u32[]{:S(2)}, u32[]{:S(2)}) collective-permute-start(bf16[4,32,2048]{2,1,0:T(8,128)(2,1)S(1)} %get-tuple-element.97), channel_id=1, source_target_pairs={{0,3},{1,0},{2,1},{3,2},{4,7},{5,4},{6,5},{7,6},{8,11},{9,8},{10,9... | collective-permute-start | bytes 1572872 | tf_op jit(solution)/shard_map/ppermute | solution.py:21
  42.5 25.9 %collective-permute-start.11 = (bf16[4,32,2048]{2,1,0:T(8,128)(2,1)S(1)}, bf16[4,32,2048]{2,1,0:T(8,128)(2,1)S(1)}, u32[]{:S(2)}, u32[]{:S(2)}) collective-permute-start(bf16[4,32,2048]{2,1,0:T(8,128)(2,1)S(1)} %get-tuple-element.99), channel_id=1, source_target_pairs={{0,4},{4,8},{8,12},{12,0},{1,5},{5,9},{9,13},{13,1},{2,6},{6,10},{... | collective-permute-start | bytes 1572872 | tf_op jit(solution)/shard_map/ppermute | solution.py:21
  42.5 28.4 %collective-permute-start.12 = (bf16[4,32,2048]{2,1,0:T(8,128)(2,1)S(1)}, bf16[4,32,2048]{2,1,0:T(8,128)(2,1)S(1)}, u32[]{:S(2)}, u32[]{:S(2)}) collective-permute-start(bf16[4,32,2048]{2,1,0:T(8,128)(2,1)S(1)} %get-tuple-element.100), channel_id=1, source_target_pairs={{0,8},{4,12},{8,0},{12,4},{1,9},{5,13},{9,1},{13,5},{2,10},{6,14},... | collective-permute-start | bytes 1572872 | tf_op jit(solution)/shard_map/ppermute | solution.py:21
  53.6 17.4 %collective-permute-start.13 = (bf16[4,32,2048]{2,1,0:T(8,128)(2,1)S(1)}, bf16[4,32,2048]{2,1,0:T(8,128)(2,1)S(1)}, u32[]{:S(2)}, u32[]{:S(2)}) collective-permute-start(bf16[4,32,2048]{2,1,0:T(8,128)(2,1)S(1)} %get-tuple-element.101), channel_id=1, source_target_pairs={{0,12},{4,0},{8,4},{12,8},{1,13},{5,1},{9,5},{13,9},{2,14},{6,2},{... | collective-permute-start | bytes 1572872 | tf_op jit(solution)/shard_map/ppermute | solution.py:21
  67.5 19.0 %collective-permute-start.14 = (bf16[4,32,2048]{2,1,0:T(8,128)(2,1)S(1)}, bf16[4,32,2048]{2,1,0:T(8,128)(2,1)S(1)}, u32[]{:S(2)}, u32[]{:S(2)}) collective-permute-start(bf16[4,32,2048]{2,1,0:T(8,128)(2,1)S(1)} %get-tuple-element.105), channel_id=1, source_target_pairs={{0,1},{1,2},{2,3},{3,0},{4,5},{5,6},{6,7},{7,4},{8,9},{9,10},{10,1... | collective-permute-start | bytes 1572872 | tf_op jit(solution)/shard_map/ppermute | solution.py:21
  67.6 25.5 %collective-permute-start.15 = (bf16[4,32,2048]{2,1,0:T(8,128)(2,1)S(1)}, bf16[4,32,2048]{2,1,0:T(8,128)(2,1)S(1)}, u32[]{:S(2)}, u32[]{:S(2)}) collective-permute-start(bf16[4,32,2048]{2,1,0:T(8,128)(2,1)S(1)} %get-tuple-element.106), channel_id=1, source_target_pairs={{0,2},{1,3},{2,0},{3,1},{4,6},{5,7},{6,4},{7,5},{8,10},{9,11},{10,... | collective-permute-start | bytes 1572872 | tf_op jit(solution)/shard_map/ppermute | solution.py:21
  68.5 24.7 %collective-permute-start.16 = (bf16[4,32,2048]{2,1,0:T(8,128)(2,1)S(1)}, bf16[4,32,2048]{2,1,0:T(8,128)(2,1)S(1)}, u32[]{:S(2)}, u32[]{:S(2)}) collective-permute-start(bf16[4,32,2048]{2,1,0:T(8,128)(2,1)S(1)} %get-tuple-element.107), channel_id=1, source_target_pairs={{0,3},{1,0},{2,1},{3,2},{4,7},{5,4},{6,5},{7,6},{8,11},{9,8},{10,9... | collective-permute-start | bytes 1572872 | tf_op jit(solution)/shard_map/ppermute | solution.py:21
  70.9 22.7 %collective-permute-start.17 = (bf16[4,32,2048]{2,1,0:T(8,128)(2,1)S(1)}, bf16[4,32,2048]{2,1,0:T(8,128)(2,1)S(1)}, u32[]{:S(2)}, u32[]{:S(2)}) collective-permute-start(bf16[4,32,2048]{2,1,0:T(8,128)(2,1)S(1)} %get-tuple-element.109), channel_id=1, source_target_pairs={{0,4},{4,8},{8,12},{12,0},{1,5},{5,9},{9,13},{13,1},{2,6},{6,10},{... | collective-permute-start | bytes 1572872 | tf_op jit(solution)/shard_map/ppermute | solution.py:21
  70.9 24.3 %collective-permute-start.19 = (bf16[4,32,2048]{2,1,0:T(8,128)(2,1)S(1)}, bf16[4,32,2048]{2,1,0:T(8,128)(2,1)S(1)}, u32[]{:S(2)}, u32[]{:S(2)}) collective-permute-start(bf16[4,32,2048]{2,1,0:T(8,128)(2,1)S(1)} %get-tuple-element.111), channel_id=1, source_target_pairs={{0,12},{4,0},{8,4},{12,8},{1,13},{5,1},{9,5},{13,9},{2,14},{6,2},{... | collective-permute-start | bytes 1572872 | tf_op jit(solution)/shard_map/ppermute | solution.py:21
  86.6 12.5 %collective-permute-start.18 = (bf16[4,32,2048]{2,1,0:T(8,128)(2,1)S(1)}, bf16[4,32,2048]{2,1,0:T(8,128)(2,1)S(1)}, u32[]{:S(2)}, u32[]{:S(2)}) collective-permute-start(bf16[4,32,2048]{2,1,0:T(8,128)(2,1)S(1)} %get-tuple-element.110), channel_id=1, source_target_pairs={{0,8},{4,12},{8,0},{12,4},{1,9},{5,13},{9,1},{13,5},{2,10},{6,14},... | collective-permute-start | bytes 1572872 | tf_op jit(solution)/shard_map/ppermute | solution.py:21
  93.1 15.7 %collective-permute-start.20 = (bf16[4,32,2048]{2,1,0:T(8,128)(2,1)S(1)}, bf16[4,32,2048]{2,1,0:T(8,128)(2,1)S(1)}, u32[]{:S(2)}, u32[]{:S(2)}) collective-permute-start(bf16[4,32,2048]{2,1,0:T(8,128)(2,1)S(1)} %get-tuple-element.112), channel_id=1, source_target_pairs={{0,3},{1,0},{2,1},{3,2},{4,7},{5,4},{6,5},{7,6},{8,11},{9,8},{10,9... | collective-permute-start | bytes 1572872 | tf_op jit(solution)/shard_map/ppermute | solution.py:21
  93.2 23.4 %collective-permute-start.21 = (bf16[4,32,2048]{2,1,0:T(8,128)(2,1)S(1)}, bf16[4,32,2048]{2,1,0:T(8,128)(2,1)S(1)}, u32[]{:S(2)}, u32[]{:S(2)}) collective-permute-start(bf16[4,32,2048]{2,1,0:T(8,128)(2,1)S(1)} %get-tuple-element.114), channel_id=1, source_target_pairs={{0,2},{1,3},{2,0},{3,1},{4,6},{5,7},{6,4},{7,5},{8,10},{9,11},{10,... | collective-permute-start | bytes 1572872 | tf_op jit(solution)/shard_map/ppermute | solution.py:21
  93.6 25.7 %collective-permute-start.22 = (bf16[4,32,2048]{2,1,0:T(8,128)(2,1)S(1)}, bf16[4,32,2048]{2,1,0:T(8,128)(2,1)S(1)}, u32[]{:S(2)}, u32[]{:S(2)}) collective-permute-start(bf16[4,32,2048]{2,1,0:T(8,128)(2,1)S(1)} %get-tuple-element.115), channel_id=1, source_target_pairs={{0,1},{1,2},{2,3},{3,0},{4,5},{5,6},{6,7},{7,4},{8,9},{9,10},{10,1... | collective-permute-start | bytes 1572872 | tf_op jit(solution)/shard_map/ppermute | solution.py:21
  95.3 25.5 %collective-permute-start.26 = (bf16[4,32,2048]{2,1,0:T(8,128)(2,1)S(1)}, bf16[4,32,2048]{2,1,0:T(8,128)(2,1)S(1)}, u32[]{:S(2)}, u32[]{:S(2)}) collective-permute-start(bf16[4,32,2048]{2,1,0:T(8,128)(2,1)S(1)} %get-tuple-element.122), channel_id=1, source_target_pairs={{0,12},{4,0},{8,4},{12,8},{1,13},{5,1},{9,5},{13,9},{2,14},{6,2},{... | collective-permute-start | bytes 1572872 | tf_op jit(solution)/shard_map/ppermute | solution.py:21
  99.0 23.1 %collective-permute-start.27 = (bf16[4,32,2048]{2,1,0:T(8,128)(2,1)S(1)}, bf16[4,32,2048]{2,1,0:T(8,128)(2,1)S(1)}, u32[]{:S(2)}, u32[]{:S(2)}) collective-permute-start(bf16[4,32,2048]{2,1,0:T(8,128)(2,1)S(1)} %get-tuple-element.123), channel_id=1, source_target_pairs={{0,8},{4,12},{8,0},{12,4},{1,9},{5,13},{9,1},{13,5},{2,10},{6,14},... | collective-permute-start | bytes 1572872 | tf_op jit(solution)/shard_map/ppermute | solution.py:21
  108.8 15.3 %collective-permute-start.28 = (bf16[4,32,2048]{2,1,0:T(8,128)(2,1)S(1)}, bf16[4,32,2048]{2,1,0:T(8,128)(2,1)S(1)}, u32[]{:S(2)}, u32[]{:S(2)}) collective-permute-start(bf16[4,32,2048]{2,1,0:T(8,128)(2,1)S(1)} %get-tuple-element.124), channel_id=1, source_target_pairs={{0,4},{4,8},{8,12},{12,0},{1,5},{5,9},{9,13},{13,1},{2,6},{6,10},{... | collective-permute-start | bytes 1572872 | tf_op jit(solution)/shard_map/ppermute | solution.py:21
  116.6 17.4 %collective-permute-start.23 = (bf16[4,32,2048]{2,1,0:T(8,128)(2,1)S(1)}, bf16[4,32,2048]{2,1,0:T(8,128)(2,1)S(1)}, u32[]{:S(2)}, u32[]{:S(2)}) collective-permute-start(bf16[4,32,2048]{2,1,0:T(8,128)(2,1)S(1)} %get-tuple-element.118), channel_id=1, source_target_pairs={{0,3},{1,0},{2,1},{3,2},{4,7},{5,4},{6,5},{7,6},{8,11},{9,8},{10,9... | collective-permute-start | bytes 1572872 | tf_op jit(solution)/shard_map/ppermute | solution.py:21
  119.3 14.7 %collective-permute-start.24 = (bf16[4,32,2048]{2,1,0:T(8,128)(2,1)S(1)}, bf16[4,32,2048]{2,1,0:T(8,128)(2,1)S(1)}, u32[]{:S(2)}, u32[]{:S(2)}) collective-permute-start(bf16[4,32,2048]{2,1,0:T(8,128)(2,1)S(1)} %get-tuple-element.119), channel_id=1, source_target_pairs={{0,2},{1,3},{2,0},{3,1},{4,6},{5,7},{6,4},{7,5},{8,10},{9,11},{10,... | collective-permute-start | bytes 1572872 | tf_op jit(solution)/shard_map/ppermute | solution.py:21
  120.8 17.6 %collective-permute-start.25 = (bf16[4,32,2048]{2,1,0:T(8,128)(2,1)S(1)}, bf16[4,32,2048]{2,1,0:T(8,128)(2,1)S(1)}, u32[]{:S(2)}, u32[]{:S(2)}) collective-permute-start(bf16[4,32,2048]{2,1,0:T(8,128)(2,1)S(1)} %get-tuple-element.120), channel_id=1, source_target_pairs={{0,1},{1,2},{2,3},{3,0},{4,5},{5,6},{6,7},{7,4},{8,9},{9,10},{10,1... | collective-permute-start | bytes 1572872 | tf_op jit(solution)/shard_map/ppermute | solution.py:21
  122.1 16.3 %collective-permute-start.29 = (bf16[4,32,2048]{2,1,0:T(8,128)(2,1)S(1)}, bf16[4,32,2048]{2,1,0:T(8,128)(2,1)S(1)}, u32[]{:S(2)}, u32[]{:S(2)}) collective-permute-start(bf16[4,32,2048]{2,1,0:T(8,128)(2,1)S(1)} %get-tuple-element.126), channel_id=1, source_target_pairs={{0,12},{4,0},{8,4},{12,8},{1,13},{5,1},{9,5},{13,9},{2,14},{6,2},{... | collective-permute-start | bytes 1572872 | tf_op jit(solution)/shard_map/ppermute | solution.py:21
  124.1 14.4 %collective-permute-start.30 = (bf16[4,32,2048]{2,1,0:T(8,128)(2,1)S(1)}, bf16[4,32,2048]{2,1,0:T(8,128)(2,1)S(1)}, u32[]{:S(2)}, u32[]{:S(2)}) collective-permute-start(bf16[4,32,2048]{2,1,0:T(8,128)(2,1)S(1)} %get-tuple-element.127), channel_id=1, source_target_pairs={{0,8},{4,12},{8,0},{12,4},{1,9},{5,13},{9,1},{13,5},{2,10},{6,14},... | collective-permute-start | bytes 1572872 | tf_op jit(solution)/shard_map/ppermute | solution.py:21
  148.4 15.0 %collective-permute-start.32 = (bf16[128,2048]{1,0:T(8,128)(2,1)S(1)}, bf16[128,2048]{1,0:T(8,128)(2,1)S(1)}, u32[]{:S(2)}, u32[]{:S(2)}) collective-permute-start(bf16[128,2048]{1,0:T(8,128)(2,1)S(1)} %get-tuple-element.130), channel_id=1, source_target_pairs={{0,12},{4,0},{8,4},{12,8},{1,13},{5,1},{9,5},{13,9},{2,14},{6,2},{... | collective-permute-start | bytes 1572872 | tf_op jit(solution)/shard_map/ppermute | solution.py:21
  151.1 12.7 %collective-permute-start.33 = (bf16[128,2048]{1,0:T(8,128)(2,1)S(1)}, bf16[128,2048]{1,0:T(8,128)(2,1)S(1)}, u32[]{:S(2)}, u32[]{:S(2)}) collective-permute-start(bf16[128,2048]{1,0:T(8,128)(2,1)S(1)} %get-tuple-element.131), channel_id=1, source_target_pairs={{0,8},{4,12},{8,0},{12,4},{1,9},{5,13},{9,1},{13,5},{2,10},{6,14},... | collective-permute-start | bytes 1572872 | tf_op jit(solution)/shard_map/ppermute | solution.py:21
  151.1 16.0 %collective-permute-start.34 = (bf16[128,2048]{1,0:T(8,128)(2,1)S(1)}, bf16[128,2048]{1,0:T(8,128)(2,1)S(1)}, u32[]{:S(2)}, u32[]{:S(2)}) collective-permute-start(bf16[128,2048]{1,0:T(8,128)(2,1)S(1)} %get-tuple-element.132), channel_id=1, source_target_pairs={{0,4},{4,8},{8,12},{12,0},{1,5},{5,9},{9,13},{13,1},{2,6},{6,10},{... | collective-permute-start | bytes 1572872 | tf_op jit(solution)/shard_map/ppermute | solution.py:21
  152.0 23.2 %collective-permute-start.35 = (bf16[128,2048]{1,0:T(8,128)(2,1)S(1)}, bf16[128,2048]{1,0:T(8,128)(2,1)S(1)}, u32[]{:S(2)}, u32[]{:S(2)}) collective-permute-start(bf16[128,2048]{1,0:T(8,128)(2,1)S(1)} %get-tuple-element.134), channel_id=1, source_target_pairs={{0,3},{1,0},{2,1},{3,2},{4,7},{5,4},{6,5},{7,6},{8,11},{9,8},{10,9... | collective-permute-start | bytes 1572872 | tf_op jit(solution)/shard_map/ppermute | solution.py:21
  163.4 15.8 %collective-permute-start.37 = (bf16[128,2048]{1,0:T(8,128)(2,1)S(1)}, bf16[128,2048]{1,0:T(8,128)(2,1)S(1)}, u32[]{:S(2)}, u32[]{:S(2)}) collective-permute-start(bf16[128,2048]{1,0:T(8,128)(2,1)S(1)} %get-tuple-element.136), channel_id=1, source_target_pairs={{0,1},{1,2},{2,3},{3,0},{4,5},{5,6},{6,7},{7,4},{8,9},{9,10},{10,1... | collective-permute-start | bytes 1572872 | tf_op jit(solution)/shard_map/ppermute | solution.py:21
  (6 other events, 61.3 us)

commit v7 on v6

v7 whole, which is shorter than its diff:
```python
import functools

import jax
import jax.numpy as jnp
from jax import lax
from jax.experimental import pallas as pl
from jax.experimental.pallas import tpu as pltpu
from jax.sharding import Mesh, PartitionSpec as P

SIDE = 4
CAP = 64
EARLY = 48
PLAN = (
    ((0, 0, EARLY), (1, 0, EARLY), (3, 0, EARLY)),
    ((0, EARLY, CAP - EARLY), (1, EARLY, CAP - EARLY), (3, EARLY, CAP - EARLY), (2, 0, CAP)),
)
TILE = 128
FF_TILE = 256
D_TILE = 1024
VMEM = 36 * 1024 * 1024


def shift(block, axis, step):
    return lax.ppermute(block, axis, [(i, (i + step) % SIDE) for i in range(SIDE)])


def gather_line(half, axis):
    rows = half.shape[0] // 2
    ahead, behind = shift(half, axis, 1), shift(half, axis, -1)
    low = shift(ahead[:rows], axis, 1)
    high = shift(behind[rows:], axis, -1)
    return [(half,), (ahead,), (low, high), (behind,)]


def load(refs, column=slice(None)):
    parts = [ref[:, column] for ref in refs]
    return parts[0] if len(parts) == 1 else jnp.concatenate(parts, axis=0)


def regroup(refs, counts):
    groups = []
    for count in counts:
        groups.append(refs[:count])
        refs = refs[count:]
    return groups


def offsets(sizes):
    return [sum(sizes[:i]) for i in range(len(sizes))]


def in_hbm(*arrays):
    return [pltpu.with_memory_space_constraint(array, pltpu.HBM) for array in arrays]


def prepare_kernel(token_ref, id_ref, gate_ref, a_ref, b_ref):
    tokens, depth = token_ref.shape
    half = depth // 2
    top = id_ref.shape[0]
    given = jnp.concatenate([id_ref[...].astype(jnp.float32), gate_ref[...]], axis=0).T
    lane = lax.broadcasted_iota(jnp.int32, (tokens, TILE), 1)
    number = lane.astype(jnp.float32)
    row = lax.broadcasted_iota(jnp.int32, (tokens, tokens), 0)
    column = lax.broadcasted_iota(jnp.int32, (tokens, tokens), 1)
    ids = [given[:, k : k + 1] for k in range(top)]
    named = jnp.zeros((tokens, TILE), jnp.float32)
    for k in range(top):
        named = jnp.where(ids[k] == number, 1.0, named)
    before = jnp.where(column < row, 1.0, 0.0).astype(jnp.bfloat16)
    rank = jnp.dot(before, named.astype(jnp.bfloat16), preferred_element_type=jnp.float32)
    facts = jnp.zeros((tokens, TILE), jnp.float32)
    for k in range(top):
        place = jnp.sum(jnp.where(ids[k] == number, rank, 0.0), axis=1, keepdims=True)
        facts = jnp.where(lane == k, ids[k], facts)
        facts = jnp.where(lane == top + k, place, facts)
        facts = jnp.where(lane == 2 * top + k, given[:, top + k : top + k + 1], facts)
    facts = facts.astype(jnp.bfloat16)
    a_ref[:, :half] = token_ref[:, :half]
    b_ref[:, :half] = token_ref[:, half:]
    a_ref[:, half:] = facts
    b_ref[:, half:] = facts


def prepare(tokens, expert_ids, gate_values):
    rows, depth = tokens.shape
    out = jax.ShapeDtypeStruct((rows, depth // 2 + TILE), jnp.bfloat16)
    top = expert_ids.shape[1]
    return pl.pallas_call(
        prepare_kernel,
        grid=(1,),
        in_specs=[
            pl.BlockSpec((rows, depth), lambda i: (0, 0)),
            pl.BlockSpec((top, rows), lambda i: (0, 0)),
            pl.BlockSpec((top, rows), lambda i: (0, 0)),
        ],
        out_specs=[pl.BlockSpec(out.shape, lambda i: (0, 0))] * 2,
        out_shape=[out, out],
        compiler_params=pltpu.CompilerParams(vmem_limit_bytes=VMEM),
        cost_estimate=pl.CostEstimate(
            flops=2 * rows * rows * TILE, bytes_accessed=4 * rows * depth, transcendentals=0
        ),
    )(*in_hbm(tokens, expert_ids.T, gate_values.T))


def codes(facts, top):
    facts = facts.astype(jnp.float32)
    return [facts[:, k : k + 1] * CAP + facts[:, top + k : top + k + 1] for k in range(top)]


def targets(experts_ref, pieces, tokens):
    count = sum(rows for _, _, rows in pieces)
    lane = lax.broadcasted_iota(jnp.int32, (tokens, count), 1)
    code = jnp.zeros((tokens, count), jnp.int32)
    low = 0
    for place, first, rows in pieces:
        value = experts_ref[place] * CAP + first + lane - low
        code = jnp.where((lane >= low) & (lane < low + rows), value, code)
        low += rows
    return code.astype(jnp.float32)


def pick_rows(experts_ref, pieces, top, refs, width):
    tokens = sum(ref.shape[0] for ref in refs)
    target = targets(experts_ref, pieces, tokens)
    pick = jnp.zeros(target.shape, jnp.float32)
    for code in codes(load(refs, slice(width, width + TILE)), top):
        pick = jnp.where(code == target, 1.0, pick)
    rows = jnp.dot(
        pick.T.astype(jnp.bfloat16),
        load(refs, slice(0, width)),
        preferred_element_type=jnp.float32,
    )
    return rows.astype(jnp.bfloat16)


def pack_a_kernel(segments, counts, top, experts_ref, *refs):
    *sources, outs = regroup(refs, counts + (SIDE,))
    width = outs[0].shape[-1]
    starts = offsets([rows for _, _, rows in segments])
    for refs, start, (_, first, rows) in zip(sources, starts, segments):
        pieces = [(dest, first, rows) for dest in range(SIDE)]
        picked = pick_rows(experts_ref, pieces, top, refs, width)
        for dest in range(SIDE):
            outs[dest][start : start + rows] = picked[dest * rows : (dest + 1) * rows]


def pack_b_kernel(segments, counts, top, experts_ref, *refs):
    *sources, outs = regroup(refs, counts + (len(segments),))
    width = outs[0].shape[-1]
    starts = offsets([rows for _, _, rows in segments])
    for source, refs in enumerate(sources):
        picked = pick_rows(experts_ref, segments, top, refs, width)
        for out, start, (_, _, rows) in zip(outs, starts, segments):
            out[source * rows : (source + 1) * rows] = picked[start : start + rows]


def pack(kernel, segments, top, experts, sources, sizes):
    tokens, width = sources[0][0].shape
    width -= TILE
    counts = tuple(len(source) for source in sources)
    blocks = [block for source in sources for block in source]
    total = sum(sizes)
    return pl.pallas_call(
        functools.partial(kernel, segments, counts, top),
        in_specs=[pl.BlockSpec(memory_space=pltpu.SMEM)]
        + [pl.BlockSpec(memory_space=pltpu.VMEM)] * len(blocks),
        out_specs=[pl.BlockSpec(memory_space=pltpu.VMEM)] * len(sizes),
        out_shape=[jax.ShapeDtypeStruct((rows, width), jnp.bfloat16) for rows in sizes],
        compiler_params=pltpu.CompilerParams(vmem_limit_bytes=VMEM),
        cost_estimate=pl.CostEstimate(
            flops=2 * total * tokens * width,
            bytes_accessed=2 * width * (tokens * len(sources) + total),
            transcendentals=0,
        ),
    )(experts, *blocks)


def hidden_kernel(segments, wg_ref, wu_ref, *refs):
    a_in, b_in, (hidden_ref, x_ref, sems) = regroup(refs, (SIDE, len(segments), 3))
    half = x_ref.shape[-1] // 2

    @pl.when(pl.program_id(0) == 0)
    def _():
        copies = []

        def move(source, target):
            copies.append(pltpu.make_async_copy(source, target, sems.at[len(copies)]))

        base = start = 0
        for ref, (_, _, rows) in zip(b_in, segments):
            move(ref, x_ref.at[base : base + SIDE * rows, half:])
            for k in range(SIDE):
                low = base + k * rows
                move(a_in[k].at[start : start + rows], x_ref.at[low : low + rows, :half])
            base += SIDE * rows
            start += rows
        for copy in copies:
            copy.start()
        for copy in copies:
            copy.wait()

    x = x_ref[...]
    gate = jnp.dot(x, wg_ref[...], preferred_element_type=jnp.float32)
    up = jnp.dot(x, wu_ref[...], preferred_element_type=jnp.float32)
    hidden_ref[...] = (gate / (1.0 + jnp.exp(-gate)) * up).astype(jnp.bfloat16)


def hidden_rows(segments, w_gate, w_up, a_in, b_in):
    depth, ff = w_gate.shape
    count = SIDE * sum(rows for _, _, rows in segments)
    weight = pl.BlockSpec((depth, FF_TILE), lambda i: (0, i))
    return pl.pallas_call(
        functools.partial(hidden_kernel, segments),
        grid=(ff // FF_TILE,),
        in_specs=[weight, weight]
        + [pl.BlockSpec(memory_space=pl.ANY)] * (SIDE + len(segments)),
        out_specs=pl.BlockSpec((count, FF_TILE), lambda i: (0, i)),
        out_shape=jax.ShapeDtypeStruct((count, ff), jnp.bfloat16),
        scratch_shapes=[
            pltpu.VMEM((count, depth), jnp.bfloat16),
            pltpu.SemaphoreType.DMA(((SIDE + 1) * len(segments),)),
        ],
        compiler_params=pltpu.CompilerParams(vmem_limit_bytes=VMEM),
        cost_estimate=pl.CostEstimate(
            flops=4 * count * depth * ff,
            bytes_accessed=4 * depth * ff + 2 * count * depth,
            transcendentals=count * ff,
        ),
    )(w_gate, w_up, *a_in, *b_in)


def down_kernel(segments, n_half, hidden_ref, wd_ref, *refs):
    a_out, b_out = refs[:SIDE], refs[SIDE:]
    out = jnp.dot(hidden_ref[...], wd_ref[...], preferred_element_type=jnp.float32)
    out = out.astype(jnp.bfloat16)

    @pl.when(pl.program_id(0) < n_half)
    def _():
        base = start = 0
        for _, _, rows in segments:
            for k in range(SIDE):
                low = base + k * rows
                a_out[k][start : start + rows] = out[low : low + rows]
            base += SIDE * rows
            start += rows

    @pl.when(pl.program_id(0) >= n_half)
    def _():
        base = 0
        for ref, (_, _, rows) in zip(b_out, segments):
            ref[...] = out[base : base + SIDE * rows]
            base += SIDE * rows


def down_rows(segments, hidden, w_down):
    count, ff = hidden.shape
    half = w_down.shape[1] // 2
    tile = min(D_TILE, half)
    n_half = half // tile
    sizes = [count // SIDE] * SIDE, [SIDE * rows for _, _, rows in segments]
    a_specs = [
        pl.BlockSpec((rows, tile), lambda i: (0, jnp.minimum(i, n_half - 1)))
        for rows in sizes[0]
    ]
    b_specs = [
        pl.BlockSpec((rows, tile), lambda i: (0, jnp.maximum(i - n_half, 0)))
        for rows in sizes[1]
    ]
    done = pl.pallas_call(
        functools.partial(down_kernel, segments, n_half),
        grid=(2 * n_half,),
        in_specs=[
            pl.BlockSpec((count, ff), lambda i: (0, 0)),
            pl.BlockSpec((ff, tile), lambda i: (0, i)),
        ],
        out_specs=a_specs + b_specs,
        out_shape=[
            jax.ShapeDtypeStruct((rows, half), jnp.bfloat16) for rows in sizes[0] + sizes[1]
        ],
        compiler_params=pltpu.CompilerParams(vmem_limit_bytes=VMEM),
        cost_estimate=pl.CostEstimate(
            flops=4 * count * half * ff,
            bytes_accessed=4 * half * ff + 4 * count * half,
            transcendentals=0,
        ),
    )(hidden, w_down)
    return done[:SIDE], done[SIDE:]


def sum_kernel(top, counts, experts_ref, *refs):
    *groups, a_out, b_out = regroup(refs, counts)
    a_in, b_in = groups[: len(PLAN)], groups[len(PLAN) : 2 * len(PLAN)]
    facts = groups[2 * len(PLAN) :]
    tokens = a_out[0].shape[0]

    def total(refs, pieces, rows, out):
        about = load(refs).astype(jnp.float32)
        target = targets(experts_ref, pieces, tokens)
        weight = jnp.zeros(target.shape, jnp.float32)
        for k, code in enumerate(codes(about, top)):
            gate = about[:, 2 * top + k : 2 * top + k + 1]
            weight = jnp.where(code == target, gate, weight)
        mixed = jnp.dot(
            weight.astype(jnp.bfloat16),
            jnp.concatenate(rows, axis=0),
            preferred_element_type=jnp.float32,
        )
        out[...] = mixed.astype(jnp.bfloat16)

    for source in range(SIDE):
        pieces, parts = [], []
        for ins, segments in zip(a_in, PLAN):
            starts = offsets([rows for _, _, rows in segments])
            for start, (distance, first, rows) in zip(starts, segments):
                if distance == source:
                    pieces += [(dest, first, rows) for dest in range(SIDE)]
                    parts += [ref[start : start + rows] for ref in ins]
        total(facts[source], pieces, parts, a_out[source])
    for source in range(SIDE):
        pieces, parts = [], []
        for ins, segments in zip(b_in, PLAN):
            for ref, (distance, first, rows) in zip(ins, segments):
                pieces.append((SIDE + distance, first, rows))
                parts.append(ref[source * rows : (source + 1) * rows])
        total(facts[SIDE + source], pieces, parts, b_out[source])


def sum_rows(top, experts, a_rows, b_rows, a_back, b_back):
    width = a_back[0][0].shape[-1]
    tokens = a_rows[0][0].shape[0]
    lines = [*a_rows, *b_rows]
    facts = [block for line in lines for block in line]
    last = width // TILE
    whole = pl.BlockSpec(memory_space=pltpu.VMEM)
    out = jax.ShapeDtypeStruct((tokens, width), jnp.bfloat16)
    groups = [*a_back, *b_back]
    blocks = [block for group in groups for block in group]
    counts = tuple(len(group) for group in groups + lines) + (SIDE, SIDE)
    done = pl.pallas_call(
        functools.partial(sum_kernel, top, counts),
        grid=(1,),
        in_specs=[pl.BlockSpec(memory_space=pltpu.SMEM)]
        + [whole] * len(blocks)
        + [pl.BlockSpec((f.shape[0], TILE), lambda i: (0, last)) for f in facts],
        out_specs=[whole] * (2 * SIDE),
        out_shape=[out] * (2 * SIDE),
        compiler_params=pltpu.CompilerParams(vmem_limit_bytes=VMEM),
        cost_estimate=pl.CostEstimate(
            flops=4 * SIDE * SIDE * CAP * tokens * width,
            bytes_accessed=4 * SIDE * width * (tokens + SIDE * CAP),
            transcendentals=0,
        ),
    )(experts, *blocks, *facts)
    return done[:SIDE], done[SIDE:]


def send(segments, a_blocks, b_blocks, a_axis, b_axis, sign):
    a_moved, b_moved = list(a_blocks), list(b_blocks)
    for k in range(1, SIDE):
        a_moved[k] = shift(a_blocks[k], a_axis, sign * k)
    for i, (distance, _, _) in enumerate(segments):
        if distance:
            b_moved[i] = shift(b_blocks[i], b_axis, sign * distance)
    return a_moved, b_moved


def local(tokens, expert_ids, gate_values, gate_weight, up_weight, down_weight):
    top = expert_ids.shape[1]
    z, x = lax.axis_index("z"), lax.axis_index("x")
    steps = jnp.arange(SIDE, dtype=jnp.int32)
    a_experts = z * SIDE + (x + steps) % SIDE
    b_experts = (z + steps) % SIDE * SIDE + x

    a_half, b_half = prepare(tokens, expert_ids, gate_values)
    b_rows = gather_line(b_half, "x")
    a_rows = gather_line(a_half, "z")

    w_gate, w_up, w_down = in_hbm(gate_weight[0], up_weight[0], down_weight[0])
    experts = jnp.concatenate([a_experts, b_experts])
    a_back, b_back, hidden = [], [], None

    def back(segments, hidden):
        a_done, b_done = down_rows(segments, hidden, w_down)
        a_home, b_home = send(segments, a_done, b_done, "x", "z", -1)
        a_back.append(a_home)
        b_back.append(b_home)

    packed = []
    for segments in PLAN:
        rows = [size for _, _, size in segments]
        sources = [a_rows[distance] for distance, _, _ in segments]
        a_out = list(
            pack(pack_a_kernel, segments, top, experts[:SIDE], sources, [sum(rows)] * SIDE)
        )
        sizes = [SIDE * size for size in rows]
        b_out = list(pack(pack_b_kernel, segments, top, experts[SIDE:], b_rows, sizes))
        experts, a_out, b_out = lax.optimization_barrier((experts, a_out, b_out))
        packed.append((a_out, b_out))

    a_in, b_in = send(PLAN[0], *packed[0], "x", "z", 1)
    a_out, b_out = packed[1]
    hidden = hidden_rows(PLAN[0], w_gate, w_up, a_in, b_in)
    b_out[2], hidden = lax.optimization_barrier((b_out[2], hidden))
    back(PLAN[0], hidden)
    a_in, b_in = send(PLAN[1], a_out, b_out, "x", "z", 1)
    hidden = hidden_rows(PLAN[1], w_gate, w_up, a_in, b_in)
    b_back[0][1], b_back[0][2], hidden = lax.optimization_barrier(
        (b_back[0][1], b_back[0][2], hidden)
    )
    back(PLAN[-1], hidden)

    a_sums, b_sums = sum_rows(top, experts, a_rows, b_rows, a_back, b_back)
    line = tuple((distance, 0, 0) for distance in range(SIDE))
    a_home, b_home = send(line, a_sums, b_sums, "z", "x", -1)
    mixed = [sum(part.astype(jnp.float32) for part in home) for home in (a_home, b_home)]
    return jnp.concatenate(mixed, axis=1).astype(jnp.bfloat16)


def solution(mesh):
    dp = mesh.devices.shape[0]
    grid = Mesh(mesh.devices.reshape(dp, SIDE, SIDE), ("dp", "z", "x"))
    rows, experts = ("dp", "z", "x"), ("z", "x")
    in_specs = (
        P(rows, None),
        P(rows, None),
        P(rows, None),
        P(experts, None, None),
        P(experts, None, None),
        P(experts, None, None),
    )
    return jax.shard_map(
        local, mesh=grid, in_specs=in_specs, out_specs=P(rows, None), check_vma=False
    )
```

time: 181 us -> 201 us (1.11); the launches traced: 181 us -> 198 us
  waiting for transfers between devices: 61.1 us -> 81.2 us
    ppermute x38 -> x36, waiting for transfers between devices: 61.1 us -> 81.2 us  [shift(): lax.ppermute(block, axis, [(i, (i + step) % SIDE) for i in range(SIDE)])]
    ppermute x38 -> x36, starting transfers between devices: 68.4 us -> 66.5 us  [shift(): lax.ppermute(block, axis, [(i, (i + step) % SIDE) for i in range(SIDE)])]
  transfers between devices with their start and end apart: 38 -> 36, of which waited for: 13 -> 9; matrix products, arithmetic and copies ran while one was open for 2% -> 1% of each run, Pallas kernels for 22% -> 21%
where the time goes in v7:
time: 201 us; the launch traced here: 198 us
  waiting for transfers between devices  81.2 us (40%)
  starting transfers between devices  66.5 us (33%)
  Pallas kernels  47 us (23%)
    ppermute x36, waiting for transfers between devices, shift(): lax.ppermute(block, axis, [(i, (i + step) % SIDE) for i in range(SIDE)])  81.2 us
    ppermute x36, starting transfers between devices, shift(): lax.ppermute(block, axis, [(i, (i + step) % SIDE) for i in range(SIDE)])  66.5 us
    pallas_call x2, Pallas kernels, hidden_rows(): pl.pallas_call(functools.partial(hidden_kernel, segments), grid=(ff // FF...  20.7 us
    pallas_call x2, Pallas kernels, down_rows(): pl.pallas_call(functools.partial(down_kernel, segments, n_half), grid=(2...  13.1 us
    pallas_call x4, Pallas kernels, pack(): pl.pallas_call(functools.partial(kernel, segments, counts, top), in_specs...  8.46 us
  transfers between devices with their start and end apart: 36, of which 9 were waited for; matrix products, arithmetic and copies ran while one was open for 1% of the time, Pallas kernels for 21%

profile of v7, /device:TPU:0, one launch (start us, length us, event | category | flops | bytes accessed | tf_op | source)
XLA Modules:
  0.0 198.4 jit_solution(6149472767032506557)
XLA Ops:
  1.8 2.9 %collective-permute-start.4 = (bf16[128,2176]{1,0:T(8,128)(2,1)S(1)}, bf16[128,2176]{1,0:T(8,128)(2,1)S(1)}, u32[]{:S(2)}, u32[]{:S(2)}) collective-permute-start(bf16[128,2176]{1,0:T(8,128)(2,1)S(1)} %get-tuple-element.72.refs_0_.refs_20_), channel_id=1, source_target_pairs={{0,3},{1,0},{2,1},{3,2},{4,7},{5,4},{6,5},{7,6},{8,11},{9,8},{10,9... | collective-permute-start | bytes 1671176 | tf_op jit(solution)/shard_map/ppermute | solution.py:24
  4.8 4.0 %collective-permute-start.1 = (bf16[128,2176]{1,0:T(8,128)(2,1)S(1)}, bf16[128,2176]{1,0:T(8,128)(2,1)S(1)}, u32[]{:S(2)}, u32[]{:S(2)}) collective-permute-start(bf16[128,2176]{1,0:T(8,128)(2,1)S(1)} %get-tuple-element.67.refs_0_.refs_15_), channel_id=1, source_target_pairs={{0,12},{4,0},{8,4},{12,8},{1,13},{5,1},{9,5},{13,9},{2,14},{6,2},{... | collective-permute-start | bytes 1671176 | tf_op jit(solution)/shard_map/ppermute | solution.py:24
  8.8 7.8 %collective-permute-done.4.refs_4_.refs_24_ = bf16[128,2176]{1,0:T(8,128)(2,1)S(1)} collective-permute-done((bf16[128,2176]{1,0:T(8,128)(2,1)S(1)}, bf16[128,2176]{1,0:T(8,128)(2,1)S(1)}, u32[]{:S(2)}, u32[]{:S(2)}) %collective-permute-start.4) | collective-permute-done | bytes 557088 | tf_op jit(solution)/shard_map/ppermute | solution.py:24
  17.4 3.7 %collective-permute-start.5 = (bf16[64,2176]{1,0:T(8,128)(2,1)}, bf16[64,2176]{1,0:T(8,128)(2,1)}, u32[]{:S(2)}, u32[]{:S(2)}) collective-permute-start(bf16[64,2176]{1,0:T(8,128)(2,1)} %slice.25), channel_id=1, source_target_pairs={{0,3},{1,0},{2,1},{3,2},{4,7},{5,4},{6,5},{7,6},{8,11},{9,8},{10,9... | collective-permute-start | bytes 835592 | tf_op jit(solution)/shard_map/ppermute | solution.py:24
  21.9 4.1 %collective-permute-start.7 = (bf16[64,2176]{1,0:T(8,128)(2,1)S(1)}, bf16[64,2176]{1,0:T(8,128)(2,1)S(1)}, u32[]{:S(2)}, u32[]{:S(2)}) collective-permute-start(bf16[64,2176]{1,0:T(8,128)(2,1)S(1)} %slice.27), channel_id=1, source_target_pairs={{0,12},{4,0},{8,4},{12,8},{1,13},{5,1},{9,5},{13,9},{2,14},{6,2},{... | collective-permute-start | bytes 835592 | tf_op jit(solution)/shard_map/ppermute | solution.py:24
  27.9 2.6 %collective-permute-done.3.refs_2_.refs_22_ = bf16[64,2176]{1,0:T(8,128)(2,1)} collective-permute-done((bf16[64,2176]{1,0:T(8,128)(2,1)}, bf16[64,2176]{1,0:T(8,128)(2,1)}, u32[]{:S(2)}, u32[]{:S(2)}) %collective-permute-start.3) | collective-permute-done | bytes 278560 | tf_op jit(solution)/shard_map/ppermute | solution.py:24
  30.6 2.5 %shard_map.66 = (bf16[192,2048]{1,0:T(8,128)(2,1)S(1)}, bf16[192,2048]{1,0:T(8,128)(2,1)S(1)}, bf16[192,2048]{1,0:T(8,128)(2,1)S(1)}) custom-call(s32[4]{0:T(128)S(1)} %get-tuple-element.132.experts_ref, bf16[128,2176]{1,0:T(8,128)(2,1)S(1)} %get-tuple-element.72.refs_0_.refs_20_, bf16[128,2176]{1,0:T(8,128)(2,1)S(1)} %collective-permute-done.2.refs_1_.refs_21_, ...), custom_call_target="tpu_custom_call" | custom-call | flops 301989888 | bytes 4456448 | tf_op jit(solution)/shard_map/pallas_call | solution.py:163
  33.1 2.0 %collective-permute-start.11 = (bf16[192,2048]{1,0:T(8,128)(2,1)S(1)}, bf16[192,2048]{1,0:T(8,128)(2,1)S(1)}, u32[]{:S(2)}, u32[]{:S(2)}) collective-permute-start(bf16[192,2048]{1,0:T(8,128)(2,1)S(1)} %get-tuple-element.92), channel_id=1, source_target_pairs={{0,4},{4,8},{8,12},{12,0},{1,5},{5,9},{9,13},{13,1},{2,6},{6,10},{... | collective-permute-start | bytes 2359304 | tf_op jit(solution)/shard_map/ppermute | solution.py:24
  35.1 2.2 %collective-permute-start.12 = (bf16[192,2048]{1,0:T(8,128)(2,1)S(1)}, bf16[192,2048]{1,0:T(8,128)(2,1)S(1)}, u32[]{:S(2)}, u32[]{:S(2)}) collective-permute-start(bf16[192,2048]{1,0:T(8,128)(2,1)S(1)} %get-tuple-element.93), channel_id=1, source_target_pairs={{0,12},{4,0},{8,4},{12,8},{1,13},{5,1},{9,5},{13,9},{2,14},{6,2},{... | collective-permute-start | bytes 2359304 | tf_op jit(solution)/shard_map/ppermute | solution.py:24
  38.5 2.1 %collective-permute-start.10 = (bf16[144,2048]{1,0:T(8,128)(2,1)S(1)}, bf16[144,2048]{1,0:T(8,128)(2,1)S(1)}, u32[]{:S(2)}, u32[]{:S(2)}) collective-permute-start(bf16[144,2048]{1,0:T(8,128)(2,1)S(1)} %get-tuple-element.90), channel_id=1, source_target_pairs={{0,3},{1,0},{2,1},{3,2},{4,7},{5,4},{6,5},{7,6},{8,11},{9,8},{10,9... | collective-permute-start | bytes 1769480 | tf_op jit(solution)/shard_map/ppermute | solution.py:24
  40.6 2.3 %shard_map.68 = (bf16[64,2048]{1,0:T(8,128)(2,1)S(1)}, bf16[64,2048]{1,0:T(8,128)(2,1)S(1)}, bf16[64,2048]{1,0:T(8,128)(2,1)S(1)}, bf16[256,2048]{1,0:T(8,128)(2,1)S(1)}) custom-call(s32[4]{0:T(128)S(1)} %get-tuple-element.129.experts_ref, bf16[128,2176]{1,0:T(8,128)(2,1)S(1)} %get-tuple-element.72.refs_0_.refs_20_, ...), custom_call_target="tpu_custom_call" | custom-call | flops 234881024 | bytes 3932160 | tf_op jit(solution)/shard_map/pallas_call | solution.py:163
  42.9 1.9 shard_map.67
  44.8 20.3 %collective-permute-done.8.refs_1_ = bf16[144,2048]{1,0:T(8,128)(2,1)S(1)} collective-permute-done((bf16[144,2048]{1,0:T(8,128)(2,1)S(1)}, bf16[144,2048]{1,0:T(8,128)(2,1)S(1)}, u32[]{:S(2)}, u32[]{:S(2)}) %collective-permute-start.8) | collective-permute-done | bytes 589856 | tf_op jit(solution)/shard_map/ppermute | solution.py:24
  66.2 2.3 %collective-permute-start.20 = (bf16[112,2048]{1,0:T(8,128)(2,1)S(1)}, bf16[112,2048]{1,0:T(8,128)(2,1)S(1)}, u32[]{:S(2)}, u32[]{:S(2)}) collective-permute-start(bf16[112,2048]{1,0:T(8,128)(2,1)S(1)} %get-tuple-element.104), channel_id=1, source_target_pairs={{0,3},{1,0},{2,1},{3,2},{4,7},{5,4},{6,5},{7,6},{8,11},{9,8},{10,9... | collective-permute-start | bytes 1376264 | tf_op jit(solution)/shard_map/ppermute | solution.py:24
  68.5 3.4 %collective-permute-start.23 = (bf16[256,2048]{1,0:T(8,128)(2,1)S(1)}, bf16[256,2048]{1,0:T(8,128)(2,1)S(1)}, u32[]{:S(2)}, u32[]{:S(2)}) collective-permute-start(bf16[256,2048]{1,0:T(8,128)(2,1)S(1)} %get-tuple-element.108), channel_id=1, source_target_pairs={{0,8},{4,12},{8,0},{12,4},{1,9},{5,13},{9,1},{13,5},{2,10},{6,14},... | collective-permute-start | bytes 3145736 | tf_op jit(solution)/shard_map/ppermute | solution.py:24
  71.9 11.1 %shard_map.69.hidden_ref = bf16[576,768]{1,0:T(8,128)(2,1)S(1)} custom-call(bf16[4096,768]{1,0:T(8,128)(2,1)} %bitcast.7, bf16[4096,768]{1,0:T(8,128)(2,1)} %bitcast.9, bf16[144,2048]{1,0:T(8,128)(2,1)S(1)} %get-tuple-element.87.refs_0_, bf16[144,2048]{1,0:T(8,128)(2,1)S(1)} %collective-permute-done.8.refs_1_, ...), custom_call_target="tpu_custom_call" | custom-call | flops 7247757312 | bytes 17301504 | tf_op jit(solution)/shard_map/pallas_call | solution.py:212
  83.9 6.9 %shard_map.70 = (bf16[144,2048]{1,0:T(8,128)(2,1)S(1)}, bf16[144,2048]{1,0:T(8,128)(2,1)S(1)}, bf16[144,2048]{1,0:T(8,128)(2,1)S(1)}, bf16[144,2048]{1,0:T(8,128...) custom-call(bf16[576,768]{1,0:T(8,128)(2,1)S(1)} %shard_map.69.hidden_ref, ...), custom_call_target="tpu_custom_call" | custom-call | flops 3623878656 | bytes 11010048 | tf_op jit(solution)/shard_map/pallas_call | solution.py:269
  90.8 9.6 %collective-permute-start.16 = (bf16[192,2048]{1,0:T(8,128)(2,1)S(1)}, bf16[192,2048]{1,0:T(8,128)(2,1)S(1)}, u32[]{:S(2)}, u32[]{:S(2)}) collective-permute-start(bf16[192,2048]{1,0:T(8,128)(2,1)S(1)} %get-tuple-element.99), channel_id=1, source_target_pairs={{0,12},{4,0},{8,4},{12,8},{1,13},{5,1},{9,5},{13,9},{2,14},{6,2},{... | collective-permute-start | bytes 2359304 | tf_op jit(solution)/shard_map/ppermute | solution.py:24
  100.5 1.8 collective-permute-done.22.refs_6_
  102.3 2.9 %collective-permute-start.14 = (bf16[144,2048]{1,0:T(8,128)(2,1)S(1)}, bf16[144,2048]{1,0:T(8,128)(2,1)S(1)}, u32[]{:S(2)}, u32[]{:S(2)}) collective-permute-start(bf16[144,2048]{1,0:T(8,128)(2,1)S(1)} %get-tuple-element.97), channel_id=1, source_target_pairs={{0,2},{1,3},{2,0},{3,1},{4,6},{5,7},{6,4},{7,5},{8,10},{9,11},{10,... | collective-permute-start | bytes 1769480 | tf_op jit(solution)/shard_map/ppermute | solution.py:24
  105.2 9.6 %shard_map.71.hidden_ref = bf16[448,768]{1,0:T(8,128)(2,1)S(1)} custom-call(bf16[4096,768]{1,0:T(8,128)(2,1)} %bitcast.8, bf16[4096,768]{1,0:T(8,128)(2,1)} %bitcast.10, bf16[112,2048]{1,0:T(8,128)(2,1)S(1)} %get-tuple-element.101.refs_0_, bf16[112,2048]{1,0:T(8,128)(2,1)S(1)} %collective-permute-done.18.refs_1_, ...), custom_call_target="tpu_custom_call" | custom-call | flops 5637144576 | bytes 16252928 | tf_op jit(solution)/shard_map/pallas_call | solution.py:212
  114.9 6.2 %shard_map.72 = (bf16[112,2048]{1,0:T(8,128)(2,1)S(1)}, bf16[112,2048]{1,0:T(8,128)(2,1)S(1)}, bf16[112,2048]{1,0:T(8,128)(2,1)S(1)}, bf16[112,2048]{1,0:T(8,128...) custom-call(bf16[448,768]{1,0:T(8,128)(2,1)S(1)} %shard_map.71.hidde, ...), custom_call_target="tpu_custom_call" | custom-call | flops 2818572288 | bytes 9961472 | tf_op jit(solution)/shard_map/pallas_call | solution.py:269
  124.5 2.0 %collective-permute-start.24 = (bf16[112,2048]{1,0:T(8,128)(2,1)S(1)}, bf16[112,2048]{1,0:T(8,128)(2,1)S(1)}, u32[]{:S(2)}, u32[]{:S(2)}) collective-permute-start(bf16[112,2048]{1,0:T(8,128)(2,1)S(1)} %get-tuple-element.111), channel_id=1, source_target_pairs={{0,3},{1,0},{2,1},{3,2},{4,7},{5,4},{6,5},{7,6},{8,11},{9,8},{10,9... | collective-permute-start | bytes 1376264 | tf_op jit(solution)/shard_map/ppermute | solution.py:24
  128.2 20.8 %collective-permute-done.27.refs_12_ = bf16[64,2048]{1,0:T(8,128)(2,1)S(1)} collective-permute-done((bf16[64,2048]{1,0:T(8,128)(2,1)S(1)}, bf16[64,2048]{1,0:T(8,128)(2,1)S(1)}, u32[]{:S(2)}, u32[]{:S(2)}) %collective-permute-start.27) | collective-permute-done | bytes 262176 | tf_op jit(solution)/shard_map/ppermute | solution.py:24
  150.6 7.4 %collective-permute-done.28.refs_13_ = bf16[64,2048]{1,0:T(8,128)(2,1)S(1)} collective-permute-done((bf16[64,2048]{1,0:T(8,128)(2,1)S(1)}, bf16[64,2048]{1,0:T(8,128)(2,1)S(1)}, u32[]{:S(2)}, u32[]{:S(2)}) %collective-permute-start.28) | collective-permute-done | bytes 262176 | tf_op jit(solution)/shard_map/ppermute | solution.py:24
  158.0 3.0 %shard_map.73 = (bf16[128,2048]{1,0:T(8,128)(2,1)S(1)}, bf16[128,2048]{1,0:T(8,128)(2,1)S(1)}, bf16[128,2048]{1,0:T(8,128)(2,1)S(1)}, bf16[128,2048]{1,0:T(8,128...) custom-call(s32[8]{0:T(128)S(1)} %pad_add_fusion.experts_ref, ...), custom_call_target="tpu_custom_call" | custom-call | flops 1073741824 | bytes 12582912 | tf_op jit(solution)/shard_map/pallas_call | solution.py:339
  161.1 2.0 %collective-permute-start.30 = (bf16[128,2048]{1,0:T(8,128)(2,1)S(1)}, bf16[128,2048]{1,0:T(8,128)(2,1)S(1)}, u32[]{:S(2)}, u32[]{:S(2)}) collective-permute-start(bf16[128,2048]{1,0:T(8,128)(2,1)S(1)} %get-tuple-element.122), channel_id=1, source_target_pairs={{0,12},{4,0},{8,4},{12,8},{1,13},{5,1},{9,5},{13,9},{2,14},{6,2},{... | collective-permute-start | bytes 1572872 | tf_op jit(solution)/shard_map/ppermute | solution.py:24
  164.0 5.0 %collective-permute-start.33 = (bf16[128,2048]{1,0:T(8,128)(2,1)S(1)}, bf16[128,2048]{1,0:T(8,128)(2,1)S(1)}, u32[]{:S(2)}, u32[]{:S(2)}) collective-permute-start(bf16[128,2048]{1,0:T(8,128)(2,1)S(1)} %get-tuple-element.126), channel_id=1, source_target_pairs={{0,3},{1,0},{2,1},{3,2},{4,7},{5,4},{6,5},{7,6},{8,11},{9,8},{10,9... | collective-permute-start | bytes 1572872 | tf_op jit(solution)/shard_map/ppermute | solution.py:24
  169.0 2.2 %collective-permute-start.34 = (bf16[128,2048]{1,0:T(8,128)(2,1)S(1)}, bf16[128,2048]{1,0:T(8,128)(2,1)S(1)}, u32[]{:S(2)}, u32[]{:S(2)}) collective-permute-start(bf16[128,2048]{1,0:T(8,128)(2,1)S(1)} %get-tuple-element.127), channel_id=1, source_target_pairs={{0,2},{1,3},{2,0},{3,1},{4,6},{5,7},{6,4},{7,5},{8,10},{9,11},{10,... | collective-permute-start | bytes 1572872 | tf_op jit(solution)/shard_map/ppermute | solution.py:24
  171.2 13.6 %collective-permute-done.30 = bf16[128,2048]{1,0:T(8,128)(2,1)S(1)} collective-permute-done((bf16[128,2048]{1,0:T(8,128)(2,1)S(1)}, bf16[128,2048]{1,0:T(8,128)(2,1)S(1)}, u32[]{:S(2)}, u32[]{:S(2)}) %collective-permute-start.30) | collective-permute-done | bytes 524320 | tf_op jit(solution)/shard_map/ppermute | solution.py:24
  184.9 5.1 %collective-permute-start.35 = (bf16[128,2048]{1,0:T(8,128)(2,1)S(1)}, bf16[128,2048]{1,0:T(8,128)(2,1)S(1)}, u32[]{:S(2)}, u32[]{:S(2)}) collective-permute-start(bf16[128,2048]{1,0:T(8,128)(2,1)S(1)} %get-tuple-element.128), channel_id=1, source_target_pairs={{0,1},{1,2},{2,3},{3,0},{4,5},{5,6},{6,7},{7,4},{8,9},{9,10},{10,1... | collective-permute-start | bytes 1572872 | tf_op jit(solution)/shard_map/ppermute | solution.py:24
  190.4 6.7 %collective-permute-done.35 = bf16[128,2048]{1,0:T(8,128)(2,1)S(1)} collective-permute-done((bf16[128,2048]{1,0:T(8,128)(2,1)S(1)}, bf16[128,2048]{1,0:T(8,128)(2,1)S(1)}, u32[]{:S(2)}, u32[]{:S(2)}) %collective-permute-start.35) | collective-permute-done | bytes 524320 | tf_op jit(solution)/shard_map/ppermute | solution.py:24
  (60 shorter events, 18.2 us)
Async XLA Ops:
  1.8 14.8 %collective-permute-start.4 = (bf16[128,2176]{1,0:T(8,128)(2,1)S(1)}, bf16[128,2176]{1,0:T(8,128)(2,1)S(1)}, u32[]{:S(2)}, u32[]{:S(2)}) collective-permute-start(bf16[128,2176]{1,0:T(8,128)(2,1)S(1)} %get-tuple-element.72.refs_0_.refs_20_), channel_id=1, source_target_pairs={{0,3},{1,0},{2,1},{3,2},{4,7},{5,4},{6,5},{7,6},{8,11},{9,8},{10,9... | collective-permute-start | bytes 1671176 | tf_op jit(solution)/shard_map/ppermute | solution.py:24
  4.7 16.3 %collective-permute-start.2 = (bf16[128,2176]{1,0:T(8,128)(2,1)S(1)}, bf16[128,2176]{1,0:T(8,128)(2,1)S(1)}, u32[]{:S(2)}, u32[]{:S(2)}) collective-permute-start(bf16[128,2176]{1,0:T(8,128)(2,1)S(1)} %get-tuple-element.72.refs_0_.refs_20_), channel_id=1, source_target_pairs={{0,1},{1,2},{2,3},{3,0},{4,5},{5,6},{6,7},{7,4},{8,9},{9,10},{10,1... | collective-permute-start | bytes 1671176 | tf_op jit(solution)/shard_map/ppermute | solution.py:24
  4.8 17.1 %collective-permute-start.1 = (bf16[128,2176]{1,0:T(8,128)(2,1)S(1)}, bf16[128,2176]{1,0:T(8,128)(2,1)S(1)}, u32[]{:S(2)}, u32[]{:S(2)}) collective-permute-start(bf16[128,2176]{1,0:T(8,128)(2,1)S(1)} %get-tuple-element.67.refs_0_.refs_15_), channel_id=1, source_target_pairs={{0,12},{4,0},{8,4},{12,8},{1,13},{5,1},{9,5},{13,9},{2,14},{6,2},{... | collective-permute-start | bytes 1671176 | tf_op jit(solution)/shard_map/ppermute | solution.py:24
  8.8 17.2 %collective-permute-start = (bf16[128,2176]{1,0:T(8,128)(2,1)S(1)}, bf16[128,2176]{1,0:T(8,128)(2,1)S(1)}, u32[]{:S(2)}, u32[]{:S(2)}) collective-permute-start(bf16[128,2176]{1,0:T(8,128)(2,1)S(1)} %get-tuple-element.67.refs_0_.refs_15_), channel_id=1, source_target_pairs={{0,4},{4,8},{8,12},{12,0},{1,5},{5,9},{9,13},{13,1},{2,6},{6,10},{... | collective-permute-start | bytes 1671176 | tf_op jit(solution)/shard_map/ppermute | solution.py:24
  21.9 15.4 %collective-permute-start.7 = (bf16[64,2176]{1,0:T(8,128)(2,1)S(1)}, bf16[64,2176]{1,0:T(8,128)(2,1)S(1)}, u32[]{:S(2)}, u32[]{:S(2)}) collective-permute-start(bf16[64,2176]{1,0:T(8,128)(2,1)S(1)} %slice.27), channel_id=1, source_target_pairs={{0,12},{4,0},{8,4},{12,8},{1,13},{5,1},{9,5},{13,9},{2,14},{6,2},{... | collective-permute-start | bytes 835592 | tf_op jit(solution)/shard_map/ppermute | solution.py:24
  26.0 12.5 %collective-permute-start.6 = (bf16[64,2176]{1,0:T(8,128)(2,1)S(1)}, bf16[64,2176]{1,0:T(8,128)(2,1)S(1)}, u32[]{:S(2)}, u32[]{:S(2)}) collective-permute-start(bf16[64,2176]{1,0:T(8,128)(2,1)S(1)} %slice.26), channel_id=1, source_target_pairs={{0,4},{4,8},{8,12},{12,0},{1,5},{5,9},{9,13},{13,1},{2,6},{6,10},{... | collective-permute-start | bytes 835592 | tf_op jit(solution)/shard_map/ppermute | solution.py:24
  33.1 33.1 %collective-permute-start.11 = (bf16[192,2048]{1,0:T(8,128)(2,1)S(1)}, bf16[192,2048]{1,0:T(8,128)(2,1)S(1)}, u32[]{:S(2)}, u32[]{:S(2)}) collective-permute-start(bf16[192,2048]{1,0:T(8,128)(2,1)S(1)} %get-tuple-element.92), channel_id=1, source_target_pairs={{0,4},{4,8},{8,12},{12,0},{1,5},{5,9},{9,13},{13,1},{2,6},{6,10},{... | collective-permute-start | bytes 2359304 | tf_op jit(solution)/shard_map/ppermute | solution.py:24
  35.1 33.4 %collective-permute-start.12 = (bf16[192,2048]{1,0:T(8,128)(2,1)S(1)}, bf16[192,2048]{1,0:T(8,128)(2,1)S(1)}, u32[]{:S(2)}, u32[]{:S(2)}) collective-permute-start(bf16[192,2048]{1,0:T(8,128)(2,1)S(1)} %get-tuple-element.93), channel_id=1, source_target_pairs={{0,12},{4,0},{8,4},{12,8},{1,13},{5,1},{9,5},{13,9},{2,14},{6,2},{... | collective-permute-start | bytes 2359304 | tf_op jit(solution)/shard_map/ppermute | solution.py:24
  37.2 27.9 %collective-permute-start.8 = (bf16[144,2048]{1,0:T(8,128)(2,1)S(1)}, bf16[144,2048]{1,0:T(8,128)(2,1)S(1)}, u32[]{:S(2)}, u32[]{:S(2)}) collective-permute-start(bf16[144,2048]{1,0:T(8,128)(2,1)S(1)} %get-tuple-element.88), channel_id=1, source_target_pairs={{0,1},{1,2},{2,3},{3,0},{4,5},{5,6},{6,7},{7,4},{8,9},{9,10},{10,1... | collective-permute-start | bytes 1769480 | tf_op jit(solution)/shard_map/ppermute | solution.py:24
  37.2 27.9 %collective-permute-start.9 = (bf16[144,2048]{1,0:T(8,128)(2,1)S(1)}, bf16[144,2048]{1,0:T(8,128)(2,1)S(1)}, u32[]{:S(2)}, u32[]{:S(2)}) collective-permute-start(bf16[144,2048]{1,0:T(8,128)(2,1)S(1)} %get-tuple-element.89), channel_id=1, source_target_pairs={{0,2},{1,3},{2,0},{3,1},{4,6},{5,7},{6,4},{7,5},{8,10},{9,11},{10,... | collective-permute-start | bytes 1769480 | tf_op jit(solution)/shard_map/ppermute | solution.py:24
  38.5 26.7 %collective-permute-start.10 = (bf16[144,2048]{1,0:T(8,128)(2,1)S(1)}, bf16[144,2048]{1,0:T(8,128)(2,1)S(1)}, u32[]{:S(2)}, u32[]{:S(2)}) collective-permute-start(bf16[144,2048]{1,0:T(8,128)(2,1)S(1)} %get-tuple-element.90), channel_id=1, source_target_pairs={{0,3},{1,0},{2,1},{3,2},{4,7},{5,4},{6,5},{7,6},{8,11},{9,8},{10,9... | collective-permute-start | bytes 1769480 | tf_op jit(solution)/shard_map/ppermute | solution.py:24
  65.1 17.8 %collective-permute-start.21 = (bf16[64,2048]{1,0:T(8,128)(2,1)S(1)}, bf16[64,2048]{1,0:T(8,128)(2,1)S(1)}, u32[]{:S(2)}, u32[]{:S(2)}) collective-permute-start(bf16[64,2048]{1,0:T(8,128)(2,1)S(1)} %get-tuple-element.106), channel_id=1, source_target_pairs={{0,4},{4,8},{8,12},{12,0},{1,5},{5,9},{9,13},{13,1},{2,6},{6,10},{... | collective-permute-start | bytes 786440 | tf_op jit(solution)/shard_map/ppermute | solution.py:24
  65.2 25.6 %collective-permute-start.18 = (bf16[112,2048]{1,0:T(8,128)(2,1)S(1)}, bf16[112,2048]{1,0:T(8,128)(2,1)S(1)}, u32[]{:S(2)}, u32[]{:S(2)}) collective-permute-start(bf16[112,2048]{1,0:T(8,128)(2,1)S(1)} %get-tuple-element.102), channel_id=1, source_target_pairs={{0,1},{1,2},{2,3},{3,0},{4,5},{5,6},{6,7},{7,4},{8,9},{9,10},{10,1... | collective-permute-start | bytes 1376264 | tf_op jit(solution)/shard_map/ppermute | solution.py:24
  65.2 35.2 %collective-permute-start.19 = (bf16[112,2048]{1,0:T(8,128)(2,1)S(1)}, bf16[112,2048]{1,0:T(8,128)(2,1)S(1)}, u32[]{:S(2)}, u32[]{:S(2)}) collective-permute-start(bf16[112,2048]{1,0:T(8,128)(2,1)S(1)} %get-tuple-element.103), channel_id=1, source_target_pairs={{0,2},{1,3},{2,0},{3,1},{4,6},{5,7},{6,4},{7,5},{8,10},{9,11},{10,... | collective-permute-start | bytes 1376264 | tf_op jit(solution)/shard_map/ppermute | solution.py:24
  66.2 34.2 %collective-permute-start.20 = (bf16[112,2048]{1,0:T(8,128)(2,1)S(1)}, bf16[112,2048]{1,0:T(8,128)(2,1)S(1)}, u32[]{:S(2)}, u32[]{:S(2)}) collective-permute-start(bf16[112,2048]{1,0:T(8,128)(2,1)S(1)} %get-tuple-element.104), channel_id=1, source_target_pairs={{0,3},{1,0},{2,1},{3,2},{4,7},{5,4},{6,5},{7,6},{8,11},{9,8},{10,9... | collective-permute-start | bytes 1376264 | tf_op jit(solution)/shard_map/ppermute | solution.py:24
  68.5 36.7 %collective-permute-start.23 = (bf16[256,2048]{1,0:T(8,128)(2,1)S(1)}, bf16[256,2048]{1,0:T(8,128)(2,1)S(1)}, u32[]{:S(2)}, u32[]{:S(2)}) collective-permute-start(bf16[256,2048]{1,0:T(8,128)(2,1)S(1)} %get-tuple-element.108), channel_id=1, source_target_pairs={{0,8},{4,12},{8,0},{12,4},{1,9},{5,13},{9,1},{13,5},{2,10},{6,14},... | collective-permute-start | bytes 3145736 | tf_op jit(solution)/shard_map/ppermute | solution.py:24
  83.0 19.3 %collective-permute-start.22 = (bf16[64,2048]{1,0:T(8,128)(2,1)S(1)}, bf16[64,2048]{1,0:T(8,128)(2,1)S(1)}, u32[]{:S(2)}, u32[]{:S(2)}) collective-permute-start(bf16[64,2048]{1,0:T(8,128)(2,1)S(1)} %get-tuple-element.107), channel_id=1, source_target_pairs={{0,12},{4,0},{8,4},{12,8},{1,13},{5,1},{9,5},{13,9},{2,14},{6,2},{... | collective-permute-start | bytes 786440 | tf_op jit(solution)/shard_map/ppermute | solution.py:24
  90.8 24.1 %collective-permute-start.16 = (bf16[192,2048]{1,0:T(8,128)(2,1)S(1)}, bf16[192,2048]{1,0:T(8,128)(2,1)S(1)}, u32[]{:S(2)}, u32[]{:S(2)}) collective-permute-start(bf16[192,2048]{1,0:T(8,128)(2,1)S(1)} %get-tuple-element.99), channel_id=1, source_target_pairs={{0,12},{4,0},{8,4},{12,8},{1,13},{5,1},{9,5},{13,9},{2,14},{6,2},{... | collective-permute-start | bytes 2359304 | tf_op jit(solution)/shard_map/ppermute | solution.py:24
  100.4 14.5 %collective-permute-start.17 = (bf16[192,2048]{1,0:T(8,128)(2,1)S(1)}, bf16[192,2048]{1,0:T(8,128)(2,1)S(1)}, u32[]{:S(2)}, u32[]{:S(2)}) collective-permute-start(bf16[192,2048]{1,0:T(8,128)(2,1)S(1)} %get-tuple-element.100), channel_id=1, source_target_pairs={{0,4},{4,8},{8,12},{12,0},{1,5},{5,9},{9,13},{13,1},{2,6},{6,10},{... | collective-permute-start | bytes 2359304 | tf_op jit(solution)/shard_map/ppermute | solution.py:24
  100.4 24.1 %collective-permute-start.13 = (bf16[144,2048]{1,0:T(8,128)(2,1)S(1)}, bf16[144,2048]{1,0:T(8,128)(2,1)S(1)}, u32[]{:S(2)}, u32[]{:S(2)}) collective-permute-start(bf16[144,2048]{1,0:T(8,128)(2,1)S(1)} %get-tuple-element.96), channel_id=1, source_target_pairs={{0,3},{1,0},{2,1},{3,2},{4,7},{5,4},{6,5},{7,6},{8,11},{9,8},{10,9... | collective-permute-start | bytes 1769480 | tf_op jit(solution)/shard_map/ppermute | solution.py:24
  102.3 24.3 %collective-permute-start.14 = (bf16[144,2048]{1,0:T(8,128)(2,1)S(1)}, bf16[144,2048]{1,0:T(8,128)(2,1)S(1)}, u32[]{:S(2)}, u32[]{:S(2)}) collective-permute-start(bf16[144,2048]{1,0:T(8,128)(2,1)S(1)} %get-tuple-element.97), channel_id=1, source_target_pairs={{0,2},{1,3},{2,0},{3,1},{4,6},{5,7},{6,4},{7,5},{8,10},{9,11},{10,... | collective-permute-start | bytes 1769480 | tf_op jit(solution)/shard_map/ppermute | solution.py:24
  105.2 22.1 %collective-permute-start.15 = (bf16[144,2048]{1,0:T(8,128)(2,1)S(1)}, bf16[144,2048]{1,0:T(8,128)(2,1)S(1)}, u32[]{:S(2)}, u32[]{:S(2)}) collective-permute-start(bf16[144,2048]{1,0:T(8,128)(2,1)S(1)} %get-tuple-element.98), channel_id=1, source_target_pairs={{0,1},{1,2},{2,3},{3,0},{4,5},{5,6},{6,7},{7,4},{8,9},{9,10},{10,1... | collective-permute-start | bytes 1769480 | tf_op jit(solution)/shard_map/ppermute | solution.py:24
  121.1 37.0 %collective-permute-start.29 = (bf16[256,2048]{1,0:T(8,128)(2,1)S(1)}, bf16[256,2048]{1,0:T(8,128)(2,1)S(1)}, u32[]{:S(2)}, u32[]{:S(2)}) collective-permute-start(bf16[256,2048]{1,0:T(8,128)(2,1)S(1)} %get-tuple-element.120), channel_id=1, source_target_pairs={{0,8},{4,12},{8,0},{12,4},{1,9},{5,13},{9,1},{13,5},{2,10},{6,14},... | collective-permute-start | bytes 3145736 | tf_op jit(solution)/shard_map/ppermute | solution.py:24
  122.7 26.2 %collective-permute-start.27 = (bf16[64,2048]{1,0:T(8,128)(2,1)S(1)}, bf16[64,2048]{1,0:T(8,128)(2,1)S(1)}, u32[]{:S(2)}, u32[]{:S(2)}) collective-permute-start(bf16[64,2048]{1,0:T(8,128)(2,1)S(1)} %get-tuple-element.118), channel_id=1, source_target_pairs={{0,12},{4,0},{8,4},{12,8},{1,13},{5,1},{9,5},{13,9},{2,14},{6,2},{... | collective-permute-start | bytes 786440 | tf_op jit(solution)/shard_map/ppermute | solution.py:24
  124.5 33.5 %collective-permute-start.24 = (bf16[112,2048]{1,0:T(8,128)(2,1)S(1)}, bf16[112,2048]{1,0:T(8,128)(2,1)S(1)}, u32[]{:S(2)}, u32[]{:S(2)}) collective-permute-start(bf16[112,2048]{1,0:T(8,128)(2,1)S(1)} %get-tuple-element.111), channel_id=1, source_target_pairs={{0,3},{1,0},{2,1},{3,2},{4,7},{5,4},{6,5},{7,6},{8,11},{9,8},{10,9... | collective-permute-start | bytes 1376264 | tf_op jit(solution)/shard_map/ppermute | solution.py:24
  126.6 31.5 %collective-permute-start.25 = (bf16[112,2048]{1,0:T(8,128)(2,1)S(1)}, bf16[112,2048]{1,0:T(8,128)(2,1)S(1)}, u32[]{:S(2)}, u32[]{:S(2)}) collective-permute-start(bf16[112,2048]{1,0:T(8,128)(2,1)S(1)} %get-tuple-element.112), channel_id=1, source_target_pairs={{0,2},{1,3},{2,0},{3,1},{4,6},{5,7},{6,4},{7,5},{8,10},{9,11},{10,... | collective-permute-start | bytes 1376264 | tf_op jit(solution)/shard_map/ppermute | solution.py:24
  127.3 30.8 %collective-permute-start.26 = (bf16[112,2048]{1,0:T(8,128)(2,1)S(1)}, bf16[112,2048]{1,0:T(8,128)(2,1)S(1)}, u32[]{:S(2)}, u32[]{:S(2)}) collective-permute-start(bf16[112,2048]{1,0:T(8,128)(2,1)S(1)} %get-tuple-element.113), channel_id=1, source_target_pairs={{0,1},{1,2},{2,3},{3,0},{4,5},{5,6},{6,7},{7,4},{8,9},{9,10},{10,1... | collective-permute-start | bytes 1376264 | tf_op jit(solution)/shard_map/ppermute | solution.py:24
  161.1 23.8 %collective-permute-start.30 = (bf16[128,2048]{1,0:T(8,128)(2,1)S(1)}, bf16[128,2048]{1,0:T(8,128)(2,1)S(1)}, u32[]{:S(2)}, u32[]{:S(2)}) collective-permute-start(bf16[128,2048]{1,0:T(8,128)(2,1)S(1)} %get-tuple-element.122), channel_id=1, source_target_pairs={{0,12},{4,0},{8,4},{12,8},{1,13},{5,1},{9,5},{13,9},{2,14},{6,2},{... | collective-permute-start | bytes 1572872 | tf_op jit(solution)/shard_map/ppermute | solution.py:24
  163.1 26.9 %collective-permute-start.31 = (bf16[128,2048]{1,0:T(8,128)(2,1)S(1)}, bf16[128,2048]{1,0:T(8,128)(2,1)S(1)}, u32[]{:S(2)}, u32[]{:S(2)}) collective-permute-start(bf16[128,2048]{1,0:T(8,128)(2,1)S(1)} %get-tuple-element.123), channel_id=1, source_target_pairs={{0,8},{4,12},{8,0},{12,4},{1,9},{5,13},{9,1},{13,5},{2,10},{6,14},... | collective-permute-start | bytes 1572872 | tf_op jit(solution)/shard_map/ppermute | solution.py:24
  163.6 26.4 %collective-permute-start.32 = (bf16[128,2048]{1,0:T(8,128)(2,1)S(1)}, bf16[128,2048]{1,0:T(8,128)(2,1)S(1)}, u32[]{:S(2)}, u32[]{:S(2)}) collective-permute-start(bf16[128,2048]{1,0:T(8,128)(2,1)S(1)} %get-tuple-element.124), channel_id=1, source_target_pairs={{0,4},{4,8},{8,12},{12,0},{1,5},{5,9},{9,13},{13,1},{2,6},{6,10},{... | collective-permute-start | bytes 1572872 | tf_op jit(solution)/shard_map/ppermute | solution.py:24
  164.0 26.3 %collective-permute-start.33 = (bf16[128,2048]{1,0:T(8,128)(2,1)S(1)}, bf16[128,2048]{1,0:T(8,128)(2,1)S(1)}, u32[]{:S(2)}, u32[]{:S(2)}) collective-permute-start(bf16[128,2048]{1,0:T(8,128)(2,1)S(1)} %get-tuple-element.126), channel_id=1, source_target_pairs={{0,3},{1,0},{2,1},{3,2},{4,7},{5,4},{6,5},{7,6},{8,11},{9,8},{10,9... | collective-permute-start | bytes 1572872 | tf_op jit(solution)/shard_map/ppermute | solution.py:24
  169.0 21.3 %collective-permute-start.34 = (bf16[128,2048]{1,0:T(8,128)(2,1)S(1)}, bf16[128,2048]{1,0:T(8,128)(2,1)S(1)}, u32[]{:S(2)}, u32[]{:S(2)}) collective-permute-start(bf16[128,2048]{1,0:T(8,128)(2,1)S(1)} %get-tuple-element.127), channel_id=1, source_target_pairs={{0,2},{1,3},{2,0},{3,1},{4,6},{5,7},{6,4},{7,5},{8,10},{9,11},{10,... | collective-permute-start | bytes 1572872 | tf_op jit(solution)/shard_map/ppermute | solution.py:24
  (4 other events, 40.6 us)

commit v8 on v6

--- a/solution.py
+++ b/solution.py
@@ -262,7 +262,10 @@
             total = jnp.dot(
                 weight.astype(jnp.bfloat16), rows, preferred_element_type=jnp.float32
             )
-            outs[source][...] = total.astype(jnp.bfloat16)
+            if first:
+                outs[0][experts_ref[2 * SIDE + source]] = total.astype(jnp.bfloat16)
+            else:
+                outs[source][...] = total.astype(jnp.bfloat16)
 
 
 def sum_rows(top, experts, a_facts, b_facts, a_blocks, b_blocks):
@@ -271,16 +274,18 @@
     facts = [*a_facts, *b_facts]
     last = width // TILE
     whole = pl.BlockSpec(memory_space=pltpu.VMEM)
-    out = jax.ShapeDtypeStruct((tokens, width), jnp.bfloat16)
-    counts = (len(a_blocks), len(b_blocks), len(a_facts), len(b_facts), SIDE, SIDE)
+    out = pltpu.HBM((tokens, width), jnp.bfloat16)
+    counts = (len(a_blocks), len(b_blocks), len(a_facts), len(b_facts), SIDE, 1)
+    line = pltpu.HBM((SIDE, tokens, width), jnp.bfloat16)
     done = pl.pallas_call(
         functools.partial(sum_kernel, top, counts),
         grid=(1,),
         in_specs=[pl.BlockSpec(memory_space=pltpu.SMEM)]
         + [whole] * (len(a_blocks) + len(b_blocks))
         + [pl.BlockSpec((f.shape[0], TILE), lambda i: (0, last)) for f in facts],
-        out_specs=[whole] * (2 * SIDE),
-        out_shape=[out] * (2 * SIDE),
+        out_specs=[pl.BlockSpec(out.shape, lambda i: (0, 0))] * SIDE
+        + [pl.BlockSpec(line.shape, lambda i: (0, 0, 0))],
+        out_shape=[out] * SIDE + [line],
         compiler_params=pltpu.CompilerParams(vmem_limit_bytes=VMEM),
         cost_estimate=pl.CostEstimate(
             flops=4 * SIDE * SIDE * CAP * tokens * width,
@@ -288,7 +293,7 @@
             transcendentals=0,
         ),
     )(experts, *a_blocks, *b_blocks, *facts)
-    return done[:SIDE], done[SIDE:]
+    return done[:SIDE], done[SIDE]
 
 
 def local(tokens, expert_ids, gate_values, gate_weight, up_weight, down_weight):
@@ -324,11 +329,13 @@
     a_back += a_home
     b_back += b_home
 
-    experts = jnp.concatenate([a_experts, b_experts])
+    experts = jnp.concatenate([a_experts, b_experts, (x - steps) % SIDE])
     a_sums, b_sums = sum_rows(top, experts, a_rows, b_rows, a_back, b_back)
-    a_home, b_home = both_ways(a_sums, b_sums, "z", "x", -1)
-    mixed = [sum(part.astype(jnp.float32) for part in home) for home in (a_home, b_home)]
-    return jnp.concatenate(mixed, axis=1).astype(jnp.bfloat16)
+    b_home = lax.all_to_all(b_sums, "x", 0, 0, tiled=True)
+    a_home = [a_sums[0]] + [shift(a_sums[k], "z", -k) for k in range(1, SIDE)]
+    a_mixed = sum(part.astype(jnp.float32) for part in a_home)
+    b_mixed = jnp.sum(b_home.astype(jnp.float32), axis=0)
+    return jnp.concatenate([a_mixed, b_mixed], axis=1).astype(jnp.bfloat16)
 
 
 def solution(mesh):

time: 181 us -> 175 us (0.967)
  starting transfers between devices: 68.4 us -> 60.7 us
  Pallas kernels: 46.2 us -> 48.1 us
    ppermute x38 -> x35, starting transfers between devices: 68.4 us -> 55.6 us  [shift(): lax.ppermute(block, axis, [(i, (i + step) % SIDE) for i in range(SIDE)])]
    all_to_all x0 -> x1, starting transfers between devices: none -> 5.06 us  [local(): b_home = lax.all_to_all(b_sums, 'x', 0, 0, tiled=True)]
    pallas_call x1, Pallas kernels: 2.96 us -> 4.8 us  [sum_rows(): pl.pallas_call(functools.partial(sum_kernel, top, counts), grid=(1,), in_...]
    ppermute x38 -> x35, waiting for transfers between devices: 61.1 us -> 59.7 us  [shift(): lax.ppermute(block, axis, [(i, (i + step) % SIDE) for i in range(SIDE)])]
  transfers between devices with their start and end apart: 38 -> 36, of which waited for: 13 -> 12; matrix products, arithmetic and copies ran while one was open for 2% -> 2% of each run, Pallas kernels for 22% -> 23%
where the time goes in v8:
time: 175 us; the launch traced here: 174 us
  starting transfers between devices  60.7 us (35%)
  waiting for transfers between devices  59.7 us (34%)
  Pallas kernels  48.1 us (27%)
  local copies, waits for them, and re-layouts  2.97 us (2%)
  other arithmetic  1.9 us (1%)
    ppermute x35, waiting for transfers between devices, shift(): lax.ppermute(block, axis, [(i, (i + step) % SIDE) for i in range(SIDE)])  59.7 us
    ppermute x35, starting transfers between devices, shift(): lax.ppermute(block, axis, [(i, (i + step) % SIDE) for i in range(SIDE)])  55.6 us
    pallas_call x2, Pallas kernels, hidden_rows(): pl.pallas_call(hidden_kernel, grid=(ff // FF_TILE,), in_specs=[weight, we...  19.5 us
    pallas_call x2, Pallas kernels, down_rows(): pl.pallas_call(functools.partial(down_kernel, n_half), grid=(2 * n_half,)...  13.1 us
    pallas_call x4, Pallas kernels, pack(): pl.pallas_call(functools.partial(pack_kernel, chunk, top), in_specs=[pl.B...  8.96 us
    all_to_all x1, starting transfers between devices, local(): b_home = lax.all_to_all(b_sums, 'x', 0, 0, tiled=True)  5.06 us
    pallas_call x1, Pallas kernels, sum_rows(): pl.pallas_call(functools.partial(sum_kernel, top, counts), grid=(1,), in_...  4.8 us
  transfers between devices with their start and end apart: 36, of which 12 were waited for; matrix products, arithmetic and copies ran while one was open for 2% of the time, Pallas kernels for 23%

profile of v8, /device:TPU:0, one launch (start us, length us, event | category | flops | bytes accessed | tf_op | source)
XLA Modules:
  0.0 173.6 jit_solution(1096517912070345672)
XLA Ops:
  1.8 2.9 %collective-permute-start.6 = (bf16[128,2176]{1,0:T(8,128)(2,1)S(1)}, bf16[128,2176]{1,0:T(8,128)(2,1)S(1)}, u32[]{:S(2)}, u32[]{:S(2)}) collective-permute-start(bf16[128,2176]{1,0:T(8,128)(2,1)S(1)} %get-tuple-element.73.refs_0_.refs_21_), channel_id=1, source_target_pairs={{0,3},{1,0},{2,1},{3,2},{4,7},{5,4},{6,5},{7,6},{8,11},{9,8},{10,9... | collective-permute-start | bytes 1671176 | tf_op jit(solution)/shard_map/ppermute | solution.py:21
  4.8 4.0 %collective-permute-start.2 = (bf16[128,2176]{1,0:T(8,128)(2,1)S(1)}, bf16[128,2176]{1,0:T(8,128)(2,1)S(1)}, u32[]{:S(2)}, u32[]{:S(2)}) collective-permute-start(bf16[128,2176]{1,0:T(8,128)(2,1)S(1)} %get-tuple-element.68.refs_0_.refs_16_), channel_id=1, source_target_pairs={{0,12},{4,0},{8,4},{12,8},{1,13},{5,1},{9,5},{13,9},{2,14},{6,2},{... | collective-permute-start | bytes 1671176 | tf_op jit(solution)/shard_map/ppermute | solution.py:21
  8.8 7.8 %collective-permute-done.6.refs_4_.refs_25_ = bf16[128,2176]{1,0:T(8,128)(2,1)S(1)} collective-permute-done((bf16[128,2176]{1,0:T(8,128)(2,1)S(1)}, bf16[128,2176]{1,0:T(8,128)(2,1)S(1)}, u32[]{:S(2)}, u32[]{:S(2)}) %collective-permute-start.6) | collective-permute-done | bytes 557088 | tf_op jit(solution)/shard_map/ppermute | solution.py:21
  17.4 3.7 %collective-permute-start.7 = (bf16[64,2176]{1,0:T(8,128)(2,1)}, bf16[64,2176]{1,0:T(8,128)(2,1)}, u32[]{:S(2)}, u32[]{:S(2)}) collective-permute-start(bf16[64,2176]{1,0:T(8,128)(2,1)} %slice.19), channel_id=1, source_target_pairs={{0,3},{1,0},{2,1},{3,2},{4,7},{5,4},{6,5},{7,6},{8,11},{9,8},{10,9... | collective-permute-start | bytes 835592 | tf_op jit(solution)/shard_map/ppermute | solution.py:21
  22.6 4.0 %collective-permute-start.3 = (bf16[64,2176]{1,0:T(8,128)(2,1)}, bf16[64,2176]{1,0:T(8,128)(2,1)}, u32[]{:S(2)}, u32[]{:S(2)}) collective-permute-start(bf16[64,2176]{1,0:T(8,128)(2,1)} %slice.17), channel_id=1, source_target_pairs={{0,12},{4,0},{8,4},{12,8},{1,13},{5,1},{9,5},{13,9},{2,14},{6,2},{... | collective-permute-start | bytes 835592 | tf_op jit(solution)/shard_map/ppermute | solution.py:21
  27.4 3.2 %collective-permute-done.5.refs_2_.refs_23_ = bf16[64,2176]{1,0:T(8,128)(2,1)} collective-permute-done((bf16[64,2176]{1,0:T(8,128)(2,1)}, bf16[64,2176]{1,0:T(8,128)(2,1)}, u32[]{:S(2)}, u32[]{:S(2)}) %collective-permute-start.5) | collective-permute-done | bytes 278560 | tf_op jit(solution)/shard_map/ppermute | solution.py:21
  30.6 2.2 %shard_map.66 = (bf16[4,32,2048]{2,1,0:T(8,128)(2,1)S(1)}, bf16[4,32,2048]{2,1,0:T(8,128)(2,1)S(1)}, bf16[4,32,2048]{2,1,0:T(8,128)(2,1)S(1)}, bf16[4,32,2048]{2,1,0:T(8,128)(2,1)S(1)}) custom-call(s32[4]{0:T(128)S(1)} %get-tuple-element.89.experts_ref, bf16[128,2176]{1,0:T(8,128)(2,1)S(1)} %get-tuple-element.73.refs_0_.refs_21_, ...), custom_call_target="tpu_custom_call" | custom-call | flops 268435456 | bytes 4194304 | tf_op jit(solution)/shard_map/pallas_call | solution.py:137
  32.8 3.0 %collective-permute-done.1.refs_2_.refs_18_ = bf16[64,2176]{1,0:T(8,128)(2,1)} collective-permute-done((bf16[64,2176]{1,0:T(8,128)(2,1)}, bf16[64,2176]{1,0:T(8,128)(2,1)}, u32[]{:S(2)}, u32[]{:S(2)}) %collective-permute-start.1) | collective-permute-done | bytes 278560 | tf_op jit(solution)/shard_map/ppermute | solution.py:21
  35.8 2.2 %shard_map.65 = (bf16[4,32,2048]{2,1,0:T(8,128)(2,1)S(1)}, bf16[4,32,2048]{2,1,0:T(8,128)(2,1)S(1)}, bf16[4,32,2048]{2,1,0:T(8,128)(2,1)S(1)}, bf16[4,32,2048]{2,1,0:T(8,128)(2,1)S(1)}) custom-call(s32[4]{0:T(128)S(1)} %get-tuple-element.88.experts_ref, bf16[128,2176]{1,0:T(8,128)(2,1)S(1)} %get-tuple-element.68.refs_0_.refs_16_, ...), custom_call_target="tpu_custom_call" | custom-call | flops 268435456 | bytes 4194304 | tf_op jit(solution)/shard_map/pallas_call | solution.py:137
  38.2 4.4 %collective-permute-start.9 = (bf16[4,32,2048]{2,1,0:T(8,128)(2,1)S(1)}, bf16[4,32,2048]{2,1,0:T(8,128)(2,1)S(1)}, u32[]{:S(2)}, u32[]{:S(2)}) collective-permute-start(bf16[4,32,2048]{2,1,0:T(8,128)(2,1)S(1)} %get-tuple-element.93), channel_id=1, source_target_pairs={{0,2},{1,3},{2,0},{3,1},{4,6},{5,7},{6,4},{7,5},{8,10},{9,11},{10,... | collective-permute-start | bytes 1572872 | tf_op jit(solution)/shard_map/ppermute | solution.py:21
  43.9 9.7 %collective-permute-done.8.refs_1_ = bf16[4,32,2048]{2,1,0:T(8,128)(2,1)S(1)} collective-permute-done((bf16[4,32,2048]{2,1,0:T(8,128)(2,1)S(1)}, bf16[4,32,2048]{2,1,0:T(8,128)(2,1)S(1)}, u32[]{:S(2)}, u32[]{:S(2)}) %collective-permute-start.8) | collective-permute-done | bytes 524320 | tf_op jit(solution)/shard_map/ppermute | solution.py:21
  53.6 9.4 %collective-permute-start.13 = (bf16[4,32,2048]{2,1,0:T(8,128)(2,1)S(1)}, bf16[4,32,2048]{2,1,0:T(8,128)(2,1)S(1)}, u32[]{:S(2)}, u32[]{:S(2)}) collective-permute-start(bf16[4,32,2048]{2,1,0:T(8,128)(2,1)S(1)} %get-tuple-element.98), channel_id=1, source_target_pairs={{0,12},{4,0},{8,4},{12,8},{1,13},{5,1},{9,5},{13,9},{2,14},{6,2},{... | collective-permute-start | bytes 1572872 | tf_op jit(solution)/shard_map/ppermute | solution.py:21
  63.0 2.2 %shard_map.67 = (bf16[4,32,2048]{2,1,0:T(8,128)(2,1)S(1)}, bf16[4,32,2048]{2,1,0:T(8,128)(2,1)S(1)}, bf16[4,32,2048]{2,1,0:T(8,128)(2,1)S(1)}, bf16[4,32,2048]{2,1,0:T(8,128)(2,1)S(1)}) custom-call(s32[4]{0:T(128)S(1)} %get-tuple-element.88.experts_ref, bf16[128,2176]{1,0:T(8,128)(2,1)S(1)} %get-tuple-element.68.refs_0_.refs_16_, ...), custom_call_target="tpu_custom_call" | custom-call | flops 268435456 | bytes 4194304 | tf_op jit(solution)/shard_map/pallas_call | solution.py:137
  65.3 2.2 %shard_map.68 = (bf16[4,32,2048]{2,1,0:T(8,128)(2,1)S(1)}, bf16[4,32,2048]{2,1,0:T(8,128)(2,1)S(1)}, bf16[4,32,2048]{2,1,0:T(8,128)(2,1)S(1)}, bf16[4,32,2048]{2,1,0:T(8,128)(2,1)S(1)}) custom-call(s32[4]{0:T(128)S(1)} %get-tuple-element.89.experts_ref, bf16[128,2176]{1,0:T(8,128)(2,1)S(1)} %get-tuple-element.73.refs_0_.refs_21_, ...), custom_call_target="tpu_custom_call" | custom-call | flops 268435456 | bytes 4194304 | tf_op jit(solution)/shard_map/pallas_call | solution.py:137
  68.5 2.4 %collective-permute-start.16 = (bf16[4,32,2048]{2,1,0:T(8,128)(2,1)S(1)}, bf16[4,32,2048]{2,1,0:T(8,128)(2,1)S(1)}, u32[]{:S(2)}, u32[]{:S(2)}) collective-permute-start(bf16[4,32,2048]{2,1,0:T(8,128)(2,1)S(1)} %get-tuple-element.104), channel_id=1, source_target_pairs={{0,3},{1,0},{2,1},{3,2},{4,7},{5,4},{6,5},{7,6},{8,11},{9,8},{10,9... | collective-permute-start | bytes 1572872 | tf_op jit(solution)/shard_map/ppermute | solution.py:21
  70.9 3.6 %collective-permute-start.19 = (bf16[4,32,2048]{2,1,0:T(8,128)(2,1)S(1)}, bf16[4,32,2048]{2,1,0:T(8,128)(2,1)S(1)}, u32[]{:S(2)}, u32[]{:S(2)}) collective-permute-start(bf16[4,32,2048]{2,1,0:T(8,128)(2,1)S(1)} %get-tuple-element.108), channel_id=1, source_target_pairs={{0,12},{4,0},{8,4},{12,8},{1,13},{5,1},{9,5},{13,9},{2,14},{6,2},{... | collective-permute-start | bytes 1572872 | tf_op jit(solution)/shard_map/ppermute | solution.py:21
  74.5 9.7 %shard_map.69.hidden_ref = bf16[512,768]{1,0:T(8,128)(2,1)S(1)} custom-call(bf16[4096,768]{1,0:T(8,128)(2,1)} %bitcast.7, bf16[4096,768]{1,0:T(8,128)(2,1)} %bitcast.9, bf16[4,32,2048]{2,1,0:T(8,128)(2,1)S(1)} %get-tuple-element.91.refs_0_, bf16[4,32,2048]{2,1,0:T(8,128)(2,1)S(1)} %collective-permute-done.8.refs_1_, ...), custom_call_target="tpu_custom_call" | custom-call | flops 6442450944 | bytes 16777216 | tf_op jit(solution)/shard_map/pallas_call | solution.py:183
  84.2 2.4 %collective-permute-done.14.refs_1_ = bf16[4,32,2048]{2,1,0:T(8,128)(2,1)S(1)} collective-permute-done((bf16[4,32,2048]{2,1,0:T(8,128)(2,1)S(1)}, bf16[4,32,2048]{2,1,0:T(8,128)(2,1)S(1)}, u32[]{:S(2)}, u32[]{:S(2)}) %collective-permute-start.14) | collective-permute-done | bytes 524320 | tf_op jit(solution)/shard_map/ppermute | solution.py:21
  86.6 6.5 %shard_map.70 = (bf16[4,32,2048]{2,1,0:T(8,128)(2,1)S(1)}, bf16[4,32,2048]{2,1,0:T(8,128)(2,1)S(1)}, bf16[4,32,2048]{2,1,0:T(8,128)(2,1)S(1)}, bf16[4,32,2048]{2...) custom-call(bf16[512,768]{1,0:T(8,128)(2,1)S(1)} %shard_map.69.hidde, ...), custom_call_target="tpu_custom_call" | custom-call | flops 3221225472 | bytes 10485760 | tf_op jit(solution)/shard_map/pallas_call | solution.py:226
  95.3 2.1 %collective-permute-start.26 = (bf16[4,32,2048]{2,1,0:T(8,128)(2,1)S(1)}, bf16[4,32,2048]{2,1,0:T(8,128)(2,1)S(1)}, u32[]{:S(2)}, u32[]{:S(2)}) collective-permute-start(bf16[4,32,2048]{2,1,0:T(8,128)(2,1)S(1)} %get-tuple-element.119), channel_id=1, source_target_pairs={{0,12},{4,0},{8,4},{12,8},{1,13},{5,1},{9,5},{13,9},{2,14},{6,2},{... | collective-permute-start | bytes 1572872 | tf_op jit(solution)/shard_map/ppermute | solution.py:21
  99.0 9.7 %shard_map.71.hidden_ref = bf16[512,768]{1,0:T(8,128)(2,1)S(1)} custom-call(bf16[4096,768]{1,0:T(8,128)(2,1)} %bitcast.8, bf16[4096,768]{1,0:T(8,128)(2,1)} %bitcast.10, bf16[4,32,2048]{2,1,0:T(8,128)(2,1)S(1)} %get-tuple-element.101.refs_0_, bf16[4,32,2048]{2,1,0:T(8,128)(2,1)S(1)} %collective-permute-done.14.refs_1_, ...), custom_call_target="tpu_custom_call" | custom-call | flops 6442450944 | bytes 16777216 | tf_op jit(solution)/shard_map/pallas_call | solution.py:183
  110.1 6.5 %shard_map.72 = (bf16[4,32,2048]{2,1,0:T(8,128)(2,1)S(1)}, bf16[4,32,2048]{2,1,0:T(8,128)(2,1)S(1)}, bf16[4,32,2048]{2,1,0:T(8,128)(2,1)S(1)}, bf16[4,32,2048]{2...) custom-call(bf16[512,768]{1,0:T(8,128)(2,1)S(1)} %shard_map.71.hidde, ...), custom_call_target="tpu_custom_call" | custom-call | flops 3221225472 | bytes 10485760 | tf_op jit(solution)/shard_map/pallas_call | solution.py:226
  116.7 2.7 %collective-permute-start.23 = (bf16[4,32,2048]{2,1,0:T(8,128)(2,1)S(1)}, bf16[4,32,2048]{2,1,0:T(8,128)(2,1)S(1)}, u32[]{:S(2)}, u32[]{:S(2)}) collective-permute-start(bf16[4,32,2048]{2,1,0:T(8,128)(2,1)S(1)} %get-tuple-element.115), channel_id=1, source_target_pairs={{0,3},{1,0},{2,1},{3,2},{4,7},{5,4},{6,5},{7,6},{8,11},{9,8},{10,9... | collective-permute-start | bytes 1572872 | tf_op jit(solution)/shard_map/ppermute | solution.py:21
  124.1 3.4 %collective-permute-start.30 = (bf16[4,32,2048]{2,1,0:T(8,128)(2,1)S(1)}, bf16[4,32,2048]{2,1,0:T(8,128)(2,1)S(1)}, u32[]{:S(2)}, u32[]{:S(2)}) collective-permute-start(bf16[4,32,2048]{2,1,0:T(8,128)(2,1)S(1)} %get-tuple-element.124), channel_id=1, source_target_pairs={{0,8},{4,12},{8,0},{12,4},{1,9},{5,13},{9,1},{13,5},{2,10},{6,14},... | collective-permute-start | bytes 1572872 | tf_op jit(solution)/shard_map/ppermute | solution.py:21
  127.5 6.6 %collective-permute-done.23.refs_5_ = bf16[4,32,2048]{2,1,0:T(8,128)(2,1)S(1)} collective-permute-done((bf16[4,32,2048]{2,1,0:T(8,128)(2,1)S(1)}, bf16[4,32,2048]{2,1,0:T(8,128)(2,1)S(1)}, u32[]{:S(2)}, u32[]{:S(2)}) %collective-permute-start.23) | collective-permute-done | bytes 524320 | tf_op jit(solution)/shard_map/ppermute | solution.py:21
  134.2 4.4 %collective-permute-done.25.refs_7_ = bf16[4,32,2048]{2,1,0:T(8,128)(2,1)S(1)} collective-permute-done((bf16[4,32,2048]{2,1,0:T(8,128)(2,1)S(1)}, bf16[4,32,2048]{2,1,0:T(8,128)(2,1)S(1)}, u32[]{:S(2)}, u32[]{:S(2)}) %collective-permute-start.25) | collective-permute-done | bytes 524320 | tf_op jit(solution)/shard_map/ppermute | solution.py:21
  138.6 5.9 %collective-permute-done.31.refs_15_ = bf16[4,32,2048]{2,1,0:T(8,128)(2,1)S(1)} collective-permute-done((bf16[4,32,2048]{2,1,0:T(8,128)(2,1)S(1)}, bf16[4,32,2048]{2,1,0:T(8,128)(2,1)S(1)}, u32[]{:S(2)}, u32[]{:S(2)}) %collective-permute-start.31) | collective-permute-done | bytes 524320 | tf_op jit(solution)/shard_map/ppermute | solution.py:21
  144.5 4.8 %shard_map.73 = (bf16[128,2048]{1,0:T(8,128)(2,1)}, bf16[128,2048]{1,0:T(8,128)(2,1)}, bf16[128,2048]{1,0:T(8,128)(2,1)}, bf16[128,2048]{1,0:T(8,128)(2,1)}, bf16[4,128,2048]{2,1,0:T(8,128)(2,1)}) custom-call(s32[12]{0:T(128)S(1)} %pad_add_fusion.experts_ref, bf16[4,32,2048]{2,1,0:T(8,128)(2,1)S(1)} %get-tuple-element.100.refs_0_, ...), custom_call_target="tpu_custom_call" | custom-call | flops 1073741824 | bytes 12582912 | tf_op jit(solution)/shard_map/pallas_call | solution.py:280
  149.3 5.1 %all-to-all-start = ((bf16[4,128,2048]{2,1,0:T(8,128)(2,1)}), bf16[4,128,2048]{2,1,0:T(8,128)(2,1)S(1)}, u32[]{:S(2)}, u32[]{:S(2)}) async-start(bf16[4,128,2048]{2,1,0:T(8,128)(2,1)} %get-tuple-element.130), calls=%async_computation | async-start | bytes 4194304 | tf_op jit(solution)/shard_map/all_to_all | solution.py:334
  156.6 7.1 %collective-permute-done.32 = bf16[128,2048]{1,0:T(8,128)(2,1)S(1)} collective-permute-done((bf16[128,2048]{1,0:T(8,128)(2,1)}, bf16[128,2048]{1,0:T(8,128)(2,1)S(1)}, u32[]{:S(2)}, u32[]{:S(2)}) %collective-permute-start.32) | collective-permute-done | bytes 524320 | tf_op jit(solution)/shard_map/ppermute | solution.py:21
  163.8 3.0 %collective-permute-done.33 = bf16[128,2048]{1,0:T(8,128)(2,1)S(1)} collective-permute-done((bf16[128,2048]{1,0:T(8,128)(2,1)}, bf16[128,2048]{1,0:T(8,128)(2,1)S(1)}, u32[]{:S(2)}, u32[]{:S(2)}) %collective-permute-start.33) | collective-permute-done | bytes 524320 | tf_op jit(solution)/shard_map/ppermute | solution.py:21
  166.8 5.0 %collective-permute-done.34 = bf16[128,2048]{1,0:T(8,128)(2,1)S(1)} collective-permute-done((bf16[128,2048]{1,0:T(8,128)(2,1)S(1)}, bf16[128,2048]{1,0:T(8,128)(2,1)S(1)}, u32[]{:S(2)}, u32[]{:S(2)}) %collective-permute-start.34) | collective-permute-done | bytes 524320 | tf_op jit(solution)/shard_map/ppermute | solution.py:21
  (64 shorter events, 21.2 us)
Async XLA Ops:
  1.8 14.8 %collective-permute-start.6 = (bf16[128,2176]{1,0:T(8,128)(2,1)S(1)}, bf16[128,2176]{1,0:T(8,128)(2,1)S(1)}, u32[]{:S(2)}, u32[]{:S(2)}) collective-permute-start(bf16[128,2176]{1,0:T(8,128)(2,1)S(1)} %get-tuple-element.73.refs_0_.refs_21_), channel_id=1, source_target_pairs={{0,3},{1,0},{2,1},{3,2},{4,7},{5,4},{6,5},{7,6},{8,11},{9,8},{10,9... | collective-permute-start | bytes 1671176 | tf_op jit(solution)/shard_map/ppermute | solution.py:21
  4.7 16.3 %collective-permute-start.4 = (bf16[128,2176]{1,0:T(8,128)(2,1)S(1)}, bf16[128,2176]{1,0:T(8,128)(2,1)S(1)}, u32[]{:S(2)}, u32[]{:S(2)}) collective-permute-start(bf16[128,2176]{1,0:T(8,128)(2,1)S(1)} %get-tuple-element.73.refs_0_.refs_21_), channel_id=1, source_target_pairs={{0,1},{1,2},{2,3},{3,0},{4,5},{5,6},{6,7},{7,4},{8,9},{9,10},{10,1... | collective-permute-start | bytes 1671176 | tf_op jit(solution)/shard_map/ppermute | solution.py:21
  4.8 17.1 %collective-permute-start.2 = (bf16[128,2176]{1,0:T(8,128)(2,1)S(1)}, bf16[128,2176]{1,0:T(8,128)(2,1)S(1)}, u32[]{:S(2)}, u32[]{:S(2)}) collective-permute-start(bf16[128,2176]{1,0:T(8,128)(2,1)S(1)} %get-tuple-element.68.refs_0_.refs_16_), channel_id=1, source_target_pairs={{0,12},{4,0},{8,4},{12,8},{1,13},{5,1},{9,5},{13,9},{2,14},{6,2},{... | collective-permute-start | bytes 1671176 | tf_op jit(solution)/shard_map/ppermute | solution.py:21
  8.8 17.8 %collective-permute-start = (bf16[128,2176]{1,0:T(8,128)(2,1)S(1)}, bf16[128,2176]{1,0:T(8,128)(2,1)S(1)}, u32[]{:S(2)}, u32[]{:S(2)}) collective-permute-start(bf16[128,2176]{1,0:T(8,128)(2,1)S(1)} %get-tuple-element.68.refs_0_.refs_16_), channel_id=1, source_target_pairs={{0,4},{4,8},{8,12},{12,0},{1,5},{5,9},{9,13},{13,1},{2,6},{6,10},{... | collective-permute-start | bytes 1671176 | tf_op jit(solution)/shard_map/ppermute | solution.py:21
  22.6 10.3 %collective-permute-start.3 = (bf16[64,2176]{1,0:T(8,128)(2,1)}, bf16[64,2176]{1,0:T(8,128)(2,1)}, u32[]{:S(2)}, u32[]{:S(2)}) collective-permute-start(bf16[64,2176]{1,0:T(8,128)(2,1)} %slice.17), channel_id=1, source_target_pairs={{0,12},{4,0},{8,4},{12,8},{1,13},{5,1},{9,5},{13,9},{2,14},{6,2},{... | collective-permute-start | bytes 835592 | tf_op jit(solution)/shard_map/ppermute | solution.py:21
  38.1 15.5 %collective-permute-start.8 = (bf16[4,32,2048]{2,1,0:T(8,128)(2,1)S(1)}, bf16[4,32,2048]{2,1,0:T(8,128)(2,1)S(1)}, u32[]{:S(2)}, u32[]{:S(2)}) collective-permute-start(bf16[4,32,2048]{2,1,0:T(8,128)(2,1)S(1)} %get-tuple-element.92), channel_id=1, source_target_pairs={{0,1},{1,2},{2,3},{3,0},{4,5},{5,6},{6,7},{7,4},{8,9},{9,10},{10,1... | collective-permute-start | bytes 1572872 | tf_op jit(solution)/shard_map/ppermute | solution.py:21
  38.2 29.3 %collective-permute-start.9 = (bf16[4,32,2048]{2,1,0:T(8,128)(2,1)S(1)}, bf16[4,32,2048]{2,1,0:T(8,128)(2,1)S(1)}, u32[]{:S(2)}, u32[]{:S(2)}) collective-permute-start(bf16[4,32,2048]{2,1,0:T(8,128)(2,1)S(1)} %get-tuple-element.93), channel_id=1, source_target_pairs={{0,2},{1,3},{2,0},{3,1},{4,6},{5,7},{6,4},{7,5},{8,10},{9,11},{10,... | collective-permute-start | bytes 1572872 | tf_op jit(solution)/shard_map/ppermute | solution.py:21
  42.6 25.0 %collective-permute-start.10 = (bf16[4,32,2048]{2,1,0:T(8,128)(2,1)S(1)}, bf16[4,32,2048]{2,1,0:T(8,128)(2,1)S(1)}, u32[]{:S(2)}, u32[]{:S(2)}) collective-permute-start(bf16[4,32,2048]{2,1,0:T(8,128)(2,1)S(1)} %get-tuple-element.94), channel_id=1, source_target_pairs={{0,3},{1,0},{2,1},{3,2},{4,7},{5,4},{6,5},{7,6},{8,11},{9,8},{10,9... | collective-permute-start | bytes 1572872 | tf_op jit(solution)/shard_map/ppermute | solution.py:21
  42.6 25.9 %collective-permute-start.11 = (bf16[4,32,2048]{2,1,0:T(8,128)(2,1)S(1)}, bf16[4,32,2048]{2,1,0:T(8,128)(2,1)S(1)}, u32[]{:S(2)}, u32[]{:S(2)}) collective-permute-start(bf16[4,32,2048]{2,1,0:T(8,128)(2,1)S(1)} %get-tuple-element.96), channel_id=1, source_target_pairs={{0,4},{4,8},{8,12},{12,0},{1,5},{5,9},{9,13},{13,1},{2,6},{6,10},{... | collective-permute-start | bytes 1572872 | tf_op jit(solution)/shard_map/ppermute | solution.py:21
  42.6 28.3 %collective-permute-start.12 = (bf16[4,32,2048]{2,1,0:T(8,128)(2,1)S(1)}, bf16[4,32,2048]{2,1,0:T(8,128)(2,1)S(1)}, u32[]{:S(2)}, u32[]{:S(2)}) collective-permute-start(bf16[4,32,2048]{2,1,0:T(8,128)(2,1)S(1)} %get-tuple-element.97), channel_id=1, source_target_pairs={{0,8},{4,12},{8,0},{12,4},{1,9},{5,13},{9,1},{13,5},{2,10},{6,14},... | collective-permute-start | bytes 1572872 | tf_op jit(solution)/shard_map/ppermute | solution.py:21
  53.6 17.3 %collective-permute-start.13 = (bf16[4,32,2048]{2,1,0:T(8,128)(2,1)S(1)}, bf16[4,32,2048]{2,1,0:T(8,128)(2,1)S(1)}, u32[]{:S(2)}, u32[]{:S(2)}) collective-permute-start(bf16[4,32,2048]{2,1,0:T(8,128)(2,1)S(1)} %get-tuple-element.98), channel_id=1, source_target_pairs={{0,12},{4,0},{8,4},{12,8},{1,13},{5,1},{9,5},{13,9},{2,14},{6,2},{... | collective-permute-start | bytes 1572872 | tf_op jit(solution)/shard_map/ppermute | solution.py:21
  67.5 19.1 %collective-permute-start.14 = (bf16[4,32,2048]{2,1,0:T(8,128)(2,1)S(1)}, bf16[4,32,2048]{2,1,0:T(8,128)(2,1)S(1)}, u32[]{:S(2)}, u32[]{:S(2)}) collective-permute-start(bf16[4,32,2048]{2,1,0:T(8,128)(2,1)S(1)} %get-tuple-element.102), channel_id=1, source_target_pairs={{0,1},{1,2},{2,3},{3,0},{4,5},{5,6},{6,7},{7,4},{8,9},{9,10},{10,1... | collective-permute-start | bytes 1572872 | tf_op jit(solution)/shard_map/ppermute | solution.py:21
  67.6 25.5 %collective-permute-start.15 = (bf16[4,32,2048]{2,1,0:T(8,128)(2,1)S(1)}, bf16[4,32,2048]{2,1,0:T(8,128)(2,1)S(1)}, u32[]{:S(2)}, u32[]{:S(2)}) collective-permute-start(bf16[4,32,2048]{2,1,0:T(8,128)(2,1)S(1)} %get-tuple-element.103), channel_id=1, source_target_pairs={{0,2},{1,3},{2,0},{3,1},{4,6},{5,7},{6,4},{7,5},{8,10},{9,11},{10,... | collective-permute-start | bytes 1572872 | tf_op jit(solution)/shard_map/ppermute | solution.py:21
  68.5 24.8 %collective-permute-start.16 = (bf16[4,32,2048]{2,1,0:T(8,128)(2,1)S(1)}, bf16[4,32,2048]{2,1,0:T(8,128)(2,1)S(1)}, u32[]{:S(2)}, u32[]{:S(2)}) collective-permute-start(bf16[4,32,2048]{2,1,0:T(8,128)(2,1)S(1)} %get-tuple-element.104), channel_id=1, source_target_pairs={{0,3},{1,0},{2,1},{3,2},{4,7},{5,4},{6,5},{7,6},{8,11},{9,8},{10,9... | collective-permute-start | bytes 1572872 | tf_op jit(solution)/shard_map/ppermute | solution.py:21
  70.9 22.7 %collective-permute-start.17 = (bf16[4,32,2048]{2,1,0:T(8,128)(2,1)S(1)}, bf16[4,32,2048]{2,1,0:T(8,128)(2,1)S(1)}, u32[]{:S(2)}, u32[]{:S(2)}) collective-permute-start(bf16[4,32,2048]{2,1,0:T(8,128)(2,1)S(1)} %get-tuple-element.106), channel_id=1, source_target_pairs={{0,4},{4,8},{8,12},{12,0},{1,5},{5,9},{9,13},{13,1},{2,6},{6,10},{... | collective-permute-start | bytes 1572872 | tf_op jit(solution)/shard_map/ppermute | solution.py:21
  70.9 24.4 %collective-permute-start.19 = (bf16[4,32,2048]{2,1,0:T(8,128)(2,1)S(1)}, bf16[4,32,2048]{2,1,0:T(8,128)(2,1)S(1)}, u32[]{:S(2)}, u32[]{:S(2)}) collective-permute-start(bf16[4,32,2048]{2,1,0:T(8,128)(2,1)S(1)} %get-tuple-element.108), channel_id=1, source_target_pairs={{0,12},{4,0},{8,4},{12,8},{1,13},{5,1},{9,5},{13,9},{2,14},{6,2},{... | collective-permute-start | bytes 1572872 | tf_op jit(solution)/shard_map/ppermute | solution.py:21
  86.6 12.4 %collective-permute-start.18 = (bf16[4,32,2048]{2,1,0:T(8,128)(2,1)S(1)}, bf16[4,32,2048]{2,1,0:T(8,128)(2,1)S(1)}, u32[]{:S(2)}, u32[]{:S(2)}) collective-permute-start(bf16[4,32,2048]{2,1,0:T(8,128)(2,1)S(1)} %get-tuple-element.107), channel_id=1, source_target_pairs={{0,8},{4,12},{8,0},{12,4},{1,9},{5,13},{9,1},{13,5},{2,10},{6,14},... | collective-permute-start | bytes 1572872 | tf_op jit(solution)/shard_map/ppermute | solution.py:21
  93.2 15.6 %collective-permute-start.20 = (bf16[4,32,2048]{2,1,0:T(8,128)(2,1)S(1)}, bf16[4,32,2048]{2,1,0:T(8,128)(2,1)S(1)}, u32[]{:S(2)}, u32[]{:S(2)}) collective-permute-start(bf16[4,32,2048]{2,1,0:T(8,128)(2,1)S(1)} %get-tuple-element.109), channel_id=1, source_target_pairs={{0,3},{1,0},{2,1},{3,2},{4,7},{5,4},{6,5},{7,6},{8,11},{9,8},{10,9... | collective-permute-start | bytes 1572872 | tf_op jit(solution)/shard_map/ppermute | solution.py:21
  93.2 23.4 %collective-permute-start.21 = (bf16[4,32,2048]{2,1,0:T(8,128)(2,1)S(1)}, bf16[4,32,2048]{2,1,0:T(8,128)(2,1)S(1)}, u32[]{:S(2)}, u32[]{:S(2)}) collective-permute-start(bf16[4,32,2048]{2,1,0:T(8,128)(2,1)S(1)} %get-tuple-element.111), channel_id=1, source_target_pairs={{0,2},{1,3},{2,0},{3,1},{4,6},{5,7},{6,4},{7,5},{8,10},{9,11},{10,... | collective-permute-start | bytes 1572872 | tf_op jit(solution)/shard_map/ppermute | solution.py:21
  93.6 25.8 %collective-permute-start.22 = (bf16[4,32,2048]{2,1,0:T(8,128)(2,1)S(1)}, bf16[4,32,2048]{2,1,0:T(8,128)(2,1)S(1)}, u32[]{:S(2)}, u32[]{:S(2)}) collective-permute-start(bf16[4,32,2048]{2,1,0:T(8,128)(2,1)S(1)} %get-tuple-element.112), channel_id=1, source_target_pairs={{0,1},{1,2},{2,3},{3,0},{4,5},{5,6},{6,7},{7,4},{8,9},{9,10},{10,1... | collective-permute-start | bytes 1572872 | tf_op jit(solution)/shard_map/ppermute | solution.py:21
  95.3 25.6 %collective-permute-start.26 = (bf16[4,32,2048]{2,1,0:T(8,128)(2,1)S(1)}, bf16[4,32,2048]{2,1,0:T(8,128)(2,1)S(1)}, u32[]{:S(2)}, u32[]{:S(2)}) collective-permute-start(bf16[4,32,2048]{2,1,0:T(8,128)(2,1)S(1)} %get-tuple-element.119), channel_id=1, source_target_pairs={{0,12},{4,0},{8,4},{12,8},{1,13},{5,1},{9,5},{13,9},{2,14},{6,2},{... | collective-permute-start | bytes 1572872 | tf_op jit(solution)/shard_map/ppermute | solution.py:21
  99.0 23.2 %collective-permute-start.27 = (bf16[4,32,2048]{2,1,0:T(8,128)(2,1)S(1)}, bf16[4,32,2048]{2,1,0:T(8,128)(2,1)S(1)}, u32[]{:S(2)}, u32[]{:S(2)}) collective-permute-start(bf16[4,32,2048]{2,1,0:T(8,128)(2,1)S(1)} %get-tuple-element.120), channel_id=1, source_target_pairs={{0,8},{4,12},{8,0},{12,4},{1,9},{5,13},{9,1},{13,5},{2,10},{6,14},... | collective-permute-start | bytes 1572872 | tf_op jit(solution)/shard_map/ppermute | solution.py:21
  108.8 15.4 %collective-permute-start.28 = (bf16[4,32,2048]{2,1,0:T(8,128)(2,1)S(1)}, bf16[4,32,2048]{2,1,0:T(8,128)(2,1)S(1)}, u32[]{:S(2)}, u32[]{:S(2)}) collective-permute-start(bf16[4,32,2048]{2,1,0:T(8,128)(2,1)S(1)} %get-tuple-element.121), channel_id=1, source_target_pairs={{0,4},{4,8},{8,12},{12,0},{1,5},{5,9},{9,13},{13,1},{2,6},{6,10},{... | collective-permute-start | bytes 1572872 | tf_op jit(solution)/shard_map/ppermute | solution.py:21
  116.7 17.4 %collective-permute-start.23 = (bf16[4,32,2048]{2,1,0:T(8,128)(2,1)S(1)}, bf16[4,32,2048]{2,1,0:T(8,128)(2,1)S(1)}, u32[]{:S(2)}, u32[]{:S(2)}) collective-permute-start(bf16[4,32,2048]{2,1,0:T(8,128)(2,1)S(1)} %get-tuple-element.115), channel_id=1, source_target_pairs={{0,3},{1,0},{2,1},{3,2},{4,7},{5,4},{6,5},{7,6},{8,11},{9,8},{10,9... | collective-permute-start | bytes 1572872 | tf_op jit(solution)/shard_map/ppermute | solution.py:21
  119.4 14.7 %collective-permute-start.24 = (bf16[4,32,2048]{2,1,0:T(8,128)(2,1)S(1)}, bf16[4,32,2048]{2,1,0:T(8,128)(2,1)S(1)}, u32[]{:S(2)}, u32[]{:S(2)}) collective-permute-start(bf16[4,32,2048]{2,1,0:T(8,128)(2,1)S(1)} %get-tuple-element.116), channel_id=1, source_target_pairs={{0,2},{1,3},{2,0},{3,1},{4,6},{5,7},{6,4},{7,5},{8,10},{9,11},{10,... | collective-permute-start | bytes 1572872 | tf_op jit(solution)/shard_map/ppermute | solution.py:21
  120.9 17.6 %collective-permute-start.25 = (bf16[4,32,2048]{2,1,0:T(8,128)(2,1)S(1)}, bf16[4,32,2048]{2,1,0:T(8,128)(2,1)S(1)}, u32[]{:S(2)}, u32[]{:S(2)}) collective-permute-start(bf16[4,32,2048]{2,1,0:T(8,128)(2,1)S(1)} %get-tuple-element.117), channel_id=1, source_target_pairs={{0,1},{1,2},{2,3},{3,0},{4,5},{5,6},{6,7},{7,4},{8,9},{9,10},{10,1... | collective-permute-start | bytes 1572872 | tf_op jit(solution)/shard_map/ppermute | solution.py:21
  122.2 16.3 %collective-permute-start.29 = (bf16[4,32,2048]{2,1,0:T(8,128)(2,1)S(1)}, bf16[4,32,2048]{2,1,0:T(8,128)(2,1)S(1)}, u32[]{:S(2)}, u32[]{:S(2)}) collective-permute-start(bf16[4,32,2048]{2,1,0:T(8,128)(2,1)S(1)} %get-tuple-element.123), channel_id=1, source_target_pairs={{0,12},{4,0},{8,4},{12,8},{1,13},{5,1},{9,5},{13,9},{2,14},{6,2},{... | collective-permute-start | bytes 1572872 | tf_op jit(solution)/shard_map/ppermute | solution.py:21
  124.1 14.4 %collective-permute-start.30 = (bf16[4,32,2048]{2,1,0:T(8,128)(2,1)S(1)}, bf16[4,32,2048]{2,1,0:T(8,128)(2,1)S(1)}, u32[]{:S(2)}, u32[]{:S(2)}) collective-permute-start(bf16[4,32,2048]{2,1,0:T(8,128)(2,1)S(1)} %get-tuple-element.124), channel_id=1, source_target_pairs={{0,8},{4,12},{8,0},{12,4},{1,9},{5,13},{9,1},{13,5},{2,10},{6,14},... | collective-permute-start | bytes 1572872 | tf_op jit(solution)/shard_map/ppermute | solution.py:21
  134.1 10.4 %collective-permute-start.31 = (bf16[4,32,2048]{2,1,0:T(8,128)(2,1)S(1)}, bf16[4,32,2048]{2,1,0:T(8,128)(2,1)S(1)}, u32[]{:S(2)}, u32[]{:S(2)}) collective-permute-start(bf16[4,32,2048]{2,1,0:T(8,128)(2,1)S(1)} %get-tuple-element.125), channel_id=1, source_target_pairs={{0,4},{4,8},{8,12},{12,0},{1,5},{5,9},{9,13},{13,1},{2,6},{6,10},{... | collective-permute-start | bytes 1572872 | tf_op jit(solution)/shard_map/ppermute | solution.py:21
  149.3 22.9 %all-to-all-start = ((bf16[4,128,2048]{2,1,0:T(8,128)(2,1)}), bf16[4,128,2048]{2,1,0:T(8,128)(2,1)S(1)}, u32[]{:S(2)}, u32[]{:S(2)}) async-start(bf16[4,128,2048]{2,1,0:T(8,128)(2,1)} %get-tuple-element.130), calls=%async_computation | async-start | bytes 4194304 | tf_op jit(solution)/shard_map/all_to_all | solution.py:334
  155.8 11.0 %collective-permute-start.33 = (bf16[128,2048]{1,0:T(8,128)(2,1)}, bf16[128,2048]{1,0:T(8,128)(2,1)S(1)}, u32[]{:S(2)}, u32[]{:S(2)}) collective-permute-start(bf16[128,2048]{1,0:T(8,128)(2,1)} %get-tuple-element.128), channel_id=1, source_target_pairs={{0,8},{4,12},{8,0},{12,4},{1,9},{5,13},{9,1},{13,5},{2,10},{6,14},... | collective-permute-start | bytes 1572872 | tf_op jit(solution)/shard_map/ppermute | solution.py:21
  155.8 16.0 %collective-permute-start.34 = (bf16[128,2048]{1,0:T(8,128)(2,1)S(1)}, bf16[128,2048]{1,0:T(8,128)(2,1)S(1)}, u32[]{:S(2)}, u32[]{:S(2)}) collective-permute-start(bf16[128,2048]{1,0:T(8,128)(2,1)S(1)} %copy-done.1), channel_id=1, source_target_pairs={{0,4},{4,8},{8,12},{12,0},{1,5},{5,9},{9,13},{13,1},{2,6},{6,10},{... | collective-permute-start | bytes 1572872 | tf_op jit(solution)/shard_map/ppermute | solution.py:21
  (6 other events, 65.8 us)

commit v9 on v7

v9 whole, which is shorter than its diff:
```python
import functools

import jax
import jax.numpy as jnp
from jax import lax
from jax.experimental import pallas as pl
from jax.experimental.pallas import tpu as pltpu
from jax.sharding import Mesh, PartitionSpec as P

SIDE = 4
CAP = 64
NEAR = tuple((i, k) for i in range(SIDE) for k in range(SIDE) if 2 not in (i, k))
FAR = tuple((i, k) for i in range(SIDE) for k in range(SIDE) if 2 in (i, k))
PLAN = (NEAR, FAR)
TILE = 128
FF_TILE = 256
D_TILE = 1024
VMEM = 36 * 1024 * 1024


def shift(block, axis, step):
    return lax.ppermute(block, axis, [(i, (i + step) % SIDE) for i in range(SIDE)])


def gather_line(half, axis):
    rows = half.shape[0] // 2
    ahead, behind = shift(half, axis, 1), shift(half, axis, -1)
    low = shift(ahead[:rows], axis, 1)
    high = shift(behind[rows:], axis, -1)
    return [(half,), (ahead,), (low, high), (behind,)]


def load(refs, column=slice(None)):
    parts = [ref[:, column] for ref in refs]
    return parts[0] if len(parts) == 1 else jnp.concatenate(parts, axis=0)


def regroup(refs, counts):
    groups = []
    for count in counts:
        groups.append(refs[:count])
        refs = refs[count:]
    return groups


def line_blocks(blocks, axis):
    lines = {}
    for number, block in enumerate(blocks):
        lines.setdefault(block[axis], []).append(number)
    return dict(sorted(lines.items()))


def in_hbm(*arrays):
    return [pltpu.with_memory_space_constraint(array, pltpu.HBM) for array in arrays]


def prepare_kernel(token_ref, id_ref, gate_ref, a_ref, b_ref):
    tokens, depth = token_ref.shape
    half = depth // 2
    top = id_ref.shape[0]
    given = jnp.concatenate([id_ref[...].astype(jnp.float32), gate_ref[...]], axis=0).T
    lane = lax.broadcasted_iota(jnp.int32, (tokens, TILE), 1)
    number = lane.astype(jnp.float32)
    row = lax.broadcasted_iota(jnp.int32, (tokens, tokens), 0)
    column = lax.broadcasted_iota(jnp.int32, (tokens, tokens), 1)
    ids = [given[:, k : k + 1] for k in range(top)]
    named = jnp.zeros((tokens, TILE), jnp.float32)
    for k in range(top):
        named = jnp.where(ids[k] == number, 1.0, named)
    before = jnp.where(column < row, 1.0, 0.0).astype(jnp.bfloat16)
    rank = jnp.dot(before, named.astype(jnp.bfloat16), preferred_element_type=jnp.float32)
    facts = jnp.zeros((tokens, TILE), jnp.float32)
    for k in range(top):
        place = jnp.sum(jnp.where(ids[k] == number, rank, 0.0), axis=1, keepdims=True)
        facts = jnp.where(lane == k, ids[k], facts)
        facts = jnp.where(lane == top + k, place, facts)
        facts = jnp.where(lane == 2 * top + k, given[:, top + k : top + k + 1], facts)
    facts = facts.astype(jnp.bfloat16)
    a_ref[:, :half] = token_ref[:, :half]
    b_ref[:, :half] = token_ref[:, half:]
    a_ref[:, half:] = facts
    b_ref[:, half:] = facts


def prepare(tokens, expert_ids, gate_values):
    rows, depth = tokens.shape
    out = jax.ShapeDtypeStruct((rows, depth // 2 + TILE), jnp.bfloat16)
    top = expert_ids.shape[1]
    return pl.pallas_call(
        prepare_kernel,
        grid=(1,),
        in_specs=[
            pl.BlockSpec((rows, depth), lambda i: (0, 0)),
            pl.BlockSpec((top, rows), lambda i: (0, 0)),
            pl.BlockSpec((top, rows), lambda i: (0, 0)),
        ],
        out_specs=[pl.BlockSpec(out.shape, lambda i: (0, 0))] * 2,
        out_shape=[out, out],
        compiler_params=pltpu.CompilerParams(vmem_limit_bytes=VMEM),
        cost_estimate=pl.CostEstimate(
            flops=2 * rows * rows * TILE, bytes_accessed=4 * rows * depth, transcendentals=0
        ),
    )(*in_hbm(tokens, expert_ids.T, gate_values.T))


def codes(facts, top):
    facts = facts.astype(jnp.float32)
    return [facts[:, k : k + 1] * CAP + facts[:, top + k : top + k + 1] for k in range(top)]


def targets(experts_ref, places, tokens):
    count = len(places) * CAP
    lane = lax.broadcasted_iota(jnp.int32, (tokens, count), 1)
    code = jnp.zeros((tokens, count), jnp.int32)
    for i, place in enumerate(places):
        low = i * CAP
        value = experts_ref[place] * CAP + lane - low
        code = jnp.where((lane >= low) & (lane < low + CAP), value, code)
    return code.astype(jnp.float32)


def pick_rows(experts_ref, places, top, refs, width):
    tokens = sum(ref.shape[0] for ref in refs)
    target = targets(experts_ref, places, tokens)
    pick = jnp.zeros(target.shape, jnp.float32)
    for code in codes(load(refs, slice(width, width + TILE)), top):
        pick = jnp.where(code == target, 1.0, pick)
    rows = jnp.dot(
        pick.T.astype(jnp.bfloat16),
        load(refs, slice(0, width)),
        preferred_element_type=jnp.float32,
    )
    return rows.astype(jnp.bfloat16)


def pack_kernel(blocks, axis, counts, top, experts_ref, *refs):
    sources, targets_to = line_blocks(blocks, axis), line_blocks(blocks, 1 - axis)
    *lines, outs = regroup(refs, counts + (len(targets_to),))
    outs = dict(zip(targets_to, outs))
    width = next(iter(outs.values())).shape[-1]
    for refs, numbers in zip(lines, sources.values()):
        to = [blocks[number][1 - axis] for number in numbers]
        places = [axis * SIDE + distance for distance in to]
        picked = pick_rows(experts_ref, places, top, refs, width)
        for i, (distance, number) in enumerate(zip(to, numbers)):
            low = targets_to[distance].index(number) * CAP
            outs[distance][low : low + CAP] = picked[i * CAP : (i + 1) * CAP]


def pack(blocks, axis, top, experts, lines):
    sources, targets_to = line_blocks(blocks, axis), line_blocks(blocks, 1 - axis)
    lines = [lines[distance] for distance in sources]
    tokens, width = lines[0][0].shape
    width -= TILE
    counts = tuple(len(line) for line in lines)
    arrays = [array for line in lines for array in line]
    sizes = [len(numbers) * CAP for numbers in targets_to.values()]
    done = pl.pallas_call(
        functools.partial(pack_kernel, blocks, axis, counts, top),
        in_specs=[pl.BlockSpec(memory_space=pltpu.SMEM)]
        + [pl.BlockSpec(memory_space=pltpu.VMEM)] * len(arrays),
        out_specs=[pl.BlockSpec(memory_space=pltpu.VMEM)] * len(sizes),
        out_shape=[jax.ShapeDtypeStruct((rows, width), jnp.bfloat16) for rows in sizes],
        compiler_params=pltpu.CompilerParams(vmem_limit_bytes=VMEM),
        cost_estimate=pl.CostEstimate(
            flops=2 * sum(sizes) * tokens * width,
            bytes_accessed=2 * width * (tokens * len(lines) + sum(sizes)),
            transcendentals=0,
        ),
    )(experts, *arrays)
    return dict(zip(targets_to, done))


def hidden_kernel(blocks, wg_ref, wu_ref, *refs):
    by_z, by_x = line_blocks(blocks, 0), line_blocks(blocks, 1)
    a_in, b_in, (hidden_ref, x_ref, sems) = regroup(refs, (len(by_x), len(by_z), 3))
    half = x_ref.shape[-1] // 2

    @pl.when(pl.program_id(0) == 0)
    def _():
        copies = []

        def move(source, target):
            copies.append(pltpu.make_async_copy(source, target, sems.at[len(copies)]))

        for ref, numbers in zip(b_in, by_z.values()):
            low = numbers[0] * CAP
            move(ref, x_ref.at[low : low + len(numbers) * CAP, half:])
        for ref, numbers in zip(a_in, by_x.values()):
            for i, number in enumerate(numbers):
                low = number * CAP
                move(ref.at[i * CAP : (i + 1) * CAP], x_ref.at[low : low + CAP, :half])
        for copy in copies:
            copy.start()
        for copy in copies:
            copy.wait()

    x = x_ref[...]
    gate = jnp.dot(x, wg_ref[...], preferred_element_type=jnp.float32)
    up = jnp.dot(x, wu_ref[...], preferred_element_type=jnp.float32)
    hidden_ref[...] = (gate / (1.0 + jnp.exp(-gate)) * up).astype(jnp.bfloat16)


def hidden_rows(blocks, w_gate, w_up, a_in, b_in):
    depth, ff = w_gate.shape
    count = len(blocks) * CAP
    weight = pl.BlockSpec((depth, FF_TILE), lambda i: (0, i))
    return pl.pallas_call(
        functools.partial(hidden_kernel, blocks),
        grid=(ff // FF_TILE,),
        in_specs=[weight, weight]
        + [pl.BlockSpec(memory_space=pl.ANY)] * (len(a_in) + len(b_in)),
        out_specs=pl.BlockSpec((count, FF_TILE), lambda i: (0, i)),
        out_shape=jax.ShapeDtypeStruct((count, ff), jnp.bfloat16),
        scratch_shapes=[
            pltpu.VMEM((count, depth), jnp.bfloat16),
            pltpu.SemaphoreType.DMA((len(b_in) + len(blocks),)),
        ],
        compiler_params=pltpu.CompilerParams(vmem_limit_bytes=VMEM),
        cost_estimate=pl.CostEstimate(
            flops=4 * count * depth * ff,
            bytes_accessed=4 * depth * ff + 2 * count * depth,
            transcendentals=count * ff,
        ),
    )(w_gate, w_up, *a_in.values(), *b_in.values())


def down_kernel(blocks, n_half, hidden_ref, wd_ref, *refs):
    by_z, by_x = line_blocks(blocks, 0), line_blocks(blocks, 1)
    a_out, b_out = regroup(refs, (len(by_x), len(by_z)))
    out = jnp.dot(hidden_ref[...], wd_ref[...], preferred_element_type=jnp.float32)
    out = out.astype(jnp.bfloat16)

    def hand(outs, lines):
        for ref, numbers in zip(outs, lines.values()):
            for i, number in enumerate(numbers):
                ref[i * CAP : (i + 1) * CAP] = out[number * CAP : (number + 1) * CAP]

    @pl.when(pl.program_id(0) < n_half)
    def _():
        hand(a_out, by_x)

    @pl.when(pl.program_id(0) >= n_half)
    def _():
        hand(b_out, by_z)


def down_rows(blocks, hidden, w_down):
    by_z, by_x = line_blocks(blocks, 0), line_blocks(blocks, 1)
    count, ff = hidden.shape
    half = w_down.shape[1] // 2
    tile = min(D_TILE, half)
    n_half = half // tile
    a_sizes = [len(numbers) * CAP for numbers in by_x.values()]
    b_sizes = [len(numbers) * CAP for numbers in by_z.values()]
    a_specs = [
        pl.BlockSpec((rows, tile), lambda i: (0, jnp.minimum(i, n_half - 1)))
        for rows in a_sizes
    ]
    b_specs = [
        pl.BlockSpec((rows, tile), lambda i: (0, jnp.maximum(i - n_half, 0)))
        for rows in b_sizes
    ]
    done = pl.pallas_call(
        functools.partial(down_kernel, blocks, n_half),
        grid=(2 * n_half,),
        in_specs=[
            pl.BlockSpec((count, ff), lambda i: (0, 0)),
            pl.BlockSpec((ff, tile), lambda i: (0, i)),
        ],
        out_specs=a_specs + b_specs,
        out_shape=[
            jax.ShapeDtypeStruct((rows, half), jnp.bfloat16) for rows in a_sizes + b_sizes
        ],
        compiler_params=pltpu.CompilerParams(vmem_limit_bytes=VMEM),
        cost_estimate=pl.CostEstimate(
            flops=4 * count * half * ff,
            bytes_accessed=4 * half * ff + 4 * count * half,
            transcendentals=0,
        ),
    )(hidden, w_down)
    return dict(zip(by_x, done[: len(by_x)])), dict(zip(by_z, done[len(by_x) :]))


def sum_kernel(top, counts, experts_ref, *refs):
    *groups, a_out, b_out = regroup(refs, counts)
    facts = groups[-2 * SIDE :]
    tokens = a_out[0].shape[0]

    def total(axis, source):
        about = load(facts[axis * SIDE + source]).astype(jnp.float32)
        places = [axis * SIDE + distance for distance in range(SIDE)]
        target = targets(experts_ref, places, tokens)
        weight = jnp.zeros(target.shape, jnp.float32)
        for k, code in enumerate(codes(about, top)):
            gate = about[:, 2 * top + k : 2 * top + k + 1]
            weight = jnp.where(code == target, gate, weight)
        rows = []
        for distance in range(SIDE):
            block = (source, distance) if axis == 0 else (distance, source)
            chunk = next(c for c, blocks in enumerate(PLAN) if block in blocks)
            lines = line_blocks(PLAN[chunk], 1 - axis)
            low = lines[distance].index(PLAN[chunk].index(block)) * CAP
            ref = groups[axis * len(PLAN) + chunk][list(lines).index(distance)]
            rows.append(ref[low : low + CAP])
        mixed = jnp.dot(
            weight.astype(jnp.bfloat16),
            jnp.concatenate(rows, axis=0),
            preferred_element_type=jnp.float32,
        )
        return mixed.astype(jnp.bfloat16)

    for source in range(SIDE):
        b_out[0][experts_ref[2 * SIDE + source]] = total(1, source)
    for source in range(SIDE):
        a_out[source][...] = total(0, source)


def sum_rows(top, experts, a_rows, b_rows, a_back, b_back):
    width = a_back[0][0].shape[-1]
    tokens = a_rows[0][0].shape[0]
    lines = [*a_rows, *b_rows]
    facts = [array for line in lines for array in line]
    last = width // TILE
    whole = pl.BlockSpec(memory_space=pltpu.VMEM)
    groups = [tuple(chunk.values()) for chunk in a_back + b_back]
    arrays = [array for group in groups for array in group]
    counts = tuple(len(group) for group in groups + lines) + (SIDE, 1)
    out = pltpu.HBM((tokens, width), jnp.bfloat16)
    line = pltpu.HBM((SIDE, tokens, width), jnp.bfloat16)
    done = pl.pallas_call(
        functools.partial(sum_kernel, top, counts),
        grid=(1,),
        in_specs=[pl.BlockSpec(memory_space=pltpu.SMEM)]
        + [whole] * len(arrays)
        + [pl.BlockSpec((f.shape[0], TILE), lambda i: (0, last)) for f in facts],
        out_specs=[pl.BlockSpec(out.shape, lambda i: (0, 0))] * SIDE
        + [pl.BlockSpec(line.shape, lambda i: (0, 0, 0))],
        out_shape=[out] * SIDE + [line],
        compiler_params=pltpu.CompilerParams(vmem_limit_bytes=VMEM),
        cost_estimate=pl.CostEstimate(
            flops=4 * SIDE * SIDE * CAP * tokens * width,
            bytes_accessed=4 * SIDE * width * (tokens + SIDE * CAP),
            transcendentals=0,
        ),
    )(experts, *arrays, *facts)
    return done[:SIDE], done[SIDE]


def send(blocks, axis, sign):
    return {
        distance: shift(block, axis, sign * distance) if distance else block
        for distance, block in blocks.items()
    }


def local(tokens, expert_ids, gate_values, gate_weight, up_weight, down_weight):
    top = expert_ids.shape[1]
    z, x = lax.axis_index("z"), lax.axis_index("x")
    steps = jnp.arange(SIDE, dtype=jnp.int32)
    experts = jnp.concatenate(
        [z * SIDE + (x + steps) % SIDE, (z + steps) % SIDE * SIDE + x, (x - steps) % SIDE]
    )

    a_half, b_half = prepare(tokens, expert_ids, gate_values)
    b_rows = gather_line(b_half, "x")
    a_rows = gather_line(a_half, "z")

    w_gate, w_up, w_down = in_hbm(gate_weight[0], up_weight[0], down_weight[0])
    packed = []
    for blocks in PLAN:
        a_out = pack(blocks, 0, top, experts, a_rows)
        b_out = pack(blocks, 1, top, experts, b_rows)
        experts, a_out, b_out = lax.optimization_barrier((experts, a_out, b_out))
        packed.append((a_out, b_out))

    (a_out, b_out), (a_late, b_late) = packed
    hidden = hidden_rows(NEAR, w_gate, w_up, send(a_out, "x", 1), send(b_out, "z", 1))
    b_late[3], hidden = lax.optimization_barrier((b_late[3], hidden))
    a_done, b_done = down_rows(NEAR, hidden, w_down)
    a_back, b_back = [send(a_done, "x", -1)], [send(b_done, "z", -1)]
    hidden = hidden_rows(FAR, w_gate, w_up, send(a_late, "x", 1), send(b_late, "z", 1))
    a_done, b_done = down_rows(FAR, hidden, w_down)
    a_back.append(send(a_done, "x", -1))
    b_back.append(send(b_done, "z", -1))

    a_sums, b_sums = sum_rows(top, experts, a_rows, b_rows, a_back, b_back)
    b_home = lax.all_to_all(b_sums, "x", 0, 0, tiled=True)
    a_home = [a_sums[0]] + [shift(a_sums[k], "z", -k) for k in range(1, SIDE)]
    a_mixed = sum(part.astype(jnp.float32) for part in a_home)
    b_mixed = jnp.sum(b_home.astype(jnp.float32), axis=0)
    return jnp.concatenate([a_mixed, b_mixed], axis=1).astype(jnp.bfloat16)


def solution(mesh):
    dp = mesh.devices.shape[0]
    grid = Mesh(mesh.devices.reshape(dp, SIDE, SIDE), ("dp", "z", "x"))
    rows, experts = ("dp", "z", "x"), ("z", "x")
    in_specs = (
        P(rows, None),
        P(rows, None),
        P(rows, None),
        P(experts, None, None),
        P(experts, None, None),
        P(experts, None, None),
    )
    return jax.shard_map(
        local, mesh=grid, in_specs=in_specs, out_specs=P(rows, None), check_vma=False
    )
```

time: 201 us -> 194 us (0.965)
  starting transfers between devices: 66.5 us -> 45 us
  waiting for transfers between devices: 81.2 us -> 99.9 us
    ppermute x36 -> x31, starting transfers between devices: 66.5 us -> 39.9 us  [shift(): lax.ppermute(block, axis, [(i, (i + step) % SIDE) for i in range(SIDE)])]
    ppermute x36 -> x31, waiting for transfers between devices: 81.2 us -> 99.9 us  [shift(): lax.ppermute(block, axis, [(i, (i + step) % SIDE) for i in range(SIDE)])]
    all_to_all x0 -> x1, starting transfers between devices: none -> 5.09 us  [local(): b_home = lax.all_to_all(b_sums, 'x', 0, 0, tiled=True)]
    pallas_call x8, Pallas kernels: 42.2 us -> 39.8 us  [the longest x2 19.7 us: hidden_rows(): pl.pallas_call(functools.partial(hidden_kernel, blocks), grid=(ff // FF_T...]
  transfers between devices with their start and end apart: 36 -> 32, of which waited for: 9 -> 9; matrix products, arithmetic and copies ran while one was open for 1% -> 0% of each run, Pallas kernels for 21% -> 21%
where the time goes in v9:
time: 194 us; the launch traced here: 193 us
  waiting for transfers between devices  99.9 us (51%)
  Pallas kernels  46.2 us (24%)
  starting transfers between devices  45 us (23%)
    ppermute x31, waiting for transfers between devices, shift(): lax.ppermute(block, axis, [(i, (i + step) % SIDE) for i in range(SIDE)])  99.9 us
    ppermute x31, starting transfers between devices, shift(): lax.ppermute(block, axis, [(i, (i + step) % SIDE) for i in range(SIDE)])  39.9 us
    pallas_call x2, Pallas kernels, hidden_rows(): pl.pallas_call(functools.partial(hidden_kernel, blocks), grid=(ff // FF_T...  19.7 us
    pallas_call x2, Pallas kernels, down_rows(): pl.pallas_call(functools.partial(down_kernel, blocks, n_half), grid=(2 *...  13.1 us
    pallas_call x4, Pallas kernels, pack(): pl.pallas_call(functools.partial(pack_kernel, blocks, axis, counts, top),...  6.95 us
    all_to_all x1, starting transfers between devices, local(): b_home = lax.all_to_all(b_sums, 'x', 0, 0, tiled=True)  5.09 us
    pallas_call x1, Pallas kernels, sum_rows(): pl.pallas_call(functools.partial(sum_kernel, top, counts), grid=(1,), in_...  4.56 us
  transfers between devices with their start and end apart: 32, of which 9 were waited for; matrix products, arithmetic and copies ran while one was open for 0% of the time, Pallas kernels for 21%

profile of v9, /device:TPU:0, one launch (start us, length us, event | category | flops | bytes accessed | tf_op | source)
XLA Modules:
  0.0 193.2 jit_solution(17443285591974005703)
XLA Ops:
  0.0 1.8 shard_map.64
  1.8 4.2 %collective-permute-start.1 = (bf16[128,2176]{1,0:T(8,128)(2,1)S(1)}, bf16[128,2176]{1,0:T(8,128)(2,1)S(1)}, u32[]{:S(2)}, u32[]{:S(2)}) collective-permute-start(bf16[128,2176]{1,0:T(8,128)(2,1)S(1)} %get-tuple-element.58.refs_0_.refs_14_), channel_id=1, source_target_pairs={{0,12},{4,0},{8,4},{12,8},{1,13},{5,1},{9,5},{13,9},{2,14},{6,2},{... | collective-permute-start | bytes 1671176 | tf_op jit(solution)/shard_map/ppermute | solution.py:22
  6.0 2.8 %collective-permute-start.3 = (bf16[128,2176]{1,0:T(8,128)(2,1)S(1)}, bf16[128,2176]{1,0:T(8,128)(2,1)S(1)}, u32[]{:S(2)}, u32[]{:S(2)}) collective-permute-start(bf16[128,2176]{1,0:T(8,128)(2,1)S(1)} %get-tuple-element.62.refs_0_.refs_19_), channel_id=1, source_target_pairs={{0,3},{1,0},{2,1},{3,2},{4,7},{5,4},{6,5},{7,6},{8,11},{9,8},{10,9... | collective-permute-start | bytes 1671176 | tf_op jit(solution)/shard_map/ppermute | solution.py:22
  8.8 9.1 %collective-permute-done.1.refs_2_.refs_4_.refs_18_ = bf16[128,2176]{1,0:T(8,128)(2,1)S(1)} collective-permute-done((bf16[128,2176]{1,0:T(8,128)(2,1)S(1)}, bf16[128,2176]{1,0:T(8,128)(2,1)S(1)}, u32[]{:S(2)}, u32[]{:S(2)}) %collective-permute-start.1) | collective-permute-done | bytes 557088 | tf_op jit(solution)/shard_map/ppermute | solution.py:22
  17.9 3.8 %collective-permute-start.5 = (bf16[64,2176]{1,0:T(8,128)(2,1)S(1)}, bf16[64,2176]{1,0:T(8,128)(2,1)S(1)}, u32[]{:S(2)}, u32[]{:S(2)}) collective-permute-start(bf16[64,2176]{1,0:T(8,128)(2,1)S(1)} %slice.17), channel_id=1, source_target_pairs={{0,12},{4,0},{8,4},{12,8},{1,13},{5,1},{9,5},{13,9},{2,14},{6,2},{... | collective-permute-start | bytes 835592 | tf_op jit(solution)/shard_map/ppermute | solution.py:22
  21.7 2.8 %collective-permute-start.7 = (bf16[64,2176]{1,0:T(8,128)(2,1)S(1)}, bf16[64,2176]{1,0:T(8,128)(2,1)S(1)}, u32[]{:S(2)}, u32[]{:S(2)}) collective-permute-start(bf16[64,2176]{1,0:T(8,128)(2,1)S(1)} %slice.19), channel_id=1, source_target_pairs={{0,3},{1,0},{2,1},{3,2},{4,7},{5,4},{6,5},{7,6},{8,11},{9,8},{10,9... | collective-permute-start | bytes 835592 | tf_op jit(solution)/shard_map/ppermute | solution.py:22
  24.7 1.8 shard_map.66
  26.4 1.8 shard_map.65
  28.3 3.2 %collective-permute-start.9 = (bf16[192,2048]{1,0:T(8,128)(2,1)S(1)}, bf16[192,2048]{1,0:T(8,128)(2,1)S(1)}, u32[]{:S(2)}, u32[]{:S(2)}) collective-permute-start(bf16[192,2048]{1,0:T(8,128)(2,1)S(1)} %get-tuple-element.79), channel_id=1, source_target_pairs={{0,3},{1,0},{2,1},{3,2},{4,7},{5,4},{6,5},{7,6},{8,11},{9,8},{10,9... | collective-permute-start | bytes 2359304 | tf_op jit(solution)/shard_map/ppermute | solution.py:22
  31.5 3.2 %collective-permute-start.11 = (bf16[192,2048]{1,0:T(8,128)(2,1)S(1)}, bf16[192,2048]{1,0:T(8,128)(2,1)S(1)}, u32[]{:S(2)}, u32[]{:S(2)}) collective-permute-start(bf16[192,2048]{1,0:T(8,128)(2,1)S(1)} %get-tuple-element.82), channel_id=1, source_target_pairs={{0,12},{4,0},{8,4},{12,8},{1,13},{5,1},{9,5},{13,9},{2,14},{6,2},{... | collective-permute-start | bytes 2359304 | tf_op jit(solution)/shard_map/ppermute | solution.py:22
  34.9 18.4 %collective-permute-done.6.refs_2_.refs_21_ = bf16[64,2176]{1,0:T(8,128)(2,1)S(1)} collective-permute-done((bf16[64,2176]{1,0:T(8,128)(2,1)S(1)}, bf16[64,2176]{1,0:T(8,128)(2,1)S(1)}, u32[]{:S(2)}, u32[]{:S(2)}) %collective-permute-start.6) | collective-permute-done | bytes 278560 | tf_op jit(solution)/shard_map/ppermute | solution.py:22
  53.3 1.7 shard_map.68
  55.0 6.0 %collective-permute-done.4.refs_2_.refs_16_ = bf16[64,2176]{1,0:T(8,128)(2,1)S(1)} collective-permute-done((bf16[64,2176]{1,0:T(8,128)(2,1)S(1)}, bf16[64,2176]{1,0:T(8,128)(2,1)S(1)}, u32[]{:S(2)}, u32[]{:S(2)}) %collective-permute-start.4) | collective-permute-done | bytes 278560 | tf_op jit(solution)/shard_map/ppermute | solution.py:22
  61.1 1.7 shard_map.67
  63.4 2.9 %collective-permute-start.16 = (bf16[64,2048]{1,0:T(8,128)(2,1)S(1)}, bf16[64,2048]{1,0:T(8,128)(2,1)S(1)}, u32[]{:S(2)}, u32[]{:S(2)}) collective-permute-start(bf16[64,2048]{1,0:T(8,128)(2,1)S(1)} %get-tuple-element.90), channel_id=1, source_target_pairs={{0,3},{1,0},{2,1},{3,2},{4,7},{5,4},{6,5},{7,6},{8,11},{9,8},{10,9... | collective-permute-start | bytes 786440 | tf_op jit(solution)/shard_map/ppermute | solution.py:22
  66.6 10.7 %shard_map.69.hidden_ref = bf16[576,768]{1,0:T(8,128)(2,1)S(1)} custom-call(bf16[4096,768]{1,0:T(8,128)(2,1)} %bitcast.7, bf16[4096,768]{1,0:T(8,128)(2,1)} %bitcast.9, bf16[192,2048]{1,0:T(8,128)(2,1)S(1)} %get-tuple-element.77.refs_0_, bf16[192,2048]{1,0:T(8,128)(2,1)S(1)} %collective-permute-done.8.refs_1_, ...), custom_call_target="tpu_custom_call" | custom-call | flops 7247757312 | bytes 17301504 | tf_op jit(solution)/shard_map/pallas_call | solution.py:208
  77.3 14.0 %collective-permute-done.14.refs_1_ = bf16[64,2048]{1,0:T(8,128)(2,1)S(1)} collective-permute-done((bf16[64,2048]{1,0:T(8,128)(2,1)S(1)}, bf16[64,2048]{1,0:T(8,128)(2,1)S(1)}, u32[]{:S(2)}, u32[]{:S(2)}) %collective-permute-start.14) | collective-permute-done | bytes 262176 | tf_op jit(solution)/shard_map/ppermute | solution.py:22
  91.3 6.9 %shard_map.70 = (bf16[192,2048]{1,0:T(8,128)(2,1)S(1)}, bf16[192,2048]{1,0:T(8,128)(2,1)S(1)}, bf16[192,2048]{1,0:T(8,128)(2,1)S(1)}, bf16[192,2048]{1,0:T(8,128...) custom-call(bf16[576,768]{1,0:T(8,128)(2,1)S(1)} %shard_map.69.hidden_ref, ...), custom_call_target="tpu_custom_call" | custom-call | flops 3623878656 | bytes 11010048 | tf_op jit(solution)/shard_map/pallas_call | solution.py:264
  102.4 9.0 %shard_map.71.hidden_ref = bf16[448,768]{1,0:T(8,128)(2,1)S(1)} custom-call(bf16[4096,768]{1,0:T(8,128)(2,1)} %bitcast.8, bf16[4096,768]{1,0:T(8,128)(2,1)} %bitcast.10, bf16[64,2048]{1,0:T(8,128)(2,1)S(1)} %get-tuple-element.87.refs_0_, bf16[64,2048]{1,0:T(8,128)(2,1)S(1)} %collective-permute-done.14.refs_1_, ...), custom_call_target="tpu_custom_call" | custom-call | flops 5637144576 | bytes 16252928 | tf_op jit(solution)/shard_map/pallas_call | solution.py:208
  111.4 6.2 %shard_map.72 = (bf16[64,2048]{1,0:T(8,128)(2,1)S(1)}, bf16[64,2048]{1,0:T(8,128)(2,1)S(1)}, bf16[256,2048]{1,0:T(8,128)(2,1)S(1)}, bf16[64,2048]{1,0:T(8,128)(2...) custom-call(bf16[448,768]{1,0:T(8,128)(2,1)S(1)} %shard_map.71.hidde, ...), custom_call_target="tpu_custom_call" | custom-call | flops 2818572288 | bytes 9961472 | tf_op jit(solution)/shard_map/pallas_call | solution.py:264
  118.1 2.0 %collective-permute-start.26 = (bf16[256,2048]{1,0:T(8,128)(2,1)S(1)}, bf16[256,2048]{1,0:T(8,128)(2,1)S(1)}, u32[]{:S(2)}, u32[]{:S(2)}) collective-permute-start(bf16[256,2048]{1,0:T(8,128)(2,1)S(1)} %get-tuple-element.104), channel_id=1, source_target_pairs={{0,8},{4,12},{8,0},{12,4},{1,9},{5,13},{9,1},{13,5},{2,10},{6,14},... | collective-permute-start | bytes 3145736 | tf_op jit(solution)/shard_map/ppermute | solution.py:22
  120.1 2.4 %collective-permute-start.20 = (bf16[64,2048]{1,0:T(8,128)(2,1)S(1)}, bf16[64,2048]{1,0:T(8,128)(2,1)S(1)}, u32[]{:S(2)}, u32[]{:S(2)}) collective-permute-start(bf16[64,2048]{1,0:T(8,128)(2,1)S(1)} %get-tuple-element.96), channel_id=1, source_target_pairs={{0,3},{1,0},{2,1},{3,2},{4,7},{5,4},{6,5},{7,6},{8,11},{9,8},{10,9... | collective-permute-start | bytes 786440 | tf_op jit(solution)/shard_map/ppermute | solution.py:22
  122.6 2.6 %collective-permute-start.25 = (bf16[64,2048]{1,0:T(8,128)(2,1)S(1)}, bf16[64,2048]{1,0:T(8,128)(2,1)S(1)}, u32[]{:S(2)}, u32[]{:S(2)}) collective-permute-start(bf16[64,2048]{1,0:T(8,128)(2,1)S(1)} %get-tuple-element.103), channel_id=1, source_target_pairs={{0,12},{4,0},{8,4},{12,8},{1,13},{5,1},{9,5},{13,9},{2,14},{6,2},{... | collective-permute-start | bytes 786440 | tf_op jit(solution)/shard_map/ppermute | solution.py:22
  125.2 22.5 %collective-permute-done.20.refs_4_ = bf16[64,2048]{1,0:T(8,128)(2,1)S(1)} collective-permute-done((bf16[64,2048]{1,0:T(8,128)(2,1)S(1)}, bf16[64,2048]{1,0:T(8,128)(2,1)S(1)}, u32[]{:S(2)}, u32[]{:S(2)}) %collective-permute-start.20) | collective-permute-done | bytes 262176 | tf_op jit(solution)/shard_map/ppermute | solution.py:22
  147.7 1.7 collective-permute-start.27
  149.4 6.7 %collective-permute-done.27.refs_13_ = bf16[64,2048]{1,0:T(8,128)(2,1)S(1)} collective-permute-done((bf16[64,2048]{1,0:T(8,128)(2,1)S(1)}, bf16[64,2048]{1,0:T(8,128)(2,1)S(1)}, u32[]{:S(2)}, u32[]{:S(2)}) %collective-permute-start.27) | collective-permute-done | bytes 262176 | tf_op jit(solution)/shard_map/ppermute | solution.py:22
  156.1 4.6 %shard_map.73 = (bf16[128,2048]{1,0:T(8,128)(2,1)}, bf16[128,2048]{1,0:T(8,128)(2,1)}, bf16[128,2048]{1,0:T(8,128)(2,1)}, bf16[128,2048]{1,0:T(8,128)(2,1)}, bf16[4,128,2048]{2,1,0:T(8,128)(2,1)}) custom-call(s32[12]{0:T(128)S(1)} %pad_add_fusion.experts_ref, bf16[192,2048]{1,0:T(8,128)(2,1)S(1)} %get-tuple-element.84.refs_0_, ...), custom_call_target="tpu_custom_call" | custom-call | flops 1073741824 | bytes 12582912 | tf_op jit(solution)/shard_map/pallas_call | solution.py:331
  160.6 5.1 %all-to-all-start = ((bf16[4,128,2048]{2,1,0:T(8,128)(2,1)}), bf16[4,128,2048]{2,1,0:T(8,128)(2,1)S(1)}, u32[]{:S(2)}, u32[]{:S(2)}) async-start(bf16[4,128,2048]{2,1,0:T(8,128)(2,1)} %get-tuple-element.110), calls=%async_computation | async-start | bytes 4194304 | tf_op jit(solution)/shard_map/all_to_all | solution.py:388
  166.0 2.2 %collective-permute-start.29 = (bf16[128,2048]{1,0:T(8,128)(2,1)}, bf16[128,2048]{1,0:T(8,128)(2,1)S(1)}, u32[]{:S(2)}, u32[]{:S(2)}) collective-permute-start(bf16[128,2048]{1,0:T(8,128)(2,1)} %get-tuple-element.108), channel_id=1, source_target_pairs={{0,8},{4,12},{8,0},{12,4},{1,9},{5,13},{9,1},{13,5},{2,10},{6,14},... | collective-permute-start | bytes 1572872 | tf_op jit(solution)/shard_map/ppermute | solution.py:22
  168.2 12.5 %collective-permute-done.28 = bf16[128,2048]{1,0:T(8,128)(2,1)S(1)} collective-permute-done((bf16[128,2048]{1,0:T(8,128)(2,1)}, bf16[128,2048]{1,0:T(8,128)(2,1)S(1)}, u32[]{:S(2)}, u32[]{:S(2)}) %collective-permute-start.28) | collective-permute-done | bytes 524320 | tf_op jit(solution)/shard_map/ppermute | solution.py:22
  180.8 1.8 collective-permute-done.29
  182.6 8.8 %collective-permute-done.30 = bf16[128,2048]{1,0:T(8,128)(2,1)S(1)} collective-permute-done((bf16[128,2048]{1,0:T(8,128)(2,1)S(1)}, bf16[128,2048]{1,0:T(8,128)(2,1)S(1)}, u32[]{:S(2)}, u32[]{:S(2)}) %collective-permute-start.30) | collective-permute-done | bytes 524320 | tf_op jit(solution)/shard_map/ppermute | solution.py:22
  (56 shorter events, 8.2 us)
Async XLA Ops:
  1.8 16.1 %collective-permute-start.1 = (bf16[128,2176]{1,0:T(8,128)(2,1)S(1)}, bf16[128,2176]{1,0:T(8,128)(2,1)S(1)}, u32[]{:S(2)}, u32[]{:S(2)}) collective-permute-start(bf16[128,2176]{1,0:T(8,128)(2,1)S(1)} %get-tuple-element.58.refs_0_.refs_14_), channel_id=1, source_target_pairs={{0,12},{4,0},{8,4},{12,8},{1,13},{5,1},{9,5},{13,9},{2,14},{6,2},{... | collective-permute-start | bytes 1671176 | tf_op jit(solution)/shard_map/ppermute | solution.py:22
  6.0 15.7 %collective-permute-start.3 = (bf16[128,2176]{1,0:T(8,128)(2,1)S(1)}, bf16[128,2176]{1,0:T(8,128)(2,1)S(1)}, u32[]{:S(2)}, u32[]{:S(2)}) collective-permute-start(bf16[128,2176]{1,0:T(8,128)(2,1)S(1)} %get-tuple-element.62.refs_0_.refs_19_), channel_id=1, source_target_pairs={{0,3},{1,0},{2,1},{3,2},{4,7},{5,4},{6,5},{7,6},{8,11},{9,8},{10,9... | collective-permute-start | bytes 1671176 | tf_op jit(solution)/shard_map/ppermute | solution.py:22
  8.8 15.9 %collective-permute-start.2 = (bf16[128,2176]{1,0:T(8,128)(2,1)S(1)}, bf16[128,2176]{1,0:T(8,128)(2,1)S(1)}, u32[]{:S(2)}, u32[]{:S(2)}) collective-permute-start(bf16[128,2176]{1,0:T(8,128)(2,1)S(1)} %get-tuple-element.62.refs_0_.refs_19_), channel_id=1, source_target_pairs={{0,1},{1,2},{2,3},{3,0},{4,5},{5,6},{6,7},{7,4},{8,9},{9,10},{10,1... | collective-permute-start | bytes 1671176 | tf_op jit(solution)/shard_map/ppermute | solution.py:22
  8.8 17.6 %collective-permute-start = (bf16[128,2176]{1,0:T(8,128)(2,1)S(1)}, bf16[128,2176]{1,0:T(8,128)(2,1)S(1)}, u32[]{:S(2)}, u32[]{:S(2)}) collective-permute-start(bf16[128,2176]{1,0:T(8,128)(2,1)S(1)} %get-tuple-element.58.refs_0_.refs_14_), channel_id=1, source_target_pairs={{0,4},{4,8},{8,12},{12,0},{1,5},{5,9},{9,13},{13,1},{2,6},{6,10},{... | collective-permute-start | bytes 1671176 | tf_op jit(solution)/shard_map/ppermute | solution.py:22
  17.9 13.6 %collective-permute-start.5 = (bf16[64,2176]{1,0:T(8,128)(2,1)S(1)}, bf16[64,2176]{1,0:T(8,128)(2,1)S(1)}, u32[]{:S(2)}, u32[]{:S(2)}) collective-permute-start(bf16[64,2176]{1,0:T(8,128)(2,1)S(1)} %slice.17), channel_id=1, source_target_pairs={{0,12},{4,0},{8,4},{12,8},{1,13},{5,1},{9,5},{13,9},{2,14},{6,2},{... | collective-permute-start | bytes 835592 | tf_op jit(solution)/shard_map/ppermute | solution.py:22
  21.7 13.0 %collective-permute-start.7 = (bf16[64,2176]{1,0:T(8,128)(2,1)S(1)}, bf16[64,2176]{1,0:T(8,128)(2,1)S(1)}, u32[]{:S(2)}, u32[]{:S(2)}) collective-permute-start(bf16[64,2176]{1,0:T(8,128)(2,1)S(1)} %slice.19), channel_id=1, source_target_pairs={{0,3},{1,0},{2,1},{3,2},{4,7},{5,4},{6,5},{7,6},{8,11},{9,8},{10,9... | collective-permute-start | bytes 835592 | tf_op jit(solution)/shard_map/ppermute | solution.py:22
  28.2 34.7 %collective-permute-start.8 = (bf16[192,2048]{1,0:T(8,128)(2,1)S(1)}, bf16[192,2048]{1,0:T(8,128)(2,1)S(1)}, u32[]{:S(2)}, u32[]{:S(2)}) collective-permute-start(bf16[192,2048]{1,0:T(8,128)(2,1)S(1)} %get-tuple-element.78), channel_id=1, source_target_pairs={{0,1},{1,2},{2,3},{3,0},{4,5},{5,6},{6,7},{7,4},{8,9},{9,10},{10,1... | collective-permute-start | bytes 2359304 | tf_op jit(solution)/shard_map/ppermute | solution.py:22
  28.3 34.7 %collective-permute-start.9 = (bf16[192,2048]{1,0:T(8,128)(2,1)S(1)}, bf16[192,2048]{1,0:T(8,128)(2,1)S(1)}, u32[]{:S(2)}, u32[]{:S(2)}) collective-permute-start(bf16[192,2048]{1,0:T(8,128)(2,1)S(1)} %get-tuple-element.79), channel_id=1, source_target_pairs={{0,3},{1,0},{2,1},{3,2},{4,7},{5,4},{6,5},{7,6},{8,11},{9,8},{10,9... | collective-permute-start | bytes 2359304 | tf_op jit(solution)/shard_map/ppermute | solution.py:22
  31.5 31.9 %collective-permute-start.10 = (bf16[192,2048]{1,0:T(8,128)(2,1)S(1)}, bf16[192,2048]{1,0:T(8,128)(2,1)S(1)}, u32[]{:S(2)}, u32[]{:S(2)}) collective-permute-start(bf16[192,2048]{1,0:T(8,128)(2,1)S(1)} %get-tuple-element.81), channel_id=1, source_target_pairs={{0,4},{4,8},{8,12},{12,0},{1,5},{5,9},{9,13},{13,1},{2,6},{6,10},{... | collective-permute-start | bytes 2359304 | tf_op jit(solution)/shard_map/ppermute | solution.py:22
  31.5 34.8 %collective-permute-start.11 = (bf16[192,2048]{1,0:T(8,128)(2,1)S(1)}, bf16[192,2048]{1,0:T(8,128)(2,1)S(1)}, u32[]{:S(2)}, u32[]{:S(2)}) collective-permute-start(bf16[192,2048]{1,0:T(8,128)(2,1)S(1)} %get-tuple-element.82), channel_id=1, source_target_pairs={{0,12},{4,0},{8,4},{12,8},{1,13},{5,1},{9,5},{13,9},{2,14},{6,2},{... | collective-permute-start | bytes 2359304 | tf_op jit(solution)/shard_map/ppermute | solution.py:22
  34.8 18.5 %collective-permute-start.6 = (bf16[64,2176]{1,0:T(8,128)(2,1)S(1)}, bf16[64,2176]{1,0:T(8,128)(2,1)S(1)}, u32[]{:S(2)}, u32[]{:S(2)}) collective-permute-start(bf16[64,2176]{1,0:T(8,128)(2,1)S(1)} %slice.18), channel_id=1, source_target_pairs={{0,1},{1,2},{2,3},{3,0},{4,5},{5,6},{6,7},{7,4},{8,9},{9,10},{10,1... | collective-permute-start | bytes 835592 | tf_op jit(solution)/shard_map/ppermute | solution.py:22
  53.3 7.8 %collective-permute-start.4 = (bf16[64,2176]{1,0:T(8,128)(2,1)S(1)}, bf16[64,2176]{1,0:T(8,128)(2,1)S(1)}, u32[]{:S(2)}, u32[]{:S(2)}) collective-permute-start(bf16[64,2176]{1,0:T(8,128)(2,1)S(1)} %slice.16), channel_id=1, source_target_pairs={{0,4},{4,8},{8,12},{12,0},{1,5},{5,9},{9,13},{13,1},{2,6},{6,10},{... | collective-permute-start | bytes 835592 | tf_op jit(solution)/shard_map/ppermute | solution.py:22
  62.8 38.1 %collective-permute-start.15 = (bf16[256,2048]{1,0:T(8,128)(2,1)S(1)}, bf16[256,2048]{1,0:T(8,128)(2,1)S(1)}, u32[]{:S(2)}, u32[]{:S(2)}) collective-permute-start(bf16[256,2048]{1,0:T(8,128)(2,1)S(1)} %get-tuple-element.89), channel_id=1, source_target_pairs={{0,2},{1,3},{2,0},{3,1},{4,6},{5,7},{6,4},{7,5},{8,10},{9,11},{10,... | collective-permute-start | bytes 3145736 | tf_op jit(solution)/shard_map/ppermute | solution.py:22
  62.9 39.5 %collective-permute-start.18 = (bf16[256,2048]{1,0:T(8,128)(2,1)S(1)}, bf16[256,2048]{1,0:T(8,128)(2,1)S(1)}, u32[]{:S(2)}, u32[]{:S(2)}) collective-permute-start(bf16[256,2048]{1,0:T(8,128)(2,1)S(1)} %get-tuple-element.93), channel_id=1, source_target_pairs={{0,8},{4,12},{8,0},{12,4},{1,9},{5,13},{9,1},{13,5},{2,10},{6,14},... | collective-permute-start | bytes 3145736 | tf_op jit(solution)/shard_map/ppermute | solution.py:22
  63.0 28.3 %collective-permute-start.14 = (bf16[64,2048]{1,0:T(8,128)(2,1)S(1)}, bf16[64,2048]{1,0:T(8,128)(2,1)S(1)}, u32[]{:S(2)}, u32[]{:S(2)}) collective-permute-start(bf16[64,2048]{1,0:T(8,128)(2,1)S(1)} %get-tuple-element.88), channel_id=1, source_target_pairs={{0,1},{1,2},{2,3},{3,0},{4,5},{5,6},{6,7},{7,4},{8,9},{9,10},{10,1... | collective-permute-start | bytes 786440 | tf_op jit(solution)/shard_map/ppermute | solution.py:22
  63.4 34.7 %collective-permute-start.16 = (bf16[64,2048]{1,0:T(8,128)(2,1)S(1)}, bf16[64,2048]{1,0:T(8,128)(2,1)S(1)}, u32[]{:S(2)}, u32[]{:S(2)}) collective-permute-start(bf16[64,2048]{1,0:T(8,128)(2,1)S(1)} %get-tuple-element.90), channel_id=1, source_target_pairs={{0,3},{1,0},{2,1},{3,2},{4,7},{5,4},{6,5},{7,6},{8,11},{9,8},{10,9... | collective-permute-start | bytes 786440 | tf_op jit(solution)/shard_map/ppermute | solution.py:22
  66.3 32.7 %collective-permute-start.17 = (bf16[64,2048]{1,0:T(8,128)(2,1)S(1)}, bf16[64,2048]{1,0:T(8,128)(2,1)S(1)}, u32[]{:S(2)}, u32[]{:S(2)}) collective-permute-start(bf16[64,2048]{1,0:T(8,128)(2,1)S(1)} %get-tuple-element.92), channel_id=1, source_target_pairs={{0,4},{4,8},{8,12},{12,0},{1,5},{5,9},{9,13},{13,1},{2,6},{6,10},{... | collective-permute-start | bytes 786440 | tf_op jit(solution)/shard_map/ppermute | solution.py:22
  91.3 9.0 %collective-permute-start.19 = (bf16[64,2048]{1,0:T(8,128)(2,1)S(1)}, bf16[64,2048]{1,0:T(8,128)(2,1)S(1)}, u32[]{:S(2)}, u32[]{:S(2)}) collective-permute-start(bf16[64,2048]{1,0:T(8,128)(2,1)S(1)} %get-tuple-element.94), channel_id=1, source_target_pairs={{0,12},{4,0},{8,4},{12,8},{1,13},{5,1},{9,5},{13,9},{2,14},{6,2},{... | collective-permute-start | bytes 786440 | tf_op jit(solution)/shard_map/ppermute | solution.py:22
  98.2 19.9 %collective-permute-start.12 = (bf16[192,2048]{1,0:T(8,128)(2,1)S(1)}, bf16[192,2048]{1,0:T(8,128)(2,1)S(1)}, u32[]{:S(2)}, u32[]{:S(2)}) collective-permute-start(bf16[192,2048]{1,0:T(8,128)(2,1)S(1)} %get-tuple-element.85), channel_id=1, source_target_pairs={{0,3},{1,0},{2,1},{3,2},{4,7},{5,4},{6,5},{7,6},{8,11},{9,8},{10,9... | collective-permute-start | bytes 2359304 | tf_op jit(solution)/shard_map/ppermute | solution.py:22
  99.0 21.2 %collective-permute-start.13 = (bf16[192,2048]{1,0:T(8,128)(2,1)S(1)}, bf16[192,2048]{1,0:T(8,128)(2,1)S(1)}, u32[]{:S(2)}, u32[]{:S(2)}) collective-permute-start(bf16[192,2048]{1,0:T(8,128)(2,1)S(1)} %get-tuple-element.86), channel_id=1, source_target_pairs={{0,1},{1,2},{2,3},{3,0},{4,5},{5,6},{6,7},{7,4},{8,9},{9,10},{10,1... | collective-permute-start | bytes 2359304 | tf_op jit(solution)/shard_map/ppermute | solution.py:22
  100.3 22.2 %collective-permute-start.23 = (bf16[192,2048]{1,0:T(8,128)(2,1)S(1)}, bf16[192,2048]{1,0:T(8,128)(2,1)S(1)}, u32[]{:S(2)}, u32[]{:S(2)}) collective-permute-start(bf16[192,2048]{1,0:T(8,128)(2,1)S(1)} %get-tuple-element.100), channel_id=1, source_target_pairs={{0,12},{4,0},{8,4},{12,8},{1,13},{5,1},{9,5},{13,9},{2,14},{6,2},{... | collective-permute-start | bytes 2359304 | tf_op jit(solution)/shard_map/ppermute | solution.py:22
  100.9 21.7 %collective-permute-start.24 = (bf16[192,2048]{1,0:T(8,128)(2,1)S(1)}, bf16[192,2048]{1,0:T(8,128)(2,1)S(1)}, u32[]{:S(2)}, u32[]{:S(2)}) collective-permute-start(bf16[192,2048]{1,0:T(8,128)(2,1)S(1)} %get-tuple-element.101), channel_id=1, source_target_pairs={{0,4},{4,8},{8,12},{12,0},{1,5},{5,9},{9,13},{13,1},{2,6},{6,10},{... | collective-permute-start | bytes 2359304 | tf_op jit(solution)/shard_map/ppermute | solution.py:22
  117.7 38.4 %collective-permute-start.21 = (bf16[256,2048]{1,0:T(8,128)(2,1)S(1)}, bf16[256,2048]{1,0:T(8,128)(2,1)S(1)}, u32[]{:S(2)}, u32[]{:S(2)}) collective-permute-start(bf16[256,2048]{1,0:T(8,128)(2,1)S(1)} %get-tuple-element.97), channel_id=1, source_target_pairs={{0,2},{1,3},{2,0},{3,1},{4,6},{5,7},{6,4},{7,5},{8,10},{9,11},{10,... | collective-permute-start | bytes 3145736 | tf_op jit(solution)/shard_map/ppermute | solution.py:22
  118.1 37.9 %collective-permute-start.26 = (bf16[256,2048]{1,0:T(8,128)(2,1)S(1)}, bf16[256,2048]{1,0:T(8,128)(2,1)S(1)}, u32[]{:S(2)}, u32[]{:S(2)}) collective-permute-start(bf16[256,2048]{1,0:T(8,128)(2,1)S(1)} %get-tuple-element.104), channel_id=1, source_target_pairs={{0,8},{4,12},{8,0},{12,4},{1,9},{5,13},{9,1},{13,5},{2,10},{6,14},... | collective-permute-start | bytes 3145736 | tf_op jit(solution)/shard_map/ppermute | solution.py:22
  120.1 27.5 %collective-permute-start.20 = (bf16[64,2048]{1,0:T(8,128)(2,1)S(1)}, bf16[64,2048]{1,0:T(8,128)(2,1)S(1)}, u32[]{:S(2)}, u32[]{:S(2)}) collective-permute-start(bf16[64,2048]{1,0:T(8,128)(2,1)S(1)} %get-tuple-element.96), channel_id=1, source_target_pairs={{0,3},{1,0},{2,1},{3,2},{4,7},{5,4},{6,5},{7,6},{8,11},{9,8},{10,9... | collective-permute-start | bytes 786440 | tf_op jit(solution)/shard_map/ppermute | solution.py:22
  122.5 26.8 %collective-permute-start.22 = (bf16[64,2048]{1,0:T(8,128)(2,1)S(1)}, bf16[64,2048]{1,0:T(8,128)(2,1)S(1)}, u32[]{:S(2)}, u32[]{:S(2)}) collective-permute-start(bf16[64,2048]{1,0:T(8,128)(2,1)S(1)} %get-tuple-element.98), channel_id=1, source_target_pairs={{0,1},{1,2},{2,3},{3,0},{4,5},{5,6},{6,7},{7,4},{8,9},{9,10},{10,1... | collective-permute-start | bytes 786440 | tf_op jit(solution)/shard_map/ppermute | solution.py:22
  122.6 26.7 %collective-permute-start.25 = (bf16[64,2048]{1,0:T(8,128)(2,1)S(1)}, bf16[64,2048]{1,0:T(8,128)(2,1)S(1)}, u32[]{:S(2)}, u32[]{:S(2)}) collective-permute-start(bf16[64,2048]{1,0:T(8,128)(2,1)S(1)} %get-tuple-element.103), channel_id=1, source_target_pairs={{0,12},{4,0},{8,4},{12,8},{1,13},{5,1},{9,5},{13,9},{2,14},{6,2},{... | collective-permute-start | bytes 786440 | tf_op jit(solution)/shard_map/ppermute | solution.py:22
  147.7 8.4 %collective-permute-start.27 = (bf16[64,2048]{1,0:T(8,128)(2,1)S(1)}, bf16[64,2048]{1,0:T(8,128)(2,1)S(1)}, u32[]{:S(2)}, u32[]{:S(2)}) collective-permute-start(bf16[64,2048]{1,0:T(8,128)(2,1)S(1)} %get-tuple-element.105), channel_id=1, source_target_pairs={{0,4},{4,8},{8,12},{12,0},{1,5},{5,9},{9,13},{13,1},{2,6},{6,10},{... | collective-permute-start | bytes 786440 | tf_op jit(solution)/shard_map/ppermute | solution.py:22
  160.6 31.1 %all-to-all-start = ((bf16[4,128,2048]{2,1,0:T(8,128)(2,1)}), bf16[4,128,2048]{2,1,0:T(8,128)(2,1)S(1)}, u32[]{:S(2)}, u32[]{:S(2)}) async-start(bf16[4,128,2048]{2,1,0:T(8,128)(2,1)} %get-tuple-element.110), calls=%async_computation | async-start | bytes 4194304 | tf_op jit(solution)/shard_map/all_to_all | solution.py:388
  165.7 15.1 %collective-permute-start.28 = (bf16[128,2048]{1,0:T(8,128)(2,1)}, bf16[128,2048]{1,0:T(8,128)(2,1)S(1)}, u32[]{:S(2)}, u32[]{:S(2)}) collective-permute-start(bf16[128,2048]{1,0:T(8,128)(2,1)} %get-tuple-element.107), channel_id=1, source_target_pairs={{0,12},{4,0},{8,4},{12,8},{1,13},{5,1},{9,5},{13,9},{2,14},{6,2},{... | collective-permute-start | bytes 1572872 | tf_op jit(solution)/shard_map/ppermute | solution.py:22
  166.0 16.6 %collective-permute-start.29 = (bf16[128,2048]{1,0:T(8,128)(2,1)}, bf16[128,2048]{1,0:T(8,128)(2,1)S(1)}, u32[]{:S(2)}, u32[]{:S(2)}) collective-permute-start(bf16[128,2048]{1,0:T(8,128)(2,1)} %get-tuple-element.108), channel_id=1, source_target_pairs={{0,8},{4,12},{8,0},{12,4},{1,9},{5,13},{9,1},{13,5},{2,10},{6,14},... | collective-permute-start | bytes 1572872 | tf_op jit(solution)/shard_map/ppermute | solution.py:22
  168.2 23.1 %collective-permute-start.30 = (bf16[128,2048]{1,0:T(8,128)(2,1)S(1)}, bf16[128,2048]{1,0:T(8,128)(2,1)S(1)}, u32[]{:S(2)}, u32[]{:S(2)}) collective-permute-start(bf16[128,2048]{1,0:T(8,128)(2,1)S(1)} %copy-done.1), channel_id=1, source_target_pairs={{0,4},{4,8},{8,12},{12,0},{1,5},{5,9},{9,13},{13,1},{2,6},{6,10},{... | collective-permute-start | bytes 1572872 | tf_op jit(solution)/shard_map/ppermute | solution.py:22
  (2 other events, 38.4 us)

commit v10 on v8

--- a/solution.py
+++ b/solution.py
@@ -155,24 +155,35 @@
     half = x_ref.shape[-1] // 2
     count = SIDE * SIDE * ROWS
 
-    @pl.when(pl.program_id(0) == 0)
+    first = pl.program_id(0) == 0
+    a_copies = [
+        pltpu.make_async_copy(a_in[k], x_ref.at[:, k, :, :half], sems.at[k])
+        for k in range(SIDE)
+    ]
+    b_copies = [
+        pltpu.make_async_copy(b_in[k], x_ref.at[k, :, :, half:], sems.at[SIDE + k])
+        for k in range(SIDE)
+    ]
+
+    @pl.when(first)
     def _():
-        copies = []
-        for k in range(SIDE):
-            copies.append(
-                pltpu.make_async_copy(a_in[k], x_ref.at[:, k, :, :half], sems.at[k])
-            )
-            copies.append(
-                pltpu.make_async_copy(b_in[k], x_ref.at[k, :, :, half:], sems.at[SIDE + k])
-            )
-        for copy in copies:
+        for copy in b_copies + a_copies:
             copy.start()
-        for copy in copies:
+        for copy in b_copies:
             copy.wait()
 
-    x = x_ref[...].reshape(count, 2 * half)
-    gate = jnp.dot(x, wg_ref[...], preferred_element_type=jnp.float32)
-    up = jnp.dot(x, wu_ref[...], preferred_element_type=jnp.float32)
+    x = x_ref[:, :, :, half:].reshape(count, half)
+    gate = jnp.dot(x, wg_ref[half:], preferred_element_type=jnp.float32)
+    up = jnp.dot(x, wu_ref[half:], preferred_element_type=jnp.float32)
+
+    @pl.when(first)
+    def _():
+        for copy in a_copies:
+            copy.wait()
+
+    x = x_ref[:, :, :, :half].reshape(count, half)
+    gate += jnp.dot(x, wg_ref[:half], preferred_element_type=jnp.float32)
+    up += jnp.dot(x, wu_ref[:half], preferred_element_type=jnp.float32)
     hidden_ref[...] = (gate / (1.0 + jnp.exp(-gate)) * up).astype(jnp.bfloat16)
 
 

time: 175 us -> 175 us (level)
  transfers between devices with their start and end apart: 36 -> 36, of which waited for: 12 -> 13; matrix products, arithmetic and copies ran while one was open for 2% -> 2% of each run, Pallas kernels for 23% -> 23%
where the time goes in v10:
time: 175 us; the launch traced here: 174 us
  starting transfers between devices  60.8 us (35%)
  waiting for transfers between devices  58.8 us (34%)
  Pallas kernels  49.7 us (28%)
  local copies, waits for them, and re-layouts  2.97 us (2%)
  other arithmetic  1.9 us (1%)
    ppermute x35, waiting for transfers between devices, shift(): lax.ppermute(block, axis, [(i, (i + step) % SIDE) for i in range(SIDE)])  58.8 us
    ppermute x35, starting transfers between devices, shift(): lax.ppermute(block, axis, [(i, (i + step) % SIDE) for i in range(SIDE)])  55.7 us
    pallas_call x2, Pallas kernels, hidden_rows(): pl.pallas_call(hidden_kernel, grid=(ff // FF_TILE,), in_specs=[weight, we...  21.1 us
    pallas_call x2, Pallas kernels, down_rows(): pl.pallas_call(functools.partial(down_kernel, n_half), grid=(2 * n_half,)...  13.1 us
    pallas_call x4, Pallas kernels, pack(): pl.pallas_call(functools.partial(pack_kernel, chunk, top), in_specs=[pl.B...  8.96 us
    all_to_all x1, starting transfers between devices, local(): b_home = lax.all_to_all(b_sums, 'x', 0, 0, tiled=True)  5.05 us
    pallas_call x1, Pallas kernels, sum_rows(): pl.pallas_call(functools.partial(sum_kernel, top, counts), grid=(1,), in_...  4.8 us
  transfers between devices with their start and end apart: 36, of which 13 were waited for; matrix products, arithmetic and copies ran while one was open for 2% of the time, Pallas kernels for 23%

profile of v10, /device:TPU:0, one launch (start us, length us, event | category | flops | bytes accessed | tf_op | source)
XLA Modules:
  0.0 174.4 jit_solution(6536172319319322967)
XLA Ops:
  0.0 1.8 %shard_map.64 = (bf16[128,2176]{1,0:T(8,128)(2,1)S(1)}, bf16[128,2176]{1,0:T(8,128)(2,1)S(1)}) custom-call(bf16[128,4096]{1,0:T(8,128)(2,1)} %token_ref.1, s32[4,128]{1,0:T(4,128)} %bitcast.5, f32[4,128]{1,0:T(4,128)} %bitcast.6), custom_call_target="tpu_custom_call" | custom-call | flops 4194304 | bytes 2097152 | tf_op jit(solution)/shard_map/pallas_call | solution.py:81
  1.8 2.9 %collective-permute-start.6 = (bf16[128,2176]{1,0:T(8,128)(2,1)S(1)}, bf16[128,2176]{1,0:T(8,128)(2,1)S(1)}, u32[]{:S(2)}, u32[]{:S(2)}) collective-permute-start(bf16[128,2176]{1,0:T(8,128)(2,1)S(1)} %get-tuple-element.73.refs_0_.refs_21_), channel_id=1, source_target_pairs={{0,3},{1,0},{2,1},{3,2},{4,7},{5,4},{6,5},{7,6},{8,11},{9,8},{10,9... | collective-permute-start | bytes 1671176 | tf_op jit(solution)/shard_map/ppermute | solution.py:21
  4.8 4.0 %collective-permute-start.2 = (bf16[128,2176]{1,0:T(8,128)(2,1)S(1)}, bf16[128,2176]{1,0:T(8,128)(2,1)S(1)}, u32[]{:S(2)}, u32[]{:S(2)}) collective-permute-start(bf16[128,2176]{1,0:T(8,128)(2,1)S(1)} %get-tuple-element.68.refs_0_.refs_16_), channel_id=1, source_target_pairs={{0,12},{4,0},{8,4},{12,8},{1,13},{5,1},{9,5},{13,9},{2,14},{6,2},{... | collective-permute-start | bytes 1671176 | tf_op jit(solution)/shard_map/ppermute | solution.py:21
  8.8 7.8 %collective-permute-done.6.refs_4_.refs_25_ = bf16[128,2176]{1,0:T(8,128)(2,1)S(1)} collective-permute-done((bf16[128,2176]{1,0:T(8,128)(2,1)S(1)}, bf16[128,2176]{1,0:T(8,128)(2,1)S(1)}, u32[]{:S(2)}, u32[]{:S(2)}) %collective-permute-start.6) | collective-permute-done | bytes 557088 | tf_op jit(solution)/shard_map/ppermute | solution.py:21
  17.4 3.7 %collective-permute-start.7 = (bf16[64,2176]{1,0:T(8,128)(2,1)}, bf16[64,2176]{1,0:T(8,128)(2,1)}, u32[]{:S(2)}, u32[]{:S(2)}) collective-permute-start(bf16[64,2176]{1,0:T(8,128)(2,1)} %slice.19), channel_id=1, source_target_pairs={{0,3},{1,0},{2,1},{3,2},{4,7},{5,4},{6,5},{7,6},{8,11},{9,8},{10,9... | collective-permute-start | bytes 835592 | tf_op jit(solution)/shard_map/ppermute | solution.py:21
  22.6 4.0 %collective-permute-start.3 = (bf16[64,2176]{1,0:T(8,128)(2,1)}, bf16[64,2176]{1,0:T(8,128)(2,1)}, u32[]{:S(2)}, u32[]{:S(2)}) collective-permute-start(bf16[64,2176]{1,0:T(8,128)(2,1)} %slice.17), channel_id=1, source_target_pairs={{0,12},{4,0},{8,4},{12,8},{1,13},{5,1},{9,5},{13,9},{2,14},{6,2},{... | collective-permute-start | bytes 835592 | tf_op jit(solution)/shard_map/ppermute | solution.py:21
  27.4 3.2 %collective-permute-done.5.refs_2_.refs_23_ = bf16[64,2176]{1,0:T(8,128)(2,1)} collective-permute-done((bf16[64,2176]{1,0:T(8,128)(2,1)}, bf16[64,2176]{1,0:T(8,128)(2,1)}, u32[]{:S(2)}, u32[]{:S(2)}) %collective-permute-start.5) | collective-permute-done | bytes 278560 | tf_op jit(solution)/shard_map/ppermute | solution.py:21
  30.6 2.2 %shard_map.66 = (bf16[4,32,2048]{2,1,0:T(8,128)(2,1)S(1)}, bf16[4,32,2048]{2,1,0:T(8,128)(2,1)S(1)}, bf16[4,32,2048]{2,1,0:T(8,128)(2,1)S(1)}, bf16[4,32,2048]{2,1,0:T(8,128)(2,1)S(1)}) custom-call(s32[4]{0:T(128)S(1)} %get-tuple-element.89.experts_ref, bf16[128,2176]{1,0:T(8,128)(2,1)S(1)} %get-tuple-element.73.refs_0_.refs_21_, ...), custom_call_target="tpu_custom_call" | custom-call | flops 268435456 | bytes 4194304 | tf_op jit(solution)/shard_map/pallas_call | solution.py:137
  32.8 3.0 %collective-permute-done.1.refs_2_.refs_18_ = bf16[64,2176]{1,0:T(8,128)(2,1)} collective-permute-done((bf16[64,2176]{1,0:T(8,128)(2,1)}, bf16[64,2176]{1,0:T(8,128)(2,1)}, u32[]{:S(2)}, u32[]{:S(2)}) %collective-permute-start.1) | collective-permute-done | bytes 278560 | tf_op jit(solution)/shard_map/ppermute | solution.py:21
  35.8 2.2 %shard_map.65 = (bf16[4,32,2048]{2,1,0:T(8,128)(2,1)S(1)}, bf16[4,32,2048]{2,1,0:T(8,128)(2,1)S(1)}, bf16[4,32,2048]{2,1,0:T(8,128)(2,1)S(1)}, bf16[4,32,2048]{2,1,0:T(8,128)(2,1)S(1)}) custom-call(s32[4]{0:T(128)S(1)} %get-tuple-element.88.experts_ref, bf16[128,2176]{1,0:T(8,128)(2,1)S(1)} %get-tuple-element.68.refs_0_.refs_16_, ...), custom_call_target="tpu_custom_call" | custom-call | flops 268435456 | bytes 4194304 | tf_op jit(solution)/shard_map/pallas_call | solution.py:137
  38.2 4.4 %collective-permute-start.9 = (bf16[4,32,2048]{2,1,0:T(8,128)(2,1)S(1)}, bf16[4,32,2048]{2,1,0:T(8,128)(2,1)S(1)}, u32[]{:S(2)}, u32[]{:S(2)}) collective-permute-start(bf16[4,32,2048]{2,1,0:T(8,128)(2,1)S(1)} %get-tuple-element.93), channel_id=1, source_target_pairs={{0,2},{1,3},{2,0},{3,1},{4,6},{5,7},{6,4},{7,5},{8,10},{9,11},{10,... | collective-permute-start | bytes 1572872 | tf_op jit(solution)/shard_map/ppermute | solution.py:21
  43.9 9.7 %collective-permute-done.8.refs_1_ = bf16[4,32,2048]{2,1,0:T(8,128)(2,1)S(1)} collective-permute-done((bf16[4,32,2048]{2,1,0:T(8,128)(2,1)S(1)}, bf16[4,32,2048]{2,1,0:T(8,128)(2,1)S(1)}, u32[]{:S(2)}, u32[]{:S(2)}) %collective-permute-start.8) | collective-permute-done | bytes 524320 | tf_op jit(solution)/shard_map/ppermute | solution.py:21
  53.6 9.4 %collective-permute-start.13 = (bf16[4,32,2048]{2,1,0:T(8,128)(2,1)S(1)}, bf16[4,32,2048]{2,1,0:T(8,128)(2,1)S(1)}, u32[]{:S(2)}, u32[]{:S(2)}) collective-permute-start(bf16[4,32,2048]{2,1,0:T(8,128)(2,1)S(1)} %get-tuple-element.98), channel_id=1, source_target_pairs={{0,12},{4,0},{8,4},{12,8},{1,13},{5,1},{9,5},{13,9},{2,14},{6,2},{... | collective-permute-start | bytes 1572872 | tf_op jit(solution)/shard_map/ppermute | solution.py:21
  63.0 2.2 %shard_map.67 = (bf16[4,32,2048]{2,1,0:T(8,128)(2,1)S(1)}, bf16[4,32,2048]{2,1,0:T(8,128)(2,1)S(1)}, bf16[4,32,2048]{2,1,0:T(8,128)(2,1)S(1)}, bf16[4,32,2048]{2,1,0:T(8,128)(2,1)S(1)}) custom-call(s32[4]{0:T(128)S(1)} %get-tuple-element.88.experts_ref, bf16[128,2176]{1,0:T(8,128)(2,1)S(1)} %get-tuple-element.68.refs_0_.refs_16_, ...), custom_call_target="tpu_custom_call" | custom-call | flops 268435456 | bytes 4194304 | tf_op jit(solution)/shard_map/pallas_call | solution.py:137
  65.3 2.2 %shard_map.68 = (bf16[4,32,2048]{2,1,0:T(8,128)(2,1)S(1)}, bf16[4,32,2048]{2,1,0:T(8,128)(2,1)S(1)}, bf16[4,32,2048]{2,1,0:T(8,128)(2,1)S(1)}, bf16[4,32,2048]{2,1,0:T(8,128)(2,1)S(1)}) custom-call(s32[4]{0:T(128)S(1)} %get-tuple-element.89.experts_ref, bf16[128,2176]{1,0:T(8,128)(2,1)S(1)} %get-tuple-element.73.refs_0_.refs_21_, ...), custom_call_target="tpu_custom_call" | custom-call | flops 268435456 | bytes 4194304 | tf_op jit(solution)/shard_map/pallas_call | solution.py:137
  68.5 2.4 %collective-permute-start.16 = (bf16[4,32,2048]{2,1,0:T(8,128)(2,1)S(1)}, bf16[4,32,2048]{2,1,0:T(8,128)(2,1)S(1)}, u32[]{:S(2)}, u32[]{:S(2)}) collective-permute-start(bf16[4,32,2048]{2,1,0:T(8,128)(2,1)S(1)} %get-tuple-element.104), channel_id=1, source_target_pairs={{0,3},{1,0},{2,1},{3,2},{4,7},{5,4},{6,5},{7,6},{8,11},{9,8},{10,9... | collective-permute-start | bytes 1572872 | tf_op jit(solution)/shard_map/ppermute | solution.py:21
  70.9 3.6 %collective-permute-start.19 = (bf16[4,32,2048]{2,1,0:T(8,128)(2,1)S(1)}, bf16[4,32,2048]{2,1,0:T(8,128)(2,1)S(1)}, u32[]{:S(2)}, u32[]{:S(2)}) collective-permute-start(bf16[4,32,2048]{2,1,0:T(8,128)(2,1)S(1)} %get-tuple-element.108), channel_id=1, source_target_pairs={{0,12},{4,0},{8,4},{12,8},{1,13},{5,1},{9,5},{13,9},{2,14},{6,2},{... | collective-permute-start | bytes 1572872 | tf_op jit(solution)/shard_map/ppermute | solution.py:21
  74.5 10.5 %shard_map.69.hidden_ref = bf16[512,768]{1,0:T(8,128)(2,1)S(1)} custom-call(bf16[4096,768]{1,0:T(8,128)(2,1)} %bitcast.7, bf16[4096,768]{1,0:T(8,128)(2,1)} %bitcast.9, bf16[4,32,2048]{2,1,0:T(8,128)(2,1)S(1)} %get-tuple-element.91.refs_0_, bf16[4,32,2048]{2,1,0:T(8,128)(2,1)S(1)} %collective-permute-done.8.refs_1_, ...), custom_call_target="tpu_custom_call" | custom-call | flops 6442450944 | bytes 16777216 | tf_op jit(solution)/shard_map/pallas_call | solution.py:194
  86.6 6.5 %shard_map.70 = (bf16[4,32,2048]{2,1,0:T(8,128)(2,1)S(1)}, bf16[4,32,2048]{2,1,0:T(8,128)(2,1)S(1)}, bf16[4,32,2048]{2,1,0:T(8,128)(2,1)S(1)}, bf16[4,32,2048]{2...) custom-call(bf16[512,768]{1,0:T(8,128)(2,1)S(1)} %shard_map.69.hidde, ...), custom_call_target="tpu_custom_call" | custom-call | flops 3221225472 | bytes 10485760 | tf_op jit(solution)/shard_map/pallas_call | solution.py:237
  99.3 10.5 %shard_map.71.hidden_ref = bf16[512,768]{1,0:T(8,128)(2,1)S(1)} custom-call(bf16[4096,768]{1,0:T(8,128)(2,1)} %bitcast.8, bf16[4096,768]{1,0:T(8,128)(2,1)} %bitcast.10, bf16[4,32,2048]{2,1,0:T(8,128)(2,1)S(1)} %get-tuple-element.101.refs_0_, bf16[4,32,2048]{2,1,0:T(8,128)(2,1)S(1)} %collective-permute-done.14.refs_1_, ...), custom_call_target="tpu_custom_call" | custom-call | flops 6442450944 | bytes 16777216 | tf_op jit(solution)/shard_map/pallas_call | solution.py:194
  111.3 6.5 %shard_map.72 = (bf16[4,32,2048]{2,1,0:T(8,128)(2,1)S(1)}, bf16[4,32,2048]{2,1,0:T(8,128)(2,1)S(1)}, bf16[4,32,2048]{2,1,0:T(8,128)(2,1)S(1)}, bf16[4,32,2048]{2...) custom-call(bf16[512,768]{1,0:T(8,128)(2,1)S(1)} %shard_map.71.hidde, ...), custom_call_target="tpu_custom_call" | custom-call | flops 3221225472 | bytes 10485760 | tf_op jit(solution)/shard_map/pallas_call | solution.py:237
  117.8 2.4 %collective-permute-start.23 = (bf16[4,32,2048]{2,1,0:T(8,128)(2,1)S(1)}, bf16[4,32,2048]{2,1,0:T(8,128)(2,1)S(1)}, u32[]{:S(2)}, u32[]{:S(2)}) collective-permute-start(bf16[4,32,2048]{2,1,0:T(8,128)(2,1)S(1)} %get-tuple-element.115), channel_id=1, source_target_pairs={{0,3},{1,0},{2,1},{3,2},{4,7},{5,4},{6,5},{7,6},{8,11},{9,8},{10,9... | collective-permute-start | bytes 1572872 | tf_op jit(solution)/shard_map/ppermute | solution.py:21
  123.0 1.9 %collective-permute-start.29 = (bf16[4,32,2048]{2,1,0:T(8,128)(2,1)S(1)}, bf16[4,32,2048]{2,1,0:T(8,128)(2,1)S(1)}, u32[]{:S(2)}, u32[]{:S(2)}) collective-permute-start(bf16[4,32,2048]{2,1,0:T(8,128)(2,1)S(1)} %get-tuple-element.123), channel_id=1, source_target_pairs={{0,12},{4,0},{8,4},{12,8},{1,13},{5,1},{9,5},{13,9},{2,14},{6,2},{... | collective-permute-start | bytes 1572872 | tf_op jit(solution)/shard_map/ppermute | solution.py:21
  124.9 3.3 %collective-permute-start.30 = (bf16[4,32,2048]{2,1,0:T(8,128)(2,1)S(1)}, bf16[4,32,2048]{2,1,0:T(8,128)(2,1)S(1)}, u32[]{:S(2)}, u32[]{:S(2)}) collective-permute-start(bf16[4,32,2048]{2,1,0:T(8,128)(2,1)S(1)} %get-tuple-element.124), channel_id=1, source_target_pairs={{0,8},{4,12},{8,0},{12,4},{1,9},{5,13},{9,1},{13,5},{2,10},{6,14},... | collective-permute-start | bytes 1572872 | tf_op jit(solution)/shard_map/ppermute | solution.py:21
  128.2 6.5 %collective-permute-done.23.refs_5_ = bf16[4,32,2048]{2,1,0:T(8,128)(2,1)S(1)} collective-permute-done((bf16[4,32,2048]{2,1,0:T(8,128)(2,1)S(1)}, bf16[4,32,2048]{2,1,0:T(8,128)(2,1)S(1)}, u32[]{:S(2)}, u32[]{:S(2)}) %collective-permute-start.23) | collective-permute-done | bytes 524320 | tf_op jit(solution)/shard_map/ppermute | solution.py:21
  134.8 3.8 %collective-permute-done.25.refs_7_ = bf16[4,32,2048]{2,1,0:T(8,128)(2,1)S(1)} collective-permute-done((bf16[4,32,2048]{2,1,0:T(8,128)(2,1)S(1)}, bf16[4,32,2048]{2,1,0:T(8,128)(2,1)S(1)}, u32[]{:S(2)}, u32[]{:S(2)}) %collective-permute-start.25) | collective-permute-done | bytes 524320 | tf_op jit(solution)/shard_map/ppermute | solution.py:21
  138.9 6.2 %collective-permute-done.31.refs_15_ = bf16[4,32,2048]{2,1,0:T(8,128)(2,1)S(1)} collective-permute-done((bf16[4,32,2048]{2,1,0:T(8,128)(2,1)S(1)}, bf16[4,32,2048]{2,1,0:T(8,128)(2,1)S(1)}, u32[]{:S(2)}, u32[]{:S(2)}) %collective-permute-start.31) | collective-permute-done | bytes 524320 | tf_op jit(solution)/shard_map/ppermute | solution.py:21
  145.1 4.8 %shard_map.73 = (bf16[128,2048]{1,0:T(8,128)(2,1)}, bf16[128,2048]{1,0:T(8,128)(2,1)}, bf16[128,2048]{1,0:T(8,128)(2,1)}, bf16[128,2048]{1,0:T(8,128)(2,1)}, bf16[4,128,2048]{2,1,0:T(8,128)(2,1)}) custom-call(s32[12]{0:T(128)S(1)} %pad_add_fusion.experts_ref, bf16[4,32,2048]{2,1,0:T(8,128)(2,1)S(1)} %get-tuple-element.100.refs_0_, ...), custom_call_target="tpu_custom_call" | custom-call | flops 1073741824 | bytes 12582912 | tf_op jit(solution)/shard_map/pallas_call | solution.py:291
  149.9 5.1 %all-to-all-start = ((bf16[4,128,2048]{2,1,0:T(8,128)(2,1)}), bf16[4,128,2048]{2,1,0:T(8,128)(2,1)S(1)}, u32[]{:S(2)}, u32[]{:S(2)}) async-start(bf16[4,128,2048]{2,1,0:T(8,128)(2,1)} %get-tuple-element.130), calls=%async_computation | async-start | bytes 4194304 | tf_op jit(solution)/shard_map/all_to_all | solution.py:345
  157.4 7.7 %collective-permute-done.32 = bf16[128,2048]{1,0:T(8,128)(2,1)S(1)} collective-permute-done((bf16[128,2048]{1,0:T(8,128)(2,1)}, bf16[128,2048]{1,0:T(8,128)(2,1)S(1)}, u32[]{:S(2)}, u32[]{:S(2)}) %collective-permute-start.32) | collective-permute-done | bytes 524320 | tf_op jit(solution)/shard_map/ppermute | solution.py:21
  165.1 2.5 %collective-permute-done.33 = bf16[128,2048]{1,0:T(8,128)(2,1)S(1)} collective-permute-done((bf16[128,2048]{1,0:T(8,128)(2,1)}, bf16[128,2048]{1,0:T(8,128)(2,1)S(1)}, u32[]{:S(2)}, u32[]{:S(2)}) %collective-permute-start.33) | collective-permute-done | bytes 524320 | tf_op jit(solution)/shard_map/ppermute | solution.py:21
  167.6 5.0 %collective-permute-done.34 = bf16[128,2048]{1,0:T(8,128)(2,1)S(1)} collective-permute-done((bf16[128,2048]{1,0:T(8,128)(2,1)S(1)}, bf16[128,2048]{1,0:T(8,128)(2,1)S(1)}, u32[]{:S(2)}, u32[]{:S(2)}) %collective-permute-start.34) | collective-permute-done | bytes 524320 | tf_op jit(solution)/shard_map/ppermute | solution.py:21
  (64 shorter events, 22.1 us)
Async XLA Ops:
  1.8 14.8 %collective-permute-start.6 = (bf16[128,2176]{1,0:T(8,128)(2,1)S(1)}, bf16[128,2176]{1,0:T(8,128)(2,1)S(1)}, u32[]{:S(2)}, u32[]{:S(2)}) collective-permute-start(bf16[128,2176]{1,0:T(8,128)(2,1)S(1)} %get-tuple-element.73.refs_0_.refs_21_), channel_id=1, source_target_pairs={{0,3},{1,0},{2,1},{3,2},{4,7},{5,4},{6,5},{7,6},{8,11},{9,8},{10,9... | collective-permute-start | bytes 1671176 | tf_op jit(solution)/shard_map/ppermute | solution.py:21
  4.7 16.3 %collective-permute-start.4 = (bf16[128,2176]{1,0:T(8,128)(2,1)S(1)}, bf16[128,2176]{1,0:T(8,128)(2,1)S(1)}, u32[]{:S(2)}, u32[]{:S(2)}) collective-permute-start(bf16[128,2176]{1,0:T(8,128)(2,1)S(1)} %get-tuple-element.73.refs_0_.refs_21_), channel_id=1, source_target_pairs={{0,1},{1,2},{2,3},{3,0},{4,5},{5,6},{6,7},{7,4},{8,9},{9,10},{10,1... | collective-permute-start | bytes 1671176 | tf_op jit(solution)/shard_map/ppermute | solution.py:21
  4.8 17.1 %collective-permute-start.2 = (bf16[128,2176]{1,0:T(8,128)(2,1)S(1)}, bf16[128,2176]{1,0:T(8,128)(2,1)S(1)}, u32[]{:S(2)}, u32[]{:S(2)}) collective-permute-start(bf16[128,2176]{1,0:T(8,128)(2,1)S(1)} %get-tuple-element.68.refs_0_.refs_16_), channel_id=1, source_target_pairs={{0,12},{4,0},{8,4},{12,8},{1,13},{5,1},{9,5},{13,9},{2,14},{6,2},{... | collective-permute-start | bytes 1671176 | tf_op jit(solution)/shard_map/ppermute | solution.py:21
  8.8 17.8 %collective-permute-start = (bf16[128,2176]{1,0:T(8,128)(2,1)S(1)}, bf16[128,2176]{1,0:T(8,128)(2,1)S(1)}, u32[]{:S(2)}, u32[]{:S(2)}) collective-permute-start(bf16[128,2176]{1,0:T(8,128)(2,1)S(1)} %get-tuple-element.68.refs_0_.refs_16_), channel_id=1, source_target_pairs={{0,4},{4,8},{8,12},{12,0},{1,5},{5,9},{9,13},{13,1},{2,6},{6,10},{... | collective-permute-start | bytes 1671176 | tf_op jit(solution)/shard_map/ppermute | solution.py:21
  22.6 10.3 %collective-permute-start.3 = (bf16[64,2176]{1,0:T(8,128)(2,1)}, bf16[64,2176]{1,0:T(8,128)(2,1)}, u32[]{:S(2)}, u32[]{:S(2)}) collective-permute-start(bf16[64,2176]{1,0:T(8,128)(2,1)} %slice.17), channel_id=1, source_target_pairs={{0,12},{4,0},{8,4},{12,8},{1,13},{5,1},{9,5},{13,9},{2,14},{6,2},{... | collective-permute-start | bytes 835592 | tf_op jit(solution)/shard_map/ppermute | solution.py:21
  38.1 15.5 %collective-permute-start.8 = (bf16[4,32,2048]{2,1,0:T(8,128)(2,1)S(1)}, bf16[4,32,2048]{2,1,0:T(8,128)(2,1)S(1)}, u32[]{:S(2)}, u32[]{:S(2)}) collective-permute-start(bf16[4,32,2048]{2,1,0:T(8,128)(2,1)S(1)} %get-tuple-element.92), channel_id=1, source_target_pairs={{0,1},{1,2},{2,3},{3,0},{4,5},{5,6},{6,7},{7,4},{8,9},{9,10},{10,1... | collective-permute-start | bytes 1572872 | tf_op jit(solution)/shard_map/ppermute | solution.py:21
  38.2 29.3 %collective-permute-start.9 = (bf16[4,32,2048]{2,1,0:T(8,128)(2,1)S(1)}, bf16[4,32,2048]{2,1,0:T(8,128)(2,1)S(1)}, u32[]{:S(2)}, u32[]{:S(2)}) collective-permute-start(bf16[4,32,2048]{2,1,0:T(8,128)(2,1)S(1)} %get-tuple-element.93), channel_id=1, source_target_pairs={{0,2},{1,3},{2,0},{3,1},{4,6},{5,7},{6,4},{7,5},{8,10},{9,11},{10,... | collective-permute-start | bytes 1572872 | tf_op jit(solution)/shard_map/ppermute | solution.py:21
  42.6 25.0 %collective-permute-start.10 = (bf16[4,32,2048]{2,1,0:T(8,128)(2,1)S(1)}, bf16[4,32,2048]{2,1,0:T(8,128)(2,1)S(1)}, u32[]{:S(2)}, u32[]{:S(2)}) collective-permute-start(bf16[4,32,2048]{2,1,0:T(8,128)(2,1)S(1)} %get-tuple-element.94), channel_id=1, source_target_pairs={{0,3},{1,0},{2,1},{3,2},{4,7},{5,4},{6,5},{7,6},{8,11},{9,8},{10,9... | collective-permute-start | bytes 1572872 | tf_op jit(solution)/shard_map/ppermute | solution.py:21
  42.6 25.9 %collective-permute-start.11 = (bf16[4,32,2048]{2,1,0:T(8,128)(2,1)S(1)}, bf16[4,32,2048]{2,1,0:T(8,128)(2,1)S(1)}, u32[]{:S(2)}, u32[]{:S(2)}) collective-permute-start(bf16[4,32,2048]{2,1,0:T(8,128)(2,1)S(1)} %get-tuple-element.96), channel_id=1, source_target_pairs={{0,4},{4,8},{8,12},{12,0},{1,5},{5,9},{9,13},{13,1},{2,6},{6,10},{... | collective-permute-start | bytes 1572872 | tf_op jit(solution)/shard_map/ppermute | solution.py:21
  42.6 28.3 %collective-permute-start.12 = (bf16[4,32,2048]{2,1,0:T(8,128)(2,1)S(1)}, bf16[4,32,2048]{2,1,0:T(8,128)(2,1)S(1)}, u32[]{:S(2)}, u32[]{:S(2)}) collective-permute-start(bf16[4,32,2048]{2,1,0:T(8,128)(2,1)S(1)} %get-tuple-element.97), channel_id=1, source_target_pairs={{0,8},{4,12},{8,0},{12,4},{1,9},{5,13},{9,1},{13,5},{2,10},{6,14},... | collective-permute-start | bytes 1572872 | tf_op jit(solution)/shard_map/ppermute | solution.py:21
  53.6 17.3 %collective-permute-start.13 = (bf16[4,32,2048]{2,1,0:T(8,128)(2,1)S(1)}, bf16[4,32,2048]{2,1,0:T(8,128)(2,1)S(1)}, u32[]{:S(2)}, u32[]{:S(2)}) collective-permute-start(bf16[4,32,2048]{2,1,0:T(8,128)(2,1)S(1)} %get-tuple-element.98), channel_id=1, source_target_pairs={{0,12},{4,0},{8,4},{12,8},{1,13},{5,1},{9,5},{13,9},{2,14},{6,2},{... | collective-permute-start | bytes 1572872 | tf_op jit(solution)/shard_map/ppermute | solution.py:21
  67.5 19.1 %collective-permute-start.14 = (bf16[4,32,2048]{2,1,0:T(8,128)(2,1)S(1)}, bf16[4,32,2048]{2,1,0:T(8,128)(2,1)S(1)}, u32[]{:S(2)}, u32[]{:S(2)}) collective-permute-start(bf16[4,32,2048]{2,1,0:T(8,128)(2,1)S(1)} %get-tuple-element.102), channel_id=1, source_target_pairs={{0,1},{1,2},{2,3},{3,0},{4,5},{5,6},{6,7},{7,4},{8,9},{9,10},{10,1... | collective-permute-start | bytes 1572872 | tf_op jit(solution)/shard_map/ppermute | solution.py:21
  67.6 25.5 %collective-permute-start.15 = (bf16[4,32,2048]{2,1,0:T(8,128)(2,1)S(1)}, bf16[4,32,2048]{2,1,0:T(8,128)(2,1)S(1)}, u32[]{:S(2)}, u32[]{:S(2)}) collective-permute-start(bf16[4,32,2048]{2,1,0:T(8,128)(2,1)S(1)} %get-tuple-element.103), channel_id=1, source_target_pairs={{0,2},{1,3},{2,0},{3,1},{4,6},{5,7},{6,4},{7,5},{8,10},{9,11},{10,... | collective-permute-start | bytes 1572872 | tf_op jit(solution)/shard_map/ppermute | solution.py:21
  68.5 24.8 %collective-permute-start.16 = (bf16[4,32,2048]{2,1,0:T(8,128)(2,1)S(1)}, bf16[4,32,2048]{2,1,0:T(8,128)(2,1)S(1)}, u32[]{:S(2)}, u32[]{:S(2)}) collective-permute-start(bf16[4,32,2048]{2,1,0:T(8,128)(2,1)S(1)} %get-tuple-element.104), channel_id=1, source_target_pairs={{0,3},{1,0},{2,1},{3,2},{4,7},{5,4},{6,5},{7,6},{8,11},{9,8},{10,9... | collective-permute-start | bytes 1572872 | tf_op jit(solution)/shard_map/ppermute | solution.py:21
  70.9 23.5 %collective-permute-start.17 = (bf16[4,32,2048]{2,1,0:T(8,128)(2,1)S(1)}, bf16[4,32,2048]{2,1,0:T(8,128)(2,1)S(1)}, u32[]{:S(2)}, u32[]{:S(2)}) collective-permute-start(bf16[4,32,2048]{2,1,0:T(8,128)(2,1)S(1)} %get-tuple-element.106), channel_id=1, source_target_pairs={{0,4},{4,8},{8,12},{12,0},{1,5},{5,9},{9,13},{13,1},{2,6},{6,10},{... | collective-permute-start | bytes 1572872 | tf_op jit(solution)/shard_map/ppermute | solution.py:21
  70.9 24.8 %collective-permute-start.19 = (bf16[4,32,2048]{2,1,0:T(8,128)(2,1)S(1)}, bf16[4,32,2048]{2,1,0:T(8,128)(2,1)S(1)}, u32[]{:S(2)}, u32[]{:S(2)}) collective-permute-start(bf16[4,32,2048]{2,1,0:T(8,128)(2,1)S(1)} %get-tuple-element.108), channel_id=1, source_target_pairs={{0,12},{4,0},{8,4},{12,8},{1,13},{5,1},{9,5},{13,9},{2,14},{6,2},{... | collective-permute-start | bytes 1572872 | tf_op jit(solution)/shard_map/ppermute | solution.py:21
  86.6 12.4 %collective-permute-start.18 = (bf16[4,32,2048]{2,1,0:T(8,128)(2,1)S(1)}, bf16[4,32,2048]{2,1,0:T(8,128)(2,1)S(1)}, u32[]{:S(2)}, u32[]{:S(2)}) collective-permute-start(bf16[4,32,2048]{2,1,0:T(8,128)(2,1)S(1)} %get-tuple-element.107), channel_id=1, source_target_pairs={{0,8},{4,12},{8,0},{12,4},{1,9},{5,13},{9,1},{13,5},{2,10},{6,14},... | collective-permute-start | bytes 1572872 | tf_op jit(solution)/shard_map/ppermute | solution.py:21
  93.2 16.7 %collective-permute-start.20 = (bf16[4,32,2048]{2,1,0:T(8,128)(2,1)S(1)}, bf16[4,32,2048]{2,1,0:T(8,128)(2,1)S(1)}, u32[]{:S(2)}, u32[]{:S(2)}) collective-permute-start(bf16[4,32,2048]{2,1,0:T(8,128)(2,1)S(1)} %get-tuple-element.109), channel_id=1, source_target_pairs={{0,3},{1,0},{2,1},{3,2},{4,7},{5,4},{6,5},{7,6},{8,11},{9,8},{10,9... | collective-permute-start | bytes 1572872 | tf_op jit(solution)/shard_map/ppermute | solution.py:21
  93.2 24.6 %collective-permute-start.21 = (bf16[4,32,2048]{2,1,0:T(8,128)(2,1)S(1)}, bf16[4,32,2048]{2,1,0:T(8,128)(2,1)S(1)}, u32[]{:S(2)}, u32[]{:S(2)}) collective-permute-start(bf16[4,32,2048]{2,1,0:T(8,128)(2,1)S(1)} %get-tuple-element.111), channel_id=1, source_target_pairs={{0,2},{1,3},{2,0},{3,1},{4,6},{5,7},{6,4},{7,5},{8,10},{9,11},{10,... | collective-permute-start | bytes 1572872 | tf_op jit(solution)/shard_map/ppermute | solution.py:21
  94.4 25.8 %collective-permute-start.22 = (bf16[4,32,2048]{2,1,0:T(8,128)(2,1)S(1)}, bf16[4,32,2048]{2,1,0:T(8,128)(2,1)S(1)}, u32[]{:S(2)}, u32[]{:S(2)}) collective-permute-start(bf16[4,32,2048]{2,1,0:T(8,128)(2,1)S(1)} %get-tuple-element.112), channel_id=1, source_target_pairs={{0,1},{1,2},{2,3},{3,0},{4,5},{5,6},{6,7},{7,4},{8,9},{9,10},{10,1... | collective-permute-start | bytes 1572872 | tf_op jit(solution)/shard_map/ppermute | solution.py:21
  95.7 26.0 %collective-permute-start.26 = (bf16[4,32,2048]{2,1,0:T(8,128)(2,1)S(1)}, bf16[4,32,2048]{2,1,0:T(8,128)(2,1)S(1)}, u32[]{:S(2)}, u32[]{:S(2)}) collective-permute-start(bf16[4,32,2048]{2,1,0:T(8,128)(2,1)S(1)} %get-tuple-element.119), channel_id=1, source_target_pairs={{0,12},{4,0},{8,4},{12,8},{1,13},{5,1},{9,5},{13,9},{2,14},{6,2},{... | collective-permute-start | bytes 1572872 | tf_op jit(solution)/shard_map/ppermute | solution.py:21
  99.0 24.0 %collective-permute-start.27 = (bf16[4,32,2048]{2,1,0:T(8,128)(2,1)S(1)}, bf16[4,32,2048]{2,1,0:T(8,128)(2,1)S(1)}, u32[]{:S(2)}, u32[]{:S(2)}) collective-permute-start(bf16[4,32,2048]{2,1,0:T(8,128)(2,1)S(1)} %get-tuple-element.120), channel_id=1, source_target_pairs={{0,8},{4,12},{8,0},{12,4},{1,9},{5,13},{9,1},{13,5},{2,10},{6,14},... | collective-permute-start | bytes 1572872 | tf_op jit(solution)/shard_map/ppermute | solution.py:21
  109.9 15.1 %collective-permute-start.28 = (bf16[4,32,2048]{2,1,0:T(8,128)(2,1)S(1)}, bf16[4,32,2048]{2,1,0:T(8,128)(2,1)S(1)}, u32[]{:S(2)}, u32[]{:S(2)}) collective-permute-start(bf16[4,32,2048]{2,1,0:T(8,128)(2,1)S(1)} %get-tuple-element.121), channel_id=1, source_target_pairs={{0,4},{4,8},{8,12},{12,0},{1,5},{5,9},{9,13},{13,1},{2,6},{6,10},{... | collective-permute-start | bytes 1572872 | tf_op jit(solution)/shard_map/ppermute | solution.py:21
  117.8 16.9 %collective-permute-start.23 = (bf16[4,32,2048]{2,1,0:T(8,128)(2,1)S(1)}, bf16[4,32,2048]{2,1,0:T(8,128)(2,1)S(1)}, u32[]{:S(2)}, u32[]{:S(2)}) collective-permute-start(bf16[4,32,2048]{2,1,0:T(8,128)(2,1)S(1)} %get-tuple-element.115), channel_id=1, source_target_pairs={{0,3},{1,0},{2,1},{3,2},{4,7},{5,4},{6,5},{7,6},{8,11},{9,8},{10,9... | collective-permute-start | bytes 1572872 | tf_op jit(solution)/shard_map/ppermute | solution.py:21
  120.2 14.6 %collective-permute-start.24 = (bf16[4,32,2048]{2,1,0:T(8,128)(2,1)S(1)}, bf16[4,32,2048]{2,1,0:T(8,128)(2,1)S(1)}, u32[]{:S(2)}, u32[]{:S(2)}) collective-permute-start(bf16[4,32,2048]{2,1,0:T(8,128)(2,1)S(1)} %get-tuple-element.116), channel_id=1, source_target_pairs={{0,2},{1,3},{2,0},{3,1},{4,6},{5,7},{6,4},{7,5},{8,10},{9,11},{10,... | collective-permute-start | bytes 1572872 | tf_op jit(solution)/shard_map/ppermute | solution.py:21
  121.7 16.8 %collective-permute-start.25 = (bf16[4,32,2048]{2,1,0:T(8,128)(2,1)S(1)}, bf16[4,32,2048]{2,1,0:T(8,128)(2,1)S(1)}, u32[]{:S(2)}, u32[]{:S(2)}) collective-permute-start(bf16[4,32,2048]{2,1,0:T(8,128)(2,1)S(1)} %get-tuple-element.117), channel_id=1, source_target_pairs={{0,1},{1,2},{2,3},{3,0},{4,5},{5,6},{6,7},{7,4},{8,9},{9,10},{10,1... | collective-permute-start | bytes 1572872 | tf_op jit(solution)/shard_map/ppermute | solution.py:21
  123.0 15.9 %collective-permute-start.29 = (bf16[4,32,2048]{2,1,0:T(8,128)(2,1)S(1)}, bf16[4,32,2048]{2,1,0:T(8,128)(2,1)S(1)}, u32[]{:S(2)}, u32[]{:S(2)}) collective-permute-start(bf16[4,32,2048]{2,1,0:T(8,128)(2,1)S(1)} %get-tuple-element.123), channel_id=1, source_target_pairs={{0,12},{4,0},{8,4},{12,8},{1,13},{5,1},{9,5},{13,9},{2,14},{6,2},{... | collective-permute-start | bytes 1572872 | tf_op jit(solution)/shard_map/ppermute | solution.py:21
  124.9 14.0 %collective-permute-start.30 = (bf16[4,32,2048]{2,1,0:T(8,128)(2,1)S(1)}, bf16[4,32,2048]{2,1,0:T(8,128)(2,1)S(1)}, u32[]{:S(2)}, u32[]{:S(2)}) collective-permute-start(bf16[4,32,2048]{2,1,0:T(8,128)(2,1)S(1)} %get-tuple-element.124), channel_id=1, source_target_pairs={{0,8},{4,12},{8,0},{12,4},{1,9},{5,13},{9,1},{13,5},{2,10},{6,14},... | collective-permute-start | bytes 1572872 | tf_op jit(solution)/shard_map/ppermute | solution.py:21
  134.7 10.4 %collective-permute-start.31 = (bf16[4,32,2048]{2,1,0:T(8,128)(2,1)S(1)}, bf16[4,32,2048]{2,1,0:T(8,128)(2,1)S(1)}, u32[]{:S(2)}, u32[]{:S(2)}) collective-permute-start(bf16[4,32,2048]{2,1,0:T(8,128)(2,1)S(1)} %get-tuple-element.125), channel_id=1, source_target_pairs={{0,4},{4,8},{8,12},{12,0},{1,5},{5,9},{9,13},{13,1},{2,6},{6,10},{... | collective-permute-start | bytes 1572872 | tf_op jit(solution)/shard_map/ppermute | solution.py:21
  149.9 23.1 %all-to-all-start = ((bf16[4,128,2048]{2,1,0:T(8,128)(2,1)}), bf16[4,128,2048]{2,1,0:T(8,128)(2,1)S(1)}, u32[]{:S(2)}, u32[]{:S(2)}) async-start(bf16[4,128,2048]{2,1,0:T(8,128)(2,1)} %get-tuple-element.130), calls=%async_computation | async-start | bytes 4194304 | tf_op jit(solution)/shard_map/all_to_all | solution.py:345
  156.6 11.0 %collective-permute-start.33 = (bf16[128,2048]{1,0:T(8,128)(2,1)}, bf16[128,2048]{1,0:T(8,128)(2,1)S(1)}, u32[]{:S(2)}, u32[]{:S(2)}) collective-permute-start(bf16[128,2048]{1,0:T(8,128)(2,1)} %get-tuple-element.128), channel_id=1, source_target_pairs={{0,8},{4,12},{8,0},{12,4},{1,9},{5,13},{9,1},{13,5},{2,10},{6,14},... | collective-permute-start | bytes 1572872 | tf_op jit(solution)/shard_map/ppermute | solution.py:21
  156.6 16.0 %collective-permute-start.34 = (bf16[128,2048]{1,0:T(8,128)(2,1)S(1)}, bf16[128,2048]{1,0:T(8,128)(2,1)S(1)}, u32[]{:S(2)}, u32[]{:S(2)}) collective-permute-start(bf16[128,2048]{1,0:T(8,128)(2,1)S(1)} %copy-done.1), channel_id=1, source_target_pairs={{0,4},{4,8},{8,12},{12,0},{1,5},{5,9},{9,13},{13,1},{2,6},{6,10},{... | collective-permute-start | bytes 1572872 | tf_op jit(solution)/shard_map/ppermute | solution.py:21
  (6 other events, 66.9 us)

commit v11 on v8

--- a/solution.py
+++ b/solution.py
@@ -323,7 +323,9 @@
             b_back += b_home
         a_in, b_in = both_ways(a_out, b_out, "x", "z", 1)
         hidden = hidden_rows(w_gate, w_up, a_in, b_in)
-    hidden, a_back[1] = lax.optimization_barrier((hidden, a_back[1]))
+    hidden, a_back[1], a_back[3] = lax.optimization_barrier(
+        (hidden, a_back[1], a_back[3])
+    )
     a_done, b_done = down_rows(hidden, w_down)
     a_home, b_home = both_ways(a_done, b_done, "x", "z", -1)
     a_back += a_home

time: 175 us -> 174 us (level)
  starting transfers between devices: 60.7 us -> 58.5 us
  waiting for transfers between devices: 59.7 us -> 61.5 us
    ppermute x35, starting transfers between devices: 55.6 us -> 53.5 us  [shift(): lax.ppermute(block, axis, [(i, (i + step) % SIDE) for i in range(SIDE)])]
    ppermute x35, waiting for transfers between devices: 59.7 us -> 61.5 us  [shift(): lax.ppermute(block, axis, [(i, (i + step) % SIDE) for i in range(SIDE)])]
  transfers between devices with their start and end apart: 36 -> 36, of which waited for: 12 -> 13; matrix products, arithmetic and copies ran while one was open for 2% -> 2% of each run, Pallas kernels for 23% -> 23%
where the time goes in v11:
time: 174 us; the launch traced here: 173 us
  waiting for transfers between devices  61.5 us (35%)
  starting transfers between devices  58.5 us (34%)
  Pallas kernels  48.1 us (28%)
  local copies, waits for them, and re-layouts  2.97 us (2%)
  other arithmetic  1.9 us (1%)
    ppermute x35, waiting for transfers between devices, shift(): lax.ppermute(block, axis, [(i, (i + step) % SIDE) for i in range(SIDE)])  61.5 us
    ppermute x35, starting transfers between devices, shift(): lax.ppermute(block, axis, [(i, (i + step) % SIDE) for i in range(SIDE)])  53.5 us
    pallas_call x2, Pallas kernels, hidden_rows(): pl.pallas_call(hidden_kernel, grid=(ff // FF_TILE,), in_specs=[weight, we...  19.5 us
    pallas_call x2, Pallas kernels, down_rows(): pl.pallas_call(functools.partial(down_kernel, n_half), grid=(2 * n_half,)...  13.1 us
    pallas_call x4, Pallas kernels, pack(): pl.pallas_call(functools.partial(pack_kernel, chunk, top), in_specs=[pl.B...  8.96 us
    all_to_all x1, starting transfers between devices, local(): b_home = lax.all_to_all(b_sums, 'x', 0, 0, tiled=True)  5.05 us
    pallas_call x1, Pallas kernels, sum_rows(): pl.pallas_call(functools.partial(sum_kernel, top, counts), grid=(1,), in_...  4.8 us
  transfers between devices with their start and end apart: 36, of which 13 were waited for; matrix products, arithmetic and copies ran while one was open for 2% of the time, Pallas kernels for 23%

profile of v11, /device:TPU:0, one launch (start us, length us, event | category | flops | bytes accessed | tf_op | source)
XLA Modules:
  0.0 173.2 jit_solution(12815022847275441939)
XLA Ops:
  1.8 2.9 %collective-permute-start.6 = (bf16[128,2176]{1,0:T(8,128)(2,1)S(1)}, bf16[128,2176]{1,0:T(8,128)(2,1)S(1)}, u32[]{:S(2)}, u32[]{:S(2)}) collective-permute-start(bf16[128,2176]{1,0:T(8,128)(2,1)S(1)} %get-tuple-element.74.refs_0_.refs_21_), channel_id=1, source_target_pairs={{0,3},{1,0},{2,1},{3,2},{4,7},{5,4},{6,5},{7,6},{8,11},{9,8},{10,9... | collective-permute-start | bytes 1671176 | tf_op jit(solution)/shard_map/ppermute | solution.py:21
  4.8 4.0 %collective-permute-start.2 = (bf16[128,2176]{1,0:T(8,128)(2,1)S(1)}, bf16[128,2176]{1,0:T(8,128)(2,1)S(1)}, u32[]{:S(2)}, u32[]{:S(2)}) collective-permute-start(bf16[128,2176]{1,0:T(8,128)(2,1)S(1)} %get-tuple-element.69.refs_0_.refs_16_), channel_id=1, source_target_pairs={{0,12},{4,0},{8,4},{12,8},{1,13},{5,1},{9,5},{13,9},{2,14},{6,2},{... | collective-permute-start | bytes 1671176 | tf_op jit(solution)/shard_map/ppermute | solution.py:21
  8.8 7.8 %collective-permute-done.6.refs_4_.refs_25_ = bf16[128,2176]{1,0:T(8,128)(2,1)S(1)} collective-permute-done((bf16[128,2176]{1,0:T(8,128)(2,1)S(1)}, bf16[128,2176]{1,0:T(8,128)(2,1)S(1)}, u32[]{:S(2)}, u32[]{:S(2)}) %collective-permute-start.6) | collective-permute-done | bytes 557088 | tf_op jit(solution)/shard_map/ppermute | solution.py:21
  17.4 3.7 %collective-permute-start.7 = (bf16[64,2176]{1,0:T(8,128)(2,1)}, bf16[64,2176]{1,0:T(8,128)(2,1)}, u32[]{:S(2)}, u32[]{:S(2)}) collective-permute-start(bf16[64,2176]{1,0:T(8,128)(2,1)} %slice.19), channel_id=1, source_target_pairs={{0,3},{1,0},{2,1},{3,2},{4,7},{5,4},{6,5},{7,6},{8,11},{9,8},{10,9... | collective-permute-start | bytes 835592 | tf_op jit(solution)/shard_map/ppermute | solution.py:21
  22.6 4.0 %collective-permute-start.3 = (bf16[64,2176]{1,0:T(8,128)(2,1)}, bf16[64,2176]{1,0:T(8,128)(2,1)}, u32[]{:S(2)}, u32[]{:S(2)}) collective-permute-start(bf16[64,2176]{1,0:T(8,128)(2,1)} %slice.17), channel_id=1, source_target_pairs={{0,12},{4,0},{8,4},{12,8},{1,13},{5,1},{9,5},{13,9},{2,14},{6,2},{... | collective-permute-start | bytes 835592 | tf_op jit(solution)/shard_map/ppermute | solution.py:21
  27.4 3.2 %collective-permute-done.5.refs_2_.refs_23_ = bf16[64,2176]{1,0:T(8,128)(2,1)} collective-permute-done((bf16[64,2176]{1,0:T(8,128)(2,1)}, bf16[64,2176]{1,0:T(8,128)(2,1)}, u32[]{:S(2)}, u32[]{:S(2)}) %collective-permute-start.5) | collective-permute-done | bytes 278560 | tf_op jit(solution)/shard_map/ppermute | solution.py:21
  30.6 2.2 %shard_map.66 = (bf16[4,32,2048]{2,1,0:T(8,128)(2,1)S(1)}, bf16[4,32,2048]{2,1,0:T(8,128)(2,1)S(1)}, bf16[4,32,2048]{2,1,0:T(8,128)(2,1)S(1)}, bf16[4,32,2048]{2,1,0:T(8,128)(2,1)S(1)}) custom-call(s32[4]{0:T(128)S(1)} %get-tuple-element.90.experts_ref, bf16[128,2176]{1,0:T(8,128)(2,1)S(1)} %get-tuple-element.74.refs_0_.refs_21_, ...), custom_call_target="tpu_custom_call" | custom-call | flops 268435456 | bytes 4194304 | tf_op jit(solution)/shard_map/pallas_call | solution.py:137
  32.8 3.0 %collective-permute-done.1.refs_2_.refs_18_ = bf16[64,2176]{1,0:T(8,128)(2,1)} collective-permute-done((bf16[64,2176]{1,0:T(8,128)(2,1)}, bf16[64,2176]{1,0:T(8,128)(2,1)}, u32[]{:S(2)}, u32[]{:S(2)}) %collective-permute-start.1) | collective-permute-done | bytes 278560 | tf_op jit(solution)/shard_map/ppermute | solution.py:21
  35.8 2.2 %shard_map.65 = (bf16[4,32,2048]{2,1,0:T(8,128)(2,1)S(1)}, bf16[4,32,2048]{2,1,0:T(8,128)(2,1)S(1)}, bf16[4,32,2048]{2,1,0:T(8,128)(2,1)S(1)}, bf16[4,32,2048]{2,1,0:T(8,128)(2,1)S(1)}) custom-call(s32[4]{0:T(128)S(1)} %get-tuple-element.89.experts_ref, bf16[128,2176]{1,0:T(8,128)(2,1)S(1)} %get-tuple-element.69.refs_0_.refs_16_, ...), custom_call_target="tpu_custom_call" | custom-call | flops 268435456 | bytes 4194304 | tf_op jit(solution)/shard_map/pallas_call | solution.py:137
  38.2 4.4 %collective-permute-start.9 = (bf16[4,32,2048]{2,1,0:T(8,128)(2,1)S(1)}, bf16[4,32,2048]{2,1,0:T(8,128)(2,1)S(1)}, u32[]{:S(2)}, u32[]{:S(2)}) collective-permute-start(bf16[4,32,2048]{2,1,0:T(8,128)(2,1)S(1)} %get-tuple-element.94), channel_id=1, source_target_pairs={{0,2},{1,3},{2,0},{3,1},{4,6},{5,7},{6,4},{7,5},{8,10},{9,11},{10,... | collective-permute-start | bytes 1572872 | tf_op jit(solution)/shard_map/ppermute | solution.py:21
  43.9 9.7 %collective-permute-done.8.refs_1_ = bf16[4,32,2048]{2,1,0:T(8,128)(2,1)S(1)} collective-permute-done((bf16[4,32,2048]{2,1,0:T(8,128)(2,1)S(1)}, bf16[4,32,2048]{2,1,0:T(8,128)(2,1)S(1)}, u32[]{:S(2)}, u32[]{:S(2)}) %collective-permute-start.8) | collective-permute-done | bytes 524320 | tf_op jit(solution)/shard_map/ppermute | solution.py:21
  53.6 9.4 %collective-permute-start.13 = (bf16[4,32,2048]{2,1,0:T(8,128)(2,1)S(1)}, bf16[4,32,2048]{2,1,0:T(8,128)(2,1)S(1)}, u32[]{:S(2)}, u32[]{:S(2)}) collective-permute-start(bf16[4,32,2048]{2,1,0:T(8,128)(2,1)S(1)} %get-tuple-element.99), channel_id=1, source_target_pairs={{0,12},{4,0},{8,4},{12,8},{1,13},{5,1},{9,5},{13,9},{2,14},{6,2},{... | collective-permute-start | bytes 1572872 | tf_op jit(solution)/shard_map/ppermute | solution.py:21
  63.0 2.2 %shard_map.67 = (bf16[4,32,2048]{2,1,0:T(8,128)(2,1)S(1)}, bf16[4,32,2048]{2,1,0:T(8,128)(2,1)S(1)}, bf16[4,32,2048]{2,1,0:T(8,128)(2,1)S(1)}, bf16[4,32,2048]{2,1,0:T(8,128)(2,1)S(1)}) custom-call(s32[4]{0:T(128)S(1)} %get-tuple-element.89.experts_ref, bf16[128,2176]{1,0:T(8,128)(2,1)S(1)} %get-tuple-element.69.refs_0_.refs_16_, ...), custom_call_target="tpu_custom_call" | custom-call | flops 268435456 | bytes 4194304 | tf_op jit(solution)/shard_map/pallas_call | solution.py:137
  65.3 2.2 %shard_map.68 = (bf16[4,32,2048]{2,1,0:T(8,128)(2,1)S(1)}, bf16[4,32,2048]{2,1,0:T(8,128)(2,1)S(1)}, bf16[4,32,2048]{2,1,0:T(8,128)(2,1)S(1)}, bf16[4,32,2048]{2,1,0:T(8,128)(2,1)S(1)}) custom-call(s32[4]{0:T(128)S(1)} %get-tuple-element.90.experts_ref, bf16[128,2176]{1,0:T(8,128)(2,1)S(1)} %get-tuple-element.74.refs_0_.refs_21_, ...), custom_call_target="tpu_custom_call" | custom-call | flops 268435456 | bytes 4194304 | tf_op jit(solution)/shard_map/pallas_call | solution.py:137
  68.5 2.4 %collective-permute-start.16 = (bf16[4,32,2048]{2,1,0:T(8,128)(2,1)S(1)}, bf16[4,32,2048]{2,1,0:T(8,128)(2,1)S(1)}, u32[]{:S(2)}, u32[]{:S(2)}) collective-permute-start(bf16[4,32,2048]{2,1,0:T(8,128)(2,1)S(1)} %get-tuple-element.105), channel_id=1, source_target_pairs={{0,3},{1,0},{2,1},{3,2},{4,7},{5,4},{6,5},{7,6},{8,11},{9,8},{10,9... | collective-permute-start | bytes 1572872 | tf_op jit(solution)/shard_map/ppermute | solution.py:21
  70.9 3.6 %collective-permute-start.19 = (bf16[4,32,2048]{2,1,0:T(8,128)(2,1)S(1)}, bf16[4,32,2048]{2,1,0:T(8,128)(2,1)S(1)}, u32[]{:S(2)}, u32[]{:S(2)}) collective-permute-start(bf16[4,32,2048]{2,1,0:T(8,128)(2,1)S(1)} %get-tuple-element.109), channel_id=1, source_target_pairs={{0,12},{4,0},{8,4},{12,8},{1,13},{5,1},{9,5},{13,9},{2,14},{6,2},{... | collective-permute-start | bytes 1572872 | tf_op jit(solution)/shard_map/ppermute | solution.py:21
  74.5 9.7 %shard_map.69.hidden_ref = bf16[512,768]{1,0:T(8,128)(2,1)S(1)} custom-call(bf16[4096,768]{1,0:T(8,128)(2,1)} %bitcast.7, bf16[4096,768]{1,0:T(8,128)(2,1)} %bitcast.9, bf16[4,32,2048]{2,1,0:T(8,128)(2,1)S(1)} %get-tuple-element.92.refs_0_, bf16[4,32,2048]{2,1,0:T(8,128)(2,1)S(1)} %collective-permute-done.8.refs_1_, ...), custom_call_target="tpu_custom_call" | custom-call | flops 6442450944 | bytes 16777216 | tf_op jit(solution)/shard_map/pallas_call | solution.py:183
  84.2 2.4 %collective-permute-done.14.refs_1_ = bf16[4,32,2048]{2,1,0:T(8,128)(2,1)S(1)} collective-permute-done((bf16[4,32,2048]{2,1,0:T(8,128)(2,1)S(1)}, bf16[4,32,2048]{2,1,0:T(8,128)(2,1)S(1)}, u32[]{:S(2)}, u32[]{:S(2)}) %collective-permute-start.14) | collective-permute-done | bytes 524320 | tf_op jit(solution)/shard_map/ppermute | solution.py:21
  86.6 6.5 %shard_map.70 = (bf16[4,32,2048]{2,1,0:T(8,128)(2,1)S(1)}, bf16[4,32,2048]{2,1,0:T(8,128)(2,1)S(1)}, bf16[4,32,2048]{2,1,0:T(8,128)(2,1)S(1)}, bf16[4,32,2048]{2...) custom-call(bf16[512,768]{1,0:T(8,128)(2,1)S(1)} %shard_map.69.hidde, ...), custom_call_target="tpu_custom_call" | custom-call | flops 3221225472 | bytes 10485760 | tf_op jit(solution)/shard_map/pallas_call | solution.py:226
  93.2 2.0 %collective-permute-start.21 = (bf16[4,32,2048]{2,1,0:T(8,128)(2,1)S(1)}, bf16[4,32,2048]{2,1,0:T(8,128)(2,1)S(1)}, u32[]{:S(2)}, u32[]{:S(2)}) collective-permute-start(bf16[4,32,2048]{2,1,0:T(8,128)(2,1)S(1)} %get-tuple-element.111), channel_id=1, source_target_pairs={{0,1},{1,2},{2,3},{3,0},{4,5},{5,6},{6,7},{7,4},{8,9},{9,10},{10,1... | collective-permute-start | bytes 1572872 | tf_op jit(solution)/shard_map/ppermute | solution.py:21
  95.5 1.9 %collective-permute-start.26 = (bf16[4,32,2048]{2,1,0:T(8,128)(2,1)S(1)}, bf16[4,32,2048]{2,1,0:T(8,128)(2,1)S(1)}, u32[]{:S(2)}, u32[]{:S(2)}) collective-permute-start(bf16[4,32,2048]{2,1,0:T(8,128)(2,1)S(1)} %get-tuple-element.121), channel_id=1, source_target_pairs={{0,12},{4,0},{8,4},{12,8},{1,13},{5,1},{9,5},{13,9},{2,14},{6,2},{... | collective-permute-start | bytes 1572872 | tf_op jit(solution)/shard_map/ppermute | solution.py:21
  99.1 9.7 %shard_map.71.hidden_ref = bf16[512,768]{1,0:T(8,128)(2,1)S(1)} custom-call(bf16[4096,768]{1,0:T(8,128)(2,1)} %bitcast.8, bf16[4096,768]{1,0:T(8,128)(2,1)} %bitcast.10, bf16[4,32,2048]{2,1,0:T(8,128)(2,1)S(1)} %get-tuple-element.102.refs_0_, bf16[4,32,2048]{2,1,0:T(8,128)(2,1)S(1)} %collective-permute-done.14.refs_1_, ...), custom_call_target="tpu_custom_call" | custom-call | flops 6442450944 | bytes 16777216 | tf_op jit(solution)/shard_map/pallas_call | solution.py:183
  110.3 6.5 %shard_map.72 = (bf16[4,32,2048]{2,1,0:T(8,128)(2,1)S(1)}, bf16[4,32,2048]{2,1,0:T(8,128)(2,1)S(1)}, bf16[4,32,2048]{2,1,0:T(8,128)(2,1)S(1)}, bf16[4,32,2048]{2...) custom-call(bf16[512,768]{1,0:T(8,128)(2,1)S(1)} %shard_map.71.hidde, ...), custom_call_target="tpu_custom_call" | custom-call | flops 3221225472 | bytes 10485760 | tf_op jit(solution)/shard_map/pallas_call | solution.py:226
  116.8 2.6 %collective-permute-start.23 = (bf16[4,32,2048]{2,1,0:T(8,128)(2,1)S(1)}, bf16[4,32,2048]{2,1,0:T(8,128)(2,1)S(1)}, u32[]{:S(2)}, u32[]{:S(2)}) collective-permute-start(bf16[4,32,2048]{2,1,0:T(8,128)(2,1)S(1)} %get-tuple-element.117), channel_id=1, source_target_pairs={{0,3},{1,0},{2,1},{3,2},{4,7},{5,4},{6,5},{7,6},{8,11},{9,8},{10,9... | collective-permute-start | bytes 1572872 | tf_op jit(solution)/shard_map/ppermute | solution.py:21
  121.6 3.3 %collective-permute-start.29 = (bf16[4,32,2048]{2,1,0:T(8,128)(2,1)S(1)}, bf16[4,32,2048]{2,1,0:T(8,128)(2,1)S(1)}, u32[]{:S(2)}, u32[]{:S(2)}) collective-permute-start(bf16[4,32,2048]{2,1,0:T(8,128)(2,1)S(1)} %get-tuple-element.125), channel_id=1, source_target_pairs={{0,12},{4,0},{8,4},{12,8},{1,13},{5,1},{9,5},{13,9},{2,14},{6,2},{... | collective-permute-start | bytes 1572872 | tf_op jit(solution)/shard_map/ppermute | solution.py:21
  125.0 9.6 %collective-permute-done.23.refs_5_ = bf16[4,32,2048]{2,1,0:T(8,128)(2,1)S(1)} collective-permute-done((bf16[4,32,2048]{2,1,0:T(8,128)(2,1)S(1)}, bf16[4,32,2048]{2,1,0:T(8,128)(2,1)S(1)}, u32[]{:S(2)}, u32[]{:S(2)}) %collective-permute-start.23) | collective-permute-done | bytes 524320 | tf_op jit(solution)/shard_map/ppermute | solution.py:21
  134.7 3.3 %collective-permute-done.25.refs_7_ = bf16[4,32,2048]{2,1,0:T(8,128)(2,1)S(1)} collective-permute-done((bf16[4,32,2048]{2,1,0:T(8,128)(2,1)S(1)}, bf16[4,32,2048]{2,1,0:T(8,128)(2,1)S(1)}, u32[]{:S(2)}, u32[]{:S(2)}) %collective-permute-start.25) | collective-permute-done | bytes 524320 | tf_op jit(solution)/shard_map/ppermute | solution.py:21
  139.4 5.6 %collective-permute-done.31.refs_15_ = bf16[4,32,2048]{2,1,0:T(8,128)(2,1)S(1)} collective-permute-done((bf16[4,32,2048]{2,1,0:T(8,128)(2,1)S(1)}, bf16[4,32,2048]{2,1,0:T(8,128)(2,1)S(1)}, u32[]{:S(2)}, u32[]{:S(2)}) %collective-permute-start.31) | collective-permute-done | bytes 524320 | tf_op jit(solution)/shard_map/ppermute | solution.py:21
  145.0 4.8 %shard_map.73 = (bf16[128,2048]{1,0:T(8,128)(2,1)}, bf16[128,2048]{1,0:T(8,128)(2,1)}, bf16[128,2048]{1,0:T(8,128)(2,1)}, bf16[128,2048]{1,0:T(8,128)(2,1)}, bf16[4,128,2048]{2,1,0:T(8,128)(2,1)}) custom-call(s32[12]{0:T(128)S(1)} %pad_add_fusion.experts_ref, bf16[4,32,2048]{2,1,0:T(8,128)(2,1)S(1)} %get-tuple-element.101.refs_0_, ...), custom_call_target="tpu_custom_call" | custom-call | flops 1073741824 | bytes 12582912 | tf_op jit(solution)/shard_map/pallas_call | solution.py:280
  149.8 5.1 %all-to-all-start = ((bf16[4,128,2048]{2,1,0:T(8,128)(2,1)}), bf16[4,128,2048]{2,1,0:T(8,128)(2,1)S(1)}, u32[]{:S(2)}, u32[]{:S(2)}) async-start(bf16[4,128,2048]{2,1,0:T(8,128)(2,1)} %get-tuple-element.132), calls=%async_computation | async-start | bytes 4194304 | tf_op jit(solution)/shard_map/all_to_all | solution.py:336
  156.9 7.4 %collective-permute-done.32 = bf16[128,2048]{1,0:T(8,128)(2,1)S(1)} collective-permute-done((bf16[128,2048]{1,0:T(8,128)(2,1)}, bf16[128,2048]{1,0:T(8,128)(2,1)S(1)}, u32[]{:S(2)}, u32[]{:S(2)}) %collective-permute-start.32) | collective-permute-done | bytes 524320 | tf_op jit(solution)/shard_map/ppermute | solution.py:21
  165.8 5.5 %collective-permute-done.34 = bf16[128,2048]{1,0:T(8,128)(2,1)S(1)} collective-permute-done((bf16[128,2048]{1,0:T(8,128)(2,1)S(1)}, bf16[128,2048]{1,0:T(8,128)(2,1)S(1)}, u32[]{:S(2)}, u32[]{:S(2)}) %collective-permute-start.34) | collective-permute-done | bytes 524320 | tf_op jit(solution)/shard_map/ppermute | solution.py:21
  (64 shorter events, 19.8 us)
Async XLA Ops:
  1.8 14.8 %collective-permute-start.6 = (bf16[128,2176]{1,0:T(8,128)(2,1)S(1)}, bf16[128,2176]{1,0:T(8,128)(2,1)S(1)}, u32[]{:S(2)}, u32[]{:S(2)}) collective-permute-start(bf16[128,2176]{1,0:T(8,128)(2,1)S(1)} %get-tuple-element.74.refs_0_.refs_21_), channel_id=1, source_target_pairs={{0,3},{1,0},{2,1},{3,2},{4,7},{5,4},{6,5},{7,6},{8,11},{9,8},{10,9... | collective-permute-start | bytes 1671176 | tf_op jit(solution)/shard_map/ppermute | solution.py:21
  4.7 16.3 %collective-permute-start.4 = (bf16[128,2176]{1,0:T(8,128)(2,1)S(1)}, bf16[128,2176]{1,0:T(8,128)(2,1)S(1)}, u32[]{:S(2)}, u32[]{:S(2)}) collective-permute-start(bf16[128,2176]{1,0:T(8,128)(2,1)S(1)} %get-tuple-element.74.refs_0_.refs_21_), channel_id=1, source_target_pairs={{0,1},{1,2},{2,3},{3,0},{4,5},{5,6},{6,7},{7,4},{8,9},{9,10},{10,1... | collective-permute-start | bytes 1671176 | tf_op jit(solution)/shard_map/ppermute | solution.py:21
  4.8 17.1 %collective-permute-start.2 = (bf16[128,2176]{1,0:T(8,128)(2,1)S(1)}, bf16[128,2176]{1,0:T(8,128)(2,1)S(1)}, u32[]{:S(2)}, u32[]{:S(2)}) collective-permute-start(bf16[128,2176]{1,0:T(8,128)(2,1)S(1)} %get-tuple-element.69.refs_0_.refs_16_), channel_id=1, source_target_pairs={{0,12},{4,0},{8,4},{12,8},{1,13},{5,1},{9,5},{13,9},{2,14},{6,2},{... | collective-permute-start | bytes 1671176 | tf_op jit(solution)/shard_map/ppermute | solution.py:21
  8.8 17.8 %collective-permute-start = (bf16[128,2176]{1,0:T(8,128)(2,1)S(1)}, bf16[128,2176]{1,0:T(8,128)(2,1)S(1)}, u32[]{:S(2)}, u32[]{:S(2)}) collective-permute-start(bf16[128,2176]{1,0:T(8,128)(2,1)S(1)} %get-tuple-element.69.refs_0_.refs_16_), channel_id=1, source_target_pairs={{0,4},{4,8},{8,12},{12,0},{1,5},{5,9},{9,13},{13,1},{2,6},{6,10},{... | collective-permute-start | bytes 1671176 | tf_op jit(solution)/shard_map/ppermute | solution.py:21
  22.6 10.3 %collective-permute-start.3 = (bf16[64,2176]{1,0:T(8,128)(2,1)}, bf16[64,2176]{1,0:T(8,128)(2,1)}, u32[]{:S(2)}, u32[]{:S(2)}) collective-permute-start(bf16[64,2176]{1,0:T(8,128)(2,1)} %slice.17), channel_id=1, source_target_pairs={{0,12},{4,0},{8,4},{12,8},{1,13},{5,1},{9,5},{13,9},{2,14},{6,2},{... | collective-permute-start | bytes 835592 | tf_op jit(solution)/shard_map/ppermute | solution.py:21
  38.1 15.5 %collective-permute-start.8 = (bf16[4,32,2048]{2,1,0:T(8,128)(2,1)S(1)}, bf16[4,32,2048]{2,1,0:T(8,128)(2,1)S(1)}, u32[]{:S(2)}, u32[]{:S(2)}) collective-permute-start(bf16[4,32,2048]{2,1,0:T(8,128)(2,1)S(1)} %get-tuple-element.93), channel_id=1, source_target_pairs={{0,1},{1,2},{2,3},{3,0},{4,5},{5,6},{6,7},{7,4},{8,9},{9,10},{10,1... | collective-permute-start | bytes 1572872 | tf_op jit(solution)/shard_map/ppermute | solution.py:21
  38.2 29.3 %collective-permute-start.9 = (bf16[4,32,2048]{2,1,0:T(8,128)(2,1)S(1)}, bf16[4,32,2048]{2,1,0:T(8,128)(2,1)S(1)}, u32[]{:S(2)}, u32[]{:S(2)}) collective-permute-start(bf16[4,32,2048]{2,1,0:T(8,128)(2,1)S(1)} %get-tuple-element.94), channel_id=1, source_target_pairs={{0,2},{1,3},{2,0},{3,1},{4,6},{5,7},{6,4},{7,5},{8,10},{9,11},{10,... | collective-permute-start | bytes 1572872 | tf_op jit(solution)/shard_map/ppermute | solution.py:21
  42.6 25.0 %collective-permute-start.10 = (bf16[4,32,2048]{2,1,0:T(8,128)(2,1)S(1)}, bf16[4,32,2048]{2,1,0:T(8,128)(2,1)S(1)}, u32[]{:S(2)}, u32[]{:S(2)}) collective-permute-start(bf16[4,32,2048]{2,1,0:T(8,128)(2,1)S(1)} %get-tuple-element.95), channel_id=1, source_target_pairs={{0,3},{1,0},{2,1},{3,2},{4,7},{5,4},{6,5},{7,6},{8,11},{9,8},{10,9... | collective-permute-start | bytes 1572872 | tf_op jit(solution)/shard_map/ppermute | solution.py:21
  42.6 25.9 %collective-permute-start.11 = (bf16[4,32,2048]{2,1,0:T(8,128)(2,1)S(1)}, bf16[4,32,2048]{2,1,0:T(8,128)(2,1)S(1)}, u32[]{:S(2)}, u32[]{:S(2)}) collective-permute-start(bf16[4,32,2048]{2,1,0:T(8,128)(2,1)S(1)} %get-tuple-element.97), channel_id=1, source_target_pairs={{0,4},{4,8},{8,12},{12,0},{1,5},{5,9},{9,13},{13,1},{2,6},{6,10},{... | collective-permute-start | bytes 1572872 | tf_op jit(solution)/shard_map/ppermute | solution.py:21
  42.6 28.3 %collective-permute-start.12 = (bf16[4,32,2048]{2,1,0:T(8,128)(2,1)S(1)}, bf16[4,32,2048]{2,1,0:T(8,128)(2,1)S(1)}, u32[]{:S(2)}, u32[]{:S(2)}) collective-permute-start(bf16[4,32,2048]{2,1,0:T(8,128)(2,1)S(1)} %get-tuple-element.98), channel_id=1, source_target_pairs={{0,8},{4,12},{8,0},{12,4},{1,9},{5,13},{9,1},{13,5},{2,10},{6,14},... | collective-permute-start | bytes 1572872 | tf_op jit(solution)/shard_map/ppermute | solution.py:21
  53.6 17.3 %collective-permute-start.13 = (bf16[4,32,2048]{2,1,0:T(8,128)(2,1)S(1)}, bf16[4,32,2048]{2,1,0:T(8,128)(2,1)S(1)}, u32[]{:S(2)}, u32[]{:S(2)}) collective-permute-start(bf16[4,32,2048]{2,1,0:T(8,128)(2,1)S(1)} %get-tuple-element.99), channel_id=1, source_target_pairs={{0,12},{4,0},{8,4},{12,8},{1,13},{5,1},{9,5},{13,9},{2,14},{6,2},{... | collective-permute-start | bytes 1572872 | tf_op jit(solution)/shard_map/ppermute | solution.py:21
  67.5 19.1 %collective-permute-start.14 = (bf16[4,32,2048]{2,1,0:T(8,128)(2,1)S(1)}, bf16[4,32,2048]{2,1,0:T(8,128)(2,1)S(1)}, u32[]{:S(2)}, u32[]{:S(2)}) collective-permute-start(bf16[4,32,2048]{2,1,0:T(8,128)(2,1)S(1)} %get-tuple-element.103), channel_id=1, source_target_pairs={{0,1},{1,2},{2,3},{3,0},{4,5},{5,6},{6,7},{7,4},{8,9},{9,10},{10,1... | collective-permute-start | bytes 1572872 | tf_op jit(solution)/shard_map/ppermute | solution.py:21
  67.6 25.5 %collective-permute-start.15 = (bf16[4,32,2048]{2,1,0:T(8,128)(2,1)S(1)}, bf16[4,32,2048]{2,1,0:T(8,128)(2,1)S(1)}, u32[]{:S(2)}, u32[]{:S(2)}) collective-permute-start(bf16[4,32,2048]{2,1,0:T(8,128)(2,1)S(1)} %get-tuple-element.104), channel_id=1, source_target_pairs={{0,2},{1,3},{2,0},{3,1},{4,6},{5,7},{6,4},{7,5},{8,10},{9,11},{10,... | collective-permute-start | bytes 1572872 | tf_op jit(solution)/shard_map/ppermute | solution.py:21
  68.5 24.8 %collective-permute-start.16 = (bf16[4,32,2048]{2,1,0:T(8,128)(2,1)S(1)}, bf16[4,32,2048]{2,1,0:T(8,128)(2,1)S(1)}, u32[]{:S(2)}, u32[]{:S(2)}) collective-permute-start(bf16[4,32,2048]{2,1,0:T(8,128)(2,1)S(1)} %get-tuple-element.105), channel_id=1, source_target_pairs={{0,3},{1,0},{2,1},{3,2},{4,7},{5,4},{6,5},{7,6},{8,11},{9,8},{10,9... | collective-permute-start | bytes 1572872 | tf_op jit(solution)/shard_map/ppermute | solution.py:21
  70.9 24.4 %collective-permute-start.17 = (bf16[4,32,2048]{2,1,0:T(8,128)(2,1)S(1)}, bf16[4,32,2048]{2,1,0:T(8,128)(2,1)S(1)}, u32[]{:S(2)}, u32[]{:S(2)}) collective-permute-start(bf16[4,32,2048]{2,1,0:T(8,128)(2,1)S(1)} %get-tuple-element.107), channel_id=1, source_target_pairs={{0,4},{4,8},{8,12},{12,0},{1,5},{5,9},{9,13},{13,1},{2,6},{6,10},{... | collective-permute-start | bytes 1572872 | tf_op jit(solution)/shard_map/ppermute | solution.py:21
  70.9 24.6 %collective-permute-start.19 = (bf16[4,32,2048]{2,1,0:T(8,128)(2,1)S(1)}, bf16[4,32,2048]{2,1,0:T(8,128)(2,1)S(1)}, u32[]{:S(2)}, u32[]{:S(2)}) collective-permute-start(bf16[4,32,2048]{2,1,0:T(8,128)(2,1)S(1)} %get-tuple-element.109), channel_id=1, source_target_pairs={{0,12},{4,0},{8,4},{12,8},{1,13},{5,1},{9,5},{13,9},{2,14},{6,2},{... | collective-permute-start | bytes 1572872 | tf_op jit(solution)/shard_map/ppermute | solution.py:21
  86.6 11.8 %collective-permute-start.18 = (bf16[4,32,2048]{2,1,0:T(8,128)(2,1)S(1)}, bf16[4,32,2048]{2,1,0:T(8,128)(2,1)S(1)}, u32[]{:S(2)}, u32[]{:S(2)}) collective-permute-start(bf16[4,32,2048]{2,1,0:T(8,128)(2,1)S(1)} %get-tuple-element.108), channel_id=1, source_target_pairs={{0,8},{4,12},{8,0},{12,4},{1,9},{5,13},{9,1},{13,5},{2,10},{6,14},... | collective-permute-start | bytes 1572872 | tf_op jit(solution)/shard_map/ppermute | solution.py:21
  93.2 15.7 %collective-permute-start.20 = (bf16[4,32,2048]{2,1,0:T(8,128)(2,1)S(1)}, bf16[4,32,2048]{2,1,0:T(8,128)(2,1)S(1)}, u32[]{:S(2)}, u32[]{:S(2)}) collective-permute-start(bf16[4,32,2048]{2,1,0:T(8,128)(2,1)S(1)} %get-tuple-element.110), channel_id=1, source_target_pairs={{0,3},{1,0},{2,1},{3,2},{4,7},{5,4},{6,5},{7,6},{8,11},{9,8},{10,9... | collective-permute-start | bytes 1572872 | tf_op jit(solution)/shard_map/ppermute | solution.py:21
  93.2 17.0 %collective-permute-start.21 = (bf16[4,32,2048]{2,1,0:T(8,128)(2,1)S(1)}, bf16[4,32,2048]{2,1,0:T(8,128)(2,1)S(1)}, u32[]{:S(2)}, u32[]{:S(2)}) collective-permute-start(bf16[4,32,2048]{2,1,0:T(8,128)(2,1)S(1)} %get-tuple-element.111), channel_id=1, source_target_pairs={{0,1},{1,2},{2,3},{3,0},{4,5},{5,6},{6,7},{7,4},{8,9},{9,10},{10,1... | collective-permute-start | bytes 1572872 | tf_op jit(solution)/shard_map/ppermute | solution.py:21
  95.3 24.2 %collective-permute-start.22 = (bf16[4,32,2048]{2,1,0:T(8,128)(2,1)S(1)}, bf16[4,32,2048]{2,1,0:T(8,128)(2,1)S(1)}, u32[]{:S(2)}, u32[]{:S(2)}) collective-permute-start(bf16[4,32,2048]{2,1,0:T(8,128)(2,1)S(1)} %get-tuple-element.113), channel_id=1, source_target_pairs={{0,2},{1,3},{2,0},{3,1},{4,6},{5,7},{6,4},{7,5},{8,10},{9,11},{10,... | collective-permute-start | bytes 1572872 | tf_op jit(solution)/shard_map/ppermute | solution.py:21
  95.5 25.4 %collective-permute-start.26 = (bf16[4,32,2048]{2,1,0:T(8,128)(2,1)S(1)}, bf16[4,32,2048]{2,1,0:T(8,128)(2,1)S(1)}, u32[]{:S(2)}, u32[]{:S(2)}) collective-permute-start(bf16[4,32,2048]{2,1,0:T(8,128)(2,1)S(1)} %get-tuple-element.121), channel_id=1, source_target_pairs={{0,12},{4,0},{8,4},{12,8},{1,13},{5,1},{9,5},{13,9},{2,14},{6,2},{... | collective-permute-start | bytes 1572872 | tf_op jit(solution)/shard_map/ppermute | solution.py:21
  98.4 23.2 %collective-permute-start.27 = (bf16[4,32,2048]{2,1,0:T(8,128)(2,1)S(1)}, bf16[4,32,2048]{2,1,0:T(8,128)(2,1)S(1)}, u32[]{:S(2)}, u32[]{:S(2)}) collective-permute-start(bf16[4,32,2048]{2,1,0:T(8,128)(2,1)S(1)} %get-tuple-element.122), channel_id=1, source_target_pairs={{0,8},{4,12},{8,0},{12,4},{1,9},{5,13},{9,1},{13,5},{2,10},{6,14},... | collective-permute-start | bytes 1572872 | tf_op jit(solution)/shard_map/ppermute | solution.py:21
  108.9 16.0 %collective-permute-start.28 = (bf16[4,32,2048]{2,1,0:T(8,128)(2,1)S(1)}, bf16[4,32,2048]{2,1,0:T(8,128)(2,1)S(1)}, u32[]{:S(2)}, u32[]{:S(2)}) collective-permute-start(bf16[4,32,2048]{2,1,0:T(8,128)(2,1)S(1)} %get-tuple-element.123), channel_id=1, source_target_pairs={{0,4},{4,8},{8,12},{12,0},{1,5},{5,9},{9,13},{13,1},{2,6},{6,10},{... | collective-permute-start | bytes 1572872 | tf_op jit(solution)/shard_map/ppermute | solution.py:21
  116.8 17.8 %collective-permute-start.23 = (bf16[4,32,2048]{2,1,0:T(8,128)(2,1)S(1)}, bf16[4,32,2048]{2,1,0:T(8,128)(2,1)S(1)}, u32[]{:S(2)}, u32[]{:S(2)}) collective-permute-start(bf16[4,32,2048]{2,1,0:T(8,128)(2,1)S(1)} %get-tuple-element.117), channel_id=1, source_target_pairs={{0,3},{1,0},{2,1},{3,2},{4,7},{5,4},{6,5},{7,6},{8,11},{9,8},{10,9... | collective-permute-start | bytes 1572872 | tf_op jit(solution)/shard_map/ppermute | solution.py:21
  119.4 15.3 %collective-permute-start.24 = (bf16[4,32,2048]{2,1,0:T(8,128)(2,1)S(1)}, bf16[4,32,2048]{2,1,0:T(8,128)(2,1)S(1)}, u32[]{:S(2)}, u32[]{:S(2)}) collective-permute-start(bf16[4,32,2048]{2,1,0:T(8,128)(2,1)S(1)} %get-tuple-element.118), channel_id=1, source_target_pairs={{0,2},{1,3},{2,0},{3,1},{4,6},{5,7},{6,4},{7,5},{8,10},{9,11},{10,... | collective-permute-start | bytes 1572872 | tf_op jit(solution)/shard_map/ppermute | solution.py:21
  120.9 17.1 %collective-permute-start.25 = (bf16[4,32,2048]{2,1,0:T(8,128)(2,1)S(1)}, bf16[4,32,2048]{2,1,0:T(8,128)(2,1)S(1)}, u32[]{:S(2)}, u32[]{:S(2)}) collective-permute-start(bf16[4,32,2048]{2,1,0:T(8,128)(2,1)S(1)} %get-tuple-element.119), channel_id=1, source_target_pairs={{0,1},{1,2},{2,3},{3,0},{4,5},{5,6},{6,7},{7,4},{8,9},{9,10},{10,1... | collective-permute-start | bytes 1572872 | tf_op jit(solution)/shard_map/ppermute | solution.py:21
  121.6 17.7 %collective-permute-start.29 = (bf16[4,32,2048]{2,1,0:T(8,128)(2,1)S(1)}, bf16[4,32,2048]{2,1,0:T(8,128)(2,1)S(1)}, u32[]{:S(2)}, u32[]{:S(2)}) collective-permute-start(bf16[4,32,2048]{2,1,0:T(8,128)(2,1)S(1)} %get-tuple-element.125), channel_id=1, source_target_pairs={{0,12},{4,0},{8,4},{12,8},{1,13},{5,1},{9,5},{13,9},{2,14},{6,2},{... | collective-permute-start | bytes 1572872 | tf_op jit(solution)/shard_map/ppermute | solution.py:21
  124.9 14.5 %collective-permute-start.30 = (bf16[4,32,2048]{2,1,0:T(8,128)(2,1)S(1)}, bf16[4,32,2048]{2,1,0:T(8,128)(2,1)S(1)}, u32[]{:S(2)}, u32[]{:S(2)}) collective-permute-start(bf16[4,32,2048]{2,1,0:T(8,128)(2,1)S(1)} %get-tuple-element.126), channel_id=1, source_target_pairs={{0,8},{4,12},{8,0},{12,4},{1,9},{5,13},{9,1},{13,5},{2,10},{6,14},... | collective-permute-start | bytes 1572872 | tf_op jit(solution)/shard_map/ppermute | solution.py:21
  134.6 10.4 %collective-permute-start.31 = (bf16[4,32,2048]{2,1,0:T(8,128)(2,1)S(1)}, bf16[4,32,2048]{2,1,0:T(8,128)(2,1)S(1)}, u32[]{:S(2)}, u32[]{:S(2)}) collective-permute-start(bf16[4,32,2048]{2,1,0:T(8,128)(2,1)S(1)} %get-tuple-element.127), channel_id=1, source_target_pairs={{0,4},{4,8},{8,12},{12,0},{1,5},{5,9},{9,13},{13,1},{2,6},{6,10},{... | collective-permute-start | bytes 1572872 | tf_op jit(solution)/shard_map/ppermute | solution.py:21
  149.8 21.9 %all-to-all-start = ((bf16[4,128,2048]{2,1,0:T(8,128)(2,1)}), bf16[4,128,2048]{2,1,0:T(8,128)(2,1)S(1)}, u32[]{:S(2)}, u32[]{:S(2)}) async-start(bf16[4,128,2048]{2,1,0:T(8,128)(2,1)} %get-tuple-element.132), calls=%async_computation | async-start | bytes 4194304 | tf_op jit(solution)/shard_map/all_to_all | solution.py:336
  154.8 11.0 %collective-permute-start.33 = (bf16[128,2048]{1,0:T(8,128)(2,1)}, bf16[128,2048]{1,0:T(8,128)(2,1)S(1)}, u32[]{:S(2)}, u32[]{:S(2)}) collective-permute-start(bf16[128,2048]{1,0:T(8,128)(2,1)} %get-tuple-element.130), channel_id=1, source_target_pairs={{0,8},{4,12},{8,0},{12,4},{1,9},{5,13},{9,1},{13,5},{2,10},{6,14},... | collective-permute-start | bytes 1572872 | tf_op jit(solution)/shard_map/ppermute | solution.py:21
  156.7 14.7 %collective-permute-start.34 = (bf16[128,2048]{1,0:T(8,128)(2,1)S(1)}, bf16[128,2048]{1,0:T(8,128)(2,1)S(1)}, u32[]{:S(2)}, u32[]{:S(2)}) collective-permute-start(bf16[128,2048]{1,0:T(8,128)(2,1)S(1)} %copy-done.1), channel_id=1, source_target_pairs={{0,4},{4,8},{8,12},{12,0},{1,5},{5,9},{9,13},{13,1},{2,6},{6,10},{... | collective-permute-start | bytes 1572872 | tf_op jit(solution)/shard_map/ppermute | solution.py:21
  (6 other events, 65.1 us)
